TPU v7x, 32 devices: a whole 2x2x4 slice. The times are simulated.
32 devices in a mesh: layer: 8 (over y, x, core), latent: 4 (over z).
Axes of the slice: x: 2, y: 2, z: 4, core: 2. Of those that a mesh axis runs over, the one named last changes fastest.
Arguments:
- layer_input: bfloat16 [8, 1024, 4096], P('layer', None, 'latent'), may hold values from -6 to 6
- enc_weight: bfloat16 [8, 4096, 512], P('layer', None, 'latent'), may hold values from -0.09375 to 0.09375
- enc_bias: float32 [8, 512], P('layer', 'latent'), may hold values from -3 to 3
- dec_weight: bfloat16 [8, 3, 512, 4096], P('layer', None, None, 'latent'), may hold values from -0.5 to 0.5
- block_lists: int32 [8, 16, 2], P('layer'), may hold values from 0 to 3, as said below
- block_counts: int32 [8, 16], P('layer'), may hold values from 1 to 2, as said below
Outputs:
- rebuilt: bfloat16 [8, 1024, 4096], P('layer', None, 'latent')
Inputs may be any that keep to these rules, and one draw needn't show every extreme that they name: `block_lists`: each list holds distinct block ids of one layer. `block_counts`: some entry equals 2 in every draw.
All inputs are finite; a program needn't handle non-finite values.
Results may differ from a plain program's by a relative error of at most 0.0055.
Values may be sent and summed in bfloat16 or wider, within the bound.
No kernel may reach another device: no remote copies, remote signals or barrier semaphores. Data moves between devices by JAX's collectives and lax.ppermute only.
A program may use at most 128 MiB of HBM per device.

v0:
```python
import jax
import jax.numpy as jnp
from jax import lax
from jax.sharding import PartitionSpec as P


def passed_along(value, axis, steps):
    count = lax.axis_size(axis)
    initial, last = (max(0, -steps), min(count, count - steps))
    return lax.ppermute(value, axis, [(source, source + steps) for source in range(initial, last)])


def shards(layer_input, enc_weight, enc_bias, dec_weight, block_lists, block_counts):
    encoder = enc_weight[0]
    tokens = layer_input.shape[1]
    block_width = encoder.shape[1]
    weight_rows = encoder
    preact = jnp.dot(
        lax.all_gather(layer_input, "latent", axis=2, tiled=True)[0],
        weight_rows,
        preferred_element_type=jnp.float32,
    )
    preact = preact + enc_bias[0][None, :]
    own_block = lax.axis_index("latent")
    active_ids = block_lists[0]
    counts = block_counts[0]
    slot_ids = jnp.arange(active_ids.shape[1])
    in_count = slot_ids[None, :] < counts[:, None]
    matched = (active_ids == own_block) & in_count
    tile_hit = jnp.any(matched, axis=1).astype(jnp.float32)
    tile_count = active_ids.shape[0]
    latent_act = (
        (
            jnp.maximum(preact, 0.0).reshape(tile_count, tokens // tile_count, block_width)
            * tile_hit[:, None, None]
        )
        .reshape(tokens, block_width)
        .astype(jnp.bfloat16)
    )
    decoder = dec_weight[0]
    targets = decoder.shape[0]
    weight_rows = decoder
    partials = jnp.einsum(
        "tk,skd->std",
        lax.all_gather(latent_act, "latent", axis=1, tiled=True),
        weight_rows,
        preferred_element_type=jnp.float32,
    )
    rebuilt = partials[0]
    for offset in range(1, targets):
        arrived = passed_along(partials[offset].astype(jnp.bfloat16), "layer", offset)
        rebuilt = rebuilt + arrived.astype(jnp.float32)
    return rebuilt.astype(jnp.bfloat16)[None]


def solution(mesh):
    placed = (
        P("layer", None, "latent"),
        P("layer", None, "latent"),
        P("layer", "latent"),
        P("layer", None, None, "latent"),
        P("layer", None, None),
        P("layer", None),
    )
    return jax.shard_map(
        shards, mesh=mesh, in_specs=placed, out_specs=P("layer", None, "latent"), check_vma=False
    )
```

profile of v0, /device:TPU:5, one launch (start us, length us, event | category | flops | bytes accessed | tf_op | source)
XLA Modules:
  0.0 281.8 jit_solution(6330996128933816814)
XLA Ops:
  6.5 0.0 copy-start
  6.5 0.0 all-gather.3.cloned.1.call-start
  6.5 0.7 all-gather.3.cloned.1.call-update
  7.3 0.0 all-gather.5.cloned.1.call-start
  7.3 0.9 fusion.21
  8.2 0.1 mul.13
  8.3 0.1 mul.14
  8.3 151.7 %all-gather.3.cloned.1.call-done = bf16[1,1024,4096]{2,1,0:T(8,128)(2,1)} async-done(((bf16[1,1024,1024]{2,1,0:T(8,128)(2,1)}), bf16[1,1024,4096]{2,1,0:T(8,128)(2,1)}) %all-gather.3.cloned.1.call-update) | async-done | bytes 8388624 | tf_op jit(solution)/shard_map/all_gather | solution.py:19
  160.0 6.8 %fusion.16 = bf16[1024,128]{1,0:T(8,128)(2,1)} fusion(bf16[1,1024,4096]{2,1,0:T(8,128)(2,1)} %all-gather.3.cloned.1.call-done, bf16[1,4096,128]{2,1,0:T(8,128)(2,1)} %param.7, f32[1024]{0:T(1024)S(1)} %mul.14, f32[128]{0:T(128)} %bitcast.49), kind=kOutput, calls=%fused_computation.14 | convolution fusion | flops 1074266112 | bytes 9703936 | tf_op jit(solution)/shard_map/dot_general | solution.py:18
  166.8 0.0 all-gather.5.cloned.1.call-update
  166.8 27.5 %all-gather.5.cloned.1.call-done = bf16[1024,512]{1,0:T(8,128)(2,1)} async-done(((bf16[1024,128]{1,0:T(8,128)(2,1)}), bf16[1024,512]{1,0:T(8,128)(2,1)}) %all-gather.5.cloned.1.call-update) | async-done | bytes 1048592 | tf_op jit(solution)/shard_map/all_gather | solution.py:45
  194.3 0.0 copy-done
  194.3 4.6 %fusion.22 = (bf16[3,1024,1024]{2,1,0:T(8,128)(2,1)S(1)}, f32[3,1024,1024]{2,1,0:T(8,128)S(1)}) fusion(bf16[1,3,512,1024]{3,2,1,0:T(8,128)(2,1)S(1)} %copy-done, bf16[1024,512]{1,0:T(8,128)(2,1)} %all-gather.5.cloned.1.call-done), kind=kOutput, calls=%fused_computation.19 | convolution fusion | flops 3224371200 | bytes 23068672 | tf_op jit(solution)/shard_map/tk,skd->std/dot_general | solution.py:43
  199.0 0.4 slice_bitcast_fusion.2
  199.5 3.4 %collective-permute-start = (bf16[1024,1024]{1,0:T(8,128)(2,1)S(1)}, bf16[1024,1024]{1,0:T(8,128)(2,1)S(1)}, u32[]{:S(2)}, u32[]{:S(2)}) collective-permute-start(bf16[1024,1024]{1,0:T(8,128)(2,1)S(1)} %get-tuple-element.5), channel_id=1, source_target_pairs={{0,4},{4,8},{8,12},{12,16},{16,20},{20,24},{24,28},{1,5},{5,9},{9,... | collective-permute-start | bytes 6291464 | tf_op jit(solution)/shard_map/ppermute | solution.py:10
  202.9 1.9 collective-permute-start.1
  204.8 40.9 %collective-permute-done = bf16[1024,1024]{1,0:T(8,128)(2,1)S(1)} collective-permute-done((bf16[1024,1024]{1,0:T(8,128)(2,1)S(1)}, bf16[1024,1024]{1,0:T(8,128)(2,1)S(1)}, u32[]{:S(2)}, u32[]{:S(2)}) %collective-permute-start) | collective-permute-done | bytes 2097184 | tf_op jit(solution)/shard_map/ppermute | solution.py:10
  245.7 26.7 %collective-permute-done.1 = bf16[1024,1024]{1,0:T(8,128)(2,1)S(1)} collective-permute-done((bf16[1024,1024]{1,0:T(8,128)(2,1)S(1)}, bf16[1024,1024]{1,0:T(8,128)(2,1)S(1)}, u32[]{:S(2)}, u32[]{:S(2)}) %collective-permute-start.1) | collective-permute-done | bytes 2097184 | tf_op jit(solution)/shard_map/ppermute | solution.py:10
  272.4 2.5 fusion.6
  (1 shorter events, 0.0 us)
Async XLA Ops:
  6.5 187.8 %copy-start = (bf16[1,3,512,1024]{3,2,1,0:T(8,128)(2,1)S(1)}, bf16[1,3,512,1024]{3,2,1,0:T(8,128)(2,1)}, u32[]{:S(2)}) copy-start(bf16[1,3,512,1024]{3,2,1,0:T(8,128)(2,1)} %param.9) | copy-start | bytes 9437188
  6.5 153.5 %all-gather.3.cloned.1.call-start = ((), (), s32[]{:S(2)}) async-start(), calls=%async_computation | async-start | bytes 10485760 | tf_op jit(solution)/shard_map/all_gather | solution.py:19
  7.3 187.1 %all-gather.5.cloned.1.call-start = ((), (), s32[]{:S(2)}) async-start(), calls=%async_computation.1 | async-start | bytes 1310720 | tf_op jit(solution)/shard_map/all_gather | solution.py:45
  199.5 46.3 %collective-permute-start = (bf16[1024,1024]{1,0:T(8,128)(2,1)S(1)}, bf16[1024,1024]{1,0:T(8,128)(2,1)S(1)}, u32[]{:S(2)}, u32[]{:S(2)}) collective-permute-start(bf16[1024,1024]{1,0:T(8,128)(2,1)S(1)} %get-tuple-element.5), channel_id=1, source_target_pairs={{0,4},{4,8},{8,12},{12,16},{16,20},{20,24},{24,28},{1,5},{5,9},{9,... | collective-permute-start | bytes 6291464 | tf_op jit(solution)/shard_map/ppermute | solution.py:10
  202.9 69.5 %collective-permute-start.1 = (bf16[1024,1024]{1,0:T(8,128)(2,1)S(1)}, bf16[1024,1024]{1,0:T(8,128)(2,1)S(1)}, u32[]{:S(2)}, u32[]{:S(2)}) collective-permute-start(bf16[1024,1024]{1,0:T(8,128)(2,1)S(1)} %get-tuple-element.6), channel_id=1, source_target_pairs={{0,8},{4,12},{8,16},{12,20},{16,24},{20,28},{1,9},{5,13},{9,17},{1... | collective-permute-start | bytes 6291464 | tf_op jit(solution)/shard_map/ppermute | solution.py:10
Sparse Core Ops, SparseCore 0:
  8.9 151.0 all-gather.2
  166.9 27.3 all-gather.4
where the time goes:
time: 282 us
  waiting for transfers between devices  248 us (88%)
  between operations  13.4 us (5%)
  matrix products  11.4 us (4%)
  starting transfers between devices  5.4 us (2%)
  other arithmetic  3.42 us (1%)
    all_gather x1, waiting for transfers between devices, shards(): lax.all_gather(layer_input, 'latent', axis=2, tiled=True)[0]  152 us
    ppermute x2, waiting for transfers between devices, passed_along(): lax.ppermute(value, axis, [(source, source + steps) for source in range(i...  67.6 us
    all_gather x1, waiting for transfers between devices, shards(): lax.all_gather(latent_act, 'latent', axis=1, tiled=True)  27.5 us
    dot_general x1, matrix products, shards(): jnp.dot(lax.all_gather(layer_input, 'latent', axis=2, tiled=True)[0], wei...  6.78 us
  transfers between devices with their start and end apart: 4, of which 4 were waited for; matrix products, arithmetic and copies ran while one was open for 0% of the time, Pallas kernels for 0%

commit v1 on v0

v1 whole, which is shorter than its diff:
```python
import functools

import jax
import jax.numpy as jnp
from jax import lax
from jax.experimental import pallas as pl
from jax.experimental.pallas import tpu as pltpu
from jax.sharding import PartitionSpec as P

VMEM = pl.BlockSpec(memory_space=pltpu.VMEM)
SMEM = pl.BlockSpec(memory_space=pltpu.SMEM)


def rotated(value, steps):
    count = lax.axis_size("latent")
    return lax.ppermute(value, "latent", [(i, (i + steps) % count) for i in range(count)])


def passed_along(value, steps):
    count = lax.axis_size("layer")
    return lax.ppermute(value, "layer", [(i, i + steps) for i in range(count - steps)])


def encode_kernel(parts, place_ref, relative_ref, bias_ref, x_ref, *refs):
    weight_refs, refs = refs[:parts], refs[parts:]
    out_refs, (wide, partial) = refs[:parts], refs[parts:]
    width = bias_ref.shape[1]
    tiles, slots, rows, _ = out_refs[0].shape
    group_rows = tiles * rows
    for source in range(parts):
        wide[:, source * width : (source + 1) * width] = weight_refs[source][...]
    for step in range(parts):
        group = lax.rem(place_ref[0] + step, parts)
        first = pl.multiple_of(group * group_rows, group_rows)
        product = jnp.dot(x_ref[pl.ds(first, group_rows), :], wide[...], preferred_element_type=jnp.float32)
        for source in range(parts):
            block = product[:, source * width : (source + 1) * width]
            partial[source] = block + bias_ref[...] if source == 0 else block
        for tile in range(tiles):
            for slot in range(slots):
                source = relative_ref[group * tiles + tile, slot]
                kept = partial[source, tile * rows : (tile + 1) * rows, :]
                out_refs[step][tile, slot] = kept.astype(out_refs[step].dtype)


def encode(place, relative, bias, x, weights, tiles):
    parts = len(weights)
    tokens, depth = x.shape
    width = bias.shape[1]
    shape = (tiles // parts, relative.shape[1], tokens // tiles, width)
    return pl.pallas_call(
        functools.partial(encode_kernel, parts),
        out_shape=[jax.ShapeDtypeStruct(shape, jnp.bfloat16 if step else jnp.float32) for step in range(parts)],
        in_specs=[SMEM, SMEM] + [VMEM] * (2 + parts),
        out_specs=[VMEM] * parts,
        scratch_shapes=[
            pltpu.VMEM((depth, parts * width), jnp.bfloat16),
            pltpu.VMEM((parts, tokens // parts, width), jnp.float32),
        ],
        compiler_params=pltpu.CompilerParams(vmem_limit_bytes=40 << 20),
        cost_estimate=pl.CostEstimate(
            flops=2 * tokens * depth * parts * width,
            bytes_accessed=2 * (tokens * depth + depth * parts * width),
            transcendentals=0,
        ),
        name="encode",
    )(place, relative, bias, x, *weights)


def decode_kernel(parts, targets, place_ref, lists_ref, *refs):
    act_refs, refs = refs[: parts * targets], refs[parts * targets :]
    decoder_refs, (out_ref, dense) = refs[:targets], refs[targets:]
    tiles, slots, rows, width = act_refs[0].shape
    step = pl.program_id(0)
    group = lax.rem(place_ref[0] - step + parts, parts)
    dense[...] = jnp.zeros_like(dense)
    for origin in range(parts):

        @pl.when(step == origin)
        def _():
            for offset in range(targets):
                for tile in range(tiles):
                    for slot in range(slots):
                        block = lists_ref[offset, group * tiles + tile, slot]
                        lanes = pl.ds(pl.multiple_of(block * width, width), width)
                        dense[offset, tile * rows : (tile + 1) * rows, lanes] = act_refs[offset * parts + origin][tile, slot]

    total = jnp.dot(dense[0], decoder_refs[0][...], preferred_element_type=jnp.float32)
    for offset in range(1, targets):
        total = total + jnp.dot(dense[offset], decoder_refs[offset][...], preferred_element_type=jnp.float32)
    out_ref[...] = total.astype(out_ref.dtype)


def decode(place, lists, acts, decoders, tokens):
    targets, parts = len(acts), len(acts[0])
    latents, features = decoders[0].shape
    group_rows = tokens // parts
    return pl.pallas_call(
        functools.partial(decode_kernel, parts, targets),
        grid_spec=pltpu.PrefetchScalarGridSpec(
            num_scalar_prefetch=2,
            grid=(parts,),
            in_specs=[VMEM] * (targets * parts + targets),
            out_specs=pl.BlockSpec(
                (group_rows, features),
                lambda step, place_ref, lists_ref: (lax.rem(place_ref[0] - step + parts, parts), 0),
            ),
            scratch_shapes=[pltpu.VMEM((targets, group_rows, latents), jnp.bfloat16)],
        ),
        out_shape=jax.ShapeDtypeStruct((tokens, features), jnp.bfloat16),
        compiler_params=pltpu.CompilerParams(vmem_limit_bytes=40 << 20),
        cost_estimate=pl.CostEstimate(
            flops=2 * tokens * latents * features * targets,
            bytes_accessed=2 * (targets * latents * features + 2 * tokens * features),
            transcendentals=0,
        ),
        name="decode",
    )(place, lists, *[part for act in acts for part in act], *decoders)


def shards(layer_input, enc_weight, enc_bias, dec_weight, block_lists, block_counts):
    parts = lax.axis_size("latent")
    place = lax.axis_index("latent")
    x, encoder, decoder = layer_input[0], enc_weight[0], dec_weight[0]
    lists, counts = block_lists[0], block_counts[0]
    tokens, depth = x.shape
    tiles, slots = lists.shape
    targets = decoder.shape[0]

    with jax.named_scope("encoder_rows"):
        pieces = [
            lax.dynamic_slice_in_dim(encoder, lax.rem(place + step, parts) * depth, depth) for step in range(parts)
        ]
        weights = [pieces[0]] + [rotated(pieces[step], step) for step in range(1, parts)]
    with jax.named_scope("decoder_weights"):
        decoders = [decoder[0]] + [passed_along(decoder[offset], offset) for offset in range(1, targets)]
        all_lists = jnp.stack([lists] + [passed_along(lists, offset) for offset in range(1, targets)])

    with jax.named_scope("encode"):
        where = place.astype(jnp.int32)[None]
        relative = lax.rem(place - lists + parts, parts)
        partials = encode(where, relative, enc_bias, x, weights, tiles)
        arrived = [rotated(partials[step], step) for step in range(1, parts)]
    with jax.named_scope("activate"):
        preact = partials[0]
        for term in arrived:
            preact = preact + term.astype(jnp.float32)
        own_counts = lax.dynamic_slice_in_dim(counts, place * (tiles // parts), tiles // parts)
        live = (jnp.arange(slots)[None, :] < own_counts[:, None]).astype(jnp.float32)
        act = (jnp.maximum(preact, 0.0) * live[:, :, None, None]).astype(jnp.bfloat16)
    with jax.named_scope("spread"):
        acts = [[act] + [rotated(act, step) for step in range(1, parts)]]
        for offset in range(1, targets):
            acts.append([passed_along(part, offset) for part in acts[0]])
    with jax.named_scope("decode"):
        return decode(where, all_lists, acts, decoders, tokens)[None]


def solution(mesh):
    placed = (
        P("layer", None, "latent"),
        P("layer", None, "latent"),
        P("layer", "latent"),
        P("layer", None, None, "latent"),
        P("layer", None, None),
        P("layer", None),
    )
    return jax.shard_map(
        shards, mesh=mesh, in_specs=placed, out_specs=P("layer", None, "latent"), check_vma=False
    )
```

time: 282 us -> 100 us (0.35)
  the two profiles are of different devices: /device:TPU:5 before, /device:TPU:4 now
where the time goes in v1:
time: 100 us; the launch traced here: 99.8 us
  waiting for transfers between devices  44.6 us (45%)
  starting transfers between devices  38.3 us (38%)
  Pallas kernels  10.6 us (11%)
  local copies, waits for them, and re-layouts  5.92 us (6%)
    ppermute x9, waiting for transfers between devices, rotated(): lax.ppermute(value, 'latent', [(i, (i + steps) % count) for i in range(co...  27.9 us
    ppermute x12, starting transfers between devices, passed_along(): lax.ppermute(value, 'layer', [(i, i + steps) for i in range(count - steps)])  25.9 us
    ppermute x12, waiting for transfers between devices, passed_along(): lax.ppermute(value, 'layer', [(i, i + steps) for i in range(count - steps)])  16.8 us
    ppermute x9, starting transfers between devices, rotated(): lax.ppermute(value, 'latent', [(i, (i + steps) % count) for i in range(co...  12.3 us
    pallas_call x1, Pallas kernels, decode(): pl.pallas_call(functools.partial(decode_kernel, parts, targets), grid_spe...  8.04 us
    squeeze x1, local copies, waits for them, and re-layouts, shards(): decoder[offset]  3.5 us
    pallas_call x1, Pallas kernels, encode(): pl.pallas_call(functools.partial(encode_kernel, parts), out_shape=[jax.Sh...  2.53 us
    dynamic_slice x1, local copies, waits for them, and re-layouts, shards(): lax.dynamic_slice_in_dim(encoder, lax.rem(place + step, parts) * depth, d...  2.16 us
  transfers between devices with their start and end apart: 21, of which 12 were waited for; matrix products, arithmetic and copies ran while one was open for 4% of the time, Pallas kernels for 3%

profile of v1, /device:TPU:4, one launch (start us, length us, event | category | flops | bytes accessed | tf_op | source)
XLA Modules:
  0.0 99.8 jit_solution(11117046537162576308)
XLA Ops:
  0.0 2.2 %dynamic-slice_bitcast_fusion = (bf16[1024,128]{1,0:T(8,128)(2,1)}, bf16[1024,128]{1,0:T(8,128)(2,1)}, bf16[1024,128]{1,0:T(8,128)(2,1)S(1)}, bf16[1024,128]{1,0:T(8,128)(2,1)}) fusion(bf16[1,4096,128]{2,1,0:T(8,128)(2,1)} %param.7, s32[]{:T(128)S(6)} %select_n.18, s32[]{:T(128)S(6)} %select_n.16, s32[]{:T(128)S(6)} %select_n.15, s32[]{:T(128)S(6)} %select_n.17), kind=kLoop, calls=%fused_computation.4 | loop fusion | bytes 2097168 | tf_op jit(solution)/shard_map/encoder_rows/dynamic_slice | solution.py:132
  2.2 3.6 %collective-permute-start.4 = (bf16[1024,128]{1,0:T(8,128)(2,1)}, bf16[1024,128]{1,0:T(8,128)(2,1)}, u32[]{:S(2)}, u32[]{:S(2)}) collective-permute-start(bf16[1024,128]{1,0:T(8,128)(2,1)} %get-tuple-element.16), channel_id=1, source_target_pairs={{0,3},{1,0},{2,1},{3,2},{4,7},{5,4},{6,5},{7,6},{8,11},{9,8},{10,9... | collective-permute-start | bytes 786440 | tf_op jit(solution)/shard_map/encoder_rows/ppermute | solution.py:16
  5.8 0.0 collective-permute-start.2
  5.8 1.0 %collective-permute-start.3 = (bf16[1024,128]{1,0:T(8,128)(2,1)}, bf16[1024,128]{1,0:T(8,128)(2,1)}, u32[]{:S(2)}, u32[]{:S(2)}) collective-permute-start(bf16[1024,128]{1,0:T(8,128)(2,1)} %get-tuple-element.19), channel_id=1, source_target_pairs={{0,2},{1,3},{2,0},{3,1},{4,6},{5,7},{6,4},{7,5},{8,10},{9,11},{10,... | collective-permute-start | bytes 786440 | tf_op jit(solution)/shard_map/encoder_rows/ppermute | solution.py:16
  6.8 3.5 %slice_bitcast_fusion = (bf16[512,1024]{1,0:T(8,128)(2,1)}, bf16[512,1024]{1,0:T(8,128)(2,1)S(1)}, bf16[512,1024]{1,0:T(8,128)(2,1)}) fusion(bf16[1,3,512,1024]{3,2,1,0:T(8,128)(2,1)} %param.9), kind=kLoop, calls=%fused_computation | loop fusion | bytes 6291456 | tf_op jit(solution)/shard_map/decoder_weights/squeeze | solution.py:136
  10.3 3.4 %collective-permute-start.20 = (bf16[512,1024]{1,0:T(8,128)(2,1)}, bf16[512,1024]{1,0:T(8,128)(2,1)}, u32[]{:S(2)}, u32[]{:S(2)}) collective-permute-start(bf16[512,1024]{1,0:T(8,128)(2,1)} %get-tuple-element.13), channel_id=1, source_target_pairs={{0,8},{4,12},{8,16},{12,20},{16,24},{20,28},{1,9},{5,13},{9,17},{1... | collective-permute-start | bytes 3145736 | tf_op jit(solution)/shard_map/decoder_weights/ppermute | solution.py:21
  13.7 1.9 %collective-permute-start.19 = (bf16[512,1024]{1,0:T(8,128)(2,1)}, bf16[512,1024]{1,0:T(8,128)(2,1)}, u32[]{:S(2)}, u32[]{:S(2)}) collective-permute-start(bf16[512,1024]{1,0:T(8,128)(2,1)} %get-tuple-element.15), channel_id=1, source_target_pairs={{0,4},{4,8},{8,12},{12,16},{16,20},{20,24},{24,28},{1,5},{5,9},{9,... | collective-permute-start | bytes 3145736 | tf_op jit(solution)/shard_map/decoder_weights/ppermute | solution.py:21
  15.6 0.1 fusion.2
  15.7 0.1 copy.11
  15.8 0.0 collective-permute-done.4.refs_3_
  15.8 3.6 %collective-permute-done.2.refs_1_ = bf16[1024,128]{1,0:T(8,128)(2,1)} collective-permute-done((bf16[1024,128]{1,0:T(8,128)(2,1)}, bf16[1024,128]{1,0:T(8,128)(2,1)}, u32[]{:S(2)}, u32[]{:S(2)}) %collective-permute-start.2) | collective-permute-done | bytes 262176 | tf_op jit(solution)/shard_map/encoder_rows/ppermute | solution.py:16
  19.4 9.0 %collective-permute-done.3.refs_2_ = bf16[1024,128]{1,0:T(8,128)(2,1)} collective-permute-done((bf16[1024,128]{1,0:T(8,128)(2,1)}, bf16[1024,128]{1,0:T(8,128)(2,1)}, u32[]{:S(2)}, u32[]{:S(2)}) %collective-permute-start.3) | collective-permute-done | bytes 262176 | tf_op jit(solution)/shard_map/encoder_rows/ppermute | solution.py:16
  28.4 2.5 %encode.1 = (f32[4,2,64,128]{3,2,1,0:T(8,128)S(1)}, bf16[4,2,64,128]{3,2,1,0:T(8,128)(2,1)S(1)}, bf16[4,2,64,128]{3,2,1,0:T(8,128)(2,1)S(1)}, bf16[4,2,64,128]{3,2,1,0:T(8,128)(2,1)S(1)}) custom-call(s32[1]{0:T(128)} %bitcast.place_ref, s32[16,2]{1,0:T(8,128)S(1)} %negate_select_fusion.relative_ref, f32[1,128]{1,0:T(1,128)S(1)} %copy-done.2, ...), custom_call_target="tpu_custom_call" | custom-call | flops 1073741824 | bytes 3145728 | tf_op jit(solution)/shard_map/encode/encode/pallas_call | solution.py:51
  30.9 0.1 collective-permute-start.5
  31.0 3.2 %collective-permute-start.6 = (bf16[4,2,64,128]{3,2,1,0:T(8,128)(2,1)S(1)}, bf16[4,2,64,128]{3,2,1,0:T(8,128)(2,1)S(1)}, u32[]{:S(2)}, u32[]{:S(2)}) collective-permute-start(bf16[4,2,64,128]{3,2,1,0:T(8,128)(2,1)S(1)} %get-tuple-element.11), channel_id=1, source_target_pairs={{0,2},{1,3},{2,0},{3,1},{4,6},{5,7},{6,4},{7,5},{8,10},{9,11},{10,... | collective-permute-start | bytes 393224 | tf_op jit(solution)/shard_map/encode/ppermute | solution.py:16
  34.2 0.6 collective-permute-start.7
  34.8 0.1 fusion.1
  34.9 4.4 %collective-permute-done.5 = bf16[4,2,64,128]{3,2,1,0:T(8,128)(2,1)S(1)} collective-permute-done((bf16[4,2,64,128]{3,2,1,0:T(8,128)(2,1)S(1)}, bf16[4,2,64,128]{3,2,1,0:T(8,128)(2,1)S(1)}, u32[]{:S(2)}, u32[]{:S(2)}) %collective-permute-start.5) | collective-permute-done | bytes 131104 | tf_op jit(solution)/shard_map/encode/ppermute | solution.py:16
  39.3 3.7 %collective-permute-done.6 = bf16[4,2,64,128]{3,2,1,0:T(8,128)(2,1)S(1)} collective-permute-done((bf16[4,2,64,128]{3,2,1,0:T(8,128)(2,1)S(1)}, bf16[4,2,64,128]{3,2,1,0:T(8,128)(2,1)S(1)}, u32[]{:S(2)}, u32[]{:S(2)}) %collective-permute-start.6) | collective-permute-done | bytes 131104 | tf_op jit(solution)/shard_map/encode/ppermute | solution.py:16
  43.0 0.0 collective-permute-done.7
  43.0 0.1 multiply_convert_fusion.refs_0_
  43.1 3.4 %collective-permute-start.15 = (bf16[4,2,64,128]{3,2,1,0:T(8,128)(2,1)S(1)}, bf16[4,2,64,128]{3,2,1,0:T(8,128)(2,1)S(1)}, u32[]{:S(2)}, u32[]{:S(2)}) collective-permute-start(bf16[4,2,64,128]{3,2,1,0:T(8,128)(2,1)S(1)} %multiply_convert_fusion.refs_0_), channel_id=1, source_target_pairs={{0,8},{4,12},{8,16},{12,20},{16,24},{20,28},{1,9},{5,13},{9,17},{1... | collective-permute-start | bytes 393224 | tf_op jit(solution)/shard_map/spread/ppermute | solution.py:21
  46.5 1.9 %collective-permute-start.11 = (bf16[4,2,64,128]{3,2,1,0:T(8,128)(2,1)S(1)}, bf16[4,2,64,128]{3,2,1,0:T(8,128)(2,1)S(1)}, u32[]{:S(2)}, u32[]{:S(2)}) collective-permute-start(bf16[4,2,64,128]{3,2,1,0:T(8,128)(2,1)S(1)} %multiply_convert_fusion.refs_0_), channel_id=1, source_target_pairs={{0,4},{4,8},{8,12},{12,16},{16,20},{20,24},{24,28},{1,5},{5,9},{9,... | collective-permute-start | bytes 393224 | tf_op jit(solution)/shard_map/spread/ppermute | solution.py:21
  48.4 1.9 %collective-permute-start.1 = (s32[16,2]{0,1:T(2,128)S(1)}, s32[16,2]{0,1:T(2,128)S(1)}, u32[]{:S(2)}, u32[]{:S(2)}) collective-permute-start(s32[16,2]{0,1:T(2,128)S(1)} %bitcast.24), channel_id=1, source_target_pairs={{0,8},{4,12},{8,16},{12,20},{16,24},{20,28},{1,9},{5,13},{9,17},{1... | collective-permute-start | bytes 392 | tf_op jit(solution)/shard_map/decoder_weights/ppermute | solution.py:21
  50.3 4.4 %collective-permute-done.1 = s32[16,2]{0,1:T(2,128)S(1)} collective-permute-done((s32[16,2]{0,1:T(2,128)S(1)}, s32[16,2]{0,1:T(2,128)S(1)}, u32[]{:S(2)}, u32[]{:S(2)}) %collective-permute-start.1) | collective-permute-done | bytes 160 | tf_op jit(solution)/shard_map/decoder_weights/ppermute | solution.py:21
  54.8 1.9 %collective-permute-start = (s32[16,2]{0,1:T(2,128)S(1)}, s32[16,2]{0,1:T(2,128)S(1)}, u32[]{:S(2)}, u32[]{:S(2)}) collective-permute-start(s32[16,2]{0,1:T(2,128)S(1)} %bitcast.25), channel_id=1, source_target_pairs={{0,4},{4,8},{8,12},{12,16},{16,20},{20,24},{24,28},{1,5},{5,9},{9,... | collective-permute-start | bytes 392 | tf_op jit(solution)/shard_map/decoder_weights/ppermute | solution.py:21
  56.7 3.9 %collective-permute-done = s32[16,2]{0,1:T(2,128)S(1)} collective-permute-done((s32[16,2]{0,1:T(2,128)S(1)}, s32[16,2]{0,1:T(2,128)S(1)}, u32[]{:S(2)}, u32[]{:S(2)}) %collective-permute-start) | collective-permute-done | bytes 160 | tf_op jit(solution)/shard_map/decoder_weights/ppermute | solution.py:21
  60.5 2.4 %collective-permute-start.10 = (bf16[4,2,64,128]{3,2,1,0:T(8,128)(2,1)S(1)}, bf16[4,2,64,128]{3,2,1,0:T(8,128)(2,1)S(1)}, u32[]{:S(2)}, u32[]{:S(2)}) collective-permute-start(bf16[4,2,64,128]{3,2,1,0:T(8,128)(2,1)S(1)} %multiply_convert_fusion.refs_0_), channel_id=1, source_target_pairs={{0,3},{1,0},{2,1},{3,2},{4,7},{5,4},{6,5},{7,6},{8,11},{9,8},{10,9... | collective-permute-start | bytes 393224 | tf_op jit(solution)/shard_map/spread/ppermute | solution.py:16
  63.0 0.0 collective-permute-done.15.refs_8_
  63.0 1.4 %collective-permute-start.9 = (bf16[4,2,64,128]{3,2,1,0:T(8,128)(2,1)S(1)}, bf16[4,2,64,128]{3,2,1,0:T(8,128)(2,1)S(1)}, u32[]{:S(2)}, u32[]{:S(2)}) collective-permute-start(bf16[4,2,64,128]{3,2,1,0:T(8,128)(2,1)S(1)} %multiply_convert_fusion.refs_0_), channel_id=1, source_target_pairs={{0,2},{1,3},{2,0},{3,1},{4,6},{5,7},{6,4},{7,5},{8,10},{9,11},{10,... | collective-permute-start | bytes 393224 | tf_op jit(solution)/shard_map/spread/ppermute | solution.py:16
  64.4 0.0 collective-permute-done.11.refs_4_
  64.4 0.0 collective-permute-start.8
  64.4 3.9 %collective-permute-done.10.refs_3_ = bf16[4,2,64,128]{3,2,1,0:T(8,128)(2,1)S(1)} collective-permute-done((bf16[4,2,64,128]{3,2,1,0:T(8,128)(2,1)S(1)}, bf16[4,2,64,128]{3,2,1,0:T(8,128)(2,1)S(1)}, u32[]{:S(2)}, u32[]{:S(2)}) %collective-permute-start.10) | collective-permute-done | bytes 131104 | tf_op jit(solution)/shard_map/spread/ppermute | solution.py:16
  68.3 1.9 %collective-permute-start.18 = (bf16[4,2,64,128]{3,2,1,0:T(8,128)(2,1)S(1)}, bf16[4,2,64,128]{3,2,1,0:T(8,128)(2,1)S(1)}, u32[]{:S(2)}, u32[]{:S(2)}) collective-permute-start(bf16[4,2,64,128]{3,2,1,0:T(8,128)(2,1)S(1)} %collective-permute-done.10.refs_3_), channel_id=1, source_target_pairs={{0,8},{4,12},{8,16},{12,20},{16,24},{20,28},{1,9},{5,13},{9,17},{1... | collective-permute-start | bytes 393224 | tf_op jit(solution)/shard_map/spread/ppermute | solution.py:21
  70.2 3.3 %collective-permute-done.9.refs_2_ = bf16[4,2,64,128]{3,2,1,0:T(8,128)(2,1)S(1)} collective-permute-done((bf16[4,2,64,128]{3,2,1,0:T(8,128)(2,1)S(1)}, bf16[4,2,64,128]{3,2,1,0:T(8,128)(2,1)S(1)}, u32[]{:S(2)}, u32[]{:S(2)}) %collective-permute-start.9) | collective-permute-done | bytes 131104 | tf_op jit(solution)/shard_map/spread/ppermute | solution.py:16
  73.5 1.9 %collective-permute-start.14 = (bf16[4,2,64,128]{3,2,1,0:T(8,128)(2,1)S(1)}, bf16[4,2,64,128]{3,2,1,0:T(8,128)(2,1)S(1)}, u32[]{:S(2)}, u32[]{:S(2)}) collective-permute-start(bf16[4,2,64,128]{3,2,1,0:T(8,128)(2,1)S(1)} %collective-permute-done.10.refs_3_), channel_id=1, source_target_pairs={{0,4},{4,8},{8,12},{12,16},{16,20},{20,24},{24,28},{1,5},{5,9},{9,... | collective-permute-start | bytes 393224 | tf_op jit(solution)/shard_map/spread/ppermute | solution.py:21
  75.4 1.9 %collective-permute-start.17 = (bf16[4,2,64,128]{3,2,1,0:T(8,128)(2,1)S(1)}, bf16[4,2,64,128]{3,2,1,0:T(8,128)(2,1)S(1)}, u32[]{:S(2)}, u32[]{:S(2)}) collective-permute-start(bf16[4,2,64,128]{3,2,1,0:T(8,128)(2,1)S(1)} %collective-permute-done.9.refs_2_), channel_id=1, source_target_pairs={{0,8},{4,12},{8,16},{12,20},{16,24},{20,28},{1,9},{5,13},{9,17},{1... | collective-permute-start | bytes 393224 | tf_op jit(solution)/shard_map/spread/ppermute | solution.py:21
  77.4 0.0 collective-permute-done.18.refs_11_
  77.4 1.9 %collective-permute-start.13 = (bf16[4,2,64,128]{3,2,1,0:T(8,128)(2,1)S(1)}, bf16[4,2,64,128]{3,2,1,0:T(8,128)(2,1)S(1)}, u32[]{:S(2)}, u32[]{:S(2)}) collective-permute-start(bf16[4,2,64,128]{3,2,1,0:T(8,128)(2,1)S(1)} %collective-permute-done.9.refs_2_), channel_id=1, source_target_pairs={{0,4},{4,8},{8,12},{12,16},{16,20},{20,24},{24,28},{1,5},{5,9},{9,... | collective-permute-start | bytes 393224 | tf_op jit(solution)/shard_map/spread/ppermute | solution.py:21
  79.3 1.4 %collective-permute-done.14.refs_7_ = bf16[4,2,64,128]{3,2,1,0:T(8,128)(2,1)S(1)} collective-permute-done((bf16[4,2,64,128]{3,2,1,0:T(8,128)(2,1)S(1)}, bf16[4,2,64,128]{3,2,1,0:T(8,128)(2,1)S(1)}, u32[]{:S(2)}, u32[]{:S(2)}) %collective-permute-start.14) | collective-permute-done | bytes 131104 | tf_op jit(solution)/shard_map/spread/ppermute | solution.py:21
  80.7 1.9 %collective-permute-start.16 = (bf16[4,2,64,128]{3,2,1,0:T(8,128)(2,1)S(1)}, bf16[4,2,64,128]{3,2,1,0:T(8,128)(2,1)S(1)}, u32[]{:S(2)}, u32[]{:S(2)}) collective-permute-start(bf16[4,2,64,128]{3,2,1,0:T(8,128)(2,1)S(1)} %collective-permute-done.8.refs_1_), channel_id=1, source_target_pairs={{0,8},{4,12},{8,16},{12,20},{16,24},{20,28},{1,9},{5,13},{9,17},{1... | collective-permute-start | bytes 393224 | tf_op jit(solution)/shard_map/spread/ppermute | solution.py:21
  82.6 1.9 %collective-permute-done.17.refs_10_ = bf16[4,2,64,128]{3,2,1,0:T(8,128)(2,1)S(1)} collective-permute-done((bf16[4,2,64,128]{3,2,1,0:T(8,128)(2,1)S(1)}, bf16[4,2,64,128]{3,2,1,0:T(8,128)(2,1)S(1)}, u32[]{:S(2)}, u32[]{:S(2)}) %collective-permute-start.17) | collective-permute-done | bytes 131104 | tf_op jit(solution)/shard_map/spread/ppermute | solution.py:21
  84.5 1.9 %collective-permute-start.12 = (bf16[4,2,64,128]{3,2,1,0:T(8,128)(2,1)S(1)}, bf16[4,2,64,128]{3,2,1,0:T(8,128)(2,1)S(1)}, u32[]{:S(2)}, u32[]{:S(2)}) collective-permute-start(bf16[4,2,64,128]{3,2,1,0:T(8,128)(2,1)S(1)} %collective-permute-done.8.refs_1_), channel_id=1, source_target_pairs={{0,4},{4,8},{8,12},{12,16},{16,20},{20,24},{24,28},{1,5},{5,9},{9,... | collective-permute-start | bytes 393224 | tf_op jit(solution)/shard_map/spread/ppermute | solution.py:21
  86.5 0.1 copy.12.lists_ref
  86.6 1.9 %collective-permute-done.16.refs_9_ = bf16[4,2,64,128]{3,2,1,0:T(8,128)(2,1)S(1)} collective-permute-done((bf16[4,2,64,128]{3,2,1,0:T(8,128)(2,1)S(1)}, bf16[4,2,64,128]{3,2,1,0:T(8,128)(2,1)S(1)}, u32[]{:S(2)}, u32[]{:S(2)}) %collective-permute-start.16) | collective-permute-done | bytes 131104 | tf_op jit(solution)/shard_map/spread/ppermute | solution.py:21
  88.4 3.3 %collective-permute-done.12.refs_5_ = bf16[4,2,64,128]{3,2,1,0:T(8,128)(2,1)S(1)} collective-permute-done((bf16[4,2,64,128]{3,2,1,0:T(8,128)(2,1)S(1)}, bf16[4,2,64,128]{3,2,1,0:T(8,128)(2,1)S(1)}, u32[]{:S(2)}, u32[]{:S(2)}) %collective-permute-start.12) | collective-permute-done | bytes 131104 | tf_op jit(solution)/shard_map/spread/ppermute | solution.py:21
  91.7 0.0 collective-permute-done.19.refs_13_
  91.7 8.0 %decode.1 = bf16[1024,1024]{1,0:T(8,128)(2,1)} custom-call(s32[1]{0:T(128)} %bitcast.place_ref, s32[3,16,2]{2,1,0:T(8,128)S(1)} %copy.12.lists_ref, bf16[4,2,64,128]{3,2,1,0:T(8,128)(2,1)S(1)} %multiply_convert_fusion.refs_0_, bf16[4,2,64,128]{3,2,1,0:T(8,128)(2,1)S(1)} %collective-permute-done.8.refs_1_, ...), custom_call_target="tpu_custom_call" | custom-call | flops 3221225472 | bytes 7340032 | tf_op jit(solution)/shard_map/decode/decode/pallas_call | solution.py:98
  (13 shorter events, 0.0 us)
Async XLA Ops:
  0.0 15.6 %copy-start = (s32[1,16]{1,0:T(1,128)S(1)}, s32[1,16]{1,0:T(1,128)}, u32[]{:S(2)}) copy-start(s32[1,16]{1,0:T(1,128)} %param.11) | copy-start | bytes 196
  2.2 13.6 %collective-permute-start.4 = (bf16[1024,128]{1,0:T(8,128)(2,1)}, bf16[1024,128]{1,0:T(8,128)(2,1)}, u32[]{:S(2)}, u32[]{:S(2)}) collective-permute-start(bf16[1024,128]{1,0:T(8,128)(2,1)} %get-tuple-element.16), channel_id=1, source_target_pairs={{0,3},{1,0},{2,1},{3,2},{4,7},{5,4},{6,5},{7,6},{8,11},{9,8},{10,9... | collective-permute-start | bytes 786440 | tf_op jit(solution)/shard_map/encoder_rows/ppermute | solution.py:16
  5.8 13.7 %collective-permute-start.2 = (bf16[1024,128]{1,0:T(8,128)(2,1)}, bf16[1024,128]{1,0:T(8,128)(2,1)}, u32[]{:S(2)}, u32[]{:S(2)}) collective-permute-start(bf16[1024,128]{1,0:T(8,128)(2,1)} %get-tuple-element.17), channel_id=1, source_target_pairs={{0,1},{1,2},{2,3},{3,0},{4,5},{5,6},{6,7},{7,4},{8,9},{9,10},{10,1... | collective-permute-start | bytes 786440 | tf_op jit(solution)/shard_map/encoder_rows/ppermute | solution.py:16
  5.8 9.9 %copy-start.3 = (s32[1,16,2]{1,2,0:T(2,128)S(1)}, s32[1,16,2]{1,2,0:T(2,128)}, u32[]{:S(2)}) copy-start(s32[1,16,2]{1,2,0:T(2,128)} %param.10) | copy-start | bytes 388
  5.8 22.6 %copy-start.1 = (bf16[1,1024,1024]{2,1,0:T(8,128)(2,1)S(1)}, bf16[1,1024,1024]{2,1,0:T(8,128)(2,1)}, u32[]{:S(2)}) copy-start(bf16[1,1024,1024]{2,1,0:T(8,128)(2,1)} %param.6) | copy-start | bytes 6291460
  5.8 22.6 %copy-start.2 = (f32[1,128]{1,0:T(1,128)S(1)}, f32[1,128]{1,0:T(1,128)}, u32[]{:S(2)}) copy-start(f32[1,128]{1,0:T(1,128)} %bias_ref.1) | copy-start | bytes 1540
  5.8 22.6 %collective-permute-start.3 = (bf16[1024,128]{1,0:T(8,128)(2,1)}, bf16[1024,128]{1,0:T(8,128)(2,1)}, u32[]{:S(2)}, u32[]{:S(2)}) collective-permute-start(bf16[1024,128]{1,0:T(8,128)(2,1)} %get-tuple-element.19), channel_id=1, source_target_pairs={{0,2},{1,3},{2,0},{3,1},{4,6},{5,7},{6,4},{7,5},{8,10},{9,11},{10,... | collective-permute-start | bytes 786440 | tf_op jit(solution)/shard_map/encoder_rows/ppermute | solution.py:16
  10.3 81.4 %collective-permute-start.20 = (bf16[512,1024]{1,0:T(8,128)(2,1)}, bf16[512,1024]{1,0:T(8,128)(2,1)}, u32[]{:S(2)}, u32[]{:S(2)}) collective-permute-start(bf16[512,1024]{1,0:T(8,128)(2,1)} %get-tuple-element.13), channel_id=1, source_target_pairs={{0,8},{4,12},{8,16},{12,20},{16,24},{20,28},{1,9},{5,13},{9,17},{1... | collective-permute-start | bytes 3145736 | tf_op jit(solution)/shard_map/decoder_weights/ppermute | solution.py:21
  13.7 78.0 %collective-permute-start.19 = (bf16[512,1024]{1,0:T(8,128)(2,1)}, bf16[512,1024]{1,0:T(8,128)(2,1)}, u32[]{:S(2)}, u32[]{:S(2)}) collective-permute-start(bf16[512,1024]{1,0:T(8,128)(2,1)} %get-tuple-element.15), channel_id=1, source_target_pairs={{0,4},{4,8},{8,12},{12,16},{16,20},{20,24},{24,28},{1,5},{5,9},{9,... | collective-permute-start | bytes 3145736 | tf_op jit(solution)/shard_map/decoder_weights/ppermute | solution.py:21
  30.9 8.3 %collective-permute-start.5 = (bf16[4,2,64,128]{3,2,1,0:T(8,128)(2,1)S(1)}, bf16[4,2,64,128]{3,2,1,0:T(8,128)(2,1)S(1)}, u32[]{:S(2)}, u32[]{:S(2)}) collective-permute-start(bf16[4,2,64,128]{3,2,1,0:T(8,128)(2,1)S(1)} %get-tuple-element.10), channel_id=1, source_target_pairs={{0,1},{1,2},{2,3},{3,0},{4,5},{5,6},{6,7},{7,4},{8,9},{9,10},{10,1... | collective-permute-start | bytes 393224 | tf_op jit(solution)/shard_map/encode/ppermute | solution.py:16
  31.0 12.0 %collective-permute-start.6 = (bf16[4,2,64,128]{3,2,1,0:T(8,128)(2,1)S(1)}, bf16[4,2,64,128]{3,2,1,0:T(8,128)(2,1)S(1)}, u32[]{:S(2)}, u32[]{:S(2)}) collective-permute-start(bf16[4,2,64,128]{3,2,1,0:T(8,128)(2,1)S(1)} %get-tuple-element.11), channel_id=1, source_target_pairs={{0,2},{1,3},{2,0},{3,1},{4,6},{5,7},{6,4},{7,5},{8,10},{9,11},{10,... | collective-permute-start | bytes 393224 | tf_op jit(solution)/shard_map/encode/ppermute | solution.py:16
  34.2 8.8 %collective-permute-start.7 = (bf16[4,2,64,128]{3,2,1,0:T(8,128)(2,1)S(1)}, bf16[4,2,64,128]{3,2,1,0:T(8,128)(2,1)S(1)}, u32[]{:S(2)}, u32[]{:S(2)}) collective-permute-start(bf16[4,2,64,128]{3,2,1,0:T(8,128)(2,1)S(1)} %get-tuple-element.12), channel_id=1, source_target_pairs={{0,3},{1,0},{2,1},{3,2},{4,7},{5,4},{6,5},{7,6},{8,11},{9,8},{10,9... | collective-permute-start | bytes 393224 | tf_op jit(solution)/shard_map/encode/ppermute | solution.py:16
  43.1 19.9 %collective-permute-start.15 = (bf16[4,2,64,128]{3,2,1,0:T(8,128)(2,1)S(1)}, bf16[4,2,64,128]{3,2,1,0:T(8,128)(2,1)S(1)}, u32[]{:S(2)}, u32[]{:S(2)}) collective-permute-start(bf16[4,2,64,128]{3,2,1,0:T(8,128)(2,1)S(1)} %multiply_convert_fusion.refs_0_), channel_id=1, source_target_pairs={{0,8},{4,12},{8,16},{12,20},{16,24},{20,28},{1,9},{5,13},{9,17},{1... | collective-permute-start | bytes 393224 | tf_op jit(solution)/shard_map/spread/ppermute | solution.py:21
  46.5 17.9 %collective-permute-start.11 = (bf16[4,2,64,128]{3,2,1,0:T(8,128)(2,1)S(1)}, bf16[4,2,64,128]{3,2,1,0:T(8,128)(2,1)S(1)}, u32[]{:S(2)}, u32[]{:S(2)}) collective-permute-start(bf16[4,2,64,128]{3,2,1,0:T(8,128)(2,1)S(1)} %multiply_convert_fusion.refs_0_), channel_id=1, source_target_pairs={{0,4},{4,8},{8,12},{12,16},{16,20},{20,24},{24,28},{1,5},{5,9},{9,... | collective-permute-start | bytes 393224 | tf_op jit(solution)/shard_map/spread/ppermute | solution.py:21
  48.4 6.4 %collective-permute-start.1 = (s32[16,2]{0,1:T(2,128)S(1)}, s32[16,2]{0,1:T(2,128)S(1)}, u32[]{:S(2)}, u32[]{:S(2)}) collective-permute-start(s32[16,2]{0,1:T(2,128)S(1)} %bitcast.24), channel_id=1, source_target_pairs={{0,8},{4,12},{8,16},{12,20},{16,24},{20,28},{1,9},{5,13},{9,17},{1... | collective-permute-start | bytes 392 | tf_op jit(solution)/shard_map/decoder_weights/ppermute | solution.py:21
  54.8 5.8 %collective-permute-start = (s32[16,2]{0,1:T(2,128)S(1)}, s32[16,2]{0,1:T(2,128)S(1)}, u32[]{:S(2)}, u32[]{:S(2)}) collective-permute-start(s32[16,2]{0,1:T(2,128)S(1)} %bitcast.25), channel_id=1, source_target_pairs={{0,4},{4,8},{8,12},{12,16},{16,20},{20,24},{24,28},{1,5},{5,9},{9,... | collective-permute-start | bytes 392 | tf_op jit(solution)/shard_map/decoder_weights/ppermute | solution.py:21
  60.5 7.7 %collective-permute-start.10 = (bf16[4,2,64,128]{3,2,1,0:T(8,128)(2,1)S(1)}, bf16[4,2,64,128]{3,2,1,0:T(8,128)(2,1)S(1)}, u32[]{:S(2)}, u32[]{:S(2)}) collective-permute-start(bf16[4,2,64,128]{3,2,1,0:T(8,128)(2,1)S(1)} %multiply_convert_fusion.refs_0_), channel_id=1, source_target_pairs={{0,3},{1,0},{2,1},{3,2},{4,7},{5,4},{6,5},{7,6},{8,11},{9,8},{10,9... | collective-permute-start | bytes 393224 | tf_op jit(solution)/shard_map/spread/ppermute | solution.py:16
  63.0 10.5 %collective-permute-start.9 = (bf16[4,2,64,128]{3,2,1,0:T(8,128)(2,1)S(1)}, bf16[4,2,64,128]{3,2,1,0:T(8,128)(2,1)S(1)}, u32[]{:S(2)}, u32[]{:S(2)}) collective-permute-start(bf16[4,2,64,128]{3,2,1,0:T(8,128)(2,1)S(1)} %multiply_convert_fusion.refs_0_), channel_id=1, source_target_pairs={{0,2},{1,3},{2,0},{3,1},{4,6},{5,7},{6,4},{7,5},{8,10},{9,11},{10,... | collective-permute-start | bytes 393224 | tf_op jit(solution)/shard_map/spread/ppermute | solution.py:16
  64.4 11.0 %collective-permute-start.8 = (bf16[4,2,64,128]{3,2,1,0:T(8,128)(2,1)S(1)}, bf16[4,2,64,128]{3,2,1,0:T(8,128)(2,1)S(1)}, u32[]{:S(2)}, u32[]{:S(2)}) collective-permute-start(bf16[4,2,64,128]{3,2,1,0:T(8,128)(2,1)S(1)} %multiply_convert_fusion.refs_0_), channel_id=1, source_target_pairs={{0,1},{1,2},{2,3},{3,0},{4,5},{5,6},{6,7},{7,4},{8,9},{9,10},{10,1... | collective-permute-start | bytes 393224 | tf_op jit(solution)/shard_map/spread/ppermute | solution.py:16
  68.3 9.1 %collective-permute-start.18 = (bf16[4,2,64,128]{3,2,1,0:T(8,128)(2,1)S(1)}, bf16[4,2,64,128]{3,2,1,0:T(8,128)(2,1)S(1)}, u32[]{:S(2)}, u32[]{:S(2)}) collective-permute-start(bf16[4,2,64,128]{3,2,1,0:T(8,128)(2,1)S(1)} %collective-permute-done.10.refs_3_), channel_id=1, source_target_pairs={{0,8},{4,12},{8,16},{12,20},{16,24},{20,28},{1,9},{5,13},{9,17},{1... | collective-permute-start | bytes 393224 | tf_op jit(solution)/shard_map/spread/ppermute | solution.py:21
  73.5 7.2 %collective-permute-start.14 = (bf16[4,2,64,128]{3,2,1,0:T(8,128)(2,1)S(1)}, bf16[4,2,64,128]{3,2,1,0:T(8,128)(2,1)S(1)}, u32[]{:S(2)}, u32[]{:S(2)}) collective-permute-start(bf16[4,2,64,128]{3,2,1,0:T(8,128)(2,1)S(1)} %collective-permute-done.10.refs_3_), channel_id=1, source_target_pairs={{0,4},{4,8},{8,12},{12,16},{16,20},{20,24},{24,28},{1,5},{5,9},{9,... | collective-permute-start | bytes 393224 | tf_op jit(solution)/shard_map/spread/ppermute | solution.py:21
  75.4 9.1 %collective-permute-start.17 = (bf16[4,2,64,128]{3,2,1,0:T(8,128)(2,1)S(1)}, bf16[4,2,64,128]{3,2,1,0:T(8,128)(2,1)S(1)}, u32[]{:S(2)}, u32[]{:S(2)}) collective-permute-start(bf16[4,2,64,128]{3,2,1,0:T(8,128)(2,1)S(1)} %collective-permute-done.9.refs_2_), channel_id=1, source_target_pairs={{0,8},{4,12},{8,16},{12,20},{16,24},{20,28},{1,9},{5,13},{9,17},{1... | collective-permute-start | bytes 393224 | tf_op jit(solution)/shard_map/spread/ppermute | solution.py:21
  77.4 9.2 %collective-permute-start.13 = (bf16[4,2,64,128]{3,2,1,0:T(8,128)(2,1)S(1)}, bf16[4,2,64,128]{3,2,1,0:T(8,128)(2,1)S(1)}, u32[]{:S(2)}, u32[]{:S(2)}) collective-permute-start(bf16[4,2,64,128]{3,2,1,0:T(8,128)(2,1)S(1)} %collective-permute-done.9.refs_2_), channel_id=1, source_target_pairs={{0,4},{4,8},{8,12},{12,16},{16,20},{20,24},{24,28},{1,5},{5,9},{9,... | collective-permute-start | bytes 393224 | tf_op jit(solution)/shard_map/spread/ppermute | solution.py:21
  80.7 7.7 %collective-permute-start.16 = (bf16[4,2,64,128]{3,2,1,0:T(8,128)(2,1)S(1)}, bf16[4,2,64,128]{3,2,1,0:T(8,128)(2,1)S(1)}, u32[]{:S(2)}, u32[]{:S(2)}) collective-permute-start(bf16[4,2,64,128]{3,2,1,0:T(8,128)(2,1)S(1)} %collective-permute-done.8.refs_1_), channel_id=1, source_target_pairs={{0,8},{4,12},{8,16},{12,20},{16,24},{20,28},{1,9},{5,13},{9,17},{1... | collective-permute-start | bytes 393224 | tf_op jit(solution)/shard_map/spread/ppermute | solution.py:21
  84.5 7.2 %collective-permute-start.12 = (bf16[4,2,64,128]{3,2,1,0:T(8,128)(2,1)S(1)}, bf16[4,2,64,128]{3,2,1,0:T(8,128)(2,1)S(1)}, u32[]{:S(2)}, u32[]{:S(2)}) collective-permute-start(bf16[4,2,64,128]{3,2,1,0:T(8,128)(2,1)S(1)} %collective-permute-done.8.refs_1_), channel_id=1, source_target_pairs={{0,4},{4,8},{8,12},{12,16},{16,20},{20,24},{24,28},{1,5},{5,9},{9,... | collective-permute-start | bytes 393224 | tf_op jit(solution)/shard_map/spread/ppermute | solution.py:21

commit v2 on v1

v2 whole, which is shorter than its diff:
```python
import functools

import jax
import jax.numpy as jnp
from jax import lax
from jax.experimental import pallas as pl
from jax.experimental.pallas import tpu as pltpu
from jax.sharding import PartitionSpec as P

VMEM = pl.BlockSpec(memory_space=pltpu.VMEM)
SMEM = pl.BlockSpec(memory_space=pltpu.SMEM)


def rotated(value, steps):
    count = lax.axis_size("latent")
    return lax.ppermute(value, "latent", [(i, (i + steps) % count) for i in range(count)])


def passed_along(value, steps):
    count = lax.axis_size("layer")
    return lax.ppermute(value, "layer", [(i, i + steps) for i in range(count - steps)])


def encode_kernel(place_ref, lists_ref, bias_ref, x_ref, weights_ref, own_ref, sent_ref, wide, partial):
    parts, tiles, slots, rows, width = sent_ref.shape
    group_rows = tiles * rows
    for block in range(parts):
        wide[:, block * width : (block + 1) * width] = weights_ref[block]
    for group in range(parts):
        product = jnp.dot(
            x_ref[group * group_rows : (group + 1) * group_rows, :], wide[...], preferred_element_type=jnp.float32
        )
        for block in range(parts):
            here = (place_ref[0] == block).astype(jnp.float32)
            partial[block] = product[:, block * width : (block + 1) * width] + here * bias_ref[...]
        for tile in range(tiles):
            for slot in range(slots):
                block = lists_ref[group * tiles + tile, slot]
                kept = partial[block, tile * rows : (tile + 1) * rows, :]
                sent_ref[group, tile, slot] = kept.astype(sent_ref.dtype)

                @pl.when(place_ref[0] == group)
                def _():
                    own_ref[tile, slot] = kept


def encode(place, lists, bias, x, weights):
    parts, depth, width = weights.shape
    tokens = x.shape[0]
    tiles, slots = lists.shape
    shape = (tiles // parts, slots, tokens // tiles, width)
    return pl.pallas_call(
        encode_kernel,
        out_shape=[jax.ShapeDtypeStruct(shape, jnp.float32), jax.ShapeDtypeStruct((parts,) + shape, jnp.bfloat16)],
        in_specs=[SMEM, SMEM] + [VMEM] * 3,
        out_specs=[VMEM] * 2,
        scratch_shapes=[
            pltpu.VMEM((depth, parts * width), jnp.bfloat16),
            pltpu.VMEM((parts, tokens // parts, width), jnp.float32),
        ],
        compiler_params=pltpu.CompilerParams(vmem_limit_bytes=40 << 20),
        cost_estimate=pl.CostEstimate(
            flops=2 * tokens * depth * parts * width,
            bytes_accessed=2 * (tokens * depth + depth * parts * width),
            transcendentals=0,
        ),
        name="encode",
    )(place, lists, bias, x, weights)


def decode_kernel(parts, targets, place_ref, lists_ref, *refs):
    first_refs, rest_refs = refs[:targets], refs[targets : 2 * targets]
    decoder_refs, (out_ref, dense) = refs[2 * targets : 3 * targets], refs[3 * targets :]
    tiles, slots, rows, width = first_refs[0].shape
    latents = dense.shape[1] // targets
    columns = out_ref.shape[1]
    step = pl.program_id(0)

    @pl.when(step == 0)
    def _():
        dense[...] = jnp.zeros_like(dense)
        for offset in range(targets):
            for origin in range(parts):
                group = lax.rem(place_ref[0] - origin + parts, parts)
                for tile in range(tiles):
                    row = pl.multiple_of((group * tiles + tile) * rows, rows)
                    for slot in range(slots):
                        block = lists_ref[offset, group * tiles + tile, slot]
                        lane = pl.multiple_of(offset * latents + block * width, width)
                        if origin:
                            kept = rest_refs[offset][(origin - 1) * tiles + tile, slot]
                        else:
                            kept = first_refs[offset][tile, slot]
                        dense[pl.ds(row, rows), pl.ds(lane, width)] = kept

    lanes = pl.ds(pl.multiple_of(step * columns, columns), columns)
    stacked = jnp.concatenate([decoder[:latents, lanes] for decoder in decoder_refs], axis=0)
    out_ref[...] = jnp.dot(dense[...], stacked, preferred_element_type=jnp.float32).astype(out_ref.dtype)


def decode(place, lists, firsts, rests, decoders, tokens, latents):
    targets = len(firsts)
    features = decoders[0].shape[1]
    columns = features // max(features // 256, 1)
    parts = tokens // (firsts[0].shape[0] * firsts[0].shape[2])
    return pl.pallas_call(
        functools.partial(decode_kernel, parts, targets),
        grid_spec=pltpu.PrefetchScalarGridSpec(
            num_scalar_prefetch=2,
            grid=(features // columns,),
            in_specs=[VMEM] * (3 * targets),
            out_specs=pl.BlockSpec((tokens, columns), lambda step, place_ref, lists_ref: (0, step)),
            scratch_shapes=[pltpu.VMEM((tokens, targets * latents), jnp.bfloat16)],
        ),
        out_shape=jax.ShapeDtypeStruct((tokens, features), jnp.bfloat16),
        compiler_params=pltpu.CompilerParams(vmem_limit_bytes=40 << 20),
        cost_estimate=pl.CostEstimate(
            flops=2 * tokens * latents * features * targets,
            bytes_accessed=2 * (targets * latents * features + 2 * tokens * features),
            transcendentals=0,
        ),
        name="decode",
    )(place, lists, *firsts, *rests, *decoders)


def with_lists(decoder, lists):
    tiles, slots = lists.shape
    ids = jnp.pad(lists.astype(decoder.dtype), ((0, -tiles % 16), (0, decoder.shape[1] - slots)))
    return jnp.concatenate([decoder, ids], axis=0)


def shards(layer_input, enc_weight, enc_bias, dec_weight, block_lists, block_counts):
    parts = lax.axis_size("latent")
    place = lax.axis_index("latent")
    x, encoder, decoder = layer_input[0], enc_weight[0], dec_weight[0]
    lists, counts = block_lists[0], block_counts[0]
    tokens, depth = x.shape
    width = encoder.shape[1]
    tiles, slots = lists.shape
    targets, latents, _ = decoder.shape

    with jax.named_scope("encoder_rows"):
        weights = lax.all_to_all(encoder.reshape(parts, depth, width), "latent", 0, 0)
    with jax.named_scope("decoder_weights"):
        decoders, all_lists = [decoder[0]], [lists]
        for offset in range(1, targets):
            arrived = passed_along(with_lists(decoder[offset], lists), offset)
            decoders.append(arrived)
            all_lists.append(arrived[latents : latents + tiles, :slots].astype(jnp.int32))

    with jax.named_scope("encode"):
        where = place.astype(jnp.int32)[None]
        own, sent = encode(where, lists, enc_bias, x, weights)
        arrived = lax.all_to_all(sent, "latent", 0, 0)
    with jax.named_scope("activate"):
        preact = own
        for origin in range(parts):
            preact = preact + jnp.where(place == origin, 0.0, arrived[origin].astype(jnp.float32))
        own_counts = lax.dynamic_slice_in_dim(counts, place * (tiles // parts), tiles // parts)
        live = (jnp.arange(slots)[None, :] < own_counts[:, None]).astype(jnp.float32)
        act = (jnp.maximum(preact, 0.0) * live[:, :, None, None]).astype(jnp.bfloat16)
    with jax.named_scope("spread"):
        rest = jnp.concatenate([rotated(act, step) for step in range(1, parts)], axis=0)
        firsts = [act] + [passed_along(act, offset) for offset in range(1, targets)]
        rest, firsts = lax.optimization_barrier((rest, firsts))
        rests = [rest] + [passed_along(rest, offset) for offset in range(1, targets)]
    with jax.named_scope("decode"):
        return decode(where, jnp.stack(all_lists), firsts, rests, decoders, tokens, latents)[None]


def solution(mesh):
    placed = (
        P("layer", None, "latent"),
        P("layer", None, "latent"),
        P("layer", "latent"),
        P("layer", None, None, "latent"),
        P("layer", None, None),
        P("layer", None),
    )
    return jax.shard_map(
        shards, mesh=mesh, in_specs=placed, out_specs=P("layer", None, "latent"), check_vma=False
    )
```

time: 100 us -> 112 us (1.12)
  the two profiles are of different devices: /device:TPU:4 before, /device:TPU:12 now
where the time goes in v2:
time: 112 us; the launch traced here: 111 us
  waiting for transfers between devices  57 us (51%)
  starting transfers between devices  34.2 us (31%)
  Pallas kernels  11.2 us (10%)
  local copies, waits for them, and re-layouts  5.26 us (5%)
  other arithmetic  3.62 us (3%)
    ppermute x6, waiting for transfers between devices, passed_along(): lax.ppermute(value, 'layer', [(i, i + steps) for i in range(count - steps)])  31.9 us
    all_to_all x1, waiting for transfers between devices, shards(): lax.all_to_all(encoder.reshape(parts, depth, width), 'latent', 0, 0)  19.2 us
    ppermute x6, starting transfers between devices, passed_along(): lax.ppermute(value, 'layer', [(i, i + steps) for i in range(count - steps)])  15 us
    pallas_call x1, Pallas kernels, decode(): pl.pallas_call(functools.partial(decode_kernel, parts, targets), grid_spe...  7.69 us
    all_to_all x1, starting transfers between devices, shards(): arrived = lax.all_to_all(sent, 'latent', 0, 0)  7.52 us
    ppermute x3, starting transfers between devices, rotated(): lax.ppermute(value, 'latent', [(i, (i + steps) % count) for i in range(co...  6.18 us
    all_to_all x1, starting transfers between devices, shards(): lax.all_to_all(encoder.reshape(parts, depth, width), 'latent', 0, 0)  5.45 us
    all_to_all x1, waiting for transfers between devices, shards(): arrived = lax.all_to_all(sent, 'latent', 0, 0)  3.74 us
  transfers between devices with their start and end apart: 11, of which 9 were waited for; matrix products, arithmetic and copies ran while one was open for 7% of the time, Pallas kernels for 0%

profile of v2, /device:TPU:12, one launch (start us, length us, event | category | flops | bytes accessed | tf_op | source)
XLA Modules:
  0.0 111.4 jit_solution(4867352120279510060)
XLA Ops:
  0.0 0.0 copy-start
  0.0 0.0 copy-start.4
  0.0 5.4 %all-to-all-start = ((bf16[4,1024,128]{2,1,0:T(8,128)(2,1)}), bf16[4,1024,128]{2,1,0:T(8,128)(2,1)S(1)}, u32[]{:S(2)}, u32[]{:S(2)}) async-start(bf16[4,1024,128]{2,1,0:T(8,128)(2,1)} %bitcast.37), calls=%async_computation | async-start | bytes 2097152 | tf_op jit(solution)/shard_map/encoder_rows/all_to_all | solution.py:143
  5.5 0.0 copy-done.4
  5.5 0.1 copy.22.lists_ref
  5.5 0.0 copy-start.2
  5.5 3.1 %slice_bitcast_fusion = (bf16[512,1024]{1,0:T(8,128)(2,1)S(1)}, bf16[512,1024]{1,0:T(8,128)(2,1)S(1)}, bf16[512,1024]{1,0:T(8,128)(2,1)}) fusion(bf16[1,3,512,1024]{3,2,1,0:T(8,128)(2,1)} %param.9), kind=kLoop, calls=%fused_computation.4 | loop fusion | bytes 6291456 | tf_op jit(solution)/shard_map/decoder_weights/squeeze | solution.py:145
  8.7 19.2 %all-to-all-done.weights_ref = bf16[4,1024,128]{2,1,0:T(8,128)(2,1)S(1)} async-done(((bf16[4,1024,128]{2,1,0:T(8,128)(2,1)}), bf16[4,1024,128]{2,1,0:T(8,128)(2,1)S(1)}, u32[]{:S(2)}, u32[]{:S(2)}) %all-to-all-start) | async-done | bytes 1048608 | tf_op jit(solution)/shard_map/encoder_rows/all_to_all | solution.py:143
  27.9 0.0 copy-done.2
  27.9 0.0 copy-start.1
  27.9 1.6 %copy-done.1 = bf16[1,1024,1024]{2,1,0:T(8,128)(2,1)S(1)} copy-done((bf16[1,1024,1024]{2,1,0:T(8,128)(2,1)S(1)}, bf16[1,1024,1024]{2,1,0:T(8,128)(2,1)}, u32[]{:S(2)}) %copy-start.1) | copy-done | bytes 2097176
  29.5 3.5 %encode.1 = (f32[4,2,64,128]{3,2,1,0:T(8,128)S(1)}, bf16[4,4,2,64,128]{4,3,2,1,0:T(8,128)(2,1)}) custom-call(s32[1]{0:T(128)} %bitcast.place_ref, s32[16,2]{1,0:T(8,128)S(1)} %copy.22.lists_ref, f32[1,128]{1,0:T(1,128)S(1)} %copy-done.2, bf16[1024,1024]{1,0:T(8,128)(2,1)S(1)} %bitcast.36, bf16[4,1024,128]{2,1,0:T(8,128)(2,1)S(1)} %all-to-all-done.weights_ref), custom_call_target="tpu_custom_call" | custom-call | flops 1073741824 | bytes 3145728 | tf_op jit(solution)/shard_map/encode/encode/pallas_call | solution.py:52
  33.0 0.0 copy-start.3
  33.0 7.5 %all-to-all-start.1 = ((bf16[4,4,2,64,128]{4,3,2,1,0:T(8,128)(2,1)}), bf16[4,4,2,64,128]{4,3,2,1,0:T(8,128)(2,1)}, u32[]{:S(2)}, u32[]{:S(2)}) async-start(bf16[4,4,2,64,128]{4,3,2,1,0:T(8,128)(2,1)} %get-tuple-element.12), calls=%async_computation.1 | async-start | bytes 1048576 | tf_op jit(solution)/shard_map/encode/all_to_all | solution.py:154
  40.6 0.1 copy.19
  40.7 0.0 copy-done.3
  40.7 1.6 %fusion.1 = (bf16[528,1024]{1,0:T(8,128)(2,1)}, bf16[528,1024]{1,0:T(8,128)(2,1)}) fusion(bf16[16,2]{1,0:T(8,128)(2,1)S(1)} %copy.19, bf16[512,1024]{1,0:T(8,128)(2,1)S(1)} %get-tuple-element.18, bf16[512,1024]{1,0:T(8,128)(2,1)S(1)} %copy-done.3), kind=kLoop, calls=%fused_computation.2 | loop fusion | flops 4866048 | bytes 4259904 | tf_op jit(solution)/shard_map/decoder_weights/concatenate | solution.py:129
  42.2 1.9 %collective-permute-start = (bf16[528,1024]{1,0:T(8,128)(2,1)}, bf16[528,1024]{1,0:T(8,128)(2,1)S(1)}, u32[]{:S(2)}, u32[]{:S(2)}) collective-permute-start(bf16[528,1024]{1,0:T(8,128)(2,1)} %get-tuple-element.20), channel_id=1, source_target_pairs={{0,4},{4,8},{8,12},{12,16},{16,20},{20,24},{24,28},{1,5},{5,9},{9,... | collective-permute-start | bytes 3244040 | tf_op jit(solution)/shard_map/decoder_weights/ppermute | solution.py:21
  44.1 3.4 %collective-permute-start.1 = (bf16[528,1024]{1,0:T(8,128)(2,1)}, bf16[528,1024]{1,0:T(8,128)(2,1)}, u32[]{:S(2)}, u32[]{:S(2)}) collective-permute-start(bf16[528,1024]{1,0:T(8,128)(2,1)} %get-tuple-element.21), channel_id=1, source_target_pairs={{0,8},{4,12},{8,16},{12,20},{16,24},{20,28},{1,9},{5,13},{9,17},{1... | collective-permute-start | bytes 3244040 | tf_op jit(solution)/shard_map/decoder_weights/ppermute | solution.py:21
  47.6 0.0 copy-done
  47.6 0.1 dynamic-slice_bitcast_fusion
  47.6 0.1 fusion.6
  47.7 3.7 %all-to-all-done.1 = bf16[4,4,2,64,128]{4,3,2,1,0:T(8,128)(2,1)} async-done(((bf16[4,4,2,64,128]{4,3,2,1,0:T(8,128)(2,1)}), bf16[4,4,2,64,128]{4,3,2,1,0:T(8,128)(2,1)}, u32[]{:S(2)}, u32[]{:S(2)}) %all-to-all-start.1) | async-done | bytes 524320 | tf_op jit(solution)/shard_map/encode/all_to_all | solution.py:154
  51.4 1.2 %fusion.5.refs_0_ = bf16[4,2,64,128]{3,2,1,0:T(8,128)(2,1)S(1)} fusion(f32[4,2,64,128]{3,2,1,0:T(8,128)S(1)} %get-tuple-element.11, bf16[4,4,2,64,128]{4,3,2,1,0:T(8,128)(2,1)} %all-to-all-done.1, f32[4,2]{1,0:T(4,128)S(1)} %fusion.6, pred[]{:T(512)S(6)} %eq.15, pred[]{:T(512)S(6)} %eq.14, pred[]{:T(512)S(6)} %eq.13, pred[]{:T(512)S(6)} %eq.12), kind=kLoop, calls=%fused_computation.11 | loop fusion | flops 983040 | bytes 917540 | tf_op jit(solution)/shard_map/activate/convert_element_type | solution.py:161
  52.7 3.3 %collective-permute-start.4 = (bf16[4,2,64,128]{3,2,1,0:T(8,128)(2,1)S(1)}, bf16[4,2,64,128]{3,2,1,0:T(8,128)(2,1)S(1)}, u32[]{:S(2)}, u32[]{:S(2)}) collective-permute-start(bf16[4,2,64,128]{3,2,1,0:T(8,128)(2,1)S(1)} %fusion.5.refs_0_), channel_id=1, source_target_pairs={{0,3},{1,0},{2,1},{3,2},{4,7},{5,4},{6,5},{7,6},{8,11},{9,8},{10,9... | collective-permute-start | bytes 393224 | tf_op jit(solution)/shard_map/spread/ppermute | solution.py:16
  55.9 0.1 collective-permute-start.3
  56.0 2.8 %collective-permute-start.2 = (bf16[4,2,64,128]{3,2,1,0:T(8,128)(2,1)S(1)}, bf16[4,2,64,128]{3,2,1,0:T(8,128)(2,1)S(1)}, u32[]{:S(2)}, u32[]{:S(2)}) collective-permute-start(bf16[4,2,64,128]{3,2,1,0:T(8,128)(2,1)S(1)} %fusion.5.refs_0_), channel_id=1, source_target_pairs={{0,1},{1,2},{2,3},{3,0},{4,5},{5,6},{6,7},{7,4},{8,9},{9,10},{10,1... | collective-permute-start | bytes 393224 | tf_op jit(solution)/shard_map/spread/ppermute | solution.py:16
  58.9 0.4 collective-permute-done.4
  59.3 3.4 %collective-permute-start.6 = (bf16[4,2,64,128]{3,2,1,0:T(8,128)(2,1)S(1)}, bf16[4,2,64,128]{3,2,1,0:T(8,128)(2,1)S(1)}, u32[]{:S(2)}, u32[]{:S(2)}) collective-permute-start(bf16[4,2,64,128]{3,2,1,0:T(8,128)(2,1)S(1)} %fusion.5.refs_0_), channel_id=1, source_target_pairs={{0,8},{4,12},{8,16},{12,20},{16,24},{20,28},{1,9},{5,13},{9,17},{1... | collective-permute-start | bytes 393224 | tf_op jit(solution)/shard_map/spread/ppermute | solution.py:21
  62.7 1.5 %collective-permute-done.3 = bf16[4,2,64,128]{3,2,1,0:T(8,128)(2,1)S(1)} collective-permute-done((bf16[4,2,64,128]{3,2,1,0:T(8,128)(2,1)S(1)}, bf16[4,2,64,128]{3,2,1,0:T(8,128)(2,1)S(1)}, u32[]{:S(2)}, u32[]{:S(2)}) %collective-permute-start.3) | collective-permute-done | bytes 131104 | tf_op jit(solution)/shard_map/spread/ppermute | solution.py:16
  64.1 1.9 %collective-permute-start.5 = (bf16[4,2,64,128]{3,2,1,0:T(8,128)(2,1)S(1)}, bf16[4,2,64,128]{3,2,1,0:T(8,128)(2,1)S(1)}, u32[]{:S(2)}, u32[]{:S(2)}) collective-permute-start(bf16[4,2,64,128]{3,2,1,0:T(8,128)(2,1)S(1)} %fusion.5.refs_0_), channel_id=1, source_target_pairs={{0,4},{4,8},{8,12},{12,16},{16,20},{20,24},{24,28},{1,5},{5,9},{9,... | collective-permute-start | bytes 393224 | tf_op jit(solution)/shard_map/spread/ppermute | solution.py:21
  66.0 0.3 collective-permute-done.2
  66.4 10.3 %collective-permute-done.6.refs_2_ = bf16[4,2,64,128]{3,2,1,0:T(8,128)(2,1)S(1)} collective-permute-done((bf16[4,2,64,128]{3,2,1,0:T(8,128)(2,1)S(1)}, bf16[4,2,64,128]{3,2,1,0:T(8,128)(2,1)S(1)}, u32[]{:S(2)}, u32[]{:S(2)}) %collective-permute-start.6) | collective-permute-done | bytes 131104 | tf_op jit(solution)/shard_map/spread/ppermute | solution.py:21
  76.7 10.4 %collective-permute-done.5.refs_1_ = bf16[4,2,64,128]{3,2,1,0:T(8,128)(2,1)S(1)} collective-permute-done((bf16[4,2,64,128]{3,2,1,0:T(8,128)(2,1)S(1)}, bf16[4,2,64,128]{3,2,1,0:T(8,128)(2,1)S(1)}, u32[]{:S(2)}, u32[]{:S(2)}) %collective-permute-start.5) | collective-permute-done | bytes 131104 | tf_op jit(solution)/shard_map/spread/ppermute | solution.py:21
  87.2 2.5 %collective-permute-start.8 = (bf16[12,2,64,128]{3,2,1,0:T(8,128)(2,1)S(1)}, bf16[12,2,64,128]{3,2,1,0:T(8,128)(2,1)S(1)}, u32[]{:S(2)}, u32[]{:S(2)}) collective-permute-start(bf16[12,2,64,128]{3,2,1,0:T(8,128)(2,1)S(1)} %pad_maximum_fusion.refs_3_), channel_id=1, source_target_pairs={{0,8},{4,12},{8,16},{12,20},{16,24},{20,28},{1,9},{5,13},{9,17},{1... | collective-permute-start | bytes 1179656 | tf_op jit(solution)/shard_map/spread/ppermute | solution.py:21
  89.7 1.9 %collective-permute-start.7 = (bf16[12,2,64,128]{3,2,1,0:T(8,128)(2,1)S(1)}, bf16[12,2,64,128]{3,2,1,0:T(8,128)(2,1)}, u32[]{:S(2)}, u32[]{:S(2)}) collective-permute-start(bf16[12,2,64,128]{3,2,1,0:T(8,128)(2,1)S(1)} %pad_maximum_fusion.refs_3_), channel_id=1, source_target_pairs={{0,4},{4,8},{8,12},{12,16},{16,20},{20,24},{24,28},{1,5},{5,9},{9,... | collective-permute-start | bytes 1179656 | tf_op jit(solution)/shard_map/spread/ppermute | solution.py:21
  91.6 0.0 collective-permute-done.refs_7_
  91.6 0.1 copy.20
  91.7 0.0 collective-permute-done.1.refs_8_
  91.7 0.7 slice_convert_fusion
  92.4 0.1 copy.21
  92.5 0.1 copy.23.lists_ref
  92.6 9.4 %collective-permute-done.8.refs_5_ = bf16[12,2,64,128]{3,2,1,0:T(8,128)(2,1)S(1)} collective-permute-done((bf16[12,2,64,128]{3,2,1,0:T(8,128)(2,1)S(1)}, bf16[12,2,64,128]{3,2,1,0:T(8,128)(2,1)S(1)}, u32[]{:S(2)}, u32[]{:S(2)}) %collective-permute-start.8) | collective-permute-done | bytes 393248 | tf_op jit(solution)/shard_map/spread/ppermute | solution.py:21
  102.0 1.7 %collective-permute-done.7.refs_4_ = bf16[12,2,64,128]{3,2,1,0:T(8,128)(2,1)} collective-permute-done((bf16[12,2,64,128]{3,2,1,0:T(8,128)(2,1)S(1)}, bf16[12,2,64,128]{3,2,1,0:T(8,128)(2,1)}, u32[]{:S(2)}, u32[]{:S(2)}) %collective-permute-start.7) | collective-permute-done | bytes 393248 | tf_op jit(solution)/shard_map/spread/ppermute | solution.py:21
  103.7 7.7 %decode.1 = bf16[1024,1024]{1,0:T(8,128)(2,1)} custom-call(s32[1]{0:T(128)} %bitcast.place_ref, s32[3,16,2]{2,1,0:T(8,128)S(1)} %copy.23.lists_ref, bf16[4,2,64,128]{3,2,1,0:T(8,128)(2,1)S(1)} %fusion.5.refs_0_, bf16[4,2,64,128]{3,2,1,0:T(8,128)(2,1)S(1)} %collective-permute-done.5.refs_1_, bf16[4,2,64,128]{3,2,1,0:T(8,128)(2,1)S(1)} %collective-permute-done.6.refs_2_, ...), custom_call_target="tpu_custom_call" | custom-call | flops 3221225472 | bytes 7340032 | tf_op jit(solution)/shard_map/decode/decode/pallas_call | solution.py:106
  (4 shorter events, 0.1 us)
Async XLA Ops:
  0.0 47.6 %copy-start = (s32[1,16]{1,0:T(1,128)S(1)}, s32[1,16]{1,0:T(1,128)}, u32[]{:S(2)}) copy-start(s32[1,16]{1,0:T(1,128)} %param.11) | copy-start | bytes 196
  0.0 5.5 %copy-start.4 = (s32[1,16,2]{1,2,0:T(2,128)S(1)}, s32[1,16,2]{1,2,0:T(2,128)}, u32[]{:S(2)}) copy-start(s32[1,16,2]{1,2,0:T(2,128)} %param.10) | copy-start | bytes 388
  0.0 27.9 %all-to-all-start = ((bf16[4,1024,128]{2,1,0:T(8,128)(2,1)}), bf16[4,1024,128]{2,1,0:T(8,128)(2,1)S(1)}, u32[]{:S(2)}, u32[]{:S(2)}) async-start(bf16[4,1024,128]{2,1,0:T(8,128)(2,1)} %bitcast.37), calls=%async_computation | async-start | bytes 2097152 | tf_op jit(solution)/shard_map/encoder_rows/all_to_all | solution.py:143
  5.5 22.4 %copy-start.2 = (f32[1,128]{1,0:T(1,128)S(1)}, f32[1,128]{1,0:T(1,128)}, u32[]{:S(2)}) copy-start(f32[1,128]{1,0:T(1,128)} %bias_ref.1) | copy-start | bytes 1540
  27.9 1.6 %copy-start.1 = (bf16[1,1024,1024]{2,1,0:T(8,128)(2,1)S(1)}, bf16[1,1024,1024]{2,1,0:T(8,128)(2,1)}, u32[]{:S(2)}) copy-start(bf16[1,1024,1024]{2,1,0:T(8,128)(2,1)} %param.6) | copy-start | bytes 6291460
  33.0 7.6 %copy-start.3 = (bf16[512,1024]{1,0:T(8,128)(2,1)S(1)}, bf16[512,1024]{1,0:T(8,128)(2,1)}, u32[]{:S(2)}) copy-start(bf16[512,1024]{1,0:T(8,128)(2,1)} %get-tuple-element.19) | copy-start | bytes 3145732
  33.0 18.4 %all-to-all-start.1 = ((bf16[4,4,2,64,128]{4,3,2,1,0:T(8,128)(2,1)}), bf16[4,4,2,64,128]{4,3,2,1,0:T(8,128)(2,1)}, u32[]{:S(2)}, u32[]{:S(2)}) async-start(bf16[4,4,2,64,128]{4,3,2,1,0:T(8,128)(2,1)} %get-tuple-element.12), calls=%async_computation.1 | async-start | bytes 1048576 | tf_op jit(solution)/shard_map/encode/all_to_all | solution.py:154
  42.2 49.4 %collective-permute-start = (bf16[528,1024]{1,0:T(8,128)(2,1)}, bf16[528,1024]{1,0:T(8,128)(2,1)S(1)}, u32[]{:S(2)}, u32[]{:S(2)}) collective-permute-start(bf16[528,1024]{1,0:T(8,128)(2,1)} %get-tuple-element.20), channel_id=1, source_target_pairs={{0,4},{4,8},{8,12},{12,16},{16,20},{20,24},{24,28},{1,5},{5,9},{9,... | collective-permute-start | bytes 3244040 | tf_op jit(solution)/shard_map/decoder_weights/ppermute | solution.py:21
  44.1 47.6 %collective-permute-start.1 = (bf16[528,1024]{1,0:T(8,128)(2,1)}, bf16[528,1024]{1,0:T(8,128)(2,1)}, u32[]{:S(2)}, u32[]{:S(2)}) collective-permute-start(bf16[528,1024]{1,0:T(8,128)(2,1)} %get-tuple-element.21), channel_id=1, source_target_pairs={{0,8},{4,12},{8,16},{12,20},{16,24},{20,28},{1,9},{5,13},{9,17},{1... | collective-permute-start | bytes 3244040 | tf_op jit(solution)/shard_map/decoder_weights/ppermute | solution.py:21
  52.7 6.6 %collective-permute-start.4 = (bf16[4,2,64,128]{3,2,1,0:T(8,128)(2,1)S(1)}, bf16[4,2,64,128]{3,2,1,0:T(8,128)(2,1)S(1)}, u32[]{:S(2)}, u32[]{:S(2)}) collective-permute-start(bf16[4,2,64,128]{3,2,1,0:T(8,128)(2,1)S(1)} %fusion.5.refs_0_), channel_id=1, source_target_pairs={{0,3},{1,0},{2,1},{3,2},{4,7},{5,4},{6,5},{7,6},{8,11},{9,8},{10,9... | collective-permute-start | bytes 393224 | tf_op jit(solution)/shard_map/spread/ppermute | solution.py:16
  55.9 8.2 %collective-permute-start.3 = (bf16[4,2,64,128]{3,2,1,0:T(8,128)(2,1)S(1)}, bf16[4,2,64,128]{3,2,1,0:T(8,128)(2,1)S(1)}, u32[]{:S(2)}, u32[]{:S(2)}) collective-permute-start(bf16[4,2,64,128]{3,2,1,0:T(8,128)(2,1)S(1)} %fusion.5.refs_0_), channel_id=1, source_target_pairs={{0,2},{1,3},{2,0},{3,1},{4,6},{5,7},{6,4},{7,5},{8,10},{9,11},{10,... | collective-permute-start | bytes 393224 | tf_op jit(solution)/shard_map/spread/ppermute | solution.py:16
  56.0 10.3 %collective-permute-start.2 = (bf16[4,2,64,128]{3,2,1,0:T(8,128)(2,1)S(1)}, bf16[4,2,64,128]{3,2,1,0:T(8,128)(2,1)S(1)}, u32[]{:S(2)}, u32[]{:S(2)}) collective-permute-start(bf16[4,2,64,128]{3,2,1,0:T(8,128)(2,1)S(1)} %fusion.5.refs_0_), channel_id=1, source_target_pairs={{0,1},{1,2},{2,3},{3,0},{4,5},{5,6},{6,7},{7,4},{8,9},{9,10},{10,1... | collective-permute-start | bytes 393224 | tf_op jit(solution)/shard_map/spread/ppermute | solution.py:16
  59.3 17.5 %collective-permute-start.6 = (bf16[4,2,64,128]{3,2,1,0:T(8,128)(2,1)S(1)}, bf16[4,2,64,128]{3,2,1,0:T(8,128)(2,1)S(1)}, u32[]{:S(2)}, u32[]{:S(2)}) collective-permute-start(bf16[4,2,64,128]{3,2,1,0:T(8,128)(2,1)S(1)} %fusion.5.refs_0_), channel_id=1, source_target_pairs={{0,8},{4,12},{8,16},{12,20},{16,24},{20,28},{1,9},{5,13},{9,17},{1... | collective-permute-start | bytes 393224 | tf_op jit(solution)/shard_map/spread/ppermute | solution.py:21
  64.1 23.0 %collective-permute-start.5 = (bf16[4,2,64,128]{3,2,1,0:T(8,128)(2,1)S(1)}, bf16[4,2,64,128]{3,2,1,0:T(8,128)(2,1)S(1)}, u32[]{:S(2)}, u32[]{:S(2)}) collective-permute-start(bf16[4,2,64,128]{3,2,1,0:T(8,128)(2,1)S(1)} %fusion.5.refs_0_), channel_id=1, source_target_pairs={{0,4},{4,8},{8,12},{12,16},{16,20},{20,24},{24,28},{1,5},{5,9},{9,... | collective-permute-start | bytes 393224 | tf_op jit(solution)/shard_map/spread/ppermute | solution.py:21
  87.2 14.8 %collective-permute-start.8 = (bf16[12,2,64,128]{3,2,1,0:T(8,128)(2,1)S(1)}, bf16[12,2,64,128]{3,2,1,0:T(8,128)(2,1)S(1)}, u32[]{:S(2)}, u32[]{:S(2)}) collective-permute-start(bf16[12,2,64,128]{3,2,1,0:T(8,128)(2,1)S(1)} %pad_maximum_fusion.refs_3_), channel_id=1, source_target_pairs={{0,8},{4,12},{8,16},{12,20},{16,24},{20,28},{1,9},{5,13},{9,17},{1... | collective-permute-start | bytes 1179656 | tf_op jit(solution)/shard_map/spread/ppermute | solution.py:21
  89.7 14.0 %collective-permute-start.7 = (bf16[12,2,64,128]{3,2,1,0:T(8,128)(2,1)S(1)}, bf16[12,2,64,128]{3,2,1,0:T(8,128)(2,1)}, u32[]{:S(2)}, u32[]{:S(2)}) collective-permute-start(bf16[12,2,64,128]{3,2,1,0:T(8,128)(2,1)S(1)} %pad_maximum_fusion.refs_3_), channel_id=1, source_target_pairs={{0,4},{4,8},{8,12},{12,16},{16,20},{20,24},{24,28},{1,5},{5,9},{9,... | collective-permute-start | bytes 1179656 | tf_op jit(solution)/shard_map/spread/ppermute | solution.py:21

commit v3 on v0

v3 whole, which is shorter than its diff:
```python
import functools

import jax
import jax.numpy as jnp
from jax import lax
from jax.experimental import pallas as pl
from jax.experimental.pallas import tpu as pltpu
from jax.sharding import PartitionSpec as P

VMEM = pl.BlockSpec(memory_space=pltpu.VMEM)
SMEM = pl.BlockSpec(memory_space=pltpu.SMEM)
ANY = pl.BlockSpec(memory_space=pl.ANY)
HBM = pl.BlockSpec(memory_space=pltpu.HBM)


def swapped(value, step):
    count = lax.axis_size("latent")
    return lax.ppermute(value, "latent", [(i, i ^ step) for i in range(count)])


def passed_along(value, steps):
    count = lax.axis_size("layer")
    return lax.ppermute(value, "layer", [(i, i + steps) for i in range(count - steps)])


def across_cores(value):
    count = lax.axis_size("layer")
    return lax.ppermute(value, "layer", [(i, i ^ 1) for i in range(count)])


def small(name, megabytes=8):
    return dict(compiler_params=pltpu.CompilerParams(vmem_limit_bytes=megabytes << 20), name=name)


def fetch_rows_kernel(place_ref, encoder_ref, *piece_refs):
    depth = piece_refs[0].shape[0]
    for step, piece in enumerate(piece_refs):
        first = pl.multiple_of(lax.bitwise_xor(place_ref[0], step) * depth, depth)
        piece[...] = encoder_ref[pl.ds(first, depth), :]


def fetch_rows(place, encoder, parts):
    depth = encoder.shape[0] // parts
    return pl.pallas_call(
        fetch_rows_kernel,
        out_shape=[jax.ShapeDtypeStruct((depth, encoder.shape[1]), encoder.dtype)] * parts,
        in_specs=[SMEM, VMEM],
        out_specs=[VMEM] * parts,
        **small("fetch_rows"),
    )(place, encoder)


def fetch_decoders_kernel(lists_ref, decoder_ref, *refs):
    out_refs, sems = refs[:-1], refs[-1]
    latents = decoder_ref.shape[1]
    copies = []
    for number, out_ref in enumerate(out_refs):
        copies.append(
            pltpu.make_async_copy(decoder_ref.at[number + 1], out_ref.at[pl.ds(0, latents)], sems.at[number])
        )
        copies[-1].start()
    for out_ref in out_refs:
        out_ref[latents:, :] = lists_ref[...]
    for copy in copies:
        copy.wait()


def fetch_decoders(lists, decoder):
    targets, latents, features = decoder.shape
    ids = jnp.pad(lists.astype(decoder.dtype), ((0, -lists.shape[0] % 16), (0, features - lists.shape[1])))
    shape = jax.ShapeDtypeStruct((latents + ids.shape[0], features), decoder.dtype)
    return pl.pallas_call(
        fetch_decoders_kernel,
        out_shape=[shape] * (targets - 1),
        in_specs=[VMEM, ANY],
        out_specs=[VMEM] * (targets - 1),
        scratch_shapes=[pltpu.SemaphoreType.DMA((targets - 1,))],
        **small("fetch_decoders"),
    )(ids, decoder)


def encode_kernel(parts, place_ref, relative_ref, bias_ref, x_ref, *refs):
    weight_refs, (kept_ref, sent_ref, partial) = refs[:parts], refs[parts:]
    width = bias_ref.shape[1]
    held, slots, rows, _ = kept_ref.shape
    tiles = 2 * held // parts
    pair = 1 + (parts > 1)
    for first in range(0, parts, pair):
        stacked = jnp.concatenate([ref[...] for ref in weight_refs[first : first + pair]], axis=1)
        product = jnp.dot(x_ref[...], stacked, preferred_element_type=jnp.float32)
        for source in range(first, first + pair):
            block = product[:, (source - first) * width : (source - first + 1) * width]
            partial[source] = block if source else block + bias_ref[...]
    for side, out_ref in ((0, kept_ref), (1, sent_ref)):
        parity = lax.bitwise_xor(lax.bitwise_and(place_ref[0], 1), side)
        for position in range(held):
            tile = (2 * (position // tiles) + parity) * tiles + position % tiles
            first = pl.multiple_of(tile * rows, rows)
            for slot in range(slots):
                source = relative_ref[tile, slot]
                out_ref[position, slot] = partial[source, pl.ds(first, rows), :].astype(out_ref.dtype)


def encode(place, relative, bias, x, weights):
    parts = len(weights)
    tokens, depth = x.shape
    width = bias.shape[1]
    tiles, slots = relative.shape
    shape = (tiles // 2, slots, tokens // tiles, width)
    return pl.pallas_call(
        functools.partial(encode_kernel, parts),
        out_shape=[jax.ShapeDtypeStruct(shape, jnp.float32), jax.ShapeDtypeStruct(shape, jnp.bfloat16)],
        in_specs=[SMEM, SMEM] + [VMEM] * (2 + parts),
        out_specs=[VMEM] * 2,
        scratch_shapes=[pltpu.VMEM((parts, tokens, width), jnp.float32)],
        cost_estimate=pl.CostEstimate(
            flops=2 * tokens * depth * parts * width,
            bytes_accessed=2 * (tokens * depth + depth * parts * width),
            transcendentals=0,
        ),
        **small("encode", 16),
    )(place, relative, bias, x, *weights)


def merge_kernel(kept_ref, arrived_ref, total_ref, sent_ref):
    total = kept_ref[...] + arrived_ref[...].astype(jnp.float32)
    total_ref[...] = total
    sent_ref[...] = total.astype(sent_ref.dtype)


def merge(kept, arrived):
    return pl.pallas_call(
        merge_kernel,
        out_shape=[jax.ShapeDtypeStruct(kept.shape, kept.dtype), jax.ShapeDtypeStruct(kept.shape, arrived.dtype)],
        in_specs=[VMEM] * 2,
        out_specs=[VMEM] * 2,
        **small("merge"),
    )(kept, arrived)


def activate_kernel(parts, place_ref, counts_ref, kept_ref, arrived_ref, act_ref):
    held, slots, _, _ = kept_ref.shape
    tiles = 2 * held // parts
    parity = lax.bitwise_and(place_ref[0], 1)
    for position in range(held):
        tile = (2 * (position // tiles) + parity) * tiles + position % tiles
        for slot in range(slots):
            live = (slot < counts_ref[tile]).astype(jnp.float32)
            preact = kept_ref[position, slot] + arrived_ref[position, slot].astype(jnp.float32)
            act_ref[position, slot] = (jnp.maximum(preact, 0.0) * live).astype(act_ref.dtype)


def activate(place, counts, kept, arrived, parts):
    return pl.pallas_call(
        functools.partial(activate_kernel, parts),
        out_shape=jax.ShapeDtypeStruct(kept.shape, arrived.dtype),
        in_specs=[SMEM, SMEM] + [VMEM] * 2,
        out_specs=VMEM,
        **small("activate"),
    )(place, counts, kept, arrived)


def choose_kernel(even_ref, *refs):
    sources, out_ref = refs[:-1], refs[-1]
    held = sources[0].shape[0]

    @pl.when(even_ref[0] == 1)
    def _():
        out_ref[:held] = sources[0][...]
        out_ref[held:] = sources[1][...]

    @pl.when(even_ref[0] != 1)
    def _():
        out_ref[:held] = sources[2][...]
        out_ref[held:] = sources[3][...]


def choose(even, own, far):
    shape = own[0].shape
    return pl.pallas_call(
        choose_kernel,
        out_shape=jax.ShapeDtypeStruct((2 * shape[0],) + shape[1:], own[0].dtype),
        in_specs=[SMEM] + [VMEM] * 4,
        out_specs=VMEM,
        **small("choose"),
    )(even, *own, *far)


def expand(dense, lists_ref, offset, groups_ref, first, act_ref):
    tiles_held, slots, rows, width = act_ref.shape
    tiles = lists_ref.shape[1] // groups_ref.shape[0]
    for held in range(tiles_held):
        for slot in range(slots):
            block = lists_ref[offset, groups_ref[first + held // tiles] * tiles + held % tiles, slot]
            lanes = pl.ds(pl.multiple_of(block * width, width), width)
            dense[held * rows : (held + 1) * rows, lanes] = act_ref[held, slot]


def column_tiles(features):
    columns = 256 if features % 256 == 0 else features
    return [slice(first, first + columns) for first in range(0, features, columns)]


def send_out(stage, out_ref, sems, groups_ref, first, rows, number, lanes):
    copies = []
    for held in range(stage.shape[0] // rows):
        row = pl.multiple_of(groups_ref[first + held] * rows, rows)
        copies.append(
            pltpu.make_async_copy(
                stage.at[held * rows : (held + 1) * rows, lanes],
                out_ref.at[pl.ds(row, rows), lanes],
                sems.at[number, held],
            )
        )
        copies[-1].start()
    return copies


def early_kernel(groups_ref, lists_ref, own_early, own_late, far, decoder_hbm, far_dec, partial_ref, own, other, own_dec, sem):
    copy = pltpu.make_async_copy(decoder_hbm.at[0], own_dec, sem)
    copy.start()
    half, latents = other.shape
    held = groups_ref.shape[0] // 2
    own[...] = jnp.zeros_like(own)
    other[...] = jnp.zeros_like(other)
    expand(own.at[:half], lists_ref, 0, groups_ref, 0, own_early)
    expand(own.at[half:], lists_ref, 0, groups_ref, held, own_late)
    expand(other, lists_ref, 2, groups_ref, 0, far)
    copy.wait()
    for lanes in column_tiles(partial_ref.shape[1]):
        total = jnp.dot(own[...], own_dec[:, lanes], preferred_element_type=jnp.float32)
        partial_ref[half:, lanes] = total[half:]
        partial_ref[:half, lanes] = total[:half] + jnp.dot(
            other[...], far_dec[:latents, lanes], preferred_element_type=jnp.float32
        )


def late_kernel(groups_ref, lists_ref, partial_ref, near, far, near_dec, far_dec, out_ref, wide, other, stage, sems):
    half, latents = other.shape
    parts = groups_ref.shape[0]
    wide[...] = jnp.zeros_like(wide)
    other[...] = jnp.zeros_like(other)
    expand(wide, lists_ref, 1, groups_ref, 0, near)
    expand(other, lists_ref, 2, groups_ref, parts // 2, far)
    copies = []
    for number, lanes in enumerate(column_tiles(partial_ref.shape[1])):
        total = partial_ref[:, lanes] + jnp.dot(
            wide[...], near_dec[:latents, lanes], preferred_element_type=jnp.float32
        )
        stage[:half, lanes] = total[:half].astype(stage.dtype)
        total = total[half:] + jnp.dot(other[...], far_dec[:latents, lanes], preferred_element_type=jnp.float32)
        stage[half:, lanes] = total.astype(stage.dtype)
        copies += send_out(stage, out_ref, sems, groups_ref, 0, 2 * half // parts, number, lanes)
    for copy in copies:
        copy.wait()


def decode_early(groups, lists, acts, decoder, far_decoder, tokens):
    _, latents, features = decoder.shape
    return pl.pallas_call(
        early_kernel,
        out_shape=jax.ShapeDtypeStruct((tokens, features), jnp.float32),
        in_specs=[SMEM, SMEM] + [VMEM] * 3 + [ANY, VMEM],
        out_specs=VMEM,
        scratch_shapes=[
            pltpu.VMEM((tokens, latents), jnp.bfloat16),
            pltpu.VMEM((tokens // 2, latents), jnp.bfloat16),
            pltpu.VMEM((latents, features), jnp.bfloat16),
            pltpu.SemaphoreType.DMA,
        ],
        cost_estimate=pl.CostEstimate(
            flops=3 * tokens * latents * features,
            bytes_accessed=2 * (2 * latents * features + 2 * tokens * features),
            transcendentals=0,
        ),
        **small("decode_early", 16),
    )(groups, lists, *acts, decoder, far_decoder)


def decode_late(groups, lists, partial, near, far, decoders, latents):
    tokens, features = partial.shape
    parts = groups.shape[0]
    return pl.pallas_call(
        late_kernel,
        out_shape=jax.ShapeDtypeStruct((tokens, features), jnp.bfloat16),
        in_specs=[SMEM, SMEM] + [VMEM] * 5,
        out_specs=ANY,
        scratch_shapes=[
            pltpu.VMEM((tokens, latents), jnp.bfloat16),
            pltpu.VMEM((tokens // 2, latents), jnp.bfloat16),
            pltpu.VMEM((tokens, features), jnp.bfloat16),
            pltpu.SemaphoreType.DMA((len(column_tiles(features)), parts)),
        ],
        cost_estimate=pl.CostEstimate(
            flops=3 * tokens * latents * features,
            bytes_accessed=2 * (2 * latents * features + 2 * tokens * features),
            transcendentals=0,
        ),
        **small("decode_late", 16),
    )(groups, lists, partial, near, far, *decoders)


def shards(layer_input, enc_weight, enc_bias, dec_weight, block_lists, block_counts):
    parts = lax.axis_size("latent")
    index = lax.axis_index("latent").astype(jnp.int32)
    place = index[None]
    x, encoder, decoder = layer_input[0], enc_weight[0], dec_weight[0]
    lists, counts = block_lists[0], block_counts[0]
    tokens = x.shape[0]
    tiles, slots = lists.shape
    targets, latents, _ = decoder.shape
    if targets != 3 or parts < 2 or parts & (parts - 1):
        raise ValueError("mesh")

    with jax.named_scope("encoder_rows"):
        pieces = fetch_rows(place, encoder, parts)
        pieces, decoder = lax.optimization_barrier((pieces, decoder))
        weights = [pieces[0]] + [None] * (parts - 1)
        for step in sorted(range(1, parts), reverse=True):
            weights[step] = swapped(pieces[step], step)
    with jax.named_scope("decoder_weights"):
        decoders, all_lists = [], [lists]
        for number, rows in enumerate(fetch_decoders(lists, decoder)):
            decoders.append(passed_along(rows, number + 1))
            all_lists.append(decoders[-1][latents : latents + tiles, :slots].astype(jnp.int32))
        all_lists = jnp.stack(all_lists)

    with jax.named_scope("encode"):
        kept, sent = encode(place, lax.bitwise_xor(index, lists), enc_bias, x, weights)
        arrived = swapped(sent, 1)
        step = 2
        while step < parts:
            kept, sent = merge(kept, arrived)
            arrived = swapped(sent, step)
            step *= 2
        own = activate(place, counts, kept, arrived, parts)
    with jax.named_scope("spread"):
        late_own = swapped(own, 1)
        far = passed_along(own, 2)
        late_far = passed_along(late_own, 2)
    with jax.named_scope("decode"):
        order = 2 * jnp.arange(parts // 2, dtype=jnp.int32)
        parity = lax.bitwise_and(index, 1)
        groups = jnp.concatenate([order + parity, order + 1 - parity])
        partial = decode_early(groups, all_lists, [own, late_own, far], decoder, decoders[1], tokens)
        partial, late_far = lax.optimization_barrier((partial, late_far))
        even = (lax.axis_index("layer") % 2 == 0).astype(jnp.int32)[None]
        near = across_cores(choose(even, [own, late_own], [far, late_far]))
        return decode_late(groups, all_lists, partial, near, late_far, decoders, latents)[None]


def solution(mesh):
    placed = (
        P("layer", None, "latent"),
        P("layer", None, "latent"),
        P("layer", "latent"),
        P("layer", None, None, "latent"),
        P("layer", None, None),
        P("layer", None),
    )
    return jax.shard_map(
        shards, mesh=mesh, in_specs=placed, out_specs=P("layer", None, "latent"), check_vma=False
    )
```

time: 282 us -> 82 us (0.29)
  waiting for transfers between devices: 248 us -> 26 us
  starting transfers between devices: 5.4 us -> 28.2 us
  Pallas kernels: 0 us -> 13.8 us
  between operations: 13.4 us -> 0.15 us
  matrix products: 11.4 us -> 0 us
  local copies, waits for them, and re-layouts: 0.59 us -> 10.1 us
    all_gather x2 -> x0, waiting for transfers between devices: 179 us -> none  [the longest x1 152 us: shards(): lax.all_gather(layer_input, 'latent', axis=2, tiled=True)[0]]
    ppermute x2 -> x11, waiting for transfers between devices: 67.6 us -> 26 us  [the longest x6 24.5 us: swapped(): return lax.ppermute(value, 'latent', [(i, i ^ step) for i in range(count)])]
    ppermute x2 -> x11, starting transfers between devices: 5.36 us -> 28.2 us  [the longest x4 12.6 us: passed_along(): lax.ppermute(value, 'layer', [(i, i + steps) for i in range(count - steps)])]
    pallas_call x0 -> x8, Pallas kernels: none -> 13.8 us  [the longest x1 4.88 us: decode_late(): pl.pallas_call(late_kernel, out_shape=jax.ShapeDtypeStruct((tokens, featu...]
    dot_general x2 -> x0, matrix products: 11.4 us -> none  [the longest x1 6.78 us: shards(): jnp.dot(lax.all_gather(layer_input, 'latent', axis=2, tiled=True)[0], wei...]
    unnamed x2 -> x26, local copies, waits for them, and re-layouts: 0.01 us -> 9.67 us
  transfers between devices with their start and end apart: 4 -> 11, of which waited for: 4 -> 5; matrix products, arithmetic and copies ran while one was open for 0% -> 3% of each run, Pallas kernels for 0% -> 10%
where the time goes in v3:
time: 82 us; the launch traced here: 80.5 us
  starting transfers between devices  28.2 us (34%)
  waiting for transfers between devices  26 us (32%)
  Pallas kernels  13.8 us (17%)
  local copies, waits for them, and re-layouts  10.1 us (12%)
  other arithmetic  2.21 us (3%)
    ppermute x6, waiting for transfers between devices, swapped(): return lax.ppermute(value, 'latent', [(i, i ^ step) for i in range(count)])  24.5 us
    ppermute x4, starting transfers between devices, passed_along(): lax.ppermute(value, 'layer', [(i, i + steps) for i in range(count - steps)])  12.6 us
    ppermute x6, starting transfers between devices, swapped(): return lax.ppermute(value, 'latent', [(i, i ^ step) for i in range(count)])  12 us
    unnamed x26, local copies, waits for them, and re-layouts  9.67 us
    pallas_call x1, Pallas kernels, decode_late(): pl.pallas_call(late_kernel, out_shape=jax.ShapeDtypeStruct((tokens, featu...  4.88 us
    ppermute x1, starting transfers between devices, across_cores(): return lax.ppermute(value, 'layer', [(i, i ^ 1) for i in range(count)])  3.58 us
    pallas_call x1, Pallas kernels, decode_early(): pl.pallas_call(early_kernel, out_shape=jax.ShapeDtypeStruct((tokens, feat...  3.54 us
    pallas_call x1, Pallas kernels, encode(): pl.pallas_call(functools.partial(encode_kernel, parts), out_shape=[jax.Sh...  1.98 us
  transfers between devices with their start and end apart: 11, of which 5 were waited for; matrix products, arithmetic and copies ran while one was open for 3% of the time, Pallas kernels for 10%

profile of v3, /device:TPU:5, one launch (start us, length us, event | category | flops | bytes accessed | tf_op | source)
XLA Modules:
  0.0 80.5 jit_solution(15037074516144338928)
XLA Ops:
  0.0 1.2 %copy-done.2 = bf16[1,4096,128]{2,1,0:T(8,128)(2,1)S(1)} copy-done((bf16[1,4096,128]{2,1,0:T(8,128)(2,1)S(1)}, bf16[1,4096,128]{2,1,0:T(8,128)(2,1)}, u32[]{:S(2)}) %copy-start.2) | copy-done | bytes 1048600
  1.2 0.1 fetch_rows.1
  1.3 1.4 %collective-permute-start.2 = (bf16[1024,128]{1,0:T(8,128)(2,1)S(1)}, bf16[1024,128]{1,0:T(8,128)(2,1)S(1)}, u32[]{:S(2)}, u32[]{:S(2)}) collective-permute-start(bf16[1024,128]{1,0:T(8,128)(2,1)S(1)} %get-tuple-element.30), channel_id=1, source_target_pairs={{0,1},{1,0},{2,3},{3,2},{4,5},{5,4},{6,7},{7,6},{8,9},{9,8},{10,11... | collective-permute-start | bytes 786440 | tf_op jit(solution)/shard_map/encoder_rows/ppermute | solution.py:18
  2.7 2.3 %collective-permute-start.3 = (bf16[1024,128]{1,0:T(8,128)(2,1)S(1)}, bf16[1024,128]{1,0:T(8,128)(2,1)S(1)}, u32[]{:S(2)}, u32[]{:S(2)}) collective-permute-start(bf16[1024,128]{1,0:T(8,128)(2,1)S(1)} %get-tuple-element.31), channel_id=1, source_target_pairs={{0,2},{1,3},{2,0},{3,1},{4,6},{5,7},{6,4},{7,5},{8,10},{9,11},{10,... | collective-permute-start | bytes 786440 | tf_op jit(solution)/shard_map/encoder_rows/ppermute | solution.py:18
  5.0 0.0 collective-permute-start.4
  5.0 0.8 xor_bitcast_fusion
  5.7 0.1 copy.20
  5.8 1.9 %copy-done = bf16[1,3,512,1024]{3,2,1,0:T(8,128)(2,1)S(1)} copy-done((bf16[1,3,512,1024]{3,2,1,0:T(8,128)(2,1)S(1)}, bf16[1,3,512,1024]{3,2,1,0:T(8,128)(2,1)}, u32[]{:S(2)}) %copy-start) | copy-done | bytes 3145752
  7.7 1.5 %fetch_decoders.1 = (bf16[528,1024]{1,0:T(8,128)(2,1)}, bf16[528,1024]{1,0:T(8,128)(2,1)}) custom-call(bf16[16,1024]{1,0:T(8,128)(2,1)S(1)} %pad.4.lists_ref, bf16[3,512,1024]{2,1,0:T(8,128)(2,1)S(1)} %bitcast.13), custom_call_target="tpu_custom_call" | custom-call | tf_op jit(solution)/shard_map/decoder_weights/fetch_decoders/pallas_call | solution.py:72
  9.3 4.5 %collective-permute-start = (bf16[528,1024]{1,0:T(8,128)(2,1)}, bf16[528,1024]{1,0:T(8,128)(2,1)}, u32[]{:S(2)}, u32[]{:S(2)}) collective-permute-start(bf16[528,1024]{1,0:T(8,128)(2,1)} %get-tuple-element.27), channel_id=1, source_target_pairs={{0,4},{4,8},{8,12},{12,16},{16,20},{20,24},{24,28},{1,5},{5,9},{9,... | collective-permute-start | bytes 3244040 | tf_op jit(solution)/shard_map/decoder_weights/ppermute | solution.py:23
  13.7 1.9 %collective-permute-start.1 = (bf16[528,1024]{1,0:T(8,128)(2,1)}, bf16[528,1024]{1,0:T(8,128)(2,1)}, u32[]{:S(2)}, u32[]{:S(2)}) collective-permute-start(bf16[528,1024]{1,0:T(8,128)(2,1)} %get-tuple-element.28), channel_id=1, source_target_pairs={{0,8},{4,12},{8,16},{12,20},{16,24},{20,28},{1,9},{5,13},{9,17},{1... | collective-permute-start | bytes 3244040 | tf_op jit(solution)/shard_map/decoder_weights/ppermute | solution.py:23
  15.7 0.1 copy.23.relative_ref
  15.8 0.0 collective-permute-done.2.refs_1_
  15.8 0.7 copy-done.5
  16.5 0.0 collective-permute-done.3.refs_2_
  16.5 0.7 copy-done.7
  17.2 4.7 %collective-permute-done.4.refs_3_ = bf16[1024,128]{1,0:T(8,128)(2,1)S(1)} collective-permute-done((bf16[1024,128]{1,0:T(8,128)(2,1)S(1)}, bf16[1024,128]{1,0:T(8,128)(2,1)S(1)}, u32[]{:S(2)}, u32[]{:S(2)}) %collective-permute-start.4) | collective-permute-done | bytes 262176 | tf_op jit(solution)/shard_map/encoder_rows/ppermute | solution.py:18
  21.8 0.7 copy-done.9
  22.5 1.6 %copy-done.4 = bf16[1,1024,1024]{2,1,0:T(8,128)(2,1)S(1)} copy-done((bf16[1,1024,1024]{2,1,0:T(8,128)(2,1)S(1)}, bf16[1,1024,1024]{2,1,0:T(8,128)(2,1)}, u32[]{:S(2)}) %copy-start.4) | copy-done | bytes 2097176
  24.1 0.9 %copy-done.6 = bf16[1024,128]{1,0:T(8,128)(2,1)S(1)} copy-done((bf16[1024,128]{1,0:T(8,128)(2,1)S(1)}, bf16[1024,128]{1,0:T(8,128)(2,1)}, u32[]{:S(2)}) %copy-start.6) | copy-done | bytes 262168
  25.1 0.9 %copy-done.8 = bf16[1024,128]{1,0:T(8,128)(2,1)S(1)} copy-done((bf16[1024,128]{1,0:T(8,128)(2,1)S(1)}, bf16[1024,128]{1,0:T(8,128)(2,1)}, u32[]{:S(2)}) %copy-start.8) | copy-done | bytes 262168
  26.0 0.9 %copy-done.10 = bf16[1024,128]{1,0:T(8,128)(2,1)S(1)} copy-done((bf16[1024,128]{1,0:T(8,128)(2,1)S(1)}, bf16[1024,128]{1,0:T(8,128)(2,1)}, u32[]{:S(2)}) %copy-start.10) | copy-done | bytes 262168
  27.0 2.0 %encode.1 = (f32[8,2,64,128]{3,2,1,0:T(8,128)S(1)}, bf16[8,2,64,128]{3,2,1,0:T(8,128)(2,1)S(1)}) custom-call(s32[1]{0:T(128)} %bitcast.1.place_ref, s32[16,2]{1,0:T(8,128)S(1)} %copy.23.relative_ref, f32[1,128]{1,0:T(1,128)S(1)} %copy-done.11, bf16[1024,1024]{1,0:T(8,128)(2,1)S(1)} %bitcast.17, bf16[1024,128]{1,0:T(8,128)(2,1)S(1)} %get-tuple-element.29.refs_0_, ...), custom_call_target="tpu_custom_call" | custom-call | flops 1073741824 | bytes 3145728 | tf_op jit(solution)/shard_map/encode/encode/pallas_call | solution.py:110
  29.0 0.0 copy-start.12
  29.0 6.0 %collective-permute-start.5 = (bf16[8,2,64,128]{3,2,1,0:T(8,128)(2,1)S(1)}, bf16[8,2,64,128]{3,2,1,0:T(8,128)(2,1)S(1)}, u32[]{:S(2)}, u32[]{:S(2)}) collective-permute-start(bf16[8,2,64,128]{3,2,1,0:T(8,128)(2,1)S(1)} %get-tuple-element.34), channel_id=1, source_target_pairs={{0,1},{1,0},{2,3},{3,2},{4,5},{5,4},{6,7},{7,6},{8,9},{9,8},{10,11... | collective-permute-start | bytes 786440 | tf_op jit(solution)/shard_map/encode/ppermute | solution.py:18
  35.0 5.0 %collective-permute-done.5.arrived_ref = bf16[8,2,64,128]{3,2,1,0:T(8,128)(2,1)S(1)} collective-permute-done((bf16[8,2,64,128]{3,2,1,0:T(8,128)(2,1)S(1)}, bf16[8,2,64,128]{3,2,1,0:T(8,128)(2,1)S(1)}, u32[]{:S(2)}, u32[]{:S(2)}) %collective-permute-start.5) | collective-permute-done | bytes 262176 | tf_op jit(solution)/shard_map/encode/ppermute | solution.py:18
  40.0 0.1 merge.1
  40.0 2.3 %collective-permute-start.6 = (bf16[8,2,64,128]{3,2,1,0:T(8,128)(2,1)S(1)}, bf16[8,2,64,128]{3,2,1,0:T(8,128)(2,1)S(1)}, u32[]{:S(2)}, u32[]{:S(2)}) collective-permute-start(bf16[8,2,64,128]{3,2,1,0:T(8,128)(2,1)S(1)} %get-tuple-element.36), channel_id=1, source_target_pairs={{0,2},{1,3},{2,0},{3,1},{4,6},{5,7},{6,4},{7,5},{8,10},{9,11},{10,... | collective-permute-start | bytes 786440 | tf_op jit(solution)/shard_map/encode/ppermute | solution.py:18
  42.3 11.6 %collective-permute-done.6.arrived_ref = bf16[8,2,64,128]{3,2,1,0:T(8,128)(2,1)S(1)} collective-permute-done((bf16[8,2,64,128]{3,2,1,0:T(8,128)(2,1)S(1)}, bf16[8,2,64,128]{3,2,1,0:T(8,128)(2,1)S(1)}, u32[]{:S(2)}, u32[]{:S(2)}) %collective-permute-start.6) | collective-permute-done | bytes 262176 | tf_op jit(solution)/shard_map/encode/ppermute | solution.py:18
  53.9 0.6 activate.1.own_early.refs_0_
  54.5 0.1 collective-permute-start.7
  54.6 0.1 pad_add_fusion.1.groups_ref
  54.7 3.1 %collective-permute-start.8 = (bf16[8,2,64,128]{3,2,1,0:T(8,128)(2,1)S(1)}, bf16[8,2,64,128]{3,2,1,0:T(8,128)(2,1)}, u32[]{:S(2)}, u32[]{:S(2)}) collective-permute-start(bf16[8,2,64,128]{3,2,1,0:T(8,128)(2,1)S(1)} %activate.1.own_early.refs_0_), channel_id=1, source_target_pairs={{0,8},{4,12},{8,16},{12,20},{16,24},{20,28},{1,9},{5,13},{9,17},{1... | collective-permute-start | bytes 786440 | tf_op jit(solution)/shard_map/spread/ppermute | solution.py:23
  57.8 3.2 %collective-permute-done.7.own_late.refs_1_ = bf16[8,2,64,128]{3,2,1,0:T(8,128)(2,1)} collective-permute-done((bf16[8,2,64,128]{3,2,1,0:T(8,128)(2,1)S(1)}, bf16[8,2,64,128]{3,2,1,0:T(8,128)(2,1)}, u32[]{:S(2)}, u32[]{:S(2)}) %collective-permute-start.7) | collective-permute-done | bytes 262176 | tf_op jit(solution)/shard_map/spread/ppermute | solution.py:18
  61.0 3.1 %collective-permute-start.9 = (bf16[8,2,64,128]{3,2,1,0:T(8,128)(2,1)}, bf16[8,2,64,128]{3,2,1,0:T(8,128)(2,1)}, u32[]{:S(2)}, u32[]{:S(2)}) collective-permute-start(bf16[8,2,64,128]{3,2,1,0:T(8,128)(2,1)} %collective-permute-done.7.own_late.refs_1_), channel_id=1, source_target_pairs={{0,8},{4,12},{8,16},{12,20},{16,24},{20,28},{1,9},{5,13},{9,17},{1... | collective-permute-start | bytes 786440 | tf_op jit(solution)/shard_map/spread/ppermute | solution.py:23
  64.2 0.0 collective-permute-done.near_dec
  64.2 0.7 slice_convert_fusion.1
  64.8 0.1 copy.21
  64.9 0.7 slice_convert_fusion
  65.6 0.1 copy.22
  65.7 0.1 copy.25.lists_ref
  65.8 0.0 collective-permute-done.8.far.refs_2_
  65.8 3.5 %decode_early.1.partial_ref = f32[1024,1024]{1,0:T(8,128)S(1)} custom-call(s32[4]{0:T(128)S(1)} %pad_add_fusion.1.groups_ref, s32[3,16,2]{2,1,0:T(8,128)S(1)} %copy.25.lists_ref, bf16[8,2,64,128]{3,2,1,0:T(8,128)(2,1)S(1)} %activate.1.own_early.refs_0_, bf16[8,2,64,128]{3,2,1,0:T(8,128)(2,1)} %collective-permute-done.7.own_late.refs_1_, ...), custom_call_target="tpu_custom_call" | custom-call | flops 1610612736 | bytes 6291456 | tf_op jit(solution)/shard_map/decode/decode_early/pallas_call | solution.py:260
  69.4 0.0 collective-permute-done.9.refs_3_.far
  69.4 1.1 %choose.1 = bf16[16,2,64,128]{3,2,1,0:T(8,128)(2,1)S(1)} custom-call(s32[1]{0:T(128)} %bitcast.9.even_ref, bf16[8,2,64,128]{3,2,1,0:T(8,128)(2,1)S(1)} %activate.1.own_early.refs_0_, bf16[8,2,64,128]{3,2,1,0:T(8,128)(2,1)} %collective-permute-done.7.own_late.refs_1_, bf16[8,2,64,128]{3,2,1,0:T(8,128)(2,1)} %collective-permute-done.8.far.refs_2_, ...), custom_call_target="tpu_custom_call" | custom-call | tf_op jit(solution)/shard_map/decode/choose/pallas_call | solution.py:180
  70.5 3.6 %collective-permute-start.10 = (bf16[16,2,64,128]{3,2,1,0:T(8,128)(2,1)S(1)}, bf16[16,2,64,128]{3,2,1,0:T(8,128)(2,1)S(1)}, u32[]{:S(2)}, u32[]{:S(2)}) collective-permute-start(bf16[16,2,64,128]{3,2,1,0:T(8,128)(2,1)S(1)} %choose.1), channel_id=1, source_target_pairs={{0,4},{4,0},{8,12},{12,8},{16,20},{20,16},{24,28},{28,24},{1,5},{5... | collective-permute-start | bytes 1572872 | tf_op jit(solution)/shard_map/decode/ppermute | solution.py:28
  74.1 1.5 %collective-permute-done.10.near = bf16[16,2,64,128]{3,2,1,0:T(8,128)(2,1)S(1)} collective-permute-done((bf16[16,2,64,128]{3,2,1,0:T(8,128)(2,1)S(1)}, bf16[16,2,64,128]{3,2,1,0:T(8,128)(2,1)S(1)}, u32[]{:S(2)}, u32[]{:S(2)}) %collective-permute-start.10) | collective-permute-done | bytes 524320 | tf_op jit(solution)/shard_map/decode/ppermute | solution.py:28
  75.6 4.9 %decode_late.1 = bf16[1024,1024]{1,0:T(8,128)(2,1)} custom-call(s32[4]{0:T(128)S(1)} %pad_add_fusion.1.groups_ref, s32[3,16,2]{2,1,0:T(8,128)S(1)} %copy.25.lists_ref, f32[1024,1024]{1,0:T(8,128)S(1)} %decode_early.1.partial_ref, bf16[16,2,64,128]{3,2,1,0:T(8,128)(2,1)S(1)} %collective-permute-done.10.near, ...), custom_call_target="tpu_custom_call" | custom-call | flops 1610612736 | bytes 6291456 | tf_op jit(solution)/shard_map/decode/decode_late/pallas_call | solution.py:283
  (20 shorter events, 0.0 us)
Async XLA Ops:
  0.0 1.2 %copy-start.2 = (bf16[1,4096,128]{2,1,0:T(8,128)(2,1)S(1)}, bf16[1,4096,128]{2,1,0:T(8,128)(2,1)}, u32[]{:S(2)}) copy-start(bf16[1,4096,128]{2,1,0:T(8,128)(2,1)} %param.7) | copy-start | bytes 3145732
  1.3 14.5 %collective-permute-start.2 = (bf16[1024,128]{1,0:T(8,128)(2,1)S(1)}, bf16[1024,128]{1,0:T(8,128)(2,1)S(1)}, u32[]{:S(2)}, u32[]{:S(2)}) collective-permute-start(bf16[1024,128]{1,0:T(8,128)(2,1)S(1)} %get-tuple-element.30), channel_id=1, source_target_pairs={{0,1},{1,0},{2,3},{3,2},{4,5},{5,4},{6,7},{7,6},{8,9},{9,8},{10,11... | collective-permute-start | bytes 786440 | tf_op jit(solution)/shard_map/encoder_rows/ppermute | solution.py:18
  2.7 13.8 %collective-permute-start.3 = (bf16[1024,128]{1,0:T(8,128)(2,1)S(1)}, bf16[1024,128]{1,0:T(8,128)(2,1)S(1)}, u32[]{:S(2)}, u32[]{:S(2)}) collective-permute-start(bf16[1024,128]{1,0:T(8,128)(2,1)S(1)} %get-tuple-element.31), channel_id=1, source_target_pairs={{0,2},{1,3},{2,0},{3,1},{4,6},{5,7},{6,4},{7,5},{8,10},{9,11},{10,... | collective-permute-start | bytes 786440 | tf_op jit(solution)/shard_map/encoder_rows/ppermute | solution.py:18
  5.0 16.9 %collective-permute-start.4 = (bf16[1024,128]{1,0:T(8,128)(2,1)S(1)}, bf16[1024,128]{1,0:T(8,128)(2,1)S(1)}, u32[]{:S(2)}, u32[]{:S(2)}) collective-permute-start(bf16[1024,128]{1,0:T(8,128)(2,1)S(1)} %get-tuple-element.32), channel_id=1, source_target_pairs={{0,3},{1,2},{2,1},{3,0},{4,7},{5,6},{6,5},{7,4},{8,11},{9,10},{10,... | collective-permute-start | bytes 786440 | tf_op jit(solution)/shard_map/encoder_rows/ppermute | solution.py:18
  5.8 1.9 %copy-start = (bf16[1,3,512,1024]{3,2,1,0:T(8,128)(2,1)S(1)}, bf16[1,3,512,1024]{3,2,1,0:T(8,128)(2,1)}, u32[]{:S(2)}) copy-start(bf16[1,3,512,1024]{3,2,1,0:T(8,128)(2,1)} %param.9) | copy-start | bytes 9437188
  7.7 14.8 %copy-start.11 = (f32[1,128]{1,0:T(1,128)S(1)}, f32[1,128]{1,0:T(1,128)}, u32[]{:S(2)}) copy-start(f32[1,128]{1,0:T(1,128)} %bias_ref.1) | copy-start | bytes 1540
  9.3 54.9 %collective-permute-start = (bf16[528,1024]{1,0:T(8,128)(2,1)}, bf16[528,1024]{1,0:T(8,128)(2,1)}, u32[]{:S(2)}, u32[]{:S(2)}) collective-permute-start(bf16[528,1024]{1,0:T(8,128)(2,1)} %get-tuple-element.27), channel_id=1, source_target_pairs={{0,4},{4,8},{8,12},{12,16},{16,20},{20,24},{24,28},{1,5},{5,9},{9,... | collective-permute-start | bytes 3244040 | tf_op jit(solution)/shard_map/decoder_weights/ppermute | solution.py:23
  13.7 51.2 %collective-permute-start.1 = (bf16[528,1024]{1,0:T(8,128)(2,1)}, bf16[528,1024]{1,0:T(8,128)(2,1)}, u32[]{:S(2)}, u32[]{:S(2)}) collective-permute-start(bf16[528,1024]{1,0:T(8,128)(2,1)} %get-tuple-element.28), channel_id=1, source_target_pairs={{0,8},{4,12},{8,16},{12,20},{16,24},{20,28},{1,9},{5,13},{9,17},{1... | collective-permute-start | bytes 3244040 | tf_op jit(solution)/shard_map/decoder_weights/ppermute | solution.py:23
  15.8 0.7 copy-start.5
  16.5 0.7 copy-start.7
  21.8 0.7 copy-start.9
  22.5 1.6 %copy-start.4 = (bf16[1,1024,1024]{2,1,0:T(8,128)(2,1)S(1)}, bf16[1,1024,1024]{2,1,0:T(8,128)(2,1)}, u32[]{:S(2)}) copy-start(bf16[1,1024,1024]{2,1,0:T(8,128)(2,1)} %param.6) | copy-start | bytes 6291460
  24.1 0.9 %copy-start.6 = (bf16[1024,128]{1,0:T(8,128)(2,1)S(1)}, bf16[1024,128]{1,0:T(8,128)(2,1)}, u32[]{:S(2)}) copy-start(bf16[1024,128]{1,0:T(8,128)(2,1)} %copy-done.5) | copy-start | bytes 786436
  25.1 0.9 %copy-start.8 = (bf16[1024,128]{1,0:T(8,128)(2,1)S(1)}, bf16[1024,128]{1,0:T(8,128)(2,1)}, u32[]{:S(2)}) copy-start(bf16[1024,128]{1,0:T(8,128)(2,1)} %copy-done.7) | copy-start | bytes 786436
  26.0 0.9 %copy-start.10 = (bf16[1024,128]{1,0:T(8,128)(2,1)S(1)}, bf16[1024,128]{1,0:T(8,128)(2,1)}, u32[]{:S(2)}) copy-start(bf16[1024,128]{1,0:T(8,128)(2,1)} %copy-done.9) | copy-start | bytes 786436
  27.0 26.9 %copy-start.3 = (s32[1,16]{1,0:T(1,128)S(1)}, s32[1,16]{1,0:T(1,128)}, u32[]{:S(2)}) copy-start(s32[1,16]{1,0:T(1,128)} %param.11) | copy-start | bytes 196
  27.0 38.8 %copy-start.1 = (bf16[1,3,512,1024]{3,2,1,0:T(8,128)(2,1)S(1)}, bf16[1,3,512,1024]{3,2,1,0:T(8,128)(2,1)}, u32[]{:S(2)}) copy-start(bf16[1,3,512,1024]{3,2,1,0:T(8,128)(2,1)} %param.9) | copy-start | bytes 9437188
  29.0 36.7 %copy-start.12 = (s32[1,16,2]{1,2,0:T(2,128)S(1)}, s32[1,16,2]{1,2,0:T(2,128)}, u32[]{:S(2)}) copy-start(s32[1,16,2]{1,2,0:T(2,128)} %param.10) | copy-start | bytes 388
  29.0 11.0 %collective-permute-start.5 = (bf16[8,2,64,128]{3,2,1,0:T(8,128)(2,1)S(1)}, bf16[8,2,64,128]{3,2,1,0:T(8,128)(2,1)S(1)}, u32[]{:S(2)}, u32[]{:S(2)}) collective-permute-start(bf16[8,2,64,128]{3,2,1,0:T(8,128)(2,1)S(1)} %get-tuple-element.34), channel_id=1, source_target_pairs={{0,1},{1,0},{2,3},{3,2},{4,5},{5,4},{6,7},{7,6},{8,9},{9,8},{10,11... | collective-permute-start | bytes 786440 | tf_op jit(solution)/shard_map/encode/ppermute | solution.py:18
  40.0 13.8 %collective-permute-start.6 = (bf16[8,2,64,128]{3,2,1,0:T(8,128)(2,1)S(1)}, bf16[8,2,64,128]{3,2,1,0:T(8,128)(2,1)S(1)}, u32[]{:S(2)}, u32[]{:S(2)}) collective-permute-start(bf16[8,2,64,128]{3,2,1,0:T(8,128)(2,1)S(1)} %get-tuple-element.36), channel_id=1, source_target_pairs={{0,2},{1,3},{2,0},{3,1},{4,6},{5,7},{6,4},{7,5},{8,10},{9,11},{10,... | collective-permute-start | bytes 786440 | tf_op jit(solution)/shard_map/encode/ppermute | solution.py:18
  54.5 6.5 %collective-permute-start.7 = (bf16[8,2,64,128]{3,2,1,0:T(8,128)(2,1)S(1)}, bf16[8,2,64,128]{3,2,1,0:T(8,128)(2,1)}, u32[]{:S(2)}, u32[]{:S(2)}) collective-permute-start(bf16[8,2,64,128]{3,2,1,0:T(8,128)(2,1)S(1)} %activate.1.own_early.refs_0_), channel_id=1, source_target_pairs={{0,1},{1,0},{2,3},{3,2},{4,5},{5,4},{6,7},{7,6},{8,9},{9,8},{10,11... | collective-permute-start | bytes 786440 | tf_op jit(solution)/shard_map/spread/ppermute | solution.py:18
  54.7 11.1 %collective-permute-start.8 = (bf16[8,2,64,128]{3,2,1,0:T(8,128)(2,1)S(1)}, bf16[8,2,64,128]{3,2,1,0:T(8,128)(2,1)}, u32[]{:S(2)}, u32[]{:S(2)}) collective-permute-start(bf16[8,2,64,128]{3,2,1,0:T(8,128)(2,1)S(1)} %activate.1.own_early.refs_0_), channel_id=1, source_target_pairs={{0,8},{4,12},{8,16},{12,20},{16,24},{20,28},{1,9},{5,13},{9,17},{1... | collective-permute-start | bytes 786440 | tf_op jit(solution)/shard_map/spread/ppermute | solution.py:23
  61.0 8.3 %collective-permute-start.9 = (bf16[8,2,64,128]{3,2,1,0:T(8,128)(2,1)}, bf16[8,2,64,128]{3,2,1,0:T(8,128)(2,1)}, u32[]{:S(2)}, u32[]{:S(2)}) collective-permute-start(bf16[8,2,64,128]{3,2,1,0:T(8,128)(2,1)} %collective-permute-done.7.own_late.refs_1_), channel_id=1, source_target_pairs={{0,8},{4,12},{8,16},{12,20},{16,24},{20,28},{1,9},{5,13},{9,17},{1... | collective-permute-start | bytes 786440 | tf_op jit(solution)/shard_map/spread/ppermute | solution.py:23
  70.5 5.1 %collective-permute-start.10 = (bf16[16,2,64,128]{3,2,1,0:T(8,128)(2,1)S(1)}, bf16[16,2,64,128]{3,2,1,0:T(8,128)(2,1)S(1)}, u32[]{:S(2)}, u32[]{:S(2)}) collective-permute-start(bf16[16,2,64,128]{3,2,1,0:T(8,128)(2,1)S(1)} %choose.1), channel_id=1, source_target_pairs={{0,4},{4,0},{8,12},{12,8},{16,20},{20,16},{24,28},{28,24},{1,5},{5... | collective-permute-start | bytes 1572872 | tf_op jit(solution)/shard_map/decode/ppermute | solution.py:28

commit v4 on v3

v4 whole, which is shorter than its diff:
```python
import functools

import jax
import jax.numpy as jnp
from jax import lax
from jax.experimental import pallas as pl
from jax.experimental.pallas import tpu as pltpu
from jax.sharding import PartitionSpec as P

VMEM = pl.BlockSpec(memory_space=pltpu.VMEM)
SMEM = pl.BlockSpec(memory_space=pltpu.SMEM)
ANY = pl.BlockSpec(memory_space=pl.ANY)
HBM = pl.BlockSpec(memory_space=pltpu.HBM)


def swapped(value, step):
    count = lax.axis_size("latent")
    return lax.ppermute(value, "latent", [(i, i ^ step) for i in range(count)])


def passed_along(value, steps):
    count = lax.axis_size("layer")
    return lax.ppermute(value, "layer", [(i, i + steps) for i in range(count - steps)])


def across_cores(value):
    count = lax.axis_size("layer")
    return lax.ppermute(value, "layer", [(i, i ^ 1) for i in range(count)])


def small(name, megabytes=8):
    return dict(compiler_params=pltpu.CompilerParams(vmem_limit_bytes=megabytes << 20), name=name)


def held_group(number, parts):
    half = parts // 2
    parity = lax.bitwise_and(lax.axis_index("latent"), 1)
    return 2 * (number % half) + (parity if number < half else 1 - parity)


def fetch_rows_kernel(encoder_ref, *piece_refs):
    depth = piece_refs[0].shape[0]
    for step, piece in enumerate(piece_refs):
        first = pl.multiple_of(lax.bitwise_xor(lax.axis_index("latent"), step) * depth, depth)
        piece[...] = encoder_ref[pl.ds(first, depth), :]


def fetch_rows(encoder, parts):
    depth = encoder.shape[0] // parts
    return pl.pallas_call(
        fetch_rows_kernel,
        out_shape=[jax.ShapeDtypeStruct((depth, encoder.shape[1]), encoder.dtype)] * parts,
        in_specs=[VMEM],
        out_specs=[VMEM] * parts,
        **small("fetch_rows"),
    )(encoder)


def fetch_decoders_kernel(lists_ref, decoder_ref, *refs):
    out_refs, sems = refs[:-1], refs[-1]
    latents = decoder_ref.shape[1]
    copies = []
    for number, out_ref in enumerate(out_refs):
        copies.append(
            pltpu.make_async_copy(decoder_ref.at[number + 1], out_ref.at[pl.ds(0, latents)], sems.at[number])
        )
        copies[-1].start()
    for out_ref in out_refs:
        out_ref[latents:, :] = lists_ref[...]
    for copy in copies:
        copy.wait()


def fetch_decoders(lists, decoder):
    targets, latents, features = decoder.shape
    ids = jnp.pad(lists.astype(decoder.dtype), ((0, -lists.shape[0] % 16), (0, features - lists.shape[1])))
    shape = jax.ShapeDtypeStruct((latents + ids.shape[0], features), decoder.dtype)
    return pl.pallas_call(
        fetch_decoders_kernel,
        out_shape=[shape] * (targets - 1),
        in_specs=[VMEM, ANY],
        out_specs=[VMEM] * (targets - 1),
        scratch_shapes=[pltpu.SemaphoreType.DMA((targets - 1,))],
        **small("fetch_decoders", 58),
    )(ids, decoder)


def encode_kernel(parts, lists_ref, bias_ref, x_ref, *refs):
    weight_refs, (kept_ref, sent_ref, partial) = refs[:parts], refs[parts:]
    width = bias_ref.shape[1]
    held, slots, rows, _ = kept_ref.shape
    tiles = 2 * held // parts
    for first in range(0, parts, 2):
        stacked = jnp.concatenate([ref[...] for ref in weight_refs[first : first + 2]], axis=1)
        product = jnp.dot(x_ref[...], stacked, preferred_element_type=jnp.float32)
        for source in range(first, first + 2):
            block = product[:, (source - first) * width : (source - first + 1) * width]
            partial[source] = block if source else block + bias_ref[...]
    for out_ref, first in ((kept_ref, 0), (sent_ref, parts // 2)):
        for position in range(held):
            tile = held_group(first + position // tiles, parts) * tiles + position % tiles
            row = pl.multiple_of(tile * rows, rows)
            for slot in range(slots):
                source = lax.bitwise_xor(lax.axis_index("latent"), lists_ref[slot, tile])
                out_ref[position, slot] = partial[source, pl.ds(row, rows), :].astype(out_ref.dtype)


def encode(lists, bias, x, weights):
    parts = len(weights)
    tokens, depth = x.shape
    width = bias.shape[1]
    slots, tiles = lists.shape
    shape = (tiles // 2, slots, tokens // tiles, width)
    return pl.pallas_call(
        functools.partial(encode_kernel, parts),
        out_shape=[jax.ShapeDtypeStruct(shape, jnp.float32), jax.ShapeDtypeStruct(shape, jnp.bfloat16)],
        in_specs=[SMEM] + [VMEM] * (2 + parts),
        out_specs=[VMEM] * 2,
        scratch_shapes=[pltpu.VMEM((parts, tokens, width), jnp.float32)],
        cost_estimate=pl.CostEstimate(
            flops=2 * tokens * depth * parts * width,
            bytes_accessed=2 * (tokens * depth + depth * parts * width),
            transcendentals=0,
        ),
        **small("encode", 16),
    )(lists, bias, x, *weights)


def merge_kernel(kept_ref, arrived_ref, total_ref, sent_ref):
    total = kept_ref[...] + arrived_ref[...].astype(jnp.float32)
    total_ref[...] = total
    sent_ref[...] = total.astype(sent_ref.dtype)


def merge(kept, arrived):
    return pl.pallas_call(
        merge_kernel,
        out_shape=[jax.ShapeDtypeStruct(kept.shape, kept.dtype), jax.ShapeDtypeStruct(kept.shape, arrived.dtype)],
        in_specs=[VMEM] * 2,
        out_specs=[VMEM] * 2,
        **small("merge"),
    )(kept, arrived)


def activate_kernel(parts, counts_ref, kept_ref, arrived_ref, act_ref):
    held, slots, _, _ = kept_ref.shape
    tiles = 2 * held // parts
    for position in range(held):
        tile = held_group(position // tiles, parts) * tiles + position % tiles
        for slot in range(slots):
            live = (slot < counts_ref[tile]).astype(jnp.float32)
            preact = kept_ref[position, slot] + arrived_ref[position, slot].astype(jnp.float32)
            act_ref[position, slot] = (jnp.maximum(preact, 0.0) * live).astype(act_ref.dtype)


def activate(counts, kept, arrived, parts):
    return pl.pallas_call(
        functools.partial(activate_kernel, parts),
        out_shape=jax.ShapeDtypeStruct(kept.shape, arrived.dtype),
        in_specs=[SMEM] + [VMEM] * 2,
        out_specs=VMEM,
        **small("activate"),
    )(counts, kept, arrived)


def choose_kernel(*refs):
    sources, out_ref = refs[:-1], refs[-1]
    held = sources[0].shape[0]
    odd = lax.bitwise_and(lax.axis_index("layer"), 1)

    @pl.when(odd == 0)
    def _():
        out_ref[:held] = sources[0][...]
        out_ref[held:] = sources[1][...]

    @pl.when(odd == 1)
    def _():
        out_ref[:held] = sources[2][...]
        out_ref[held:] = sources[3][...]


def choose(own, far):
    shape = own[0].shape
    return pl.pallas_call(
        choose_kernel,
        out_shape=jax.ShapeDtypeStruct((2 * shape[0],) + shape[1:], own[0].dtype),
        in_specs=[VMEM] * 4,
        out_specs=VMEM,
        **small("choose"),
    )(*own, *far)


def expand(dense, lists_ref, parts, first, act_ref):
    held, slots, rows, width = act_ref.shape
    tiles = lists_ref.shape[1] // parts
    for position in range(held):
        tile = held_group(first + position // tiles, parts) * tiles + position % tiles
        for slot in range(slots):
            lanes = pl.ds(pl.multiple_of(lists_ref[slot, tile] * width, width), width)
            dense[position * rows : (position + 1) * rows, lanes] = act_ref[position, slot]


def column_tiles(features):
    columns = 256 if features % 256 == 0 else features
    return [slice(first, first + columns) for first in range(0, features, columns)]


def early_kernel(parts, lists_ref, far_lists, own_early, own_late, far, decoder_hbm, far_dec, *refs):
    early_ref, late_ref, own, other, own_dec, sem = refs
    copy = pltpu.make_async_copy(decoder_hbm.at[0], own_dec, sem)
    copy.start()
    half, latents = other.shape
    own[...] = jnp.zeros_like(own)
    other[...] = jnp.zeros_like(other)
    expand(own.at[:half], lists_ref, parts, 0, own_early)
    expand(own.at[half:], lists_ref, parts, parts // 2, own_late)
    expand(other, far_lists, parts, 0, far)
    copy.wait()
    for lanes in column_tiles(early_ref.shape[1]):
        total = jnp.dot(own[...], own_dec[:, lanes], preferred_element_type=jnp.float32)
        late_ref[:, lanes] = total[half:]
        early_ref[:, lanes] = total[:half] + jnp.dot(
            other[...], far_dec[:latents, lanes], preferred_element_type=jnp.float32
        )


def decode_early(lists, far_lists, acts, decoder, far_decoder, parts):
    _, latents, features = decoder.shape
    half = acts[0].shape[0] * acts[0].shape[2]
    return pl.pallas_call(
        functools.partial(early_kernel, parts),
        out_shape=[jax.ShapeDtypeStruct((half, features), jnp.float32)] * 2,
        in_specs=[SMEM, SMEM] + [VMEM] * 3 + [ANY, VMEM],
        out_specs=[VMEM] * 2,
        scratch_shapes=[
            pltpu.VMEM((2 * half, latents), jnp.bfloat16),
            pltpu.VMEM((half, latents), jnp.bfloat16),
            pltpu.VMEM((latents, features), jnp.bfloat16),
            pltpu.SemaphoreType.DMA,
        ],
        cost_estimate=pl.CostEstimate(
            flops=6 * half * latents * features,
            bytes_accessed=2 * (2 * latents * features + 4 * half * features),
            transcendentals=0,
        ),
        **small("decode_early", 16),
    )(lists, far_lists, *acts, decoder, far_decoder)


def middle_kernel(parts, lists_ref, partial_ref, far, far_dec, total_ref, dense):
    latents = dense.shape[1]
    dense[...] = jnp.zeros_like(dense)
    expand(dense, lists_ref, parts, parts // 2, far)
    for lanes in column_tiles(partial_ref.shape[1]):
        total_ref[:, lanes] = partial_ref[:, lanes] + jnp.dot(
            dense[...], far_dec[:latents, lanes], preferred_element_type=jnp.float32
        )


def decode_middle(lists, partial, far, decoder, latents, parts):
    half, features = partial.shape
    return pl.pallas_call(
        functools.partial(middle_kernel, parts),
        out_shape=jax.ShapeDtypeStruct(partial.shape, partial.dtype),
        in_specs=[SMEM] + [VMEM] * 3,
        out_specs=VMEM,
        scratch_shapes=[pltpu.VMEM((half, latents), jnp.bfloat16)],
        cost_estimate=pl.CostEstimate(
            flops=2 * half * latents * features,
            bytes_accessed=2 * (latents * features + 4 * half * features),
            transcendentals=0,
        ),
        **small("decode_middle", 16),
    )(lists, partial, far, decoder)


def late_kernel(parts, lists_ref, early_ref, late_ref, near, near_dec, out_ref, dense, stage, sems):
    tokens, latents = dense.shape
    half, rows = tokens // 2, tokens // parts
    dense[...] = jnp.zeros_like(dense)
    expand(dense, lists_ref, parts, 0, near)
    copies = []
    for number, lanes in enumerate(column_tiles(early_ref.shape[1])):
        total = jnp.dot(dense[...], near_dec[:latents, lanes], preferred_element_type=jnp.float32)
        stage[:half, lanes] = (total[:half] + early_ref[:, lanes]).astype(stage.dtype)
        stage[half:, lanes] = (total[half:] + late_ref[:, lanes]).astype(stage.dtype)
        for held in range(parts):
            row = pl.multiple_of(held_group(held, parts) * rows, rows)
            copies.append(
                pltpu.make_async_copy(
                    stage.at[held * rows : (held + 1) * rows, lanes],
                    out_ref.at[pl.ds(row, rows), lanes],
                    sems.at[number, held],
                )
            )
            copies[-1].start()
    for copy in copies:
        copy.wait()


def decode_late(lists, early, late, near, decoder, latents, parts):
    half, features = early.shape
    return pl.pallas_call(
        functools.partial(late_kernel, parts),
        out_shape=jax.ShapeDtypeStruct((2 * half, features), jnp.bfloat16),
        in_specs=[SMEM] + [VMEM] * 4,
        out_specs=ANY,
        scratch_shapes=[
            pltpu.VMEM((2 * half, latents), jnp.bfloat16),
            pltpu.VMEM((2 * half, features), jnp.bfloat16),
            pltpu.SemaphoreType.DMA((len(column_tiles(features)), parts)),
        ],
        cost_estimate=pl.CostEstimate(
            flops=4 * half * latents * features,
            bytes_accessed=2 * (latents * features + 6 * half * features),
            transcendentals=0,
        ),
        **small("decode_late", 16),
    )(lists, early, late, near, decoder)


def shards(layer_input, enc_weight, enc_bias, dec_weight, block_lists, block_counts):
    parts = lax.axis_size("latent")
    x, encoder, decoder = layer_input[0], enc_weight[0], dec_weight[0]
    lists, counts = block_lists[0].T, block_counts[0]
    slots, tiles = lists.shape
    targets, latents, _ = decoder.shape
    if targets != 3 or parts < 2 or parts & (parts - 1):
        raise ValueError("mesh")

    with jax.named_scope("encoder_rows"):
        pieces = fetch_rows(encoder, parts)
        pieces, decoder = lax.optimization_barrier((pieces, decoder))
        weights = [pieces[0]] + [None] * (parts - 1)
        for step in sorted(range(1, parts), reverse=True):
            weights[step] = swapped(pieces[step], step)
    with jax.named_scope("decoder_weights"):
        near_rows, far_rows = fetch_decoders(lists, decoder)
        near_decoder, far_decoder = passed_along(near_rows, 1), passed_along(far_rows, 2)
        near_lists, far_lists = [
            rows[latents : latents + slots, :tiles].astype(jnp.int32) for rows in (near_decoder, far_decoder)
        ]

    with jax.named_scope("encode"):
        kept, sent = encode(lists, enc_bias, x, weights)
        arrived = swapped(sent, 1)
        step = 2
        while step < parts:
            kept, sent = merge(kept, arrived)
            arrived = swapped(sent, step)
            step *= 2
        own = activate(counts, kept, arrived, parts)
    with jax.named_scope("spread"):
        late_own = swapped(own, 1)
        far = passed_along(own, 2)
        late_far = passed_along(late_own, 2)
    with jax.named_scope("decode"):
        early, late = decode_early(lists, far_lists, [own, late_own, far], decoder, far_decoder, parts)
        early, late, late_far = lax.optimization_barrier((early, late, late_far))
        near = across_cores(choose([own, late_own], [far, late_far]))
        late = decode_middle(far_lists, late, late_far, far_decoder, latents, parts)
        return decode_late(near_lists, early, late, near, near_decoder, latents, parts)[None]


def solution(mesh):
    placed = (
        P("layer", None, "latent"),
        P("layer", None, "latent"),
        P("layer", "latent"),
        P("layer", None, None, "latent"),
        P("layer", None, None),
        P("layer", None),
    )
    return jax.shard_map(
        shards, mesh=mesh, in_specs=placed, out_specs=P("layer", None, "latent"), check_vma=False
    )
```

time: 82 us -> 73.5 us (0.90); the launches traced: 80.5 us -> 73.2 us
  local copies, waits for them, and re-layouts: 10.1 us -> 1.87 us
  waiting for transfers between devices: 26 us -> 27.8 us
  other arithmetic: 2.21 us -> 0.69 us
  starting transfers between devices: 28.2 us -> 29.1 us
    unnamed x26 -> x14, local copies, waits for them, and re-layouts: 9.67 us -> 1.25 us
    ppermute x4, waiting for transfers between devices: 0.01 us -> 5.33 us  [passed_along(): lax.ppermute(value, 'layer', [(i, i + steps) for i in range(count - steps)])]
    ppermute x4, starting transfers between devices: 12.6 us -> 15.4 us  [passed_along(): lax.ppermute(value, 'layer', [(i, i + steps) for i in range(count - steps)])]
    ppermute x6, waiting for transfers between devices: 24.5 us -> 22.3 us  [swapped(): return lax.ppermute(value, 'latent', [(i, i ^ step) for i in range(count)])]
    pallas_call x1, Pallas kernels: 1.52 us -> 3.67 us  [fetch_decoders(): pl.pallas_call(fetch_decoders_kernel, out_shape=[shape] * (targets - 1),...]
    ppermute x1, starting transfers between devices: 3.58 us -> 1.89 us  [across_cores(): return lax.ppermute(value, 'layer', [(i, i ^ 1) for i in range(count)])]
    another operation x3 -> x0, other arithmetic: 1.37 us -> none  [shards(): all_lists = jnp.stack(all_lists)]
    ppermute x1, waiting for transfers between devices: 1.54 us -> 0.2 us  [across_cores(): return lax.ppermute(value, 'layer', [(i, i ^ 1) for i in range(count)])]
  transfers between devices with their start and end apart: 11 -> 11, of which waited for: 5 -> 8; matrix products, arithmetic and copies ran while one was open for 3% -> 2% of each run, Pallas kernels for 10% -> 14%
where the time goes in v4:
time: 73.5 us; the launch traced here: 73.2 us
  starting transfers between devices  29.1 us (40%)
  waiting for transfers between devices  27.8 us (38%)
  Pallas kernels  13.5 us (18%)
  local copies, waits for them, and re-layouts  1.87 us (3%)
    ppermute x6, waiting for transfers between devices, swapped(): return lax.ppermute(value, 'latent', [(i, i ^ step) for i in range(count)])  22.3 us
    ppermute x4, starting transfers between devices, passed_along(): lax.ppermute(value, 'layer', [(i, i + steps) for i in range(count - steps)])  15.4 us
    ppermute x6, starting transfers between devices, swapped(): return lax.ppermute(value, 'latent', [(i, i ^ step) for i in range(count)])  11.9 us
    ppermute x4, waiting for transfers between devices, passed_along(): lax.ppermute(value, 'layer', [(i, i + steps) for i in range(count - steps)])  5.33 us
    pallas_call x1, Pallas kernels, fetch_decoders(): pl.pallas_call(fetch_decoders_kernel, out_shape=[shape] * (targets - 1),...  3.67 us
    pallas_call x1, Pallas kernels, decode_late(): pl.pallas_call(functools.partial(late_kernel, parts), out_shape=jax.Shape...  3.16 us
    pallas_call x1, Pallas kernels, decode_early(): pl.pallas_call(functools.partial(early_kernel, parts), out_shape=[jax.Sha...  2.69 us
    ppermute x1, starting transfers between devices, across_cores(): return lax.ppermute(value, 'layer', [(i, i ^ 1) for i in range(count)])  1.89 us
  transfers between devices with their start and end apart: 11, of which 8 were waited for; matrix products, arithmetic and copies ran while one was open for 2% of the time, Pallas kernels for 14%

profile of v4, /device:TPU:5, one launch (start us, length us, event | category | flops | bytes accessed | tf_op | source)
XLA Modules:
  0.0 73.2 jit_solution(17080598308375436741)
XLA Ops:
  0.0 0.0 copy-start.1
  0.0 1.2 %copy-done.1 = bf16[1,4096,128]{2,1,0:T(8,128)(2,1)S(1)} copy-done((bf16[1,4096,128]{2,1,0:T(8,128)(2,1)S(1)}, bf16[1,4096,128]{2,1,0:T(8,128)(2,1)}, u32[]{:S(2)}) %copy-start.1) | copy-done | bytes 1048600
  1.2 0.0 copy-start.3
  1.2 0.0 copy-start.4
  1.2 0.0 copy-start.5
  1.2 0.1 fetch_rows.1
  1.3 1.4 %collective-permute-start.2 = (bf16[1024,128]{1,0:T(8,128)(2,1)S(1)}, bf16[1024,128]{1,0:T(8,128)(2,1)S(1)}, u32[]{:S(2)}, u32[]{:S(2)}) collective-permute-start(bf16[1024,128]{1,0:T(8,128)(2,1)S(1)} %get-tuple-element.33), channel_id=1, source_target_pairs={{0,1},{1,0},{2,3},{3,2},{4,5},{5,4},{6,7},{7,6},{8,9},{9,8},{10,11... | collective-permute-start | bytes 786440 | tf_op jit(solution)/shard_map/encoder_rows/ppermute | solution.py:18
  2.7 2.3 %collective-permute-start.3 = (bf16[1024,128]{1,0:T(8,128)(2,1)S(1)}, bf16[1024,128]{1,0:T(8,128)(2,1)S(1)}, u32[]{:S(2)}, u32[]{:S(2)}) collective-permute-start(bf16[1024,128]{1,0:T(8,128)(2,1)S(1)} %get-tuple-element.34), channel_id=1, source_target_pairs={{0,2},{1,3},{2,0},{3,1},{4,6},{5,7},{6,4},{7,5},{8,10},{9,11},{10,... | collective-permute-start | bytes 786440 | tf_op jit(solution)/shard_map/encoder_rows/ppermute | solution.py:18
  5.0 0.0 collective-permute-start.4
  5.0 0.7 bitcast_convert_fusion
  5.7 0.6 pad.4.lists_ref
  6.3 3.7 %fetch_decoders.1 = (bf16[528,1024]{1,0:T(8,128)(2,1)}, bf16[528,1024]{1,0:T(8,128)(2,1)}) custom-call(bf16[16,1024]{1,0:T(8,128)(2,1)} %pad.4.lists_ref, bf16[3,512,1024]{2,1,0:T(8,128)(2,1)} %bitcast.9), custom_call_target="tpu_custom_call" | custom-call | tf_op jit(solution)/shard_map/decoder_weights/fetch_decoders/pallas_call | solution.py:78
  10.0 3.1 %collective-permute-start.1 = (bf16[528,1024]{1,0:T(8,128)(2,1)}, bf16[528,1024]{1,0:T(8,128)(2,1)S(1)}, u32[]{:S(2)}, u32[]{:S(2)}) collective-permute-start(bf16[528,1024]{1,0:T(8,128)(2,1)} %get-tuple-element.31), channel_id=1, source_target_pairs={{0,8},{4,12},{8,16},{12,20},{16,24},{20,28},{1,9},{5,13},{9,17},{1... | collective-permute-start | bytes 3244040 | tf_op jit(solution)/shard_map/decoder_weights/ppermute | solution.py:23
  13.1 0.3 collective-permute-done.2.refs_1_
  13.4 0.0 collective-permute-done.3.refs_2_
  13.4 8.5 %collective-permute-done.4.refs_3_ = bf16[1024,128]{1,0:T(8,128)(2,1)S(1)} collective-permute-done((bf16[1024,128]{1,0:T(8,128)(2,1)S(1)}, bf16[1024,128]{1,0:T(8,128)(2,1)S(1)}, u32[]{:S(2)}, u32[]{:S(2)}) %collective-permute-start.4) | collective-permute-done | bytes 262176 | tf_op jit(solution)/shard_map/encoder_rows/ppermute | solution.py:18
  21.9 0.0 copy-done.3
  21.9 0.0 copy-done.4
  21.9 0.0 copy-done.5
  21.9 0.0 copy-start.6
  21.9 0.0 copy-start.2
  21.9 0.0 copy-start
  21.9 1.9 %encode.1 = (f32[8,2,64,128]{3,2,1,0:T(8,128)S(1)}, bf16[8,2,64,128]{3,2,1,0:T(8,128)(2,1)S(1)}) custom-call(s32[2,16]{1,0:T(2,128)S(1)} %bitcast.14, f32[1,128]{1,0:T(1,128)S(1)} %copy-done.5, bf16[1024,1024]{1,0:T(8,128)(2,1)S(1)} %bitcast.13, bf16[1024,128]{1,0:T(8,128)(2,1)S(1)} %get-tuple-element.32.refs_0_, ...), custom_call_target="tpu_custom_call" | custom-call | flops 1073741824 | bytes 3145728 | tf_op jit(solution)/shard_map/encode/encode/pallas_call | solution.py:114
  23.8 5.9 %collective-permute-start.5 = (bf16[8,2,64,128]{3,2,1,0:T(8,128)(2,1)S(1)}, bf16[8,2,64,128]{3,2,1,0:T(8,128)(2,1)S(1)}, u32[]{:S(2)}, u32[]{:S(2)}) collective-permute-start(bf16[8,2,64,128]{3,2,1,0:T(8,128)(2,1)S(1)} %get-tuple-element.37), channel_id=1, source_target_pairs={{0,1},{1,0},{2,3},{3,2},{4,5},{5,4},{6,7},{7,6},{8,9},{9,8},{10,11... | collective-permute-start | bytes 786440 | tf_op jit(solution)/shard_map/encode/ppermute | solution.py:18
  29.6 4.8 %collective-permute-done.5.arrived_ref = bf16[8,2,64,128]{3,2,1,0:T(8,128)(2,1)S(1)} collective-permute-done((bf16[8,2,64,128]{3,2,1,0:T(8,128)(2,1)S(1)}, bf16[8,2,64,128]{3,2,1,0:T(8,128)(2,1)S(1)}, u32[]{:S(2)}, u32[]{:S(2)}) %collective-permute-start.5) | collective-permute-done | bytes 262176 | tf_op jit(solution)/shard_map/encode/ppermute | solution.py:18
  34.4 0.1 merge.1
  34.5 2.3 %collective-permute-start.6 = (bf16[8,2,64,128]{3,2,1,0:T(8,128)(2,1)S(1)}, bf16[8,2,64,128]{3,2,1,0:T(8,128)(2,1)S(1)}, u32[]{:S(2)}, u32[]{:S(2)}) collective-permute-start(bf16[8,2,64,128]{3,2,1,0:T(8,128)(2,1)S(1)} %get-tuple-element.39), channel_id=1, source_target_pairs={{0,2},{1,3},{2,0},{3,1},{4,6},{5,7},{6,4},{7,5},{8,10},{9,11},{10,... | collective-permute-start | bytes 786440 | tf_op jit(solution)/shard_map/encode/ppermute | solution.py:18
  36.8 0.0 copy-done.6
  36.8 6.0 %collective-permute-start = (bf16[528,1024]{1,0:T(8,128)(2,1)S(1)}, bf16[528,1024]{1,0:T(8,128)(2,1)S(1)}, u32[]{:S(2)}, u32[]{:S(2)}) collective-permute-start(bf16[528,1024]{1,0:T(8,128)(2,1)S(1)} %copy-done.6), channel_id=1, source_target_pairs={{0,4},{4,8},{8,12},{12,16},{16,20},{20,24},{24,28},{1,5},{5,9},{9,... | collective-permute-start | bytes 3244040 | tf_op jit(solution)/shard_map/decoder_weights/ppermute | solution.py:23
  42.8 5.6 %collective-permute-done.6.arrived_ref = bf16[8,2,64,128]{3,2,1,0:T(8,128)(2,1)S(1)} collective-permute-done((bf16[8,2,64,128]{3,2,1,0:T(8,128)(2,1)S(1)}, bf16[8,2,64,128]{3,2,1,0:T(8,128)(2,1)S(1)}, u32[]{:S(2)}, u32[]{:S(2)}) %collective-permute-start.6) | collective-permute-done | bytes 262176 | tf_op jit(solution)/shard_map/encode/ppermute | solution.py:18
  48.4 0.0 copy-done.2
  48.4 0.6 activate.1.own_early.refs_0_
  49.0 0.1 collective-permute-start.7
  49.1 3.1 %collective-permute-start.8 = (bf16[8,2,64,128]{3,2,1,0:T(8,128)(2,1)S(1)}, bf16[8,2,64,128]{3,2,1,0:T(8,128)(2,1)S(1)}, u32[]{:S(2)}, u32[]{:S(2)}) collective-permute-start(bf16[8,2,64,128]{3,2,1,0:T(8,128)(2,1)S(1)} %activate.1.own_early.refs_0_), channel_id=1, source_target_pairs={{0,8},{4,12},{8,16},{12,20},{16,24},{20,28},{1,9},{5,13},{9,17},{1... | collective-permute-start | bytes 786440 | tf_op jit(solution)/shard_map/spread/ppermute | solution.py:23
  52.2 3.2 %collective-permute-done.7.own_late.refs_1_ = bf16[8,2,64,128]{3,2,1,0:T(8,128)(2,1)S(1)} collective-permute-done((bf16[8,2,64,128]{3,2,1,0:T(8,128)(2,1)S(1)}, bf16[8,2,64,128]{3,2,1,0:T(8,128)(2,1)S(1)}, u32[]{:S(2)}, u32[]{:S(2)}) %collective-permute-start.7) | collective-permute-done | bytes 262176 | tf_op jit(solution)/shard_map/spread/ppermute | solution.py:18
  55.4 3.1 %collective-permute-start.9 = (bf16[8,2,64,128]{3,2,1,0:T(8,128)(2,1)S(1)}, bf16[8,2,64,128]{3,2,1,0:T(8,128)(2,1)S(1)}, u32[]{:S(2)}, u32[]{:S(2)}) collective-permute-start(bf16[8,2,64,128]{3,2,1,0:T(8,128)(2,1)S(1)} %collective-permute-done.7.own_late.refs_1_), channel_id=1, source_target_pairs={{0,8},{4,12},{8,16},{12,20},{16,24},{20,28},{1,9},{5,13},{9,17},{1... | collective-permute-start | bytes 786440 | tf_op jit(solution)/shard_map/spread/ppermute | solution.py:23
  58.5 0.0 collective-permute-done.1.far_dec
  58.5 3.6 %collective-permute-done.8.far.refs_2_ = bf16[8,2,64,128]{3,2,1,0:T(8,128)(2,1)S(1)} collective-permute-done((bf16[8,2,64,128]{3,2,1,0:T(8,128)(2,1)S(1)}, bf16[8,2,64,128]{3,2,1,0:T(8,128)(2,1)S(1)}, u32[]{:S(2)}, u32[]{:S(2)}) %collective-permute-start.8) | collective-permute-done | bytes 262176 | tf_op jit(solution)/shard_map/spread/ppermute | solution.py:23
  62.2 0.0 copy-done
  62.2 2.7 %decode_early.1 = (f32[512,1024]{1,0:T(8,128)S(1)}, f32[512,1024]{1,0:T(8,128)S(1)}) custom-call(s32[2,16]{1,0:T(2,128)S(1)} %bitcast.15, s32[2,16]{1,0:T(2,128)S(1)} %slice_convert_fusion.far_lists.lists_ref, bf16[8,2,64,128]{3,2,1,0:T(8,128)(2,1)S(1)} %activate.1.own_early.refs_0_, bf16[8,2,64,128]{3,2,1,0:T(8,128)(2,1)S(1)} %collective-permute-done.7.own_late.refs_1_, ...), custom_call_target="tpu_custom_call" | custom-call | flops 1610612736 | bytes 6291456 | tf_op jit(solution)/shard_map/decode/decode_early/pallas_call | solution.py:230
  64.9 1.7 %collective-permute-done.9.far.refs_3_ = bf16[8,2,64,128]{3,2,1,0:T(8,128)(2,1)S(1)} collective-permute-done((bf16[8,2,64,128]{3,2,1,0:T(8,128)(2,1)S(1)}, bf16[8,2,64,128]{3,2,1,0:T(8,128)(2,1)S(1)}, u32[]{:S(2)}, u32[]{:S(2)}) %collective-permute-start.9) | collective-permute-done | bytes 262176 | tf_op jit(solution)/shard_map/spread/ppermute | solution.py:23
  66.6 1.9 %collective-permute-start.10 = (bf16[16,2,64,128]{3,2,1,0:T(8,128)(2,1)S(1)}, bf16[16,2,64,128]{3,2,1,0:T(8,128)(2,1)S(1)}, u32[]{:S(2)}, u32[]{:S(2)}) collective-permute-start(bf16[16,2,64,128]{3,2,1,0:T(8,128)(2,1)S(1)} %choose.1), channel_id=1, source_target_pairs={{0,4},{4,0},{8,12},{12,8},{16,20},{20,16},{24,28},{28,24},{1,5},{5... | collective-permute-start | bytes 1572872 | tf_op jit(solution)/shard_map/decode/ppermute | solution.py:28
  68.5 0.0 collective-permute-done.near_dec
  68.5 1.3 %decode_middle.1.late_ref = f32[512,1024]{1,0:T(8,128)S(1)} custom-call(s32[2,16]{1,0:T(2,128)S(1)} %slice_convert_fusion.far_lists.lists_ref, f32[512,1024]{1,0:T(8,128)S(1)} %get-tuple-element.43.partial_ref, bf16[8,2,64,128]{3,2,1,0:T(8,128)(2,1)S(1)} %collective-permute-done.9.far.refs_3_, bf16[528,1024]{1,0:T(8,128)(2,1)S(1)} %collective-permute-done.1.far_dec), custom_call_target="tpu_custom_call" | custom-call | flops 536870912 | bytes 5242880 | tf_op jit(solution)/shard_map/decode/decode_middle/pallas_call | solution.py:262
  69.8 0.2 collective-permute-done.10.near
  70.0 3.2 %decode_late.1 = bf16[1024,1024]{1,0:T(8,128)(2,1)} custom-call(s32[2,16]{1,0:T(2,128)S(1)} %slice_convert_fusion.1.lists_ref, f32[512,1024]{1,0:T(8,128)S(1)} %get-tuple-element.42.early_ref, f32[512,1024]{1,0:T(8,128)S(1)} %decode_middle.1.late_ref, bf16[16,2,64,128]{3,2,1,0:T(8,128)(2,1)S(1)} %collective-permute-done.10.near, ...), custom_call_target="tpu_custom_call" | custom-call | flops 1073741824 | bytes 7340032 | tf_op jit(solution)/shard_map/decode/decode_late/pallas_call | solution.py:303
  (3 shorter events, 0.0 us)
Async XLA Ops:
  0.0 1.2 %copy-start.1 = (bf16[1,4096,128]{2,1,0:T(8,128)(2,1)S(1)}, bf16[1,4096,128]{2,1,0:T(8,128)(2,1)}, u32[]{:S(2)}) copy-start(bf16[1,4096,128]{2,1,0:T(8,128)(2,1)} %param.7) | copy-start | bytes 3145732
  1.2 20.6 %copy-start.3 = (bf16[1,1024,1024]{2,1,0:T(8,128)(2,1)S(1)}, bf16[1,1024,1024]{2,1,0:T(8,128)(2,1)}, u32[]{:S(2)}) copy-start(bf16[1,1024,1024]{2,1,0:T(8,128)(2,1)} %param.6) | copy-start | bytes 6291460
  1.2 20.6 %copy-start.4 = (s32[1,16,2]{1,2,0:T(2,128)S(1)}, s32[1,16,2]{1,2,0:T(2,128)}, u32[]{:S(2)}) copy-start(s32[1,16,2]{1,2,0:T(2,128)} %param.10) | copy-start | bytes 388
  1.2 20.6 %copy-start.5 = (f32[1,128]{1,0:T(1,128)S(1)}, f32[1,128]{1,0:T(1,128)}, u32[]{:S(2)}) copy-start(f32[1,128]{1,0:T(1,128)} %bias_ref.1) | copy-start | bytes 1540
  1.3 12.1 %collective-permute-start.2 = (bf16[1024,128]{1,0:T(8,128)(2,1)S(1)}, bf16[1024,128]{1,0:T(8,128)(2,1)S(1)}, u32[]{:S(2)}, u32[]{:S(2)}) collective-permute-start(bf16[1024,128]{1,0:T(8,128)(2,1)S(1)} %get-tuple-element.33), channel_id=1, source_target_pairs={{0,1},{1,0},{2,3},{3,2},{4,5},{5,4},{6,7},{7,6},{8,9},{9,8},{10,11... | collective-permute-start | bytes 786440 | tf_op jit(solution)/shard_map/encoder_rows/ppermute | solution.py:18
  2.7 10.7 %collective-permute-start.3 = (bf16[1024,128]{1,0:T(8,128)(2,1)S(1)}, bf16[1024,128]{1,0:T(8,128)(2,1)S(1)}, u32[]{:S(2)}, u32[]{:S(2)}) collective-permute-start(bf16[1024,128]{1,0:T(8,128)(2,1)S(1)} %get-tuple-element.34), channel_id=1, source_target_pairs={{0,2},{1,3},{2,0},{3,1},{4,6},{5,7},{6,4},{7,5},{8,10},{9,11},{10,... | collective-permute-start | bytes 786440 | tf_op jit(solution)/shard_map/encoder_rows/ppermute | solution.py:18
  5.0 16.9 %collective-permute-start.4 = (bf16[1024,128]{1,0:T(8,128)(2,1)S(1)}, bf16[1024,128]{1,0:T(8,128)(2,1)S(1)}, u32[]{:S(2)}, u32[]{:S(2)}) collective-permute-start(bf16[1024,128]{1,0:T(8,128)(2,1)S(1)} %get-tuple-element.35), channel_id=1, source_target_pairs={{0,3},{1,2},{2,1},{3,0},{4,7},{5,6},{6,5},{7,4},{8,11},{9,10},{10,... | collective-permute-start | bytes 786440 | tf_op jit(solution)/shard_map/encoder_rows/ppermute | solution.py:18
  10.0 48.6 %collective-permute-start.1 = (bf16[528,1024]{1,0:T(8,128)(2,1)}, bf16[528,1024]{1,0:T(8,128)(2,1)S(1)}, u32[]{:S(2)}, u32[]{:S(2)}) collective-permute-start(bf16[528,1024]{1,0:T(8,128)(2,1)} %get-tuple-element.31), channel_id=1, source_target_pairs={{0,8},{4,12},{8,16},{12,20},{16,24},{20,28},{1,9},{5,13},{9,17},{1... | collective-permute-start | bytes 3244040 | tf_op jit(solution)/shard_map/decoder_weights/ppermute | solution.py:23
  21.9 14.9 %copy-start.6 = (bf16[528,1024]{1,0:T(8,128)(2,1)S(1)}, bf16[528,1024]{1,0:T(8,128)(2,1)}, u32[]{:S(2)}) copy-start(bf16[528,1024]{1,0:T(8,128)(2,1)} %get-tuple-element.30) | copy-start | bytes 3244036
  21.9 26.5 %copy-start.2 = (s32[1,16]{1,0:T(1,128)S(1)}, s32[1,16]{1,0:T(1,128)}, u32[]{:S(2)}) copy-start(s32[1,16]{1,0:T(1,128)} %param.11) | copy-start | bytes 196
  21.9 40.3 %copy-start = (bf16[1,3,512,1024]{3,2,1,0:T(8,128)(2,1)S(1)}, bf16[1,3,512,1024]{3,2,1,0:T(8,128)(2,1)}, u32[]{:S(2)}) copy-start(bf16[1,3,512,1024]{3,2,1,0:T(8,128)(2,1)} %param.9) | copy-start | bytes 9437188
  23.8 10.7 %collective-permute-start.5 = (bf16[8,2,64,128]{3,2,1,0:T(8,128)(2,1)S(1)}, bf16[8,2,64,128]{3,2,1,0:T(8,128)(2,1)S(1)}, u32[]{:S(2)}, u32[]{:S(2)}) collective-permute-start(bf16[8,2,64,128]{3,2,1,0:T(8,128)(2,1)S(1)} %get-tuple-element.37), channel_id=1, source_target_pairs={{0,1},{1,0},{2,3},{3,2},{4,5},{5,4},{6,7},{7,6},{8,9},{9,8},{10,11... | collective-permute-start | bytes 786440 | tf_op jit(solution)/shard_map/encode/ppermute | solution.py:18
  34.5 13.8 %collective-permute-start.6 = (bf16[8,2,64,128]{3,2,1,0:T(8,128)(2,1)S(1)}, bf16[8,2,64,128]{3,2,1,0:T(8,128)(2,1)S(1)}, u32[]{:S(2)}, u32[]{:S(2)}) collective-permute-start(bf16[8,2,64,128]{3,2,1,0:T(8,128)(2,1)S(1)} %get-tuple-element.39), channel_id=1, source_target_pairs={{0,2},{1,3},{2,0},{3,1},{4,6},{5,7},{6,4},{7,5},{8,10},{9,11},{10,... | collective-permute-start | bytes 786440 | tf_op jit(solution)/shard_map/encode/ppermute | solution.py:18
  36.8 31.7 %collective-permute-start = (bf16[528,1024]{1,0:T(8,128)(2,1)S(1)}, bf16[528,1024]{1,0:T(8,128)(2,1)S(1)}, u32[]{:S(2)}, u32[]{:S(2)}) collective-permute-start(bf16[528,1024]{1,0:T(8,128)(2,1)S(1)} %copy-done.6), channel_id=1, source_target_pairs={{0,4},{4,8},{8,12},{12,16},{16,20},{20,24},{24,28},{1,5},{5,9},{9,... | collective-permute-start | bytes 3244040 | tf_op jit(solution)/shard_map/decoder_weights/ppermute | solution.py:23
  49.0 6.4 %collective-permute-start.7 = (bf16[8,2,64,128]{3,2,1,0:T(8,128)(2,1)S(1)}, bf16[8,2,64,128]{3,2,1,0:T(8,128)(2,1)S(1)}, u32[]{:S(2)}, u32[]{:S(2)}) collective-permute-start(bf16[8,2,64,128]{3,2,1,0:T(8,128)(2,1)S(1)} %activate.1.own_early.refs_0_), channel_id=1, source_target_pairs={{0,1},{1,0},{2,3},{3,2},{4,5},{5,4},{6,7},{7,6},{8,9},{9,8},{10,11... | collective-permute-start | bytes 786440 | tf_op jit(solution)/shard_map/spread/ppermute | solution.py:18
  49.1 13.1 %collective-permute-start.8 = (bf16[8,2,64,128]{3,2,1,0:T(8,128)(2,1)S(1)}, bf16[8,2,64,128]{3,2,1,0:T(8,128)(2,1)S(1)}, u32[]{:S(2)}, u32[]{:S(2)}) collective-permute-start(bf16[8,2,64,128]{3,2,1,0:T(8,128)(2,1)S(1)} %activate.1.own_early.refs_0_), channel_id=1, source_target_pairs={{0,8},{4,12},{8,16},{12,20},{16,24},{20,28},{1,9},{5,13},{9,17},{1... | collective-permute-start | bytes 786440 | tf_op jit(solution)/shard_map/spread/ppermute | solution.py:23
  55.4 11.2 %collective-permute-start.9 = (bf16[8,2,64,128]{3,2,1,0:T(8,128)(2,1)S(1)}, bf16[8,2,64,128]{3,2,1,0:T(8,128)(2,1)S(1)}, u32[]{:S(2)}, u32[]{:S(2)}) collective-permute-start(bf16[8,2,64,128]{3,2,1,0:T(8,128)(2,1)S(1)} %collective-permute-done.7.own_late.refs_1_), channel_id=1, source_target_pairs={{0,8},{4,12},{8,16},{12,20},{16,24},{20,28},{1,9},{5,13},{9,17},{1... | collective-permute-start | bytes 786440 | tf_op jit(solution)/shard_map/spread/ppermute | solution.py:23
  66.6 3.4 %collective-permute-start.10 = (bf16[16,2,64,128]{3,2,1,0:T(8,128)(2,1)S(1)}, bf16[16,2,64,128]{3,2,1,0:T(8,128)(2,1)S(1)}, u32[]{:S(2)}, u32[]{:S(2)}) collective-permute-start(bf16[16,2,64,128]{3,2,1,0:T(8,128)(2,1)S(1)} %choose.1), channel_id=1, source_target_pairs={{0,4},{4,0},{8,12},{12,8},{16,20},{20,16},{24,28},{28,24},{1,5},{5... | collective-permute-start | bytes 1572872 | tf_op jit(solution)/shard_map/decode/ppermute | solution.py:28

commit v5 on v4

--- a/solution.py
+++ b/solution.py
@@ -18,6 +18,11 @@
     return lax.ppermute(value, "latent", [(i, i ^ step) for i in range(count)])
 
 
+def rotated(value, step):
+    count = lax.axis_size("latent")
+    return lax.ppermute(value, "latent", [(i, (i + step) % count) for i in range(count)])
+
+
 def passed_along(value, steps):
     count = lax.axis_size("layer")
     return lax.ppermute(value, "layer", [(i, i + steps) for i in range(count - steps)])
@@ -41,7 +46,7 @@
 def fetch_rows_kernel(encoder_ref, *piece_refs):
     depth = piece_refs[0].shape[0]
     for step, piece in enumerate(piece_refs):
-        first = pl.multiple_of(lax.bitwise_xor(lax.axis_index("latent"), step) * depth, depth)
+        first = pl.multiple_of(lax.rem(lax.axis_index("latent") + step, len(piece_refs)) * depth, depth)
         piece[...] = encoder_ref[pl.ds(first, depth), :]
 
 
@@ -85,7 +90,7 @@
     )(ids, decoder)
 
 
-def encode_kernel(parts, lists_ref, bias_ref, x_ref, *refs):
+def encode_kernel(parts, lists_ref, counts_ref, bias_ref, x_ref, *refs):
     weight_refs, (kept_ref, sent_ref, partial) = refs[:parts], refs[parts:]
     width = bias_ref.shape[1]
     held, slots, rows, _ = kept_ref.shape
@@ -101,11 +106,14 @@
             tile = held_group(first + position // tiles, parts) * tiles + position % tiles
             row = pl.multiple_of(tile * rows, rows)
             for slot in range(slots):
-                source = lax.bitwise_xor(lax.axis_index("latent"), lists_ref[slot, tile])
-                out_ref[position, slot] = partial[source, pl.ds(row, rows), :].astype(out_ref.dtype)
-
-
-def encode(lists, bias, x, weights):
+                source = lax.rem(lax.axis_index("latent") - lists_ref[slot, tile] + parts, parts)
+                kept = partial[source, pl.ds(row, rows), :]
+                if out_ref is kept_ref:
+                    kept = kept + jnp.where(slot < counts_ref[tile], 0.0, -1e30)
+                out_ref[position, slot] = kept.astype(out_ref.dtype)
+
+
+def encode(lists, counts, bias, x, weights):
     parts = len(weights)
     tokens, depth = x.shape
     width = bias.shape[1]
@@ -114,7 +122,7 @@
     return pl.pallas_call(
         functools.partial(encode_kernel, parts),
         out_shape=[jax.ShapeDtypeStruct(shape, jnp.float32), jax.ShapeDtypeStruct(shape, jnp.bfloat16)],
-        in_specs=[SMEM] + [VMEM] * (2 + parts),
+        in_specs=[SMEM] * 2 + [VMEM] * (2 + parts),
         out_specs=[VMEM] * 2,
         scratch_shapes=[pltpu.VMEM((parts, tokens, width), jnp.float32)],
         cost_estimate=pl.CostEstimate(
@@ -123,7 +131,7 @@
             transcendentals=0,
         ),
         **small("encode", 16),
-    )(lists, bias, x, *weights)
+    )(lists, counts, bias, x, *weights)
 
 
 def merge_kernel(kept_ref, arrived_ref, total_ref, sent_ref):
@@ -142,25 +150,19 @@
     )(kept, arrived)
 
 
-def activate_kernel(parts, counts_ref, kept_ref, arrived_ref, act_ref):
-    held, slots, _, _ = kept_ref.shape
-    tiles = 2 * held // parts
-    for position in range(held):
-        tile = held_group(position // tiles, parts) * tiles + position % tiles
-        for slot in range(slots):
-            live = (slot < counts_ref[tile]).astype(jnp.float32)
-            preact = kept_ref[position, slot] + arrived_ref[position, slot].astype(jnp.float32)
-            act_ref[position, slot] = (jnp.maximum(preact, 0.0) * live).astype(act_ref.dtype)
-
-
-def activate(counts, kept, arrived, parts):
-    return pl.pallas_call(
-        functools.partial(activate_kernel, parts),
+def activate_kernel(kept_ref, arrived_ref, act_ref):
+    preact = kept_ref[...] + arrived_ref[...].astype(jnp.float32)
+    act_ref[...] = jnp.maximum(preact, 0.0).astype(act_ref.dtype)
+
+
+def activate(kept, arrived):
+    return pl.pallas_call(
+        activate_kernel,
         out_shape=jax.ShapeDtypeStruct(kept.shape, arrived.dtype),
-        in_specs=[SMEM] + [VMEM] * 2,
+        in_specs=[VMEM] * 2,
         out_specs=VMEM,
         **small("activate"),
-    )(counts, kept, arrived)
+    )(kept, arrived)
 
 
 def choose_kernel(*refs):
@@ -333,7 +335,7 @@
         pieces, decoder = lax.optimization_barrier((pieces, decoder))
         weights = [pieces[0]] + [None] * (parts - 1)
         for step in sorted(range(1, parts), reverse=True):
-            weights[step] = swapped(pieces[step], step)
+            weights[step] = rotated(pieces[step], step)
     with jax.named_scope("decoder_weights"):
         near_rows, far_rows = fetch_decoders(lists, decoder)
         near_decoder, far_decoder = passed_along(near_rows, 1), passed_along(far_rows, 2)
@@ -342,14 +344,14 @@
         ]
 
     with jax.named_scope("encode"):
-        kept, sent = encode(lists, enc_bias, x, weights)
+        kept, sent = encode(lists, counts, enc_bias, x, weights)
         arrived = swapped(sent, 1)
         step = 2
         while step < parts:
             kept, sent = merge(kept, arrived)
             arrived = swapped(sent, step)
             step *= 2
-        own = activate(counts, kept, arrived, parts)
+        own = activate(kept, arrived)
     with jax.named_scope("spread"):
         late_own = swapped(own, 1)
         far = passed_along(own, 2)

time: 73.5 us -> 74 us (level)
  waiting for transfers between devices: 27.8 us -> 29.5 us
    ppermute x0 -> x3, waiting for transfers between devices: none -> 8.58 us  [rotated(): lax.ppermute(value, 'latent', [(i, (i + step) % count) for i in range(cou...]
    ppermute x6 -> x3, starting transfers between devices: 11.9 us -> 6.1 us  [swapped(): return lax.ppermute(value, 'latent', [(i, i ^ step) for i in range(count)])]
    ppermute x0 -> x3, starting transfers between devices: none -> 4.73 us  [rotated(): lax.ppermute(value, 'latent', [(i, (i + step) % count) for i in range(cou...]
    ppermute x6 -> x3, waiting for transfers between devices: 22.3 us -> 18.6 us  [swapped(): return lax.ppermute(value, 'latent', [(i, i ^ step) for i in range(count)])]
    ppermute x4, waiting for transfers between devices: 5.33 us -> 2.14 us  [passed_along(): lax.ppermute(value, 'layer', [(i, i + steps) for i in range(count - steps)])]
    ppermute x1, starting transfers between devices: 1.89 us -> 3.57 us  [across_cores(): return lax.ppermute(value, 'layer', [(i, i ^ 1) for i in range(count)])]
    ppermute x4, starting transfers between devices: 15.4 us -> 14.1 us  [passed_along(): lax.ppermute(value, 'layer', [(i, i + steps) for i in range(count - steps)])]
  transfers between devices with their start and end apart: 11 -> 11, of which waited for: 8 -> 6; matrix products, arithmetic and copies ran while one was open for 2% -> 2% of each run, Pallas kernels for 14% -> 13%
where the time goes in v5:
time: 74 us; the launch traced here: 73.7 us
  waiting for transfers between devices  29.5 us (40%)
  starting transfers between devices  28.4 us (38%)
  Pallas kernels  13 us (18%)
  local copies, waits for them, and re-layouts  1.87 us (3%)
    ppermute x3, waiting for transfers between devices, swapped(): return lax.ppermute(value, 'latent', [(i, i ^ step) for i in range(count)])  18.6 us
    ppermute x4, starting transfers between devices, passed_along(): lax.ppermute(value, 'layer', [(i, i + steps) for i in range(count - steps)])  14.1 us
    ppermute x3, waiting for transfers between devices, rotated(): lax.ppermute(value, 'latent', [(i, (i + step) % count) for i in range(cou...  8.58 us
    ppermute x3, starting transfers between devices, swapped(): return lax.ppermute(value, 'latent', [(i, i ^ step) for i in range(count)])  6.1 us
    ppermute x3, starting transfers between devices, rotated(): lax.ppermute(value, 'latent', [(i, (i + step) % count) for i in range(cou...  4.73 us
    pallas_call x1, Pallas kernels, fetch_decoders(): pl.pallas_call(fetch_decoders_kernel, out_shape=[shape] * (targets - 1),...  3.67 us
    ppermute x1, starting transfers between devices, across_cores(): return lax.ppermute(value, 'layer', [(i, i ^ 1) for i in range(count)])  3.57 us
    pallas_call x1, Pallas kernels, decode_late(): pl.pallas_call(functools.partial(late_kernel, parts), out_shape=jax.Shape...  3.16 us
  transfers between devices with their start and end apart: 11, of which 6 were waited for; matrix products, arithmetic and copies ran while one was open for 2% of the time, Pallas kernels for 13%

profile of v5, /device:TPU:5, one launch (start us, length us, event | category | flops | bytes accessed | tf_op | source)
XLA Modules:
  0.0 73.7 jit_solution(1693557954218813779)
XLA Ops:
  0.0 0.0 copy-start.1
  0.0 1.2 %copy-done.1 = bf16[1,4096,128]{2,1,0:T(8,128)(2,1)S(1)} copy-done((bf16[1,4096,128]{2,1,0:T(8,128)(2,1)S(1)}, bf16[1,4096,128]{2,1,0:T(8,128)(2,1)}, u32[]{:S(2)}) %copy-start.1) | copy-done | bytes 1048600
  1.2 0.0 copy-start.2
  1.2 0.0 copy-start.3
  1.2 0.0 copy-start.4
  1.2 0.0 copy-start.5
  1.2 0.1 fetch_rows.1
  1.3 1.3 %collective-permute-start.2 = (bf16[1024,128]{1,0:T(8,128)(2,1)S(1)}, bf16[1024,128]{1,0:T(8,128)(2,1)S(1)}, u32[]{:S(2)}, u32[]{:S(2)}) collective-permute-start(bf16[1024,128]{1,0:T(8,128)(2,1)S(1)} %get-tuple-element.33), channel_id=1, source_target_pairs={{0,1},{1,2},{2,3},{3,0},{4,5},{5,6},{6,7},{7,4},{8,9},{9,10},{10,1... | collective-permute-start | bytes 786440 | tf_op jit(solution)/shard_map/encoder_rows/ppermute | solution.py:23
  2.7 2.3 %collective-permute-start.3 = (bf16[1024,128]{1,0:T(8,128)(2,1)S(1)}, bf16[1024,128]{1,0:T(8,128)(2,1)S(1)}, u32[]{:S(2)}, u32[]{:S(2)}) collective-permute-start(bf16[1024,128]{1,0:T(8,128)(2,1)S(1)} %get-tuple-element.34), channel_id=1, source_target_pairs={{0,2},{1,3},{2,0},{3,1},{4,6},{5,7},{6,4},{7,5},{8,10},{9,11},{10,... | collective-permute-start | bytes 786440 | tf_op jit(solution)/shard_map/encoder_rows/ppermute | solution.py:23
  5.0 1.1 %collective-permute-start.4 = (bf16[1024,128]{1,0:T(8,128)(2,1)S(1)}, bf16[1024,128]{1,0:T(8,128)(2,1)S(1)}, u32[]{:S(2)}, u32[]{:S(2)}) collective-permute-start(bf16[1024,128]{1,0:T(8,128)(2,1)S(1)} %get-tuple-element.35), channel_id=1, source_target_pairs={{0,3},{1,0},{2,1},{3,2},{4,7},{5,4},{6,5},{7,6},{8,11},{9,8},{10,9... | collective-permute-start | bytes 786440 | tf_op jit(solution)/shard_map/encoder_rows/ppermute | solution.py:23
  6.1 0.7 bitcast_convert_fusion
  6.7 0.6 pad.4.lists_ref
  7.4 3.7 %fetch_decoders.1 = (bf16[528,1024]{1,0:T(8,128)(2,1)}, bf16[528,1024]{1,0:T(8,128)(2,1)}) custom-call(bf16[16,1024]{1,0:T(8,128)(2,1)} %pad.4.lists_ref, bf16[3,512,1024]{2,1,0:T(8,128)(2,1)} %bitcast.9), custom_call_target="tpu_custom_call" | custom-call | tf_op jit(solution)/shard_map/decoder_weights/fetch_decoders/pallas_call | solution.py:83
  11.0 3.1 %collective-permute-start.1 = (bf16[528,1024]{1,0:T(8,128)(2,1)}, bf16[528,1024]{1,0:T(8,128)(2,1)S(1)}, u32[]{:S(2)}, u32[]{:S(2)}) collective-permute-start(bf16[528,1024]{1,0:T(8,128)(2,1)} %get-tuple-element.31), channel_id=1, source_target_pairs={{0,8},{4,12},{8,16},{12,20},{16,24},{20,28},{1,9},{5,13},{9,17},{1... | collective-permute-start | bytes 3244040 | tf_op jit(solution)/shard_map/decoder_weights/ppermute | solution.py:28
  14.2 0.0 collective-permute-done.2.refs_1_
  14.2 8.6 %collective-permute-done.3.refs_2_ = bf16[1024,128]{1,0:T(8,128)(2,1)S(1)} collective-permute-done((bf16[1024,128]{1,0:T(8,128)(2,1)S(1)}, bf16[1024,128]{1,0:T(8,128)(2,1)S(1)}, u32[]{:S(2)}, u32[]{:S(2)}) %collective-permute-start.3) | collective-permute-done | bytes 262176 | tf_op jit(solution)/shard_map/encoder_rows/ppermute | solution.py:23
  22.7 0.0 collective-permute-done.4.refs_3_
  22.8 0.0 copy-done.2
  22.8 0.0 copy-done.3
  22.8 0.0 copy-done.4
  22.8 0.0 copy-done.5
  22.8 0.0 copy-start.6
  22.8 0.0 copy-start
  22.8 1.9 %encode.1 = (f32[8,2,64,128]{3,2,1,0:T(8,128)S(1)}, bf16[8,2,64,128]{3,2,1,0:T(8,128)(2,1)S(1)}) custom-call(s32[2,16]{1,0:T(2,128)S(1)} %bitcast.13, s32[16]{0:T(128)S(1)} %bitcast.15, f32[1,128]{1,0:T(1,128)S(1)} %copy-done.5, bf16[1024,1024]{1,0:T(8,128)(2,1)S(1)} %bitcast.12, bf16[1024,128]{1,0:T(8,128)(2,1)S(1)} %get-tuple-element.32.refs_0_, ...), custom_call_target="tpu_custom_call" | custom-call | flops 1073741824 | bytes 3145728 | tf_op jit(solution)/shard_map/encode/encode/pallas_call | solution.py:122
  24.7 6.0 %collective-permute-start.5 = (bf16[8,2,64,128]{3,2,1,0:T(8,128)(2,1)S(1)}, bf16[8,2,64,128]{3,2,1,0:T(8,128)(2,1)S(1)}, u32[]{:S(2)}, u32[]{:S(2)}) collective-permute-start(bf16[8,2,64,128]{3,2,1,0:T(8,128)(2,1)S(1)} %get-tuple-element.37), channel_id=1, source_target_pairs={{0,1},{1,0},{2,3},{3,2},{4,5},{5,4},{6,7},{7,6},{8,9},{9,8},{10,11... | collective-permute-start | bytes 786440 | tf_op jit(solution)/shard_map/encode/ppermute | solution.py:18
  30.7 6.2 %collective-permute-done.5.arrived_ref = bf16[8,2,64,128]{3,2,1,0:T(8,128)(2,1)S(1)} collective-permute-done((bf16[8,2,64,128]{3,2,1,0:T(8,128)(2,1)S(1)}, bf16[8,2,64,128]{3,2,1,0:T(8,128)(2,1)S(1)}, u32[]{:S(2)}, u32[]{:S(2)}) %collective-permute-start.5) | collective-permute-done | bytes 262176 | tf_op jit(solution)/shard_map/encode/ppermute | solution.py:18
  36.9 0.1 merge.1
  37.0 0.1 collective-permute-start.6
  37.1 0.0 copy-done.6
  37.1 4.7 %collective-permute-start = (bf16[528,1024]{1,0:T(8,128)(2,1)S(1)}, bf16[528,1024]{1,0:T(8,128)(2,1)S(1)}, u32[]{:S(2)}, u32[]{:S(2)}) collective-permute-start(bf16[528,1024]{1,0:T(8,128)(2,1)S(1)} %copy-done.6), channel_id=1, source_target_pairs={{0,4},{4,8},{8,12},{12,16},{16,20},{20,24},{24,28},{1,5},{5,9},{9,... | collective-permute-start | bytes 3244040 | tf_op jit(solution)/shard_map/decoder_weights/ppermute | solution.py:28
  41.8 9.1 %collective-permute-done.6.arrived_ref = bf16[8,2,64,128]{3,2,1,0:T(8,128)(2,1)S(1)} collective-permute-done((bf16[8,2,64,128]{3,2,1,0:T(8,128)(2,1)S(1)}, bf16[8,2,64,128]{3,2,1,0:T(8,128)(2,1)S(1)}, u32[]{:S(2)}, u32[]{:S(2)}) %collective-permute-start.6) | collective-permute-done | bytes 262176 | tf_op jit(solution)/shard_map/encode/ppermute | solution.py:18
  50.9 0.1 activate.1.own_early.refs_0_
  50.9 0.1 collective-permute-start.7
  51.0 3.1 %collective-permute-start.8 = (bf16[8,2,64,128]{3,2,1,0:T(8,128)(2,1)S(1)}, bf16[8,2,64,128]{3,2,1,0:T(8,128)(2,1)S(1)}, u32[]{:S(2)}, u32[]{:S(2)}) collective-permute-start(bf16[8,2,64,128]{3,2,1,0:T(8,128)(2,1)S(1)} %activate.1.own_early.refs_0_), channel_id=1, source_target_pairs={{0,8},{4,12},{8,16},{12,20},{16,24},{20,28},{1,9},{5,13},{9,17},{1... | collective-permute-start | bytes 786440 | tf_op jit(solution)/shard_map/spread/ppermute | solution.py:28
  54.2 3.2 %collective-permute-done.7.own_late.refs_1_ = bf16[8,2,64,128]{3,2,1,0:T(8,128)(2,1)S(1)} collective-permute-done((bf16[8,2,64,128]{3,2,1,0:T(8,128)(2,1)S(1)}, bf16[8,2,64,128]{3,2,1,0:T(8,128)(2,1)S(1)}, u32[]{:S(2)}, u32[]{:S(2)}) %collective-permute-start.7) | collective-permute-done | bytes 262176 | tf_op jit(solution)/shard_map/spread/ppermute | solution.py:18
  57.4 3.1 %collective-permute-start.9 = (bf16[8,2,64,128]{3,2,1,0:T(8,128)(2,1)S(1)}, bf16[8,2,64,128]{3,2,1,0:T(8,128)(2,1)S(1)}, u32[]{:S(2)}, u32[]{:S(2)}) collective-permute-start(bf16[8,2,64,128]{3,2,1,0:T(8,128)(2,1)S(1)} %collective-permute-done.7.own_late.refs_1_), channel_id=1, source_target_pairs={{0,8},{4,12},{8,16},{12,20},{16,24},{20,28},{1,9},{5,13},{9,17},{1... | collective-permute-start | bytes 786440 | tf_op jit(solution)/shard_map/spread/ppermute | solution.py:28
  60.5 0.0 collective-permute-done.1.far_dec
  60.5 0.0 collective-permute-done.8.far.refs_2_
  60.5 0.0 copy-done
  60.5 2.7 %decode_early.1 = (f32[512,1024]{1,0:T(8,128)S(1)}, f32[512,1024]{1,0:T(8,128)S(1)}) custom-call(s32[2,16]{1,0:T(2,128)S(1)} %bitcast.14, s32[2,16]{1,0:T(2,128)S(1)} %slice_convert_fusion.far_lists.lists_ref, bf16[8,2,64,128]{3,2,1,0:T(8,128)(2,1)S(1)} %activate.1.own_early.refs_0_, bf16[8,2,64,128]{3,2,1,0:T(8,128)(2,1)S(1)} %collective-permute-done.7.own_late.refs_1_, ...), custom_call_target="tpu_custom_call" | custom-call | flops 1610612736 | bytes 6291456 | tf_op jit(solution)/shard_map/decode/decode_early/pallas_call | solution.py:232
  63.3 2.1 %collective-permute-done.9.far.refs_3_ = bf16[8,2,64,128]{3,2,1,0:T(8,128)(2,1)S(1)} collective-permute-done((bf16[8,2,64,128]{3,2,1,0:T(8,128)(2,1)S(1)}, bf16[8,2,64,128]{3,2,1,0:T(8,128)(2,1)S(1)}, u32[]{:S(2)}, u32[]{:S(2)}) %collective-permute-start.9) | collective-permute-done | bytes 262176 | tf_op jit(solution)/shard_map/spread/ppermute | solution.py:28
  65.4 3.6 %collective-permute-start.10 = (bf16[16,2,64,128]{3,2,1,0:T(8,128)(2,1)S(1)}, bf16[16,2,64,128]{3,2,1,0:T(8,128)(2,1)S(1)}, u32[]{:S(2)}, u32[]{:S(2)}) collective-permute-start(bf16[16,2,64,128]{3,2,1,0:T(8,128)(2,1)S(1)} %choose.1), channel_id=1, source_target_pairs={{0,4},{4,0},{8,12},{12,8},{16,20},{20,16},{24,28},{28,24},{1,5},{5... | collective-permute-start | bytes 1572872 | tf_op jit(solution)/shard_map/decode/ppermute | solution.py:33
  69.0 0.0 collective-permute-done.near_dec
  69.0 1.3 %decode_middle.1.late_ref = f32[512,1024]{1,0:T(8,128)S(1)} custom-call(s32[2,16]{1,0:T(2,128)S(1)} %slice_convert_fusion.far_lists.lists_ref, f32[512,1024]{1,0:T(8,128)S(1)} %get-tuple-element.43.partial_ref, bf16[8,2,64,128]{3,2,1,0:T(8,128)(2,1)S(1)} %collective-permute-done.9.far.refs_3_, bf16[528,1024]{1,0:T(8,128)(2,1)S(1)} %collective-permute-done.1.far_dec), custom_call_target="tpu_custom_call" | custom-call | flops 536870912 | bytes 5242880 | tf_op jit(solution)/shard_map/decode/decode_middle/pallas_call | solution.py:264
  70.3 0.2 collective-permute-done.10.near
  70.5 3.2 %decode_late.1 = bf16[1024,1024]{1,0:T(8,128)(2,1)} custom-call(s32[2,16]{1,0:T(2,128)S(1)} %slice_convert_fusion.1.lists_ref, f32[512,1024]{1,0:T(8,128)S(1)} %get-tuple-element.42.early_ref, f32[512,1024]{1,0:T(8,128)S(1)} %decode_middle.1.late_ref, bf16[16,2,64,128]{3,2,1,0:T(8,128)(2,1)S(1)} %collective-permute-done.10.near, ...), custom_call_target="tpu_custom_call" | custom-call | flops 1073741824 | bytes 7340032 | tf_op jit(solution)/shard_map/decode/decode_late/pallas_call | solution.py:305
  (3 shorter events, 0.0 us)
Async XLA Ops:
  0.0 1.2 %copy-start.1 = (bf16[1,4096,128]{2,1,0:T(8,128)(2,1)S(1)}, bf16[1,4096,128]{2,1,0:T(8,128)(2,1)}, u32[]{:S(2)}) copy-start(bf16[1,4096,128]{2,1,0:T(8,128)(2,1)} %param.7) | copy-start | bytes 3145732
  1.2 21.5 %copy-start.2 = (bf16[1,1024,1024]{2,1,0:T(8,128)(2,1)S(1)}, bf16[1,1024,1024]{2,1,0:T(8,128)(2,1)}, u32[]{:S(2)}) copy-start(bf16[1,1024,1024]{2,1,0:T(8,128)(2,1)} %param.6) | copy-start | bytes 6291460
  1.2 21.5 %copy-start.3 = (s32[1,16,2]{1,2,0:T(2,128)S(1)}, s32[1,16,2]{1,2,0:T(2,128)}, u32[]{:S(2)}) copy-start(s32[1,16,2]{1,2,0:T(2,128)} %param.10) | copy-start | bytes 388
  1.2 21.5 %copy-start.4 = (s32[1,16]{1,0:T(1,128)S(1)}, s32[1,16]{1,0:T(1,128)}, u32[]{:S(2)}) copy-start(s32[1,16]{1,0:T(1,128)} %param.11) | copy-start | bytes 196
  1.2 21.5 %copy-start.5 = (f32[1,128]{1,0:T(1,128)S(1)}, f32[1,128]{1,0:T(1,128)}, u32[]{:S(2)}) copy-start(f32[1,128]{1,0:T(1,128)} %bias_ref.1) | copy-start | bytes 1540
  1.3 12.8 %collective-permute-start.2 = (bf16[1024,128]{1,0:T(8,128)(2,1)S(1)}, bf16[1024,128]{1,0:T(8,128)(2,1)S(1)}, u32[]{:S(2)}, u32[]{:S(2)}) collective-permute-start(bf16[1024,128]{1,0:T(8,128)(2,1)S(1)} %get-tuple-element.33), channel_id=1, source_target_pairs={{0,1},{1,2},{2,3},{3,0},{4,5},{5,6},{6,7},{7,4},{8,9},{9,10},{10,1... | collective-permute-start | bytes 786440 | tf_op jit(solution)/shard_map/encoder_rows/ppermute | solution.py:23
  2.7 20.1 %collective-permute-start.3 = (bf16[1024,128]{1,0:T(8,128)(2,1)S(1)}, bf16[1024,128]{1,0:T(8,128)(2,1)S(1)}, u32[]{:S(2)}, u32[]{:S(2)}) collective-permute-start(bf16[1024,128]{1,0:T(8,128)(2,1)S(1)} %get-tuple-element.34), channel_id=1, source_target_pairs={{0,2},{1,3},{2,0},{3,1},{4,6},{5,7},{6,4},{7,5},{8,10},{9,11},{10,... | collective-permute-start | bytes 786440 | tf_op jit(solution)/shard_map/encoder_rows/ppermute | solution.py:23
  5.0 17.8 %collective-permute-start.4 = (bf16[1024,128]{1,0:T(8,128)(2,1)S(1)}, bf16[1024,128]{1,0:T(8,128)(2,1)S(1)}, u32[]{:S(2)}, u32[]{:S(2)}) collective-permute-start(bf16[1024,128]{1,0:T(8,128)(2,1)S(1)} %get-tuple-element.35), channel_id=1, source_target_pairs={{0,3},{1,0},{2,1},{3,2},{4,7},{5,4},{6,5},{7,6},{8,11},{9,8},{10,9... | collective-permute-start | bytes 786440 | tf_op jit(solution)/shard_map/encoder_rows/ppermute | solution.py:23
  11.0 49.5 %collective-permute-start.1 = (bf16[528,1024]{1,0:T(8,128)(2,1)}, bf16[528,1024]{1,0:T(8,128)(2,1)S(1)}, u32[]{:S(2)}, u32[]{:S(2)}) collective-permute-start(bf16[528,1024]{1,0:T(8,128)(2,1)} %get-tuple-element.31), channel_id=1, source_target_pairs={{0,8},{4,12},{8,16},{12,20},{16,24},{20,28},{1,9},{5,13},{9,17},{1... | collective-permute-start | bytes 3244040 | tf_op jit(solution)/shard_map/decoder_weights/ppermute | solution.py:28
  22.8 14.3 %copy-start.6 = (bf16[528,1024]{1,0:T(8,128)(2,1)S(1)}, bf16[528,1024]{1,0:T(8,128)(2,1)}, u32[]{:S(2)}) copy-start(bf16[528,1024]{1,0:T(8,128)(2,1)} %get-tuple-element.30) | copy-start | bytes 3244036
  22.8 37.8 %copy-start = (bf16[1,3,512,1024]{3,2,1,0:T(8,128)(2,1)S(1)}, bf16[1,3,512,1024]{3,2,1,0:T(8,128)(2,1)}, u32[]{:S(2)}) copy-start(bf16[1,3,512,1024]{3,2,1,0:T(8,128)(2,1)} %param.9) | copy-start | bytes 9437188
  24.7 12.2 %collective-permute-start.5 = (bf16[8,2,64,128]{3,2,1,0:T(8,128)(2,1)S(1)}, bf16[8,2,64,128]{3,2,1,0:T(8,128)(2,1)S(1)}, u32[]{:S(2)}, u32[]{:S(2)}) collective-permute-start(bf16[8,2,64,128]{3,2,1,0:T(8,128)(2,1)S(1)} %get-tuple-element.37), channel_id=1, source_target_pairs={{0,1},{1,0},{2,3},{3,2},{4,5},{5,4},{6,7},{7,6},{8,9},{9,8},{10,11... | collective-permute-start | bytes 786440 | tf_op jit(solution)/shard_map/encode/ppermute | solution.py:18
  37.0 13.9 %collective-permute-start.6 = (bf16[8,2,64,128]{3,2,1,0:T(8,128)(2,1)S(1)}, bf16[8,2,64,128]{3,2,1,0:T(8,128)(2,1)S(1)}, u32[]{:S(2)}, u32[]{:S(2)}) collective-permute-start(bf16[8,2,64,128]{3,2,1,0:T(8,128)(2,1)S(1)} %get-tuple-element.39), channel_id=1, source_target_pairs={{0,2},{1,3},{2,0},{3,1},{4,6},{5,7},{6,4},{7,5},{8,10},{9,11},{10,... | collective-permute-start | bytes 786440 | tf_op jit(solution)/shard_map/encode/ppermute | solution.py:18
  37.1 31.9 %collective-permute-start = (bf16[528,1024]{1,0:T(8,128)(2,1)S(1)}, bf16[528,1024]{1,0:T(8,128)(2,1)S(1)}, u32[]{:S(2)}, u32[]{:S(2)}) collective-permute-start(bf16[528,1024]{1,0:T(8,128)(2,1)S(1)} %copy-done.6), channel_id=1, source_target_pairs={{0,4},{4,8},{8,12},{12,16},{16,20},{20,24},{24,28},{1,5},{5,9},{9,... | collective-permute-start | bytes 3244040 | tf_op jit(solution)/shard_map/decoder_weights/ppermute | solution.py:28
  50.9 6.4 %collective-permute-start.7 = (bf16[8,2,64,128]{3,2,1,0:T(8,128)(2,1)S(1)}, bf16[8,2,64,128]{3,2,1,0:T(8,128)(2,1)S(1)}, u32[]{:S(2)}, u32[]{:S(2)}) collective-permute-start(bf16[8,2,64,128]{3,2,1,0:T(8,128)(2,1)S(1)} %activate.1.own_early.refs_0_), channel_id=1, source_target_pairs={{0,1},{1,0},{2,3},{3,2},{4,5},{5,4},{6,7},{7,6},{8,9},{9,8},{10,11... | collective-permute-start | bytes 786440 | tf_op jit(solution)/shard_map/spread/ppermute | solution.py:18
  51.0 9.5 %collective-permute-start.8 = (bf16[8,2,64,128]{3,2,1,0:T(8,128)(2,1)S(1)}, bf16[8,2,64,128]{3,2,1,0:T(8,128)(2,1)S(1)}, u32[]{:S(2)}, u32[]{:S(2)}) collective-permute-start(bf16[8,2,64,128]{3,2,1,0:T(8,128)(2,1)S(1)} %activate.1.own_early.refs_0_), channel_id=1, source_target_pairs={{0,8},{4,12},{8,16},{12,20},{16,24},{20,28},{1,9},{5,13},{9,17},{1... | collective-permute-start | bytes 786440 | tf_op jit(solution)/shard_map/spread/ppermute | solution.py:28
  57.4 8.0 %collective-permute-start.9 = (bf16[8,2,64,128]{3,2,1,0:T(8,128)(2,1)S(1)}, bf16[8,2,64,128]{3,2,1,0:T(8,128)(2,1)S(1)}, u32[]{:S(2)}, u32[]{:S(2)}) collective-permute-start(bf16[8,2,64,128]{3,2,1,0:T(8,128)(2,1)S(1)} %collective-permute-done.7.own_late.refs_1_), channel_id=1, source_target_pairs={{0,8},{4,12},{8,16},{12,20},{16,24},{20,28},{1,9},{5,13},{9,17},{1... | collective-permute-start | bytes 786440 | tf_op jit(solution)/shard_map/spread/ppermute | solution.py:28
  65.4 5.1 %collective-permute-start.10 = (bf16[16,2,64,128]{3,2,1,0:T(8,128)(2,1)S(1)}, bf16[16,2,64,128]{3,2,1,0:T(8,128)(2,1)S(1)}, u32[]{:S(2)}, u32[]{:S(2)}) collective-permute-start(bf16[16,2,64,128]{3,2,1,0:T(8,128)(2,1)S(1)} %choose.1), channel_id=1, source_target_pairs={{0,4},{4,0},{8,12},{12,8},{16,20},{20,16},{24,28},{28,24},{1,5},{5... | collective-permute-start | bytes 1572872 | tf_op jit(solution)/shard_map/decode/ppermute | solution.py:33

commit v6 on v5

--- a/solution.py
+++ b/solution.py
@@ -62,32 +62,28 @@
 
 
 def fetch_decoders_kernel(lists_ref, decoder_ref, *refs):
-    out_refs, sems = refs[:-1], refs[-1]
+    out_refs, ids = refs[:-1], refs[-1]
     latents = decoder_ref.shape[1]
-    copies = []
+    slots, tiles = lists_ref.shape
+    ids[...] = jnp.zeros_like(ids)
+    ids[:slots, :tiles] = lists_ref[...].astype(jnp.float32)
     for number, out_ref in enumerate(out_refs):
-        copies.append(
-            pltpu.make_async_copy(decoder_ref.at[number + 1], out_ref.at[pl.ds(0, latents)], sems.at[number])
-        )
-        copies[-1].start()
-    for out_ref in out_refs:
-        out_ref[latents:, :] = lists_ref[...]
-    for copy in copies:
-        copy.wait()
+        out_ref[:latents, :] = decoder_ref[number + 1]
+        out_ref[latents:, :] = ids[...].astype(out_ref.dtype)
 
 
 def fetch_decoders(lists, decoder):
     targets, latents, features = decoder.shape
-    ids = jnp.pad(lists.astype(decoder.dtype), ((0, -lists.shape[0] % 16), (0, features - lists.shape[1])))
-    shape = jax.ShapeDtypeStruct((latents + ids.shape[0], features), decoder.dtype)
+    rows = lists.shape[0] + -lists.shape[0] % 16
+    shape = jax.ShapeDtypeStruct((latents + rows, features), decoder.dtype)
     return pl.pallas_call(
         fetch_decoders_kernel,
         out_shape=[shape] * (targets - 1),
-        in_specs=[VMEM, ANY],
+        in_specs=[VMEM, VMEM],
         out_specs=[VMEM] * (targets - 1),
-        scratch_shapes=[pltpu.SemaphoreType.DMA((targets - 1,))],
-        **small("fetch_decoders", 58),
-    )(ids, decoder)
+        scratch_shapes=[pltpu.VMEM((rows, features), jnp.float32)],
+        **small("fetch_decoders", 16),
+    )(lists, decoder)
 
 
 def encode_kernel(parts, lists_ref, counts_ref, bias_ref, x_ref, *refs):
@@ -339,6 +335,7 @@
     with jax.named_scope("decoder_weights"):
         near_rows, far_rows = fetch_decoders(lists, decoder)
         near_decoder, far_decoder = passed_along(near_rows, 1), passed_along(far_rows, 2)
+        near_decoder, far_decoder = lax.optimization_barrier((near_decoder, far_decoder))
         near_lists, far_lists = [
             rows[latents : latents + slots, :tiles].astype(jnp.int32) for rows in (near_decoder, far_decoder)
         ]

time: 74 us -> 73.9 us (level)
  Pallas kernels: 13 us -> 9.46 us
  waiting for transfers between devices: 29.5 us -> 33 us
  local copies, waits for them, and re-layouts: 1.87 us -> 3.81 us
  starting transfers between devices: 28.4 us -> 27.2 us
    ppermute x3, waiting for transfers between devices: 18.6 us -> 23.3 us  [swapped(): return lax.ppermute(value, 'latent', [(i, i ^ step) for i in range(count)])]
    pallas_call x1, Pallas kernels: 3.67 us -> 0.14 us  [fetch_decoders(): pl.pallas_call(fetch_decoders_kernel, out_shape=[shape] * (targets - 1),...]
    unnamed x14, local copies, waits for them, and re-layouts: 1.25 us -> 3.81 us
    ppermute x4, starting transfers between devices: 14.1 us -> 12.8 us  [passed_along(): lax.ppermute(value, 'layer', [(i, i + steps) for i in range(count - steps)])]
    ppermute x3, waiting for transfers between devices: 8.58 us -> 7.38 us  [rotated(): lax.ppermute(value, 'latent', [(i, (i + step) % count) for i in range(cou...]
  transfers between devices with their start and end apart: 11 -> 11, of which waited for: 6 -> 6; matrix products, arithmetic and copies ran while one was open for 2% -> 0% of each run, Pallas kernels for 13% -> 8%
where the time goes in v6:
time: 73.9 us; the launch traced here: 73.6 us
  waiting for transfers between devices  33 us (45%)
  starting transfers between devices  27.2 us (37%)
  Pallas kernels  9.46 us (13%)
  local copies, waits for them, and re-layouts  3.81 us (5%)
    ppermute x3, waiting for transfers between devices, swapped(): return lax.ppermute(value, 'latent', [(i, i ^ step) for i in range(count)])  23.3 us
    ppermute x4, starting transfers between devices, passed_along(): lax.ppermute(value, 'layer', [(i, i + steps) for i in range(count - steps)])  12.8 us
    ppermute x3, waiting for transfers between devices, rotated(): lax.ppermute(value, 'latent', [(i, (i + step) % count) for i in range(cou...  7.38 us
    ppermute x3, starting transfers between devices, swapped(): return lax.ppermute(value, 'latent', [(i, i ^ step) for i in range(count)])  6.1 us
    ppermute x3, starting transfers between devices, rotated(): lax.ppermute(value, 'latent', [(i, (i + step) % count) for i in range(cou...  4.73 us
    unnamed x14, local copies, waits for them, and re-layouts  3.81 us
    ppermute x1, starting transfers between devices, across_cores(): return lax.ppermute(value, 'layer', [(i, i ^ 1) for i in range(count)])  3.57 us
    pallas_call x1, Pallas kernels, decode_late(): pl.pallas_call(functools.partial(late_kernel, parts), out_shape=jax.Shape...  3.14 us
  transfers between devices with their start and end apart: 11, of which 6 were waited for; matrix products, arithmetic and copies ran while one was open for 0% of the time, Pallas kernels for 8%

profile of v6, /device:TPU:5, one launch (start us, length us, event | category | flops | bytes accessed | tf_op | source)
XLA Modules:
  0.0 73.6 jit_solution(16586905592534607123)
XLA Ops:
  0.0 0.0 copy-start.2
  0.0 1.2 %copy-done.2 = bf16[1,4096,128]{2,1,0:T(8,128)(2,1)S(1)} copy-done((bf16[1,4096,128]{2,1,0:T(8,128)(2,1)S(1)}, bf16[1,4096,128]{2,1,0:T(8,128)(2,1)}, u32[]{:S(2)}) %copy-start.2) | copy-done | bytes 1048600
  1.2 0.0 copy-start.5
  1.2 0.0 copy-start.6
  1.2 0.1 fetch_rows.1
  1.3 1.3 %collective-permute-start.2 = (bf16[1024,128]{1,0:T(8,128)(2,1)S(1)}, bf16[1024,128]{1,0:T(8,128)(2,1)S(1)}, u32[]{:S(2)}, u32[]{:S(2)}) collective-permute-start(bf16[1024,128]{1,0:T(8,128)(2,1)S(1)} %get-tuple-element.37), channel_id=1, source_target_pairs={{0,1},{1,2},{2,3},{3,0},{4,5},{5,6},{6,7},{7,4},{8,9},{9,10},{10,1... | collective-permute-start | bytes 786440 | tf_op jit(solution)/shard_map/encoder_rows/ppermute | solution.py:23
  2.7 2.3 %collective-permute-start.3 = (bf16[1024,128]{1,0:T(8,128)(2,1)S(1)}, bf16[1024,128]{1,0:T(8,128)(2,1)S(1)}, u32[]{:S(2)}, u32[]{:S(2)}) collective-permute-start(bf16[1024,128]{1,0:T(8,128)(2,1)S(1)} %get-tuple-element.38), channel_id=1, source_target_pairs={{0,2},{1,3},{2,0},{3,1},{4,6},{5,7},{6,4},{7,5},{8,10},{9,11},{10,... | collective-permute-start | bytes 786440 | tf_op jit(solution)/shard_map/encoder_rows/ppermute | solution.py:23
  5.0 1.1 %collective-permute-start.4 = (bf16[1024,128]{1,0:T(8,128)(2,1)S(1)}, bf16[1024,128]{1,0:T(8,128)(2,1)S(1)}, u32[]{:S(2)}, u32[]{:S(2)}) collective-permute-start(bf16[1024,128]{1,0:T(8,128)(2,1)S(1)} %get-tuple-element.39), channel_id=1, source_target_pairs={{0,3},{1,0},{2,1},{3,2},{4,7},{5,4},{6,5},{7,6},{8,11},{9,8},{10,9... | collective-permute-start | bytes 786440 | tf_op jit(solution)/shard_map/encoder_rows/ppermute | solution.py:23
  6.0 0.0 copy-start
  6.0 1.9 %copy-done = bf16[1,3,512,1024]{3,2,1,0:T(8,128)(2,1)S(1)} copy-done((bf16[1,3,512,1024]{3,2,1,0:T(8,128)(2,1)S(1)}, bf16[1,3,512,1024]{3,2,1,0:T(8,128)(2,1)}, u32[]{:S(2)}) %copy-start) | copy-done | bytes 3145752
  7.9 0.0 copy-start.3
  7.9 0.7 copy-done.3
  8.6 0.0 copy-start.4
  8.6 0.1 fetch_decoders.1
  8.7 4.7 %collective-permute-start = (bf16[528,1024]{1,0:T(8,128)(2,1)S(1)}, bf16[528,1024]{1,0:T(8,128)(2,1)S(1)}, u32[]{:S(2)}, u32[]{:S(2)}) collective-permute-start(bf16[528,1024]{1,0:T(8,128)(2,1)S(1)} %get-tuple-element.32), channel_id=1, source_target_pairs={{0,4},{4,8},{8,12},{12,16},{16,20},{20,24},{24,28},{1,5},{5,9},{9,... | collective-permute-start | bytes 3244040 | tf_op jit(solution)/shard_map/decoder_weights/ppermute | solution.py:28
  13.4 1.9 %collective-permute-start.1 = (bf16[528,1024]{1,0:T(8,128)(2,1)S(1)}, bf16[528,1024]{1,0:T(8,128)(2,1)S(1)}, u32[]{:S(2)}, u32[]{:S(2)}) collective-permute-start(bf16[528,1024]{1,0:T(8,128)(2,1)S(1)} %get-tuple-element.33), channel_id=1, source_target_pairs={{0,8},{4,12},{8,16},{12,20},{16,24},{20,28},{1,9},{5,13},{9,17},{1... | collective-permute-start | bytes 3244040 | tf_op jit(solution)/shard_map/decoder_weights/ppermute | solution.py:28
  15.3 0.0 collective-permute-done.2.refs_1_
  15.3 7.4 %collective-permute-done.3.refs_2_ = bf16[1024,128]{1,0:T(8,128)(2,1)S(1)} collective-permute-done((bf16[1024,128]{1,0:T(8,128)(2,1)S(1)}, bf16[1024,128]{1,0:T(8,128)(2,1)S(1)}, u32[]{:S(2)}, u32[]{:S(2)}) %collective-permute-start.3) | collective-permute-done | bytes 262176 | tf_op jit(solution)/shard_map/encoder_rows/ppermute | solution.py:23
  22.7 0.0 collective-permute-done.4.refs_3_
  22.7 0.0 copy-done.5
  22.7 0.0 copy-done.6
  22.7 0.0 copy-done.4
  22.7 0.0 copy-start.1
  22.8 1.9 %encode.1 = (f32[8,2,64,128]{3,2,1,0:T(8,128)S(1)}, bf16[8,2,64,128]{3,2,1,0:T(8,128)(2,1)S(1)}) custom-call(s32[2,16]{1,0:T(2,128)S(1)} %bitcast.12, s32[16]{0:T(128)S(1)} %bitcast.15, f32[1,128]{1,0:T(1,128)S(1)} %copy-done.6, bf16[1024,1024]{1,0:T(8,128)(2,1)S(1)} %bitcast.14, bf16[1024,128]{1,0:T(8,128)(2,1)S(1)} %get-tuple-element.36.refs_0_, ...), custom_call_target="tpu_custom_call" | custom-call | flops 1073741824 | bytes 3145728 | tf_op jit(solution)/shard_map/encode/encode/pallas_call | solution.py:118
  24.7 6.0 %collective-permute-start.5 = (bf16[8,2,64,128]{3,2,1,0:T(8,128)(2,1)S(1)}, bf16[8,2,64,128]{3,2,1,0:T(8,128)(2,1)S(1)}, u32[]{:S(2)}, u32[]{:S(2)}) collective-permute-start(bf16[8,2,64,128]{3,2,1,0:T(8,128)(2,1)S(1)} %get-tuple-element.41), channel_id=1, source_target_pairs={{0,1},{1,0},{2,3},{3,2},{4,5},{5,4},{6,7},{7,6},{8,9},{9,8},{10,11... | collective-permute-start | bytes 786440 | tf_op jit(solution)/shard_map/encode/ppermute | solution.py:18
  30.6 6.2 %collective-permute-done.5.arrived_ref = bf16[8,2,64,128]{3,2,1,0:T(8,128)(2,1)S(1)} collective-permute-done((bf16[8,2,64,128]{3,2,1,0:T(8,128)(2,1)S(1)}, bf16[8,2,64,128]{3,2,1,0:T(8,128)(2,1)S(1)}, u32[]{:S(2)}, u32[]{:S(2)}) %collective-permute-start.5) | collective-permute-done | bytes 262176 | tf_op jit(solution)/shard_map/encode/ppermute | solution.py:18
  36.9 0.1 merge.1
  36.9 0.1 collective-permute-start.6
  37.0 13.8 %collective-permute-done.6.arrived_ref = bf16[8,2,64,128]{3,2,1,0:T(8,128)(2,1)S(1)} collective-permute-done((bf16[8,2,64,128]{3,2,1,0:T(8,128)(2,1)S(1)}, bf16[8,2,64,128]{3,2,1,0:T(8,128)(2,1)S(1)}, u32[]{:S(2)}, u32[]{:S(2)}) %collective-permute-start.6) | collective-permute-done | bytes 262176 | tf_op jit(solution)/shard_map/encode/ppermute | solution.py:18
  50.8 0.1 activate.1.own_early.refs_0_
  50.9 0.1 collective-permute-start.7
  51.0 3.1 %collective-permute-start.8 = (bf16[8,2,64,128]{3,2,1,0:T(8,128)(2,1)S(1)}, bf16[8,2,64,128]{3,2,1,0:T(8,128)(2,1)S(1)}, u32[]{:S(2)}, u32[]{:S(2)}) collective-permute-start(bf16[8,2,64,128]{3,2,1,0:T(8,128)(2,1)S(1)} %activate.1.own_early.refs_0_), channel_id=1, source_target_pairs={{0,8},{4,12},{8,16},{12,20},{16,24},{20,28},{1,9},{5,13},{9,17},{1... | collective-permute-start | bytes 786440 | tf_op jit(solution)/shard_map/spread/ppermute | solution.py:28
  54.1 3.2 %collective-permute-done.7.own_late.refs_1_ = bf16[8,2,64,128]{3,2,1,0:T(8,128)(2,1)S(1)} collective-permute-done((bf16[8,2,64,128]{3,2,1,0:T(8,128)(2,1)S(1)}, bf16[8,2,64,128]{3,2,1,0:T(8,128)(2,1)S(1)}, u32[]{:S(2)}, u32[]{:S(2)}) %collective-permute-start.7) | collective-permute-done | bytes 262176 | tf_op jit(solution)/shard_map/spread/ppermute | solution.py:18
  57.3 3.1 %collective-permute-start.9 = (bf16[8,2,64,128]{3,2,1,0:T(8,128)(2,1)S(1)}, bf16[8,2,64,128]{3,2,1,0:T(8,128)(2,1)S(1)}, u32[]{:S(2)}, u32[]{:S(2)}) collective-permute-start(bf16[8,2,64,128]{3,2,1,0:T(8,128)(2,1)S(1)} %collective-permute-done.7.own_late.refs_1_), channel_id=1, source_target_pairs={{0,8},{4,12},{8,16},{12,20},{16,24},{20,28},{1,9},{5,13},{9,17},{1... | collective-permute-start | bytes 786440 | tf_op jit(solution)/shard_map/spread/ppermute | solution.py:28
  60.5 0.0 collective-permute-done.near_dec
  60.5 0.0 collective-permute-done.1.far_dec
  60.5 0.0 collective-permute-done.8.far.refs_2_
  60.5 0.0 copy-done.1
  60.5 2.7 %decode_early.1 = (f32[512,1024]{1,0:T(8,128)S(1)}, f32[512,1024]{1,0:T(8,128)S(1)}) custom-call(s32[2,16]{1,0:T(2,128)S(1)} %bitcast.13, s32[2,16]{1,0:T(2,128)S(1)} %slice_convert_fusion.far_lists.lists_ref, bf16[8,2,64,128]{3,2,1,0:T(8,128)(2,1)S(1)} %activate.1.own_early.refs_0_, bf16[8,2,64,128]{3,2,1,0:T(8,128)(2,1)S(1)} %collective-permute-done.7.own_late.refs_1_, ...), custom_call_target="tpu_custom_call" | custom-call | flops 1610612736 | bytes 6291456 | tf_op jit(solution)/shard_map/decode/decode_early/pallas_call | solution.py:228
  63.2 2.1 %collective-permute-done.9.far.refs_3_ = bf16[8,2,64,128]{3,2,1,0:T(8,128)(2,1)S(1)} collective-permute-done((bf16[8,2,64,128]{3,2,1,0:T(8,128)(2,1)S(1)}, bf16[8,2,64,128]{3,2,1,0:T(8,128)(2,1)S(1)}, u32[]{:S(2)}, u32[]{:S(2)}) %collective-permute-start.9) | collective-permute-done | bytes 262176 | tf_op jit(solution)/shard_map/spread/ppermute | solution.py:28
  65.4 3.6 %collective-permute-start.10 = (bf16[16,2,64,128]{3,2,1,0:T(8,128)(2,1)S(1)}, bf16[16,2,64,128]{3,2,1,0:T(8,128)(2,1)S(1)}, u32[]{:S(2)}, u32[]{:S(2)}) collective-permute-start(bf16[16,2,64,128]{3,2,1,0:T(8,128)(2,1)S(1)} %choose.1), channel_id=1, source_target_pairs={{0,4},{4,0},{8,12},{12,8},{16,20},{20,16},{24,28},{28,24},{1,5},{5... | collective-permute-start | bytes 1572872 | tf_op jit(solution)/shard_map/decode/ppermute | solution.py:33
  69.0 1.3 %decode_middle.1.late_ref = f32[512,1024]{1,0:T(8,128)S(1)} custom-call(s32[2,16]{1,0:T(2,128)S(1)} %slice_convert_fusion.far_lists.lists_ref, f32[512,1024]{1,0:T(8,128)S(1)} %get-tuple-element.47.partial_ref, bf16[8,2,64,128]{3,2,1,0:T(8,128)(2,1)S(1)} %collective-permute-done.9.far.refs_3_, bf16[528,1024]{1,0:T(8,128)(2,1)S(1)} %collective-permute-done.1.far_dec), custom_call_target="tpu_custom_call" | custom-call | flops 536870912 | bytes 5242880 | tf_op jit(solution)/shard_map/decode/decode_middle/pallas_call | solution.py:260
  70.3 0.2 collective-permute-done.10.near
  70.5 3.1 %decode_late.1 = bf16[1024,1024]{1,0:T(8,128)(2,1)} custom-call(s32[2,16]{1,0:T(2,128)S(1)} %slice_convert_fusion.1.lists_ref, f32[512,1024]{1,0:T(8,128)S(1)} %get-tuple-element.46.early_ref, f32[512,1024]{1,0:T(8,128)S(1)} %decode_middle.1.late_ref, bf16[16,2,64,128]{3,2,1,0:T(8,128)(2,1)S(1)} %collective-permute-done.10.near, ...), custom_call_target="tpu_custom_call" | custom-call | flops 1073741824 | bytes 7340032 | tf_op jit(solution)/shard_map/decode/decode_late/pallas_call | solution.py:301
  (3 shorter events, 0.0 us)
Async XLA Ops:
  0.0 1.2 %copy-start.2 = (bf16[1,4096,128]{2,1,0:T(8,128)(2,1)S(1)}, bf16[1,4096,128]{2,1,0:T(8,128)(2,1)}, u32[]{:S(2)}) copy-start(bf16[1,4096,128]{2,1,0:T(8,128)(2,1)} %param.7) | copy-start | bytes 3145732
  1.2 21.5 %copy-start.5 = (s32[1,16]{1,0:T(1,128)S(1)}, s32[1,16]{1,0:T(1,128)}, u32[]{:S(2)}) copy-start(s32[1,16]{1,0:T(1,128)} %param.11) | copy-start | bytes 196
  1.2 21.5 %copy-start.6 = (f32[1,128]{1,0:T(1,128)S(1)}, f32[1,128]{1,0:T(1,128)}, u32[]{:S(2)}) copy-start(f32[1,128]{1,0:T(1,128)} %bias_ref.1) | copy-start | bytes 1540
  1.3 14.0 %collective-permute-start.2 = (bf16[1024,128]{1,0:T(8,128)(2,1)S(1)}, bf16[1024,128]{1,0:T(8,128)(2,1)S(1)}, u32[]{:S(2)}, u32[]{:S(2)}) collective-permute-start(bf16[1024,128]{1,0:T(8,128)(2,1)S(1)} %get-tuple-element.37), channel_id=1, source_target_pairs={{0,1},{1,2},{2,3},{3,0},{4,5},{5,6},{6,7},{7,4},{8,9},{9,10},{10,1... | collective-permute-start | bytes 786440 | tf_op jit(solution)/shard_map/encoder_rows/ppermute | solution.py:23
  2.7 20.1 %collective-permute-start.3 = (bf16[1024,128]{1,0:T(8,128)(2,1)S(1)}, bf16[1024,128]{1,0:T(8,128)(2,1)S(1)}, u32[]{:S(2)}, u32[]{:S(2)}) collective-permute-start(bf16[1024,128]{1,0:T(8,128)(2,1)S(1)} %get-tuple-element.38), channel_id=1, source_target_pairs={{0,2},{1,3},{2,0},{3,1},{4,6},{5,7},{6,4},{7,5},{8,10},{9,11},{10,... | collective-permute-start | bytes 786440 | tf_op jit(solution)/shard_map/encoder_rows/ppermute | solution.py:23
  5.0 17.8 %collective-permute-start.4 = (bf16[1024,128]{1,0:T(8,128)(2,1)S(1)}, bf16[1024,128]{1,0:T(8,128)(2,1)S(1)}, u32[]{:S(2)}, u32[]{:S(2)}) collective-permute-start(bf16[1024,128]{1,0:T(8,128)(2,1)S(1)} %get-tuple-element.39), channel_id=1, source_target_pairs={{0,3},{1,0},{2,1},{3,2},{4,7},{5,4},{6,5},{7,6},{8,11},{9,8},{10,9... | collective-permute-start | bytes 786440 | tf_op jit(solution)/shard_map/encoder_rows/ppermute | solution.py:23
  6.0 1.9 %copy-start = (bf16[1,3,512,1024]{3,2,1,0:T(8,128)(2,1)S(1)}, bf16[1,3,512,1024]{3,2,1,0:T(8,128)(2,1)}, u32[]{:S(2)}) copy-start(bf16[1,3,512,1024]{3,2,1,0:T(8,128)(2,1)} %param.9) | copy-start | bytes 9437188
  7.9 0.7 copy-start.3
  8.6 14.1 %copy-start.4 = (bf16[1,1024,1024]{2,1,0:T(8,128)(2,1)S(1)}, bf16[1,1024,1024]{2,1,0:T(8,128)(2,1)}, u32[]{:S(2)}) copy-start(bf16[1,1024,1024]{2,1,0:T(8,128)(2,1)} %param.6) | copy-start | bytes 6291460
  8.7 51.7 %collective-permute-start = (bf16[528,1024]{1,0:T(8,128)(2,1)S(1)}, bf16[528,1024]{1,0:T(8,128)(2,1)S(1)}, u32[]{:S(2)}, u32[]{:S(2)}) collective-permute-start(bf16[528,1024]{1,0:T(8,128)(2,1)S(1)} %get-tuple-element.32), channel_id=1, source_target_pairs={{0,4},{4,8},{8,12},{12,16},{16,20},{20,24},{24,28},{1,5},{5,9},{9,... | collective-permute-start | bytes 3244040 | tf_op jit(solution)/shard_map/decoder_weights/ppermute | solution.py:28
  13.4 47.1 %collective-permute-start.1 = (bf16[528,1024]{1,0:T(8,128)(2,1)S(1)}, bf16[528,1024]{1,0:T(8,128)(2,1)S(1)}, u32[]{:S(2)}, u32[]{:S(2)}) collective-permute-start(bf16[528,1024]{1,0:T(8,128)(2,1)S(1)} %get-tuple-element.33), channel_id=1, source_target_pairs={{0,8},{4,12},{8,16},{12,20},{16,24},{20,28},{1,9},{5,13},{9,17},{1... | collective-permute-start | bytes 3244040 | tf_op jit(solution)/shard_map/decoder_weights/ppermute | solution.py:28
  22.7 37.8 %copy-start.1 = (bf16[1,3,512,1024]{3,2,1,0:T(8,128)(2,1)S(1)}, bf16[1,3,512,1024]{3,2,1,0:T(8,128)(2,1)}, u32[]{:S(2)}) copy-start(bf16[1,3,512,1024]{3,2,1,0:T(8,128)(2,1)} %param.9) | copy-start | bytes 9437188
  24.7 12.2 %collective-permute-start.5 = (bf16[8,2,64,128]{3,2,1,0:T(8,128)(2,1)S(1)}, bf16[8,2,64,128]{3,2,1,0:T(8,128)(2,1)S(1)}, u32[]{:S(2)}, u32[]{:S(2)}) collective-permute-start(bf16[8,2,64,128]{3,2,1,0:T(8,128)(2,1)S(1)} %get-tuple-element.41), channel_id=1, source_target_pairs={{0,1},{1,0},{2,3},{3,2},{4,5},{5,4},{6,7},{7,6},{8,9},{9,8},{10,11... | collective-permute-start | bytes 786440 | tf_op jit(solution)/shard_map/encode/ppermute | solution.py:18
  36.9 13.9 %collective-permute-start.6 = (bf16[8,2,64,128]{3,2,1,0:T(8,128)(2,1)S(1)}, bf16[8,2,64,128]{3,2,1,0:T(8,128)(2,1)S(1)}, u32[]{:S(2)}, u32[]{:S(2)}) collective-permute-start(bf16[8,2,64,128]{3,2,1,0:T(8,128)(2,1)S(1)} %get-tuple-element.43), channel_id=1, source_target_pairs={{0,2},{1,3},{2,0},{3,1},{4,6},{5,7},{6,4},{7,5},{8,10},{9,11},{10,... | collective-permute-start | bytes 786440 | tf_op jit(solution)/shard_map/encode/ppermute | solution.py:18
  50.9 6.4 %collective-permute-start.7 = (bf16[8,2,64,128]{3,2,1,0:T(8,128)(2,1)S(1)}, bf16[8,2,64,128]{3,2,1,0:T(8,128)(2,1)S(1)}, u32[]{:S(2)}, u32[]{:S(2)}) collective-permute-start(bf16[8,2,64,128]{3,2,1,0:T(8,128)(2,1)S(1)} %activate.1.own_early.refs_0_), channel_id=1, source_target_pairs={{0,1},{1,0},{2,3},{3,2},{4,5},{5,4},{6,7},{7,6},{8,9},{9,8},{10,11... | collective-permute-start | bytes 786440 | tf_op jit(solution)/shard_map/spread/ppermute | solution.py:18
  51.0 9.5 %collective-permute-start.8 = (bf16[8,2,64,128]{3,2,1,0:T(8,128)(2,1)S(1)}, bf16[8,2,64,128]{3,2,1,0:T(8,128)(2,1)S(1)}, u32[]{:S(2)}, u32[]{:S(2)}) collective-permute-start(bf16[8,2,64,128]{3,2,1,0:T(8,128)(2,1)S(1)} %activate.1.own_early.refs_0_), channel_id=1, source_target_pairs={{0,8},{4,12},{8,16},{12,20},{16,24},{20,28},{1,9},{5,13},{9,17},{1... | collective-permute-start | bytes 786440 | tf_op jit(solution)/shard_map/spread/ppermute | solution.py:28
  57.3 8.0 %collective-permute-start.9 = (bf16[8,2,64,128]{3,2,1,0:T(8,128)(2,1)S(1)}, bf16[8,2,64,128]{3,2,1,0:T(8,128)(2,1)S(1)}, u32[]{:S(2)}, u32[]{:S(2)}) collective-permute-start(bf16[8,2,64,128]{3,2,1,0:T(8,128)(2,1)S(1)} %collective-permute-done.7.own_late.refs_1_), channel_id=1, source_target_pairs={{0,8},{4,12},{8,16},{12,20},{16,24},{20,28},{1,9},{5,13},{9,17},{1... | collective-permute-start | bytes 786440 | tf_op jit(solution)/shard_map/spread/ppermute | solution.py:28
  65.4 5.1 %collective-permute-start.10 = (bf16[16,2,64,128]{3,2,1,0:T(8,128)(2,1)S(1)}, bf16[16,2,64,128]{3,2,1,0:T(8,128)(2,1)S(1)}, u32[]{:S(2)}, u32[]{:S(2)}) collective-permute-start(bf16[16,2,64,128]{3,2,1,0:T(8,128)(2,1)S(1)} %choose.1), channel_id=1, source_target_pairs={{0,4},{4,0},{8,12},{12,8},{16,20},{20,16},{24,28},{28,24},{1,5},{5... | collective-permute-start | bytes 1572872 | tf_op jit(solution)/shard_map/decode/ppermute | solution.py:33

commit v7 on v6

v7 whole, which is shorter than its diff:
```python
import functools

import jax
import jax.numpy as jnp
from jax import lax
from jax.experimental import pallas as pl
from jax.experimental.pallas import tpu as pltpu
from jax.sharding import PartitionSpec as P

VMEM = pl.BlockSpec(memory_space=pltpu.VMEM)
SMEM = pl.BlockSpec(memory_space=pltpu.SMEM)
ANY = pl.BlockSpec(memory_space=pl.ANY)
HBM = pl.BlockSpec(memory_space=pltpu.HBM)


def swapped(value, step):
    count = lax.axis_size("latent")
    return lax.ppermute(value, "latent", [(i, i ^ step) for i in range(count)])


def passed_along(value, steps):
    count = lax.axis_size("layer")
    return lax.ppermute(value, "layer", [(i, i + steps) for i in range(count - steps)])


def across_cores(value):
    count = lax.axis_size("layer")
    return lax.ppermute(value, "layer", [(i, i ^ 1) for i in range(count)])


def small(name, megabytes=8):
    return dict(compiler_params=pltpu.CompilerParams(vmem_limit_bytes=megabytes << 20), name=name)


def held_tile(position, tiles, parts):
    each = tiles // parts
    number, half = position // each, parts // 2
    parity = lax.bitwise_and(lax.axis_index("latent"), 1)
    return (2 * (number % half) + (parity if number < half else 1 - parity)) * each + position % each


def fetch_rows_kernel(encoder_ref, *piece_refs):
    depth = piece_refs[0].shape[0]
    for step, piece in enumerate(piece_refs):
        first = pl.multiple_of(lax.bitwise_xor(lax.axis_index("latent"), step) * depth, depth)
        piece[...] = encoder_ref[pl.ds(first, depth), :]


def fetch_rows(encoder, parts):
    depth = encoder.shape[0] // parts
    return pl.pallas_call(
        fetch_rows_kernel,
        out_shape=[jax.ShapeDtypeStruct((depth, encoder.shape[1]), encoder.dtype)] * parts,
        in_specs=[VMEM],
        out_specs=[VMEM] * parts,
        **small("fetch_rows"),
    )(encoder)


def fetch_decoders_kernel(lists_ref, decoder_ref, *refs):
    out_refs, ids = refs[:-1], refs[-1]
    latents = decoder_ref.shape[1]
    slots, tiles = lists_ref.shape
    ids[...] = jnp.zeros_like(ids)
    ids[:slots, :tiles] = lists_ref[...].astype(jnp.float32)
    for number, out_ref in enumerate(out_refs):
        out_ref[:latents, :] = decoder_ref[number + 1]
        out_ref[latents:, :] = ids[...].astype(out_ref.dtype)


def fetch_decoders(lists, decoder):
    targets, latents, features = decoder.shape
    rows = lists.shape[0] + -lists.shape[0] % 16
    shape = jax.ShapeDtypeStruct((latents + rows, features), decoder.dtype)
    return pl.pallas_call(
        fetch_decoders_kernel,
        out_shape=[shape] * (targets - 1),
        in_specs=[VMEM, VMEM],
        out_specs=[VMEM] * (targets - 1),
        scratch_shapes=[pltpu.VMEM((rows, features), jnp.float32)],
        **small("fetch_decoders", 16),
    )(lists, decoder)


def encode_kernel(parts, lists_ref, counts_ref, bias_ref, x_ref, *refs):
    weight_refs, out_refs, partial = refs[:parts], refs[parts:-1], refs[-1]
    width = bias_ref.shape[1]
    count, slots, rows, _ = out_refs[0].shape
    tiles = lists_ref.shape[1]
    for first in range(0, parts, 2):
        stacked = jnp.concatenate([ref[...] for ref in weight_refs[first : first + 2]], axis=1)
        product = jnp.dot(x_ref[...], stacked, preferred_element_type=jnp.float32)
        for source in range(first, first + 2):
            block = product[:, (source - first) * width : (source - first + 1) * width]
            partial[source] = block if source else block + bias_ref[...]
    for number, out_ref in enumerate(out_refs):
        for position in range(count):
            tile = held_tile(number * count + position, tiles, parts)
            row = pl.multiple_of(tile * rows, rows)
            for slot in range(slots):
                source = lax.bitwise_xor(lax.axis_index("latent"), lists_ref[slot, tile])
                kept = partial[source, pl.ds(row, rows), :]
                if number < 2:
                    kept = kept + jnp.where(slot < counts_ref[tile], 0.0, -1e30)
                out_ref[position, slot] = kept.astype(out_ref.dtype)


def encode(lists, counts, bias, x, weights):
    parts = len(weights)
    tokens, depth = x.shape
    width = bias.shape[1]
    slots, tiles = lists.shape
    shape = (tiles // 4, slots, tokens // tiles, width)
    return pl.pallas_call(
        functools.partial(encode_kernel, parts),
        out_shape=[jax.ShapeDtypeStruct(shape, jnp.float32)] * 2 + [jax.ShapeDtypeStruct(shape, jnp.bfloat16)] * 2,
        in_specs=[SMEM] * 2 + [VMEM] * (2 + parts),
        out_specs=[VMEM] * 4,
        scratch_shapes=[pltpu.VMEM((parts, tokens, width), jnp.float32)],
        cost_estimate=pl.CostEstimate(
            flops=32 * tokens * depth * parts * width,
            bytes_accessed=2 * (tokens * depth + depth * parts * width),
            transcendentals=0,
        ),
        **small("encode", 16),
    )(lists, counts, bias, x, *weights)


def merge_kernel(kept_ref, arrived_ref, total_ref, sent_ref):
    total = kept_ref[...] + arrived_ref[...].astype(jnp.float32)
    total_ref[...] = total
    sent_ref[...] = total.astype(sent_ref.dtype)


def merge(kept, arrived):
    return pl.pallas_call(
        merge_kernel,
        out_shape=[jax.ShapeDtypeStruct(kept.shape, kept.dtype), jax.ShapeDtypeStruct(kept.shape, arrived.dtype)],
        in_specs=[VMEM] * 2,
        out_specs=[VMEM] * 2,
        **small("merge"),
    )(kept, arrived)


def activate_kernel(kept_ref, arrived_ref, act_ref):
    preact = kept_ref[...] + arrived_ref[...].astype(jnp.float32)
    act_ref[...] = jnp.maximum(preact, 0.0).astype(act_ref.dtype)


def activate(kept, arrived):
    return pl.pallas_call(
        activate_kernel,
        out_shape=jax.ShapeDtypeStruct(kept.shape, arrived.dtype),
        in_specs=[VMEM] * 2,
        out_specs=VMEM,
        **small("activate"),
    )(kept, arrived)


def choose_kernel(*refs):
    sources, out_ref = refs[:-1], refs[-1]
    count = sources[0].shape[0]
    odd = lax.bitwise_and(lax.axis_index("layer"), 1)

    @pl.when(odd == 0)
    def _():
        for number in range(4):
            out_ref[number * count : (number + 1) * count] = sources[number][...]

    @pl.when(odd == 1)
    def _():
        out_ref[:count] = sources[4][...]
        out_ref[count : 3 * count] = sources[5][...]
        out_ref[3 * count :] = sources[6][...]


def choose(own, far):
    shape = own[0].shape
    return pl.pallas_call(
        choose_kernel,
        out_shape=jax.ShapeDtypeStruct((4 * shape[0],) + shape[1:], own[0].dtype),
        in_specs=[VMEM] * 7,
        out_specs=VMEM,
        **small("choose"),
    )(*own, *far)


def join_kernel(first_ref, second_ref, out_ref):
    count = first_ref.shape[0]
    out_ref[:count] = first_ref[...]
    out_ref[count:] = second_ref[...]


def join(first, second):
    return pl.pallas_call(
        join_kernel,
        out_shape=jax.ShapeDtypeStruct((2 * first.shape[0],) + first.shape[1:], first.dtype),
        in_specs=[VMEM] * 2,
        out_specs=VMEM,
        **small("join"),
    )(first, second)


def expand(dense, lists_ref, parts, first, act_refs):
    row = 0
    for act_ref in act_refs:
        count, slots, rows, width = act_ref.shape
        for position in range(count):
            tile = held_tile(first + position, lists_ref.shape[1], parts)
            for slot in range(slots):
                lanes = pl.ds(pl.multiple_of(lists_ref[slot, tile] * width, width), width)
                dense[row : row + rows, lanes] = act_ref[position, slot]
            row += rows
        first += count


def column_tiles(features):
    columns = 256 if features % 256 == 0 else features
    return [slice(first, first + columns) for first in range(0, features, columns)]


def early_kernel(parts, lists_ref, far_lists, *refs):
    own_refs, far_refs, (decoder_hbm, far_dec), refs = refs[:4], refs[4:6], refs[6:8], refs[8:]
    early_ref, late_a, late_b, own, other, own_dec, sem = refs
    copy = pltpu.make_async_copy(decoder_hbm.at[0], own_dec, sem)
    copy.start()
    quarter, latents = late_a.shape[0], own.shape[1]
    own[...] = jnp.zeros_like(own)
    other[...] = jnp.zeros_like(other)
    expand(own, lists_ref, parts, 0, own_refs)
    expand(other, far_lists, parts, 0, far_refs)
    copy.wait()
    for lanes in column_tiles(early_ref.shape[1]):
        total = jnp.dot(own[...], own_dec[:, lanes], preferred_element_type=jnp.float32)
        late_b[:, lanes] = total[3 * quarter :]
        total = total[: 3 * quarter] + jnp.dot(
            other[...], far_dec[:latents, lanes], preferred_element_type=jnp.float32
        )
        early_ref[:, lanes] = total[: 2 * quarter]
        late_a[:, lanes] = total[2 * quarter :]


def decode_early(lists, far_lists, acts, decoder, far_decoder, parts):
    _, latents, features = decoder.shape
    quarter = acts[0].shape[0] * acts[0].shape[2]
    return pl.pallas_call(
        functools.partial(early_kernel, parts),
        out_shape=[jax.ShapeDtypeStruct((count * quarter, features), jnp.float32) for count in (2, 1, 1)],
        in_specs=[SMEM, SMEM] + [VMEM] * 6 + [ANY, VMEM],
        out_specs=[VMEM] * 3,
        scratch_shapes=[
            pltpu.VMEM((4 * quarter, latents), jnp.bfloat16),
            pltpu.VMEM((3 * quarter, latents), jnp.bfloat16),
            pltpu.VMEM((latents, features), jnp.bfloat16),
            pltpu.SemaphoreType.DMA,
        ],
        cost_estimate=pl.CostEstimate(
            flops=14 * quarter * latents * features,
            bytes_accessed=2 * (2 * latents * features + 8 * quarter * features),
            transcendentals=0,
        ),
        **small("decode_early", 16),
    )(lists, far_lists, *acts, decoder, far_decoder)


def middle_kernel(parts, lists_ref, partial_ref, far, far_dec, total_ref, dense):
    latents = dense.shape[1]
    dense[...] = jnp.zeros_like(dense)
    expand(dense, lists_ref, parts, 3 * far.shape[0], [far])
    for lanes in column_tiles(partial_ref.shape[1]):
        total_ref[:, lanes] = partial_ref[:, lanes] + jnp.dot(
            dense[...], far_dec[:latents, lanes], preferred_element_type=jnp.float32
        )


def decode_middle(lists, partial, far, decoder, latents, parts):
    quarter, features = partial.shape
    return pl.pallas_call(
        functools.partial(middle_kernel, parts),
        out_shape=jax.ShapeDtypeStruct(partial.shape, partial.dtype),
        in_specs=[SMEM] + [VMEM] * 3,
        out_specs=VMEM,
        scratch_shapes=[pltpu.VMEM((quarter, latents), jnp.bfloat16)],
        cost_estimate=pl.CostEstimate(
            flops=2 * quarter * latents * features,
            bytes_accessed=2 * (latents * features + 4 * quarter * features),
            transcendentals=0,
        ),
        **small("decode_middle", 16),
    )(lists, partial, far, decoder)


def late_kernel(parts, lists_ref, early_ref, late_a, late_b, near, near_dec, out_ref, dense, stage, sems):
    tokens, latents = dense.shape
    quarter, rows = tokens // 4, tokens // parts
    dense[...] = jnp.zeros_like(dense)
    expand(dense, lists_ref, parts, 0, [near])
    copies = []
    for number, lanes in enumerate(column_tiles(early_ref.shape[1])):
        total = jnp.dot(dense[...], near_dec[:latents, lanes], preferred_element_type=jnp.float32)
        before = ((0, early_ref), (2 * quarter, late_a), (3 * quarter, late_b))
        for first, ref in before:
            last = first + ref.shape[0]
            stage[first:last, lanes] = (total[first:last] + ref[:, lanes]).astype(stage.dtype)
        for held in range(parts):
            tiles = lists_ref.shape[1]
            row = pl.multiple_of(held_tile(held * (tiles // parts), tiles, parts) * (tokens // tiles), rows)
            copies.append(
                pltpu.make_async_copy(
                    stage.at[held * rows : (held + 1) * rows, lanes],
                    out_ref.at[pl.ds(row, rows), lanes],
                    sems.at[number, held],
                )
            )
            copies[-1].start()
    for copy in copies:
        copy.wait()


def decode_late(lists, partials, near, decoder, latents, parts):
    features = decoder.shape[1]
    tokens = near.shape[0] * near.shape[2]
    return pl.pallas_call(
        functools.partial(late_kernel, parts),
        out_shape=jax.ShapeDtypeStruct((tokens, features), jnp.bfloat16),
        in_specs=[SMEM] + [VMEM] * 5,
        out_specs=ANY,
        scratch_shapes=[
            pltpu.VMEM((tokens, latents), jnp.bfloat16),
            pltpu.VMEM((tokens, features), jnp.bfloat16),
            pltpu.SemaphoreType.DMA((len(column_tiles(features)), parts)),
        ],
        cost_estimate=pl.CostEstimate(
            flops=2 * tokens * latents * features,
            bytes_accessed=2 * (latents * features + 3 * tokens * features),
            transcendentals=0,
        ),
        **small("decode_late", 16),
    )(lists, *partials, near, decoder)


def shards(layer_input, enc_weight, enc_bias, dec_weight, block_lists, block_counts):
    parts = lax.axis_size("latent")
    x, encoder, decoder = layer_input[0], enc_weight[0], dec_weight[0]
    lists, counts = block_lists[0].T, block_counts[0]
    slots, tiles = lists.shape
    targets, latents, _ = decoder.shape
    if targets != 3 or parts < 2 or parts & (parts - 1) or tiles % 4:
        raise ValueError("mesh")

    with jax.named_scope("encoder_rows"):
        pieces = fetch_rows(encoder, parts)
        pieces, decoder = lax.optimization_barrier((pieces, decoder))
        weights = [pieces[0]] + [None] * (parts - 1)
        for step in sorted(range(1, parts), reverse=True):
            weights[step] = swapped(pieces[step], step)
    with jax.named_scope("decoder_weights"):
        near_rows, far_rows = fetch_decoders(lists, decoder)
        near_decoder, far_decoder = passed_along(near_rows, 1), passed_along(far_rows, 2)
        near_decoder, far_decoder = lax.optimization_barrier((near_decoder, far_decoder))
        near_lists, far_lists = [
            rows[latents : latents + slots, :tiles].astype(jnp.int32) for rows in (near_decoder, far_decoder)
        ]

    with jax.named_scope("encode"):
        kept_a, kept_b, sent_a, sent_b = encode(lists, counts, enc_bias, x, weights)
        arrived_a, arrived_b = swapped(sent_a, 1), swapped(sent_b, 1)
        step = 2
        while step < parts:
            kept_a, sent_a = merge(kept_a, arrived_a)
            kept_b, sent_b = merge(kept_b, arrived_b)
            arrived_a, arrived_b = swapped(sent_a, step), swapped(sent_b, step)
            step *= 2
        own_a, own_b = activate(kept_a, arrived_a), activate(kept_b, arrived_b)
    with jax.named_scope("spread"):
        late_a, late_b = swapped(own_a, 1), swapped(own_b, 1)
        own = [own_a, own_b, late_a, late_b]
        far_a = passed_along(own_a, 2)
        late_a, far_a = lax.optimization_barrier((late_a, far_a))
        far = [far_a] + [passed_along(piece, 2) for piece in (join(own_b, late_a), late_b)]
    with jax.named_scope("decode"):
        early, late_a, late_b = decode_early(lists, far_lists, own + far[:2], decoder, far_decoder, parts)
        early, late_a, late_b, far[2] = lax.optimization_barrier((early, late_a, late_b, far[2]))
        near = across_cores(choose(own, far))
        late_b = decode_middle(far_lists, late_b, far[2], far_decoder, latents, parts)
        return decode_late(near_lists, [early, late_a, late_b], near, near_decoder, latents, parts)[None]


def solution(mesh):
    placed = (
        P("layer", None, "latent"),
        P("layer", None, "latent"),
        P("layer", "latent"),
        P("layer", None, None, "latent"),
        P("layer", None, None),
        P("layer", None),
    )
    return jax.shard_map(
        shards, mesh=mesh, in_specs=placed, out_specs=P("layer", None, "latent"), check_vma=False
    )
```

time: 73.9 us -> 72.5 us (0.981)
  waiting for transfers between devices: 33 us -> 22.8 us
  starting transfers between devices: 27.2 us -> 35.9 us
    ppermute x3 -> x9, starting transfers between devices: 6.1 us -> 16.6 us  [swapped(): return lax.ppermute(value, 'latent', [(i, i ^ step) for i in range(count)])]
    ppermute x3 -> x9, waiting for transfers between devices: 23.3 us -> 13.8 us  [swapped(): return lax.ppermute(value, 'latent', [(i, i ^ step) for i in range(count)])]
    ppermute x3 -> x0, waiting for transfers between devices: 7.38 us -> none  [rotated(): lax.ppermute(value, 'latent', [(i, (i + step) % count) for i in range(cou...]
    ppermute x4 -> x5, waiting for transfers between devices: 2.14 us -> 8.5 us  [passed_along(): lax.ppermute(value, 'layer', [(i, i + steps) for i in range(count - steps)])]
    ppermute x3 -> x0, starting transfers between devices: 4.73 us -> none  [rotated(): lax.ppermute(value, 'latent', [(i, (i + step) % count) for i in range(cou...]
    ppermute x1, starting transfers between devices: 3.57 us -> 5.87 us  [across_cores(): return lax.ppermute(value, 'layer', [(i, i ^ 1) for i in range(count)])]
    ppermute x4 -> x5, starting transfers between devices: 12.8 us -> 13.5 us  [passed_along(): lax.ppermute(value, 'layer', [(i, i + steps) for i in range(count - steps)])]
  transfers between devices with their start and end apart: 11 -> 15, of which waited for: 6 -> 7; matrix products, arithmetic and copies ran while one was open for 0% -> 0% of each run, Pallas kernels for 8% -> 9%
where the time goes in v7:
time: 72.5 us; the launch traced here: 72.2 us
  starting transfers between devices  35.9 us (50%)
  waiting for transfers between devices  22.8 us (31%)
  Pallas kernels  9.46 us (13%)
  local copies, waits for them, and re-layouts  3.81 us (5%)
    ppermute x9, starting transfers between devices, swapped(): return lax.ppermute(value, 'latent', [(i, i ^ step) for i in range(count)])  16.6 us
    ppermute x9, waiting for transfers between devices, swapped(): return lax.ppermute(value, 'latent', [(i, i ^ step) for i in range(count)])  13.8 us
    ppermute x5, starting transfers between devices, passed_along(): lax.ppermute(value, 'layer', [(i, i + steps) for i in range(count - steps)])  13.5 us
    ppermute x5, waiting for transfers between devices, passed_along(): lax.ppermute(value, 'layer', [(i, i + steps) for i in range(count - steps)])  8.5 us
    ppermute x1, starting transfers between devices, across_cores(): return lax.ppermute(value, 'layer', [(i, i ^ 1) for i in range(count)])  5.87 us
    unnamed x14, local copies, waits for them, and re-layouts  3.81 us
    pallas_call x1, Pallas kernels, decode_late(): pl.pallas_call(functools.partial(late_kernel, parts), out_shape=jax.Shape...  3.14 us
    pallas_call x1, Pallas kernels, decode_early(): pl.pallas_call(functools.partial(early_kernel, parts), out_shape=[jax.Sha...  3.01 us
  transfers between devices with their start and end apart: 15, of which 7 were waited for; matrix products, arithmetic and copies ran while one was open for 0% of the time, Pallas kernels for 9%

profile of v7, /device:TPU:5, one launch (start us, length us, event | category | flops | bytes accessed | tf_op | source)
XLA Modules:
  0.0 72.2 jit_solution(16466687506822106582)
XLA Ops:
  0.0 0.0 copy-start.2
  0.0 1.2 %copy-done.2 = bf16[1,4096,128]{2,1,0:T(8,128)(2,1)S(1)} copy-done((bf16[1,4096,128]{2,1,0:T(8,128)(2,1)S(1)}, bf16[1,4096,128]{2,1,0:T(8,128)(2,1)}, u32[]{:S(2)}) %copy-start.2) | copy-done | bytes 1048600
  1.2 0.1 fetch_rows.1
  1.3 1.4 %collective-permute-start.2 = (bf16[1024,128]{1,0:T(8,128)(2,1)S(1)}, bf16[1024,128]{1,0:T(8,128)(2,1)S(1)}, u32[]{:S(2)}, u32[]{:S(2)}) collective-permute-start(bf16[1024,128]{1,0:T(8,128)(2,1)S(1)} %get-tuple-element.45), channel_id=1, source_target_pairs={{0,1},{1,0},{2,3},{3,2},{4,5},{5,4},{6,7},{7,6},{8,9},{9,8},{10,11... | collective-permute-start | bytes 786440 | tf_op jit(solution)/shard_map/encoder_rows/ppermute | solution.py:18
  2.7 2.3 %collective-permute-start.3 = (bf16[1024,128]{1,0:T(8,128)(2,1)S(1)}, bf16[1024,128]{1,0:T(8,128)(2,1)S(1)}, u32[]{:S(2)}, u32[]{:S(2)}) collective-permute-start(bf16[1024,128]{1,0:T(8,128)(2,1)S(1)} %get-tuple-element.46), channel_id=1, source_target_pairs={{0,2},{1,3},{2,0},{3,1},{4,6},{5,7},{6,4},{7,5},{8,10},{9,11},{10,... | collective-permute-start | bytes 786440 | tf_op jit(solution)/shard_map/encoder_rows/ppermute | solution.py:18
  5.0 0.0 collective-permute-start.4
  5.0 0.0 copy-start
  5.0 1.9 %copy-done = bf16[1,3,512,1024]{3,2,1,0:T(8,128)(2,1)S(1)} copy-done((bf16[1,3,512,1024]{3,2,1,0:T(8,128)(2,1)S(1)}, bf16[1,3,512,1024]{3,2,1,0:T(8,128)(2,1)}, u32[]{:S(2)}) %copy-start) | copy-done | bytes 3145752
  6.9 0.0 copy-start.3
  6.9 0.7 copy-done.3
  7.5 0.1 fetch_decoders.1
  7.7 4.6 %collective-permute-start = (bf16[528,1024]{1,0:T(8,128)(2,1)S(1)}, bf16[528,1024]{1,0:T(8,128)(2,1)S(1)}, u32[]{:S(2)}, u32[]{:S(2)}) collective-permute-start(bf16[528,1024]{1,0:T(8,128)(2,1)S(1)} %get-tuple-element.40), channel_id=1, source_target_pairs={{0,4},{4,8},{8,12},{12,16},{16,20},{20,24},{24,28},{1,5},{5,9},{9,... | collective-permute-start | bytes 3244040 | tf_op jit(solution)/shard_map/decoder_weights/ppermute | solution.py:23
  12.3 1.9 %collective-permute-start.1 = (bf16[528,1024]{1,0:T(8,128)(2,1)S(1)}, bf16[528,1024]{1,0:T(8,128)(2,1)S(1)}, u32[]{:S(2)}, u32[]{:S(2)}) collective-permute-start(bf16[528,1024]{1,0:T(8,128)(2,1)S(1)} %get-tuple-element.41), channel_id=1, source_target_pairs={{0,8},{4,12},{8,16},{12,20},{16,24},{20,28},{1,9},{5,13},{9,17},{1... | collective-permute-start | bytes 3244040 | tf_op jit(solution)/shard_map/decoder_weights/ppermute | solution.py:23
  14.2 0.0 collective-permute-done.2.refs_1_
  14.2 0.0 collective-permute-done.3.refs_2_
  14.3 7.6 %collective-permute-done.4.refs_3_ = bf16[1024,128]{1,0:T(8,128)(2,1)S(1)} collective-permute-done((bf16[1024,128]{1,0:T(8,128)(2,1)S(1)}, bf16[1024,128]{1,0:T(8,128)(2,1)S(1)}, u32[]{:S(2)}, u32[]{:S(2)}) %collective-permute-start.4) | collective-permute-done | bytes 262176 | tf_op jit(solution)/shard_map/encoder_rows/ppermute | solution.py:18
  21.8 0.0 copy-done.4
  21.8 0.0 copy-done.5
  21.9 0.0 copy-done.6
  21.9 0.0 copy-start.1
  21.9 1.9 %encode.1 = (f32[4,2,64,128]{3,2,1,0:T(8,128)S(1)}, f32[4,2,64,128]{3,2,1,0:T(8,128)S(1)}, bf16[4,2,64,128]{3,2,1,0:T(8,128)(2,1)S(1)}, bf16[4,2,64,128]{3,2,1,0:T(8,128)(2,1)S(1)}) custom-call(s32[2,16]{1,0:T(2,128)S(1)} %bitcast.12, s32[16]{0:T(128)S(1)} %bitcast.15, f32[1,128]{1,0:T(1,128)S(1)} %copy-done.6, bf16[1024,1024]{1,0:T(8,128)(2,1)S(1)} %bitcast.14, ...), custom_call_target="tpu_custom_call" | custom-call | flops 17179869184 | bytes 3145728 | tf_op jit(solution)/shard_map/encode/encode/pallas_call | solution.py:114
  23.7 5.9 %collective-permute-start.5 = (bf16[4,2,64,128]{3,2,1,0:T(8,128)(2,1)S(1)}, bf16[4,2,64,128]{3,2,1,0:T(8,128)(2,1)S(1)}, u32[]{:S(2)}, u32[]{:S(2)}) collective-permute-start(bf16[4,2,64,128]{3,2,1,0:T(8,128)(2,1)S(1)} %get-tuple-element.49), channel_id=1, source_target_pairs={{0,1},{1,0},{2,3},{3,2},{4,5},{5,4},{6,7},{7,6},{8,9},{9,8},{10,11... | collective-permute-start | bytes 393224 | tf_op jit(solution)/shard_map/encode/ppermute | solution.py:18
  29.6 0.1 collective-permute-start.7
  29.7 2.6 %collective-permute-done.5.arrived_ref = bf16[4,2,64,128]{3,2,1,0:T(8,128)(2,1)S(1)} collective-permute-done((bf16[4,2,64,128]{3,2,1,0:T(8,128)(2,1)S(1)}, bf16[4,2,64,128]{3,2,1,0:T(8,128)(2,1)S(1)}, u32[]{:S(2)}, u32[]{:S(2)}) %collective-permute-start.5) | collective-permute-done | bytes 131104 | tf_op jit(solution)/shard_map/encode/ppermute | solution.py:18
  32.3 2.5 %collective-permute-start.6 = (bf16[4,2,64,128]{3,2,1,0:T(8,128)(2,1)S(1)}, bf16[4,2,64,128]{3,2,1,0:T(8,128)(2,1)S(1)}, u32[]{:S(2)}, u32[]{:S(2)}) collective-permute-start(bf16[4,2,64,128]{3,2,1,0:T(8,128)(2,1)S(1)} %get-tuple-element.51), channel_id=1, source_target_pairs={{0,2},{1,3},{2,0},{3,1},{4,6},{5,7},{6,4},{7,5},{8,10},{9,11},{10,... | collective-permute-start | bytes 393224 | tf_op jit(solution)/shard_map/encode/ppermute | solution.py:18
  34.8 0.0 collective-permute-done.7.arrived_ref
  34.9 1.8 %collective-permute-start.8 = (bf16[4,2,64,128]{3,2,1,0:T(8,128)(2,1)S(1)}, bf16[4,2,64,128]{3,2,1,0:T(8,128)(2,1)S(1)}, u32[]{:S(2)}, u32[]{:S(2)}) collective-permute-start(bf16[4,2,64,128]{3,2,1,0:T(8,128)(2,1)S(1)} %get-tuple-element.55), channel_id=1, source_target_pairs={{0,2},{1,3},{2,0},{3,1},{4,6},{5,7},{6,4},{7,5},{8,10},{9,11},{10,... | collective-permute-start | bytes 393224 | tf_op jit(solution)/shard_map/encode/ppermute | solution.py:18
  36.7 1.1 %collective-permute-done.6.arrived_ref = bf16[4,2,64,128]{3,2,1,0:T(8,128)(2,1)S(1)} collective-permute-done((bf16[4,2,64,128]{3,2,1,0:T(8,128)(2,1)S(1)}, bf16[4,2,64,128]{3,2,1,0:T(8,128)(2,1)S(1)}, u32[]{:S(2)}, u32[]{:S(2)}) %collective-permute-start.6) | collective-permute-done | bytes 131104 | tf_op jit(solution)/shard_map/encode/ppermute | solution.py:18
  37.9 2.8 %collective-permute-start.11 = (bf16[4,2,64,128]{3,2,1,0:T(8,128)(2,1)S(1)}, bf16[4,2,64,128]{3,2,1,0:T(8,128)(2,1)S(1)}, u32[]{:S(2)}, u32[]{:S(2)}) collective-permute-start(bf16[4,2,64,128]{3,2,1,0:T(8,128)(2,1)S(1)} %activate.2.refs_0_), channel_id=1, source_target_pairs={{0,8},{4,12},{8,16},{12,20},{16,24},{20,28},{1,9},{5,13},{9,17},{1... | collective-permute-start | bytes 393224 | tf_op jit(solution)/shard_map/spread/ppermute | solution.py:23
  40.7 2.5 %collective-permute-start.9 = (bf16[4,2,64,128]{3,2,1,0:T(8,128)(2,1)S(1)}, bf16[4,2,64,128]{3,2,1,0:T(8,128)(2,1)S(1)}, u32[]{:S(2)}, u32[]{:S(2)}) collective-permute-start(bf16[4,2,64,128]{3,2,1,0:T(8,128)(2,1)S(1)} %activate.2.refs_0_), channel_id=1, source_target_pairs={{0,1},{1,0},{2,3},{3,2},{4,5},{5,4},{6,7},{7,6},{8,9},{9,8},{10,11... | collective-permute-start | bytes 393224 | tf_op jit(solution)/shard_map/spread/ppermute | solution.py:18
  43.3 2.5 %collective-permute-done.8.arrived_ref = bf16[4,2,64,128]{3,2,1,0:T(8,128)(2,1)S(1)} collective-permute-done((bf16[4,2,64,128]{3,2,1,0:T(8,128)(2,1)S(1)}, bf16[4,2,64,128]{3,2,1,0:T(8,128)(2,1)S(1)}, u32[]{:S(2)}, u32[]{:S(2)}) %collective-permute-start.8) | collective-permute-done | bytes 131104 | tf_op jit(solution)/shard_map/encode/ppermute | solution.py:18
  45.8 0.1 collective-permute-start.10
  45.8 4.7 %collective-permute-done.11.refs_4_ = bf16[4,2,64,128]{3,2,1,0:T(8,128)(2,1)S(1)} collective-permute-done((bf16[4,2,64,128]{3,2,1,0:T(8,128)(2,1)S(1)}, bf16[4,2,64,128]{3,2,1,0:T(8,128)(2,1)S(1)}, u32[]{:S(2)}, u32[]{:S(2)}) %collective-permute-start.11) | collective-permute-done | bytes 131104 | tf_op jit(solution)/shard_map/spread/ppermute | solution.py:23
  50.5 0.0 collective-permute-done.9.second_ref.refs_2_
  50.6 2.2 %collective-permute-start.12 = (bf16[8,2,64,128]{3,2,1,0:T(8,128)(2,1)S(1)}, bf16[8,2,64,128]{3,2,1,0:T(8,128)(2,1)S(1)}, u32[]{:S(2)}, u32[]{:S(2)}) collective-permute-start(bf16[8,2,64,128]{3,2,1,0:T(8,128)(2,1)S(1)} %join.1), channel_id=1, source_target_pairs={{0,8},{4,12},{8,16},{12,20},{16,24},{20,28},{1,9},{5,13},{9,17},{1... | collective-permute-start | bytes 786440 | tf_op jit(solution)/shard_map/spread/ppermute | solution.py:23
  52.8 0.0 collective-permute-done.10.refs_3_
  52.8 1.9 %collective-permute-start.13 = (bf16[4,2,64,128]{3,2,1,0:T(8,128)(2,1)S(1)}, bf16[4,2,64,128]{3,2,1,0:T(8,128)(2,1)S(1)}, u32[]{:S(2)}, u32[]{:S(2)}) collective-permute-start(bf16[4,2,64,128]{3,2,1,0:T(8,128)(2,1)S(1)} %collective-permute-done.10.refs_3_), channel_id=1, source_target_pairs={{0,8},{4,12},{8,16},{12,20},{16,24},{20,28},{1,9},{5,13},{9,17},{1... | collective-permute-start | bytes 393224 | tf_op jit(solution)/shard_map/spread/ppermute | solution.py:23
  54.7 0.0 collective-permute-done.near_dec
  54.8 0.0 collective-permute-done.1.refs_7_.far_dec
  54.8 3.8 %collective-permute-done.12.refs_5_ = bf16[8,2,64,128]{3,2,1,0:T(8,128)(2,1)S(1)} collective-permute-done((bf16[8,2,64,128]{3,2,1,0:T(8,128)(2,1)S(1)}, bf16[8,2,64,128]{3,2,1,0:T(8,128)(2,1)S(1)}, u32[]{:S(2)}, u32[]{:S(2)}) %collective-permute-start.12) | collective-permute-done | bytes 262176 | tf_op jit(solution)/shard_map/spread/ppermute | solution.py:23
  58.6 0.0 copy-done.1
  58.6 3.0 %decode_early.1 = (f32[512,1024]{1,0:T(8,128)S(1)}, f32[256,1024]{1,0:T(8,128)S(1)}, f32[256,1024]{1,0:T(8,128)S(1)}) custom-call(s32[2,16]{1,0:T(2,128)S(1)} %bitcast.13, s32[2,16]{1,0:T(2,128)S(1)} %slice_convert_fusion.far_lists.lists_ref, bf16[4,2,64,128]{3,2,1,0:T(8,128)(2,1)S(1)} %activate.2.refs_0_, ...), custom_call_target="tpu_custom_call" | custom-call | flops 1879048192 | bytes 6291456 | tf_op jit(solution)/shard_map/decode/decode_early/pallas_call | solution.py:246
  61.6 0.0 collective-permute-done.13.far.refs_6_
  61.6 0.1 choose.1
  61.7 5.9 %collective-permute-start.14 = (bf16[16,2,64,128]{3,2,1,0:T(8,128)(2,1)S(1)}, bf16[16,2,64,128]{3,2,1,0:T(8,128)(2,1)S(1)}, u32[]{:S(2)}, u32[]{:S(2)}) collective-permute-start(bf16[16,2,64,128]{3,2,1,0:T(8,128)(2,1)S(1)} %choose.1), channel_id=1, source_target_pairs={{0,4},{4,0},{8,12},{12,8},{16,20},{20,16},{24,28},{28,24},{1,5},{5... | collective-permute-start | bytes 1572872 | tf_op jit(solution)/shard_map/decode/ppermute | solution.py:28
  67.5 1.0 %decode_middle.1.late_b = f32[256,1024]{1,0:T(8,128)S(1)} custom-call(s32[2,16]{1,0:T(2,128)S(1)} %slice_convert_fusion.far_lists.lists_ref, f32[256,1024]{1,0:T(8,128)S(1)} %get-tuple-element.63.partial_ref, bf16[4,2,64,128]{3,2,1,0:T(8,128)(2,1)S(1)} %collective-permute-done.13.far.refs_6_, bf16[528,1024]{1,0:T(8,128)(2,1)S(1)} %collective-permute-done.1.refs_7_.far_dec), custom_call_target="tpu_custom_call" | custom-call | flops 268435456 | bytes 3145728 | tf_op jit(solution)/shard_map/decode/decode_middle/pallas_call | solution.py:278
  68.6 0.5 collective-permute-done.14.near
  69.1 3.1 %decode_late.1 = bf16[1024,1024]{1,0:T(8,128)(2,1)} custom-call(s32[2,16]{1,0:T(2,128)S(1)} %slice_convert_fusion.1.lists_ref, f32[512,1024]{1,0:T(8,128)S(1)} %get-tuple-element.61.early_ref, f32[256,1024]{1,0:T(8,128)S(1)} %get-tuple-element.62.late_a, f32[256,1024]{1,0:T(8,128)S(1)} %decode_middle.1.late_b, ...), custom_call_target="tpu_custom_call" | custom-call | flops 1073741824 | bytes 7340032 | tf_op jit(solution)/shard_map/decode/decode_late/pallas_call | solution.py:323
  (10 shorter events, 0.2 us)
Async XLA Ops:
  0.0 1.2 %copy-start.2 = (bf16[1,4096,128]{2,1,0:T(8,128)(2,1)S(1)}, bf16[1,4096,128]{2,1,0:T(8,128)(2,1)}, u32[]{:S(2)}) copy-start(bf16[1,4096,128]{2,1,0:T(8,128)(2,1)} %param.7) | copy-start | bytes 3145732
  1.3 12.9 %collective-permute-start.2 = (bf16[1024,128]{1,0:T(8,128)(2,1)S(1)}, bf16[1024,128]{1,0:T(8,128)(2,1)S(1)}, u32[]{:S(2)}, u32[]{:S(2)}) collective-permute-start(bf16[1024,128]{1,0:T(8,128)(2,1)S(1)} %get-tuple-element.45), channel_id=1, source_target_pairs={{0,1},{1,0},{2,3},{3,2},{4,5},{5,4},{6,7},{7,6},{8,9},{9,8},{10,11... | collective-permute-start | bytes 786440 | tf_op jit(solution)/shard_map/encoder_rows/ppermute | solution.py:18
  2.7 11.6 %collective-permute-start.3 = (bf16[1024,128]{1,0:T(8,128)(2,1)S(1)}, bf16[1024,128]{1,0:T(8,128)(2,1)S(1)}, u32[]{:S(2)}, u32[]{:S(2)}) collective-permute-start(bf16[1024,128]{1,0:T(8,128)(2,1)S(1)} %get-tuple-element.46), channel_id=1, source_target_pairs={{0,2},{1,3},{2,0},{3,1},{4,6},{5,7},{6,4},{7,5},{8,10},{9,11},{10,... | collective-permute-start | bytes 786440 | tf_op jit(solution)/shard_map/encoder_rows/ppermute | solution.py:18
  5.0 16.9 %collective-permute-start.4 = (bf16[1024,128]{1,0:T(8,128)(2,1)S(1)}, bf16[1024,128]{1,0:T(8,128)(2,1)S(1)}, u32[]{:S(2)}, u32[]{:S(2)}) collective-permute-start(bf16[1024,128]{1,0:T(8,128)(2,1)S(1)} %get-tuple-element.47), channel_id=1, source_target_pairs={{0,3},{1,2},{2,1},{3,0},{4,7},{5,6},{6,5},{7,4},{8,11},{9,10},{10,... | collective-permute-start | bytes 786440 | tf_op jit(solution)/shard_map/encoder_rows/ppermute | solution.py:18
  5.0 1.9 %copy-start = (bf16[1,3,512,1024]{3,2,1,0:T(8,128)(2,1)S(1)}, bf16[1,3,512,1024]{3,2,1,0:T(8,128)(2,1)}, u32[]{:S(2)}) copy-start(bf16[1,3,512,1024]{3,2,1,0:T(8,128)(2,1)} %param.9) | copy-start | bytes 9437188
  6.9 0.7 copy-start.3
  7.5 14.3 %copy-start.4 = (bf16[1,1024,1024]{2,1,0:T(8,128)(2,1)S(1)}, bf16[1,1024,1024]{2,1,0:T(8,128)(2,1)}, u32[]{:S(2)}) copy-start(bf16[1,1024,1024]{2,1,0:T(8,128)(2,1)} %param.6) | copy-start | bytes 6291460
  7.5 14.3 %copy-start.5 = (s32[1,16]{1,0:T(1,128)S(1)}, s32[1,16]{1,0:T(1,128)}, u32[]{:S(2)}) copy-start(s32[1,16]{1,0:T(1,128)} %param.11) | copy-start | bytes 196
  7.5 14.3 %copy-start.6 = (f32[1,128]{1,0:T(1,128)S(1)}, f32[1,128]{1,0:T(1,128)}, u32[]{:S(2)}) copy-start(f32[1,128]{1,0:T(1,128)} %bias_ref.1) | copy-start | bytes 1540
  7.7 47.1 %collective-permute-start = (bf16[528,1024]{1,0:T(8,128)(2,1)S(1)}, bf16[528,1024]{1,0:T(8,128)(2,1)S(1)}, u32[]{:S(2)}, u32[]{:S(2)}) collective-permute-start(bf16[528,1024]{1,0:T(8,128)(2,1)S(1)} %get-tuple-element.40), channel_id=1, source_target_pairs={{0,4},{4,8},{8,12},{12,16},{16,20},{20,24},{24,28},{1,5},{5,9},{9,... | collective-permute-start | bytes 3244040 | tf_op jit(solution)/shard_map/decoder_weights/ppermute | solution.py:23
  12.3 42.5 %collective-permute-start.1 = (bf16[528,1024]{1,0:T(8,128)(2,1)S(1)}, bf16[528,1024]{1,0:T(8,128)(2,1)S(1)}, u32[]{:S(2)}, u32[]{:S(2)}) collective-permute-start(bf16[528,1024]{1,0:T(8,128)(2,1)S(1)} %get-tuple-element.41), channel_id=1, source_target_pairs={{0,8},{4,12},{8,16},{12,20},{16,24},{20,28},{1,9},{5,13},{9,17},{1... | collective-permute-start | bytes 3244040 | tf_op jit(solution)/shard_map/decoder_weights/ppermute | solution.py:23
  21.9 36.7 %copy-start.1 = (bf16[1,3,512,1024]{3,2,1,0:T(8,128)(2,1)S(1)}, bf16[1,3,512,1024]{3,2,1,0:T(8,128)(2,1)}, u32[]{:S(2)}) copy-start(bf16[1,3,512,1024]{3,2,1,0:T(8,128)(2,1)} %param.9) | copy-start | bytes 9437188
  23.7 8.5 %collective-permute-start.5 = (bf16[4,2,64,128]{3,2,1,0:T(8,128)(2,1)S(1)}, bf16[4,2,64,128]{3,2,1,0:T(8,128)(2,1)S(1)}, u32[]{:S(2)}, u32[]{:S(2)}) collective-permute-start(bf16[4,2,64,128]{3,2,1,0:T(8,128)(2,1)S(1)} %get-tuple-element.49), channel_id=1, source_target_pairs={{0,1},{1,0},{2,3},{3,2},{4,5},{5,4},{6,7},{7,6},{8,9},{9,8},{10,11... | collective-permute-start | bytes 393224 | tf_op jit(solution)/shard_map/encode/ppermute | solution.py:18
  29.6 5.2 %collective-permute-start.7 = (bf16[4,2,64,128]{3,2,1,0:T(8,128)(2,1)S(1)}, bf16[4,2,64,128]{3,2,1,0:T(8,128)(2,1)S(1)}, u32[]{:S(2)}, u32[]{:S(2)}) collective-permute-start(bf16[4,2,64,128]{3,2,1,0:T(8,128)(2,1)S(1)} %get-tuple-element.53), channel_id=1, source_target_pairs={{0,1},{1,0},{2,3},{3,2},{4,5},{5,4},{6,7},{7,6},{8,9},{9,8},{10,11... | collective-permute-start | bytes 393224 | tf_op jit(solution)/shard_map/encode/ppermute | solution.py:18
  32.3 5.5 %collective-permute-start.6 = (bf16[4,2,64,128]{3,2,1,0:T(8,128)(2,1)S(1)}, bf16[4,2,64,128]{3,2,1,0:T(8,128)(2,1)S(1)}, u32[]{:S(2)}, u32[]{:S(2)}) collective-permute-start(bf16[4,2,64,128]{3,2,1,0:T(8,128)(2,1)S(1)} %get-tuple-element.51), channel_id=1, source_target_pairs={{0,2},{1,3},{2,0},{3,1},{4,6},{5,7},{6,4},{7,5},{8,10},{9,11},{10,... | collective-permute-start | bytes 393224 | tf_op jit(solution)/shard_map/encode/ppermute | solution.py:18
  34.9 10.8 %collective-permute-start.8 = (bf16[4,2,64,128]{3,2,1,0:T(8,128)(2,1)S(1)}, bf16[4,2,64,128]{3,2,1,0:T(8,128)(2,1)S(1)}, u32[]{:S(2)}, u32[]{:S(2)}) collective-permute-start(bf16[4,2,64,128]{3,2,1,0:T(8,128)(2,1)S(1)} %get-tuple-element.55), channel_id=1, source_target_pairs={{0,2},{1,3},{2,0},{3,1},{4,6},{5,7},{6,4},{7,5},{8,10},{9,11},{10,... | collective-permute-start | bytes 393224 | tf_op jit(solution)/shard_map/encode/ppermute | solution.py:18
  37.9 12.7 %collective-permute-start.11 = (bf16[4,2,64,128]{3,2,1,0:T(8,128)(2,1)S(1)}, bf16[4,2,64,128]{3,2,1,0:T(8,128)(2,1)S(1)}, u32[]{:S(2)}, u32[]{:S(2)}) collective-permute-start(bf16[4,2,64,128]{3,2,1,0:T(8,128)(2,1)S(1)} %activate.2.refs_0_), channel_id=1, source_target_pairs={{0,8},{4,12},{8,16},{12,20},{16,24},{20,28},{1,9},{5,13},{9,17},{1... | collective-permute-start | bytes 393224 | tf_op jit(solution)/shard_map/spread/ppermute | solution.py:23
  40.7 9.8 %collective-permute-start.9 = (bf16[4,2,64,128]{3,2,1,0:T(8,128)(2,1)S(1)}, bf16[4,2,64,128]{3,2,1,0:T(8,128)(2,1)S(1)}, u32[]{:S(2)}, u32[]{:S(2)}) collective-permute-start(bf16[4,2,64,128]{3,2,1,0:T(8,128)(2,1)S(1)} %activate.2.refs_0_), channel_id=1, source_target_pairs={{0,1},{1,0},{2,3},{3,2},{4,5},{5,4},{6,7},{7,6},{8,9},{9,8},{10,11... | collective-permute-start | bytes 393224 | tf_op jit(solution)/shard_map/spread/ppermute | solution.py:18
  45.8 7.0 %collective-permute-start.10 = (bf16[4,2,64,128]{3,2,1,0:T(8,128)(2,1)S(1)}, bf16[4,2,64,128]{3,2,1,0:T(8,128)(2,1)S(1)}, u32[]{:S(2)}, u32[]{:S(2)}) collective-permute-start(bf16[4,2,64,128]{3,2,1,0:T(8,128)(2,1)S(1)} %activate.3.first_ref.refs_1_), channel_id=1, source_target_pairs={{0,1},{1,0},{2,3},{3,2},{4,5},{5,4},{6,7},{7,6},{8,9},{9,8},{10,11... | collective-permute-start | bytes 393224 | tf_op jit(solution)/shard_map/spread/ppermute | solution.py:18
  50.6 8.0 %collective-permute-start.12 = (bf16[8,2,64,128]{3,2,1,0:T(8,128)(2,1)S(1)}, bf16[8,2,64,128]{3,2,1,0:T(8,128)(2,1)S(1)}, u32[]{:S(2)}, u32[]{:S(2)}) collective-permute-start(bf16[8,2,64,128]{3,2,1,0:T(8,128)(2,1)S(1)} %join.1), channel_id=1, source_target_pairs={{0,8},{4,12},{8,16},{12,20},{16,24},{20,28},{1,9},{5,13},{9,17},{1... | collective-permute-start | bytes 786440 | tf_op jit(solution)/shard_map/spread/ppermute | solution.py:23
  52.8 8.8 %collective-permute-start.13 = (bf16[4,2,64,128]{3,2,1,0:T(8,128)(2,1)S(1)}, bf16[4,2,64,128]{3,2,1,0:T(8,128)(2,1)S(1)}, u32[]{:S(2)}, u32[]{:S(2)}) collective-permute-start(bf16[4,2,64,128]{3,2,1,0:T(8,128)(2,1)S(1)} %collective-permute-done.10.refs_3_), channel_id=1, source_target_pairs={{0,8},{4,12},{8,16},{12,20},{16,24},{20,28},{1,9},{5,13},{9,17},{1... | collective-permute-start | bytes 393224 | tf_op jit(solution)/shard_map/spread/ppermute | solution.py:23
  61.7 7.4 %collective-permute-start.14 = (bf16[16,2,64,128]{3,2,1,0:T(8,128)(2,1)S(1)}, bf16[16,2,64,128]{3,2,1,0:T(8,128)(2,1)S(1)}, u32[]{:S(2)}, u32[]{:S(2)}) collective-permute-start(bf16[16,2,64,128]{3,2,1,0:T(8,128)(2,1)S(1)} %choose.1), channel_id=1, source_target_pairs={{0,4},{4,0},{8,12},{12,8},{16,20},{20,16},{24,28},{28,24},{1,5},{5... | collective-permute-start | bytes 1572872 | tf_op jit(solution)/shard_map/decode/ppermute | solution.py:28

commit v8 on v7

--- a/solution.py
+++ b/solution.py
@@ -369,15 +369,19 @@
         while step < parts:
             kept_a, sent_a = merge(kept_a, arrived_a)
             kept_b, sent_b = merge(kept_b, arrived_b)
-            arrived_a, arrived_b = swapped(sent_a, step), swapped(sent_b, step)
+            arrived_a = swapped(sent_a, step)
+            arrived_a, sent_b = lax.optimization_barrier((arrived_a, sent_b))
+            arrived_b = swapped(sent_b, step)
             step *= 2
         own_a, own_b = activate(kept_a, arrived_a), activate(kept_b, arrived_b)
     with jax.named_scope("spread"):
-        late_a, late_b = swapped(own_a, 1), swapped(own_b, 1)
+        late_a = swapped(own_a, 1)
+        far_a = passed_along(own_a, 2)
+        late_b = swapped(own_b, 1)
+        joined = join(own_b, late_a)
+        late_b, far_a = lax.optimization_barrier((late_b, far_a))
         own = [own_a, own_b, late_a, late_b]
-        far_a = passed_along(own_a, 2)
-        late_a, far_a = lax.optimization_barrier((late_a, far_a))
-        far = [far_a] + [passed_along(piece, 2) for piece in (join(own_b, late_a), late_b)]
+        far = [far_a] + [passed_along(piece, 2) for piece in (joined, late_b)]
     with jax.named_scope("decode"):
         early, late_a, late_b = decode_early(lists, far_lists, own + far[:2], decoder, far_decoder, parts)
         early, late_a, late_b, far[2] = lax.optimization_barrier((early, late_a, late_b, far[2]))

time: 72.5 us -> 69.6 us (0.960)
  waiting for transfers between devices: 22.8 us -> 18.6 us
  starting transfers between devices: 35.9 us -> 37 us
    ppermute x5, waiting for transfers between devices: 8.5 us -> 2.46 us  [passed_along(): lax.ppermute(value, 'layer', [(i, i + steps) for i in range(count - steps)])]
    ppermute x5, starting transfers between devices: 13.5 us -> 15.6 us  [passed_along(): lax.ppermute(value, 'layer', [(i, i + steps) for i in range(count - steps)])]
    ppermute x9, waiting for transfers between devices: 13.8 us -> 15.6 us  [swapped(): return lax.ppermute(value, 'latent', [(i, i ^ step) for i in range(count)])]
    ppermute x9, starting transfers between devices: 16.6 us -> 14.8 us  [swapped(): return lax.ppermute(value, 'latent', [(i, i ^ step) for i in range(count)])]
    ppermute x1, starting transfers between devices: 5.87 us -> 6.64 us  [across_cores(): return lax.ppermute(value, 'layer', [(i, i ^ 1) for i in range(count)])]
  transfers between devices with their start and end apart: 15 -> 15, of which waited for: 7 -> 8; matrix products, arithmetic and copies ran while one was open for 0% -> 0% of each run, Pallas kernels for 9% -> 9%
where the time goes in v8:
time: 69.6 us; the launch traced here: 69 us
  starting transfers between devices  37 us (53%)
  waiting for transfers between devices  18.6 us (27%)
  Pallas kernels  9.45 us (14%)
  local copies, waits for them, and re-layouts  3.81 us (5%)
    ppermute x9, waiting for transfers between devices, swapped(): return lax.ppermute(value, 'latent', [(i, i ^ step) for i in range(count)])  15.6 us
    ppermute x5, starting transfers between devices, passed_along(): lax.ppermute(value, 'layer', [(i, i + steps) for i in range(count - steps)])  15.6 us
    ppermute x9, starting transfers between devices, swapped(): return lax.ppermute(value, 'latent', [(i, i ^ step) for i in range(count)])  14.8 us
    ppermute x1, starting transfers between devices, across_cores(): return lax.ppermute(value, 'layer', [(i, i ^ 1) for i in range(count)])  6.64 us
    unnamed x14, local copies, waits for them, and re-layouts  3.81 us
    pallas_call x1, Pallas kernels, decode_late(): pl.pallas_call(functools.partial(late_kernel, parts), out_shape=jax.Shape...  3.14 us
    pallas_call x1, Pallas kernels, decode_early(): pl.pallas_call(functools.partial(early_kernel, parts), out_shape=[jax.Sha...  3.02 us
    ppermute x5, waiting for transfers between devices, passed_along(): lax.ppermute(value, 'layer', [(i, i + steps) for i in range(count - steps)])  2.46 us
  transfers between devices with their start and end apart: 15, of which 8 were waited for; matrix products, arithmetic and copies ran while one was open for 0% of the time, Pallas kernels for 9%

profile of v8, /device:TPU:5, one launch (start us, length us, event | category | flops | bytes accessed | tf_op | source)
XLA Modules:
  0.0 69.0 jit_solution(5942481384636908309)
XLA Ops:
  0.0 0.0 copy-start.2
  0.0 1.2 %copy-done.2 = bf16[1,4096,128]{2,1,0:T(8,128)(2,1)S(1)} copy-done((bf16[1,4096,128]{2,1,0:T(8,128)(2,1)S(1)}, bf16[1,4096,128]{2,1,0:T(8,128)(2,1)}, u32[]{:S(2)}) %copy-start.2) | copy-done | bytes 1048600
  1.2 0.1 fetch_rows.1
  1.3 1.4 %collective-permute-start.2 = (bf16[1024,128]{1,0:T(8,128)(2,1)S(1)}, bf16[1024,128]{1,0:T(8,128)(2,1)S(1)}, u32[]{:S(2)}, u32[]{:S(2)}) collective-permute-start(bf16[1024,128]{1,0:T(8,128)(2,1)S(1)} %get-tuple-element.47), channel_id=1, source_target_pairs={{0,1},{1,0},{2,3},{3,2},{4,5},{5,4},{6,7},{7,6},{8,9},{9,8},{10,11... | collective-permute-start | bytes 786440 | tf_op jit(solution)/shard_map/encoder_rows/ppermute | solution.py:18
  2.7 2.3 %collective-permute-start.3 = (bf16[1024,128]{1,0:T(8,128)(2,1)S(1)}, bf16[1024,128]{1,0:T(8,128)(2,1)S(1)}, u32[]{:S(2)}, u32[]{:S(2)}) collective-permute-start(bf16[1024,128]{1,0:T(8,128)(2,1)S(1)} %get-tuple-element.48), channel_id=1, source_target_pairs={{0,2},{1,3},{2,0},{3,1},{4,6},{5,7},{6,4},{7,5},{8,10},{9,11},{10,... | collective-permute-start | bytes 786440 | tf_op jit(solution)/shard_map/encoder_rows/ppermute | solution.py:18
  5.0 0.0 collective-permute-start.4
  5.0 0.0 copy-start
  5.0 1.9 %copy-done = bf16[1,3,512,1024]{3,2,1,0:T(8,128)(2,1)S(1)} copy-done((bf16[1,3,512,1024]{3,2,1,0:T(8,128)(2,1)S(1)}, bf16[1,3,512,1024]{3,2,1,0:T(8,128)(2,1)}, u32[]{:S(2)}) %copy-start) | copy-done | bytes 3145752
  6.9 0.0 copy-start.3
  6.9 0.7 copy-done.3
  7.5 0.0 copy-start.4
  7.5 0.1 fetch_decoders.1
  7.7 4.6 %collective-permute-start = (bf16[528,1024]{1,0:T(8,128)(2,1)S(1)}, bf16[528,1024]{1,0:T(8,128)(2,1)S(1)}, u32[]{:S(2)}, u32[]{:S(2)}) collective-permute-start(bf16[528,1024]{1,0:T(8,128)(2,1)S(1)} %get-tuple-element.42), channel_id=1, source_target_pairs={{0,4},{4,8},{8,12},{12,16},{16,20},{20,24},{24,28},{1,5},{5,9},{9,... | collective-permute-start | bytes 3244040 | tf_op jit(solution)/shard_map/decoder_weights/ppermute | solution.py:23
  12.3 1.9 %collective-permute-start.1 = (bf16[528,1024]{1,0:T(8,128)(2,1)S(1)}, bf16[528,1024]{1,0:T(8,128)(2,1)S(1)}, u32[]{:S(2)}, u32[]{:S(2)}) collective-permute-start(bf16[528,1024]{1,0:T(8,128)(2,1)S(1)} %get-tuple-element.43), channel_id=1, source_target_pairs={{0,8},{4,12},{8,16},{12,20},{16,24},{20,28},{1,9},{5,13},{9,17},{1... | collective-permute-start | bytes 3244040 | tf_op jit(solution)/shard_map/decoder_weights/ppermute | solution.py:23
  14.2 0.0 collective-permute-done.2.refs_1_
  14.2 0.0 collective-permute-done.3.refs_2_
  14.3 7.6 %collective-permute-done.4.refs_3_ = bf16[1024,128]{1,0:T(8,128)(2,1)S(1)} collective-permute-done((bf16[1024,128]{1,0:T(8,128)(2,1)S(1)}, bf16[1024,128]{1,0:T(8,128)(2,1)S(1)}, u32[]{:S(2)}, u32[]{:S(2)}) %collective-permute-start.4) | collective-permute-done | bytes 262176 | tf_op jit(solution)/shard_map/encoder_rows/ppermute | solution.py:18
  21.8 0.0 copy-done.4
  21.8 0.0 copy-done.5
  21.9 0.0 copy-done.6
  21.9 0.0 copy-start.1
  21.9 1.9 %encode.1 = (f32[4,2,64,128]{3,2,1,0:T(8,128)S(1)}, f32[4,2,64,128]{3,2,1,0:T(8,128)S(1)}, bf16[4,2,64,128]{3,2,1,0:T(8,128)(2,1)S(1)}, bf16[4,2,64,128]{3,2,1,0:T(8,128)(2,1)S(1)}) custom-call(s32[2,16]{1,0:T(2,128)S(1)} %bitcast.12, s32[16]{0:T(128)S(1)} %bitcast.15, f32[1,128]{1,0:T(1,128)S(1)} %copy-done.6, bf16[1024,1024]{1,0:T(8,128)(2,1)S(1)} %bitcast.14, ...), custom_call_target="tpu_custom_call" | custom-call | flops 17179869184 | bytes 3145728 | tf_op jit(solution)/shard_map/encode/encode/pallas_call | solution.py:114
  23.7 5.9 %collective-permute-start.5 = (bf16[4,2,64,128]{3,2,1,0:T(8,128)(2,1)S(1)}, bf16[4,2,64,128]{3,2,1,0:T(8,128)(2,1)S(1)}, u32[]{:S(2)}, u32[]{:S(2)}) collective-permute-start(bf16[4,2,64,128]{3,2,1,0:T(8,128)(2,1)S(1)} %get-tuple-element.51), channel_id=1, source_target_pairs={{0,1},{1,0},{2,3},{3,2},{4,5},{5,4},{6,7},{7,6},{8,9},{9,8},{10,11... | collective-permute-start | bytes 393224 | tf_op jit(solution)/shard_map/encode/ppermute | solution.py:18
  29.6 0.1 collective-permute-start.7
  29.7 2.6 %collective-permute-done.5.arrived_ref = bf16[4,2,64,128]{3,2,1,0:T(8,128)(2,1)S(1)} collective-permute-done((bf16[4,2,64,128]{3,2,1,0:T(8,128)(2,1)S(1)}, bf16[4,2,64,128]{3,2,1,0:T(8,128)(2,1)S(1)}, u32[]{:S(2)}, u32[]{:S(2)}) %collective-permute-start.5) | collective-permute-done | bytes 131104 | tf_op jit(solution)/shard_map/encode/ppermute | solution.py:18
  32.3 2.5 %collective-permute-start.6 = (bf16[4,2,64,128]{3,2,1,0:T(8,128)(2,1)S(1)}, bf16[4,2,64,128]{3,2,1,0:T(8,128)(2,1)S(1)}, u32[]{:S(2)}, u32[]{:S(2)}) collective-permute-start(bf16[4,2,64,128]{3,2,1,0:T(8,128)(2,1)S(1)} %get-tuple-element.53), channel_id=1, source_target_pairs={{0,2},{1,3},{2,0},{3,1},{4,6},{5,7},{6,4},{7,5},{8,10},{9,11},{10,... | collective-permute-start | bytes 393224 | tf_op jit(solution)/shard_map/encode/ppermute | solution.py:18
  34.8 0.0 collective-permute-done.7.arrived_ref
  34.9 3.0 %collective-permute-done.6.arrived_ref = bf16[4,2,64,128]{3,2,1,0:T(8,128)(2,1)S(1)} collective-permute-done((bf16[4,2,64,128]{3,2,1,0:T(8,128)(2,1)S(1)}, bf16[4,2,64,128]{3,2,1,0:T(8,128)(2,1)S(1)}, u32[]{:S(2)}, u32[]{:S(2)}) %collective-permute-start.6) | collective-permute-done | bytes 131104 | tf_op jit(solution)/shard_map/encode/ppermute | solution.py:18
  37.8 2.4 %collective-permute-start.8 = (bf16[4,2,64,128]{3,2,1,0:T(8,128)(2,1)S(1)}, bf16[4,2,64,128]{3,2,1,0:T(8,128)(2,1)S(1)}, u32[]{:S(2)}, u32[]{:S(2)}) collective-permute-start(bf16[4,2,64,128]{3,2,1,0:T(8,128)(2,1)S(1)} %get-tuple-element.59), channel_id=1, source_target_pairs={{0,2},{1,3},{2,0},{3,1},{4,6},{5,7},{6,4},{7,5},{8,10},{9,11},{10,... | collective-permute-start | bytes 393224 | tf_op jit(solution)/shard_map/encode/ppermute | solution.py:18
  40.3 0.1 collective-permute-start.9
  40.4 2.8 %collective-permute-start.11 = (bf16[4,2,64,128]{3,2,1,0:T(8,128)(2,1)S(1)}, bf16[4,2,64,128]{3,2,1,0:T(8,128)(2,1)S(1)}, u32[]{:S(2)}, u32[]{:S(2)}) collective-permute-start(bf16[4,2,64,128]{3,2,1,0:T(8,128)(2,1)S(1)} %activate.2.refs_0_), channel_id=1, source_target_pairs={{0,8},{4,12},{8,16},{12,20},{16,24},{20,28},{1,9},{5,13},{9,17},{1... | collective-permute-start | bytes 393224 | tf_op jit(solution)/shard_map/spread/ppermute | solution.py:23
  43.2 1.9 %collective-permute-done.8.arrived_ref = bf16[4,2,64,128]{3,2,1,0:T(8,128)(2,1)S(1)} collective-permute-done((bf16[4,2,64,128]{3,2,1,0:T(8,128)(2,1)S(1)}, bf16[4,2,64,128]{3,2,1,0:T(8,128)(2,1)S(1)}, u32[]{:S(2)}, u32[]{:S(2)}) %collective-permute-start.8) | collective-permute-done | bytes 131104 | tf_op jit(solution)/shard_map/encode/ppermute | solution.py:18
  45.2 0.1 collective-permute-start.10
  45.3 0.0 collective-permute-done.9.second_ref.refs_2_
  45.3 3.1 %collective-permute-start.12 = (bf16[8,2,64,128]{3,2,1,0:T(8,128)(2,1)S(1)}, bf16[8,2,64,128]{3,2,1,0:T(8,128)(2,1)S(1)}, u32[]{:S(2)}, u32[]{:S(2)}) collective-permute-start(bf16[8,2,64,128]{3,2,1,0:T(8,128)(2,1)S(1)} %join.1), channel_id=1, source_target_pairs={{0,8},{4,12},{8,16},{12,20},{16,24},{20,28},{1,9},{5,13},{9,17},{1... | collective-permute-start | bytes 786440 | tf_op jit(solution)/shard_map/spread/ppermute | solution.py:23
  48.5 2.1 %collective-permute-done.11.refs_4_ = bf16[4,2,64,128]{3,2,1,0:T(8,128)(2,1)S(1)} collective-permute-done((bf16[4,2,64,128]{3,2,1,0:T(8,128)(2,1)S(1)}, bf16[4,2,64,128]{3,2,1,0:T(8,128)(2,1)S(1)}, u32[]{:S(2)}, u32[]{:S(2)}) %collective-permute-start.11) | collective-permute-done | bytes 131104 | tf_op jit(solution)/shard_map/spread/ppermute | solution.py:23
  50.5 0.5 collective-permute-done.10.refs_3_
  51.1 3.1 %collective-permute-start.13 = (bf16[4,2,64,128]{3,2,1,0:T(8,128)(2,1)S(1)}, bf16[4,2,64,128]{3,2,1,0:T(8,128)(2,1)S(1)}, u32[]{:S(2)}, u32[]{:S(2)}) collective-permute-start(bf16[4,2,64,128]{3,2,1,0:T(8,128)(2,1)S(1)} %collective-permute-done.10.refs_3_), channel_id=1, source_target_pairs={{0,8},{4,12},{8,16},{12,20},{16,24},{20,28},{1,9},{5,13},{9,17},{1... | collective-permute-start | bytes 393224 | tf_op jit(solution)/shard_map/spread/ppermute | solution.py:23
  54.2 0.0 collective-permute-done.near_dec
  54.2 0.0 collective-permute-done.1.refs_7_.far_dec
  54.3 0.0 collective-permute-done.12.refs_5_
  54.3 0.0 copy-done.1
  54.3 3.0 %decode_early.1 = (f32[512,1024]{1,0:T(8,128)S(1)}, f32[256,1024]{1,0:T(8,128)S(1)}, f32[256,1024]{1,0:T(8,128)S(1)}) custom-call(s32[2,16]{1,0:T(2,128)S(1)} %bitcast.13, s32[2,16]{1,0:T(2,128)S(1)} %slice_convert_fusion.far_lists.lists_ref, bf16[4,2,64,128]{3,2,1,0:T(8,128)(2,1)S(1)} %activate.2.refs_0_, ...), custom_call_target="tpu_custom_call" | custom-call | flops 1879048192 | bytes 6291456 | tf_op jit(solution)/shard_map/decode/decode_early/pallas_call | solution.py:246
  57.3 0.4 collective-permute-done.13.far.refs_6_
  57.7 6.6 %collective-permute-start.14 = (bf16[16,2,64,128]{3,2,1,0:T(8,128)(2,1)S(1)}, bf16[16,2,64,128]{3,2,1,0:T(8,128)(2,1)S(1)}, u32[]{:S(2)}, u32[]{:S(2)}) collective-permute-start(bf16[16,2,64,128]{3,2,1,0:T(8,128)(2,1)S(1)} %choose.1), channel_id=1, source_target_pairs={{0,4},{4,0},{8,12},{12,8},{16,20},{20,16},{24,28},{28,24},{1,5},{5... | collective-permute-start | bytes 1572872 | tf_op jit(solution)/shard_map/decode/ppermute | solution.py:28
  64.4 1.0 %decode_middle.1.late_b = f32[256,1024]{1,0:T(8,128)S(1)} custom-call(s32[2,16]{1,0:T(2,128)S(1)} %slice_convert_fusion.far_lists.lists_ref, f32[256,1024]{1,0:T(8,128)S(1)} %get-tuple-element.67.partial_ref, bf16[4,2,64,128]{3,2,1,0:T(8,128)(2,1)S(1)} %collective-permute-done.13.far.refs_6_, bf16[528,1024]{1,0:T(8,128)(2,1)S(1)} %collective-permute-done.1.refs_7_.far_dec), custom_call_target="tpu_custom_call" | custom-call | flops 268435456 | bytes 3145728 | tf_op jit(solution)/shard_map/decode/decode_middle/pallas_call | solution.py:278
  65.4 0.5 collective-permute-done.14.near
  65.9 3.1 %decode_late.1 = bf16[1024,1024]{1,0:T(8,128)(2,1)} custom-call(s32[2,16]{1,0:T(2,128)S(1)} %slice_convert_fusion.1.lists_ref, f32[512,1024]{1,0:T(8,128)S(1)} %get-tuple-element.65.early_ref, f32[256,1024]{1,0:T(8,128)S(1)} %get-tuple-element.66.late_a, f32[256,1024]{1,0:T(8,128)S(1)} %decode_middle.1.late_b, ...), custom_call_target="tpu_custom_call" | custom-call | flops 1073741824 | bytes 7340032 | tf_op jit(solution)/shard_map/decode/decode_late/pallas_call | solution.py:323
  (10 shorter events, 0.2 us)
Async XLA Ops:
  0.0 1.2 %copy-start.2 = (bf16[1,4096,128]{2,1,0:T(8,128)(2,1)S(1)}, bf16[1,4096,128]{2,1,0:T(8,128)(2,1)}, u32[]{:S(2)}) copy-start(bf16[1,4096,128]{2,1,0:T(8,128)(2,1)} %param.7) | copy-start | bytes 3145732
  1.3 12.9 %collective-permute-start.2 = (bf16[1024,128]{1,0:T(8,128)(2,1)S(1)}, bf16[1024,128]{1,0:T(8,128)(2,1)S(1)}, u32[]{:S(2)}, u32[]{:S(2)}) collective-permute-start(bf16[1024,128]{1,0:T(8,128)(2,1)S(1)} %get-tuple-element.47), channel_id=1, source_target_pairs={{0,1},{1,0},{2,3},{3,2},{4,5},{5,4},{6,7},{7,6},{8,9},{9,8},{10,11... | collective-permute-start | bytes 786440 | tf_op jit(solution)/shard_map/encoder_rows/ppermute | solution.py:18
  2.7 11.6 %collective-permute-start.3 = (bf16[1024,128]{1,0:T(8,128)(2,1)S(1)}, bf16[1024,128]{1,0:T(8,128)(2,1)S(1)}, u32[]{:S(2)}, u32[]{:S(2)}) collective-permute-start(bf16[1024,128]{1,0:T(8,128)(2,1)S(1)} %get-tuple-element.48), channel_id=1, source_target_pairs={{0,2},{1,3},{2,0},{3,1},{4,6},{5,7},{6,4},{7,5},{8,10},{9,11},{10,... | collective-permute-start | bytes 786440 | tf_op jit(solution)/shard_map/encoder_rows/ppermute | solution.py:18
  5.0 16.9 %collective-permute-start.4 = (bf16[1024,128]{1,0:T(8,128)(2,1)S(1)}, bf16[1024,128]{1,0:T(8,128)(2,1)S(1)}, u32[]{:S(2)}, u32[]{:S(2)}) collective-permute-start(bf16[1024,128]{1,0:T(8,128)(2,1)S(1)} %get-tuple-element.49), channel_id=1, source_target_pairs={{0,3},{1,2},{2,1},{3,0},{4,7},{5,6},{6,5},{7,4},{8,11},{9,10},{10,... | collective-permute-start | bytes 786440 | tf_op jit(solution)/shard_map/encoder_rows/ppermute | solution.py:18
  5.0 1.9 %copy-start = (bf16[1,3,512,1024]{3,2,1,0:T(8,128)(2,1)S(1)}, bf16[1,3,512,1024]{3,2,1,0:T(8,128)(2,1)}, u32[]{:S(2)}) copy-start(bf16[1,3,512,1024]{3,2,1,0:T(8,128)(2,1)} %param.9) | copy-start | bytes 9437188
  6.9 0.7 copy-start.3
  7.5 14.3 %copy-start.4 = (bf16[1,1024,1024]{2,1,0:T(8,128)(2,1)S(1)}, bf16[1,1024,1024]{2,1,0:T(8,128)(2,1)}, u32[]{:S(2)}) copy-start(bf16[1,1024,1024]{2,1,0:T(8,128)(2,1)} %param.6) | copy-start | bytes 6291460
  7.5 14.3 %copy-start.5 = (s32[1,16]{1,0:T(1,128)S(1)}, s32[1,16]{1,0:T(1,128)}, u32[]{:S(2)}) copy-start(s32[1,16]{1,0:T(1,128)} %param.11) | copy-start | bytes 196
  7.5 14.3 %copy-start.6 = (f32[1,128]{1,0:T(1,128)S(1)}, f32[1,128]{1,0:T(1,128)}, u32[]{:S(2)}) copy-start(f32[1,128]{1,0:T(1,128)} %bias_ref.1) | copy-start | bytes 1540
  7.7 46.5 %collective-permute-start = (bf16[528,1024]{1,0:T(8,128)(2,1)S(1)}, bf16[528,1024]{1,0:T(8,128)(2,1)S(1)}, u32[]{:S(2)}, u32[]{:S(2)}) collective-permute-start(bf16[528,1024]{1,0:T(8,128)(2,1)S(1)} %get-tuple-element.42), channel_id=1, source_target_pairs={{0,4},{4,8},{8,12},{12,16},{16,20},{20,24},{24,28},{1,5},{5,9},{9,... | collective-permute-start | bytes 3244040 | tf_op jit(solution)/shard_map/decoder_weights/ppermute | solution.py:23
  12.3 41.9 %collective-permute-start.1 = (bf16[528,1024]{1,0:T(8,128)(2,1)S(1)}, bf16[528,1024]{1,0:T(8,128)(2,1)S(1)}, u32[]{:S(2)}, u32[]{:S(2)}) collective-permute-start(bf16[528,1024]{1,0:T(8,128)(2,1)S(1)} %get-tuple-element.43), channel_id=1, source_target_pairs={{0,8},{4,12},{8,16},{12,20},{16,24},{20,28},{1,9},{5,13},{9,17},{1... | collective-permute-start | bytes 3244040 | tf_op jit(solution)/shard_map/decoder_weights/ppermute | solution.py:23
  21.9 32.4 %copy-start.1 = (bf16[1,3,512,1024]{3,2,1,0:T(8,128)(2,1)S(1)}, bf16[1,3,512,1024]{3,2,1,0:T(8,128)(2,1)}, u32[]{:S(2)}) copy-start(bf16[1,3,512,1024]{3,2,1,0:T(8,128)(2,1)} %param.9) | copy-start | bytes 9437188
  23.7 8.5 %collective-permute-start.5 = (bf16[4,2,64,128]{3,2,1,0:T(8,128)(2,1)S(1)}, bf16[4,2,64,128]{3,2,1,0:T(8,128)(2,1)S(1)}, u32[]{:S(2)}, u32[]{:S(2)}) collective-permute-start(bf16[4,2,64,128]{3,2,1,0:T(8,128)(2,1)S(1)} %get-tuple-element.51), channel_id=1, source_target_pairs={{0,1},{1,0},{2,3},{3,2},{4,5},{5,4},{6,7},{7,6},{8,9},{9,8},{10,11... | collective-permute-start | bytes 393224 | tf_op jit(solution)/shard_map/encode/ppermute | solution.py:18
  29.6 5.2 %collective-permute-start.7 = (bf16[4,2,64,128]{3,2,1,0:T(8,128)(2,1)S(1)}, bf16[4,2,64,128]{3,2,1,0:T(8,128)(2,1)S(1)}, u32[]{:S(2)}, u32[]{:S(2)}) collective-permute-start(bf16[4,2,64,128]{3,2,1,0:T(8,128)(2,1)S(1)} %get-tuple-element.55), channel_id=1, source_target_pairs={{0,1},{1,0},{2,3},{3,2},{4,5},{5,4},{6,7},{7,6},{8,9},{9,8},{10,11... | collective-permute-start | bytes 393224 | tf_op jit(solution)/shard_map/encode/ppermute | solution.py:18
  32.3 5.5 %collective-permute-start.6 = (bf16[4,2,64,128]{3,2,1,0:T(8,128)(2,1)S(1)}, bf16[4,2,64,128]{3,2,1,0:T(8,128)(2,1)S(1)}, u32[]{:S(2)}, u32[]{:S(2)}) collective-permute-start(bf16[4,2,64,128]{3,2,1,0:T(8,128)(2,1)S(1)} %get-tuple-element.53), channel_id=1, source_target_pairs={{0,2},{1,3},{2,0},{3,1},{4,6},{5,7},{6,4},{7,5},{8,10},{9,11},{10,... | collective-permute-start | bytes 393224 | tf_op jit(solution)/shard_map/encode/ppermute | solution.py:18
  37.8 7.3 %collective-permute-start.8 = (bf16[4,2,64,128]{3,2,1,0:T(8,128)(2,1)S(1)}, bf16[4,2,64,128]{3,2,1,0:T(8,128)(2,1)S(1)}, u32[]{:S(2)}, u32[]{:S(2)}) collective-permute-start(bf16[4,2,64,128]{3,2,1,0:T(8,128)(2,1)S(1)} %get-tuple-element.59), channel_id=1, source_target_pairs={{0,2},{1,3},{2,0},{3,1},{4,6},{5,7},{6,4},{7,5},{8,10},{9,11},{10,... | collective-permute-start | bytes 393224 | tf_op jit(solution)/shard_map/encode/ppermute | solution.py:18
  40.3 5.0 %collective-permute-start.9 = (bf16[4,2,64,128]{3,2,1,0:T(8,128)(2,1)S(1)}, bf16[4,2,64,128]{3,2,1,0:T(8,128)(2,1)S(1)}, u32[]{:S(2)}, u32[]{:S(2)}) collective-permute-start(bf16[4,2,64,128]{3,2,1,0:T(8,128)(2,1)S(1)} %activate.2.refs_0_), channel_id=1, source_target_pairs={{0,1},{1,0},{2,3},{3,2},{4,5},{5,4},{6,7},{7,6},{8,9},{9,8},{10,11... | collective-permute-start | bytes 393224 | tf_op jit(solution)/shard_map/spread/ppermute | solution.py:18
  40.4 10.1 %collective-permute-start.11 = (bf16[4,2,64,128]{3,2,1,0:T(8,128)(2,1)S(1)}, bf16[4,2,64,128]{3,2,1,0:T(8,128)(2,1)S(1)}, u32[]{:S(2)}, u32[]{:S(2)}) collective-permute-start(bf16[4,2,64,128]{3,2,1,0:T(8,128)(2,1)S(1)} %activate.2.refs_0_), channel_id=1, source_target_pairs={{0,8},{4,12},{8,16},{12,20},{16,24},{20,28},{1,9},{5,13},{9,17},{1... | collective-permute-start | bytes 393224 | tf_op jit(solution)/shard_map/spread/ppermute | solution.py:23
  45.2 5.9 %collective-permute-start.10 = (bf16[4,2,64,128]{3,2,1,0:T(8,128)(2,1)S(1)}, bf16[4,2,64,128]{3,2,1,0:T(8,128)(2,1)S(1)}, u32[]{:S(2)}, u32[]{:S(2)}) collective-permute-start(bf16[4,2,64,128]{3,2,1,0:T(8,128)(2,1)S(1)} %activate.3.first_ref.refs_1_), channel_id=1, source_target_pairs={{0,1},{1,0},{2,3},{3,2},{4,5},{5,4},{6,7},{7,6},{8,9},{9,8},{10,11... | collective-permute-start | bytes 393224 | tf_op jit(solution)/shard_map/spread/ppermute | solution.py:18
  45.3 8.9 %collective-permute-start.12 = (bf16[8,2,64,128]{3,2,1,0:T(8,128)(2,1)S(1)}, bf16[8,2,64,128]{3,2,1,0:T(8,128)(2,1)S(1)}, u32[]{:S(2)}, u32[]{:S(2)}) collective-permute-start(bf16[8,2,64,128]{3,2,1,0:T(8,128)(2,1)S(1)} %join.1), channel_id=1, source_target_pairs={{0,8},{4,12},{8,16},{12,20},{16,24},{20,28},{1,9},{5,13},{9,17},{1... | collective-permute-start | bytes 786440 | tf_op jit(solution)/shard_map/spread/ppermute | solution.py:23
  51.1 6.6 %collective-permute-start.13 = (bf16[4,2,64,128]{3,2,1,0:T(8,128)(2,1)S(1)}, bf16[4,2,64,128]{3,2,1,0:T(8,128)(2,1)S(1)}, u32[]{:S(2)}, u32[]{:S(2)}) collective-permute-start(bf16[4,2,64,128]{3,2,1,0:T(8,128)(2,1)S(1)} %collective-permute-done.10.refs_3_), channel_id=1, source_target_pairs={{0,8},{4,12},{8,16},{12,20},{16,24},{20,28},{1,9},{5,13},{9,17},{1... | collective-permute-start | bytes 393224 | tf_op jit(solution)/shard_map/spread/ppermute | solution.py:23
  57.7 8.2 %collective-permute-start.14 = (bf16[16,2,64,128]{3,2,1,0:T(8,128)(2,1)S(1)}, bf16[16,2,64,128]{3,2,1,0:T(8,128)(2,1)S(1)}, u32[]{:S(2)}, u32[]{:S(2)}) collective-permute-start(bf16[16,2,64,128]{3,2,1,0:T(8,128)(2,1)S(1)} %choose.1), channel_id=1, source_target_pairs={{0,4},{4,0},{8,12},{12,8},{16,20},{20,16},{24,28},{28,24},{1,5},{5... | collective-permute-start | bytes 1572872 | tf_op jit(solution)/shard_map/decode/ppermute | solution.py:28

commit v9 on v8

--- a/solution.py
+++ b/solution.py
@@ -220,24 +220,22 @@
 
 
 def early_kernel(parts, lists_ref, far_lists, *refs):
-    own_refs, far_refs, (decoder_hbm, far_dec), refs = refs[:4], refs[4:6], refs[6:8], refs[8:]
-    early_ref, late_a, late_b, own, other, own_dec, sem = refs
+    own_refs, far_ref, (decoder_hbm, far_dec), refs = refs[:4], refs[4], refs[5:7], refs[7:]
+    first_ref, rest_ref, own, other, own_dec, sem = refs
     copy = pltpu.make_async_copy(decoder_hbm.at[0], own_dec, sem)
     copy.start()
-    quarter, latents = late_a.shape[0], own.shape[1]
+    quarter, latents = other.shape
     own[...] = jnp.zeros_like(own)
     other[...] = jnp.zeros_like(other)
     expand(own, lists_ref, parts, 0, own_refs)
-    expand(other, far_lists, parts, 0, far_refs)
+    expand(other, far_lists, parts, 0, [far_ref])
     copy.wait()
-    for lanes in column_tiles(early_ref.shape[1]):
+    for lanes in column_tiles(first_ref.shape[1]):
         total = jnp.dot(own[...], own_dec[:, lanes], preferred_element_type=jnp.float32)
-        late_b[:, lanes] = total[3 * quarter :]
-        total = total[: 3 * quarter] + jnp.dot(
+        rest_ref[:, lanes] = total[quarter:]
+        first_ref[:, lanes] = total[:quarter] + jnp.dot(
             other[...], far_dec[:latents, lanes], preferred_element_type=jnp.float32
         )
-        early_ref[:, lanes] = total[: 2 * quarter]
-        late_a[:, lanes] = total[2 * quarter :]
 
 
 def decode_early(lists, far_lists, acts, decoder, far_decoder, parts):
@@ -245,17 +243,17 @@
     quarter = acts[0].shape[0] * acts[0].shape[2]
     return pl.pallas_call(
         functools.partial(early_kernel, parts),
-        out_shape=[jax.ShapeDtypeStruct((count * quarter, features), jnp.float32) for count in (2, 1, 1)],
-        in_specs=[SMEM, SMEM] + [VMEM] * 6 + [ANY, VMEM],
-        out_specs=[VMEM] * 3,
+        out_shape=[jax.ShapeDtypeStruct((count * quarter, features), jnp.float32) for count in (1, 3)],
+        in_specs=[SMEM, SMEM] + [VMEM] * 5 + [ANY, VMEM],
+        out_specs=[VMEM] * 2,
         scratch_shapes=[
             pltpu.VMEM((4 * quarter, latents), jnp.bfloat16),
-            pltpu.VMEM((3 * quarter, latents), jnp.bfloat16),
+            pltpu.VMEM((quarter, latents), jnp.bfloat16),
             pltpu.VMEM((latents, features), jnp.bfloat16),
             pltpu.SemaphoreType.DMA,
         ],
         cost_estimate=pl.CostEstimate(
-            flops=14 * quarter * latents * features,
+            flops=10 * quarter * latents * features,
             bytes_accessed=2 * (2 * latents * features + 8 * quarter * features),
             transcendentals=0,
         ),
@@ -263,45 +261,43 @@
     )(lists, far_lists, *acts, decoder, far_decoder)
 
 
-def middle_kernel(parts, lists_ref, partial_ref, far, far_dec, total_ref, dense):
+def middle_kernel(parts, lists_ref, rest_ref, second, third, far_dec, total_ref, dense):
     latents = dense.shape[1]
     dense[...] = jnp.zeros_like(dense)
-    expand(dense, lists_ref, parts, 3 * far.shape[0], [far])
-    for lanes in column_tiles(partial_ref.shape[1]):
-        total_ref[:, lanes] = partial_ref[:, lanes] + jnp.dot(
+    expand(dense, lists_ref, parts, third.shape[0], [second, third])
+    for lanes in column_tiles(rest_ref.shape[1]):
+        total_ref[:, lanes] = rest_ref[:, lanes] + jnp.dot(
             dense[...], far_dec[:latents, lanes], preferred_element_type=jnp.float32
         )
 
 
-def decode_middle(lists, partial, far, decoder, latents, parts):
-    quarter, features = partial.shape
+def decode_middle(lists, rest, far, decoder, latents, parts):
+    rows, features = rest.shape
     return pl.pallas_call(
         functools.partial(middle_kernel, parts),
-        out_shape=jax.ShapeDtypeStruct(partial.shape, partial.dtype),
-        in_specs=[SMEM] + [VMEM] * 3,
+        out_shape=jax.ShapeDtypeStruct(rest.shape, rest.dtype),
+        in_specs=[SMEM] + [VMEM] * 4,
         out_specs=VMEM,
-        scratch_shapes=[pltpu.VMEM((quarter, latents), jnp.bfloat16)],
+        scratch_shapes=[pltpu.VMEM((rows, latents), jnp.bfloat16)],
         cost_estimate=pl.CostEstimate(
-            flops=2 * quarter * latents * features,
-            bytes_accessed=2 * (latents * features + 4 * quarter * features),
+            flops=2 * rows * latents * features,
+            bytes_accessed=2 * (latents * features + 4 * rows * features),
             transcendentals=0,
         ),
         **small("decode_middle", 16),
-    )(lists, partial, far, decoder)
-
-
-def late_kernel(parts, lists_ref, early_ref, late_a, late_b, near, near_dec, out_ref, dense, stage, sems):
+    )(lists, rest, *far, decoder)
+
+
+def late_kernel(parts, lists_ref, first_ref, rest_ref, near, near_dec, out_ref, dense, stage, sems):
     tokens, latents = dense.shape
     quarter, rows = tokens // 4, tokens // parts
     dense[...] = jnp.zeros_like(dense)
     expand(dense, lists_ref, parts, 0, [near])
     copies = []
-    for number, lanes in enumerate(column_tiles(early_ref.shape[1])):
+    for number, lanes in enumerate(column_tiles(first_ref.shape[1])):
         total = jnp.dot(dense[...], near_dec[:latents, lanes], preferred_element_type=jnp.float32)
-        before = ((0, early_ref), (2 * quarter, late_a), (3 * quarter, late_b))
-        for first, ref in before:
-            last = first + ref.shape[0]
-            stage[first:last, lanes] = (total[first:last] + ref[:, lanes]).astype(stage.dtype)
+        stage[:quarter, lanes] = (total[:quarter] + first_ref[:, lanes]).astype(stage.dtype)
+        stage[quarter:, lanes] = (total[quarter:] + rest_ref[:, lanes]).astype(stage.dtype)
         for held in range(parts):
             tiles = lists_ref.shape[1]
             row = pl.multiple_of(held_tile(held * (tiles // parts), tiles, parts) * (tokens // tiles), rows)
@@ -323,7 +319,7 @@
     return pl.pallas_call(
         functools.partial(late_kernel, parts),
         out_shape=jax.ShapeDtypeStruct((tokens, features), jnp.bfloat16),
-        in_specs=[SMEM] + [VMEM] * 5,
+        in_specs=[SMEM] + [VMEM] * 4,
         out_specs=ANY,
         scratch_shapes=[
             pltpu.VMEM((tokens, latents), jnp.bfloat16),
@@ -383,11 +379,11 @@
         own = [own_a, own_b, late_a, late_b]
         far = [far_a] + [passed_along(piece, 2) for piece in (joined, late_b)]
     with jax.named_scope("decode"):
-        early, late_a, late_b = decode_early(lists, far_lists, own + far[:2], decoder, far_decoder, parts)
-        early, late_a, late_b, far[2] = lax.optimization_barrier((early, late_a, late_b, far[2]))
+        first, rest = decode_early(lists, far_lists, own + far[:1], decoder, far_decoder, parts)
+        first, rest, far[2] = lax.optimization_barrier((first, rest, far[2]))
         near = across_cores(choose(own, far))
-        late_b = decode_middle(far_lists, late_b, far[2], far_decoder, latents, parts)
-        return decode_late(near_lists, [early, late_a, late_b], near, near_decoder, latents, parts)[None]
+        rest = decode_middle(far_lists, rest, far[1:], far_decoder, latents, parts)
+        return decode_late(near_lists, [first, rest], near, near_decoder, latents, parts)[None]
 
 
 def solution(mesh):

time: 69.6 us -> 69.1 us (level)
  transfers between devices with their start and end apart: 15 -> 15, of which waited for: 8 -> 7; matrix products, arithmetic and copies ran while one was open for 0% -> 0% of each run, Pallas kernels for 9% -> 9%
where the time goes in v9:
time: 69.1 us; the launch traced here: 68.8 us
  starting transfers between devices  36.6 us (53%)
  waiting for transfers between devices  18.7 us (27%)
  Pallas kernels  9.47 us (14%)
  local copies, waits for them, and re-layouts  3.81 us (6%)
    ppermute x9, waiting for transfers between devices, swapped(): return lax.ppermute(value, 'latent', [(i, i ^ step) for i in range(count)])  15.6 us
    ppermute x5, starting transfers between devices, passed_along(): lax.ppermute(value, 'layer', [(i, i + steps) for i in range(count - steps)])  15.6 us
    ppermute x9, starting transfers between devices, swapped(): return lax.ppermute(value, 'latent', [(i, i ^ step) for i in range(count)])  14.8 us
    ppermute x1, starting transfers between devices, across_cores(): return lax.ppermute(value, 'layer', [(i, i ^ 1) for i in range(count)])  6.26 us
    unnamed x14, local copies, waits for them, and re-layouts  3.81 us
    pallas_call x1, Pallas kernels, decode_late(): pl.pallas_call(functools.partial(late_kernel, parts), out_shape=jax.Shape...  3.18 us
    ppermute x5, waiting for transfers between devices, passed_along(): lax.ppermute(value, 'layer', [(i, i + steps) for i in range(count - steps)])  3.1 us
    pallas_call x1, Pallas kernels, decode_early(): pl.pallas_call(functools.partial(early_kernel, parts), out_shape=[jax.Sha...  2.38 us
  transfers between devices with their start and end apart: 15, of which 7 were waited for; matrix products, arithmetic and copies ran while one was open for 0% of the time, Pallas kernels for 9%

profile of v9, /device:TPU:5, one launch (start us, length us, event | category | flops | bytes accessed | tf_op | source)
XLA Modules:
  0.0 68.8 jit_solution(17981306134917178435)
XLA Ops:
  0.0 0.0 copy-start.2
  0.0 1.2 %copy-done.2 = bf16[1,4096,128]{2,1,0:T(8,128)(2,1)S(1)} copy-done((bf16[1,4096,128]{2,1,0:T(8,128)(2,1)S(1)}, bf16[1,4096,128]{2,1,0:T(8,128)(2,1)}, u32[]{:S(2)}) %copy-start.2) | copy-done | bytes 1048600
  1.2 0.1 fetch_rows.1
  1.3 1.4 %collective-permute-start.2 = (bf16[1024,128]{1,0:T(8,128)(2,1)S(1)}, bf16[1024,128]{1,0:T(8,128)(2,1)S(1)}, u32[]{:S(2)}, u32[]{:S(2)}) collective-permute-start(bf16[1024,128]{1,0:T(8,128)(2,1)S(1)} %get-tuple-element.45), channel_id=1, source_target_pairs={{0,1},{1,0},{2,3},{3,2},{4,5},{5,4},{6,7},{7,6},{8,9},{9,8},{10,11... | collective-permute-start | bytes 786440 | tf_op jit(solution)/shard_map/encoder_rows/ppermute | solution.py:18
  2.7 2.3 %collective-permute-start.3 = (bf16[1024,128]{1,0:T(8,128)(2,1)S(1)}, bf16[1024,128]{1,0:T(8,128)(2,1)S(1)}, u32[]{:S(2)}, u32[]{:S(2)}) collective-permute-start(bf16[1024,128]{1,0:T(8,128)(2,1)S(1)} %get-tuple-element.46), channel_id=1, source_target_pairs={{0,2},{1,3},{2,0},{3,1},{4,6},{5,7},{6,4},{7,5},{8,10},{9,11},{10,... | collective-permute-start | bytes 786440 | tf_op jit(solution)/shard_map/encoder_rows/ppermute | solution.py:18
  5.0 0.0 collective-permute-start.4
  5.0 0.0 copy-start
  5.0 1.9 %copy-done = bf16[1,3,512,1024]{3,2,1,0:T(8,128)(2,1)S(1)} copy-done((bf16[1,3,512,1024]{3,2,1,0:T(8,128)(2,1)S(1)}, bf16[1,3,512,1024]{3,2,1,0:T(8,128)(2,1)}, u32[]{:S(2)}) %copy-start) | copy-done | bytes 3145752
  6.9 0.0 copy-start.3
  6.9 0.7 copy-done.3
  7.5 0.0 copy-start.4
  7.5 0.1 fetch_decoders.1
  7.7 4.6 %collective-permute-start = (bf16[528,1024]{1,0:T(8,128)(2,1)S(1)}, bf16[528,1024]{1,0:T(8,128)(2,1)S(1)}, u32[]{:S(2)}, u32[]{:S(2)}) collective-permute-start(bf16[528,1024]{1,0:T(8,128)(2,1)S(1)} %get-tuple-element.40), channel_id=1, source_target_pairs={{0,4},{4,8},{8,12},{12,16},{16,20},{20,24},{24,28},{1,5},{5,9},{9,... | collective-permute-start | bytes 3244040 | tf_op jit(solution)/shard_map/decoder_weights/ppermute | solution.py:23
  12.3 1.9 %collective-permute-start.1 = (bf16[528,1024]{1,0:T(8,128)(2,1)S(1)}, bf16[528,1024]{1,0:T(8,128)(2,1)S(1)}, u32[]{:S(2)}, u32[]{:S(2)}) collective-permute-start(bf16[528,1024]{1,0:T(8,128)(2,1)S(1)} %get-tuple-element.41), channel_id=1, source_target_pairs={{0,8},{4,12},{8,16},{12,20},{16,24},{20,28},{1,9},{5,13},{9,17},{1... | collective-permute-start | bytes 3244040 | tf_op jit(solution)/shard_map/decoder_weights/ppermute | solution.py:23
  14.2 0.0 collective-permute-done.2.refs_1_
  14.2 0.0 collective-permute-done.3.refs_2_
  14.3 7.6 %collective-permute-done.4.refs_3_ = bf16[1024,128]{1,0:T(8,128)(2,1)S(1)} collective-permute-done((bf16[1024,128]{1,0:T(8,128)(2,1)S(1)}, bf16[1024,128]{1,0:T(8,128)(2,1)S(1)}, u32[]{:S(2)}, u32[]{:S(2)}) %collective-permute-start.4) | collective-permute-done | bytes 262176 | tf_op jit(solution)/shard_map/encoder_rows/ppermute | solution.py:18
  21.8 0.0 copy-done.4
  21.8 0.0 copy-done.5
  21.9 0.0 copy-done.6
  21.9 0.0 copy-start.1
  21.9 1.9 %encode.1 = (f32[4,2,64,128]{3,2,1,0:T(8,128)S(1)}, f32[4,2,64,128]{3,2,1,0:T(8,128)S(1)}, bf16[4,2,64,128]{3,2,1,0:T(8,128)(2,1)S(1)}, bf16[4,2,64,128]{3,2,1,0:T(8,128)(2,1)S(1)}) custom-call(s32[2,16]{1,0:T(2,128)S(1)} %bitcast.12, s32[16]{0:T(128)S(1)} %bitcast.15, f32[1,128]{1,0:T(1,128)S(1)} %copy-done.6, bf16[1024,1024]{1,0:T(8,128)(2,1)S(1)} %bitcast.14, ...), custom_call_target="tpu_custom_call" | custom-call | flops 17179869184 | bytes 3145728 | tf_op jit(solution)/shard_map/encode/encode/pallas_call | solution.py:114
  23.7 5.9 %collective-permute-start.5 = (bf16[4,2,64,128]{3,2,1,0:T(8,128)(2,1)S(1)}, bf16[4,2,64,128]{3,2,1,0:T(8,128)(2,1)S(1)}, u32[]{:S(2)}, u32[]{:S(2)}) collective-permute-start(bf16[4,2,64,128]{3,2,1,0:T(8,128)(2,1)S(1)} %get-tuple-element.49), channel_id=1, source_target_pairs={{0,1},{1,0},{2,3},{3,2},{4,5},{5,4},{6,7},{7,6},{8,9},{9,8},{10,11... | collective-permute-start | bytes 393224 | tf_op jit(solution)/shard_map/encode/ppermute | solution.py:18
  29.6 0.1 collective-permute-start.7
  29.7 2.6 %collective-permute-done.5.arrived_ref = bf16[4,2,64,128]{3,2,1,0:T(8,128)(2,1)S(1)} collective-permute-done((bf16[4,2,64,128]{3,2,1,0:T(8,128)(2,1)S(1)}, bf16[4,2,64,128]{3,2,1,0:T(8,128)(2,1)S(1)}, u32[]{:S(2)}, u32[]{:S(2)}) %collective-permute-start.5) | collective-permute-done | bytes 131104 | tf_op jit(solution)/shard_map/encode/ppermute | solution.py:18
  32.3 2.5 %collective-permute-start.6 = (bf16[4,2,64,128]{3,2,1,0:T(8,128)(2,1)S(1)}, bf16[4,2,64,128]{3,2,1,0:T(8,128)(2,1)S(1)}, u32[]{:S(2)}, u32[]{:S(2)}) collective-permute-start(bf16[4,2,64,128]{3,2,1,0:T(8,128)(2,1)S(1)} %get-tuple-element.51), channel_id=1, source_target_pairs={{0,2},{1,3},{2,0},{3,1},{4,6},{5,7},{6,4},{7,5},{8,10},{9,11},{10,... | collective-permute-start | bytes 393224 | tf_op jit(solution)/shard_map/encode/ppermute | solution.py:18
  34.8 0.0 collective-permute-done.7.arrived_ref
  34.9 3.0 %collective-permute-done.6.arrived_ref = bf16[4,2,64,128]{3,2,1,0:T(8,128)(2,1)S(1)} collective-permute-done((bf16[4,2,64,128]{3,2,1,0:T(8,128)(2,1)S(1)}, bf16[4,2,64,128]{3,2,1,0:T(8,128)(2,1)S(1)}, u32[]{:S(2)}, u32[]{:S(2)}) %collective-permute-start.6) | collective-permute-done | bytes 131104 | tf_op jit(solution)/shard_map/encode/ppermute | solution.py:18
  37.8 2.4 %collective-permute-start.8 = (bf16[4,2,64,128]{3,2,1,0:T(8,128)(2,1)S(1)}, bf16[4,2,64,128]{3,2,1,0:T(8,128)(2,1)S(1)}, u32[]{:S(2)}, u32[]{:S(2)}) collective-permute-start(bf16[4,2,64,128]{3,2,1,0:T(8,128)(2,1)S(1)} %get-tuple-element.57), channel_id=1, source_target_pairs={{0,2},{1,3},{2,0},{3,1},{4,6},{5,7},{6,4},{7,5},{8,10},{9,11},{10,... | collective-permute-start | bytes 393224 | tf_op jit(solution)/shard_map/encode/ppermute | solution.py:18
  40.3 0.1 collective-permute-start.9
  40.4 2.8 %collective-permute-start.11 = (bf16[4,2,64,128]{3,2,1,0:T(8,128)(2,1)S(1)}, bf16[4,2,64,128]{3,2,1,0:T(8,128)(2,1)S(1)}, u32[]{:S(2)}, u32[]{:S(2)}) collective-permute-start(bf16[4,2,64,128]{3,2,1,0:T(8,128)(2,1)S(1)} %activate.2.refs_0_), channel_id=1, source_target_pairs={{0,8},{4,12},{8,16},{12,20},{16,24},{20,28},{1,9},{5,13},{9,17},{1... | collective-permute-start | bytes 393224 | tf_op jit(solution)/shard_map/spread/ppermute | solution.py:23
  43.2 1.9 %collective-permute-done.8.arrived_ref = bf16[4,2,64,128]{3,2,1,0:T(8,128)(2,1)S(1)} collective-permute-done((bf16[4,2,64,128]{3,2,1,0:T(8,128)(2,1)S(1)}, bf16[4,2,64,128]{3,2,1,0:T(8,128)(2,1)S(1)}, u32[]{:S(2)}, u32[]{:S(2)}) %collective-permute-start.8) | collective-permute-done | bytes 131104 | tf_op jit(solution)/shard_map/encode/ppermute | solution.py:18
  45.2 0.1 collective-permute-start.10
  45.3 0.0 collective-permute-done.9.refs_2_.second_ref
  45.3 3.1 %collective-permute-start.13 = (bf16[8,2,64,128]{3,2,1,0:T(8,128)(2,1)S(1)}, bf16[8,2,64,128]{3,2,1,0:T(8,128)(2,1)S(1)}, u32[]{:S(2)}, u32[]{:S(2)}) collective-permute-start(bf16[8,2,64,128]{3,2,1,0:T(8,128)(2,1)S(1)} %join.1), channel_id=1, source_target_pairs={{0,8},{4,12},{8,16},{12,20},{16,24},{20,28},{1,9},{5,13},{9,17},{1... | collective-permute-start | bytes 786440 | tf_op jit(solution)/shard_map/spread/ppermute | solution.py:23
  48.5 2.1 %collective-permute-done.11.refs_4_ = bf16[4,2,64,128]{3,2,1,0:T(8,128)(2,1)S(1)} collective-permute-done((bf16[4,2,64,128]{3,2,1,0:T(8,128)(2,1)S(1)}, bf16[4,2,64,128]{3,2,1,0:T(8,128)(2,1)S(1)}, u32[]{:S(2)}, u32[]{:S(2)}) %collective-permute-start.11) | collective-permute-done | bytes 131104 | tf_op jit(solution)/shard_map/spread/ppermute | solution.py:23
  50.5 0.5 collective-permute-done.10.refs_3_
  51.1 3.1 %collective-permute-start.12 = (bf16[4,2,64,128]{3,2,1,0:T(8,128)(2,1)S(1)}, bf16[4,2,64,128]{3,2,1,0:T(8,128)(2,1)S(1)}, u32[]{:S(2)}, u32[]{:S(2)}) collective-permute-start(bf16[4,2,64,128]{3,2,1,0:T(8,128)(2,1)S(1)} %collective-permute-done.10.refs_3_), channel_id=1, source_target_pairs={{0,8},{4,12},{8,16},{12,20},{16,24},{20,28},{1,9},{5,13},{9,17},{1... | collective-permute-start | bytes 393224 | tf_op jit(solution)/shard_map/spread/ppermute | solution.py:23
  54.2 0.0 collective-permute-done.near_dec
  54.2 0.0 collective-permute-done.1.refs_6_.far_dec
  54.3 0.0 copy-done.1
  54.3 2.4 %decode_early.1 = (f32[256,1024]{1,0:T(8,128)S(1)}, f32[768,1024]{1,0:T(8,128)S(1)}) custom-call(s32[2,16]{1,0:T(2,128)S(1)} %bitcast.13, s32[2,16]{1,0:T(2,128)S(1)} %slice_convert_fusion.far_lists.lists_ref, bf16[4,2,64,128]{3,2,1,0:T(8,128)(2,1)S(1)} %activate.2.refs_0_, bf16[4,2,64,128]{3,2,1,0:T(8,128)(2,1)S(1)} %activate.3.refs_1_.first_ref, ...), custom_call_target="tpu_custom_call" | custom-call | flops 1342177280 | bytes 6291456 | tf_op jit(solution)/shard_map/decode/decode_early/pallas_call | solution.py:244
  56.7 1.0 %collective-permute-done.12.third.refs_6_ = bf16[4,2,64,128]{3,2,1,0:T(8,128)(2,1)S(1)} collective-permute-done((bf16[4,2,64,128]{3,2,1,0:T(8,128)(2,1)S(1)}, bf16[4,2,64,128]{3,2,1,0:T(8,128)(2,1)S(1)}, u32[]{:S(2)}, u32[]{:S(2)}) %collective-permute-start.12) | collective-permute-done | bytes 131104 | tf_op jit(solution)/shard_map/spread/ppermute | solution.py:23
  57.7 0.0 collective-permute-done.13.second.refs_5_
  57.7 6.3 %collective-permute-start.14 = (bf16[16,2,64,128]{3,2,1,0:T(8,128)(2,1)S(1)}, bf16[16,2,64,128]{3,2,1,0:T(8,128)(2,1)S(1)}, u32[]{:S(2)}, u32[]{:S(2)}) collective-permute-start(bf16[16,2,64,128]{3,2,1,0:T(8,128)(2,1)S(1)} %choose.1), channel_id=1, source_target_pairs={{0,4},{4,0},{8,12},{12,8},{16,20},{20,16},{24,28},{28,24},{1,5},{5... | collective-permute-start | bytes 1572872 | tf_op jit(solution)/shard_map/decode/ppermute | solution.py:28
  64.0 1.6 %decode_middle.1.rest_ref = f32[768,1024]{1,0:T(8,128)S(1)} custom-call(s32[2,16]{1,0:T(2,128)S(1)} %slice_convert_fusion.far_lists.lists_ref, f32[768,1024]{1,0:T(8,128)S(1)} %get-tuple-element.63.rest_ref, bf16[8,2,64,128]{3,2,1,0:T(8,128)(2,1)S(1)} %collective-permute-done.13.second.refs_5_, ...), custom_call_target="tpu_custom_call" | custom-call | flops 805306368 | bytes 7340032 | tf_op jit(solution)/shard_map/decode/decode_middle/pallas_call | solution.py:276
  65.6 0.0 collective-permute-done.14.near
  65.6 3.2 %decode_late.1 = bf16[1024,1024]{1,0:T(8,128)(2,1)} custom-call(s32[2,16]{1,0:T(2,128)S(1)} %slice_convert_fusion.1.lists_ref, f32[256,1024]{1,0:T(8,128)S(1)} %get-tuple-element.62.first_ref, f32[768,1024]{1,0:T(8,128)S(1)} %decode_middle.1.rest_ref, bf16[16,2,64,128]{3,2,1,0:T(8,128)(2,1)S(1)} %collective-permute-done.14.near, ...), custom_call_target="tpu_custom_call" | custom-call | flops 1073741824 | bytes 7340032 | tf_op jit(solution)/shard_map/decode/decode_late/pallas_call | solution.py:319
  (10 shorter events, 0.2 us)
Async XLA Ops:
  0.0 1.2 %copy-start.2 = (bf16[1,4096,128]{2,1,0:T(8,128)(2,1)S(1)}, bf16[1,4096,128]{2,1,0:T(8,128)(2,1)}, u32[]{:S(2)}) copy-start(bf16[1,4096,128]{2,1,0:T(8,128)(2,1)} %param.7) | copy-start | bytes 3145732
  1.3 12.9 %collective-permute-start.2 = (bf16[1024,128]{1,0:T(8,128)(2,1)S(1)}, bf16[1024,128]{1,0:T(8,128)(2,1)S(1)}, u32[]{:S(2)}, u32[]{:S(2)}) collective-permute-start(bf16[1024,128]{1,0:T(8,128)(2,1)S(1)} %get-tuple-element.45), channel_id=1, source_target_pairs={{0,1},{1,0},{2,3},{3,2},{4,5},{5,4},{6,7},{7,6},{8,9},{9,8},{10,11... | collective-permute-start | bytes 786440 | tf_op jit(solution)/shard_map/encoder_rows/ppermute | solution.py:18
  2.7 11.6 %collective-permute-start.3 = (bf16[1024,128]{1,0:T(8,128)(2,1)S(1)}, bf16[1024,128]{1,0:T(8,128)(2,1)S(1)}, u32[]{:S(2)}, u32[]{:S(2)}) collective-permute-start(bf16[1024,128]{1,0:T(8,128)(2,1)S(1)} %get-tuple-element.46), channel_id=1, source_target_pairs={{0,2},{1,3},{2,0},{3,1},{4,6},{5,7},{6,4},{7,5},{8,10},{9,11},{10,... | collective-permute-start | bytes 786440 | tf_op jit(solution)/shard_map/encoder_rows/ppermute | solution.py:18
  5.0 16.9 %collective-permute-start.4 = (bf16[1024,128]{1,0:T(8,128)(2,1)S(1)}, bf16[1024,128]{1,0:T(8,128)(2,1)S(1)}, u32[]{:S(2)}, u32[]{:S(2)}) collective-permute-start(bf16[1024,128]{1,0:T(8,128)(2,1)S(1)} %get-tuple-element.47), channel_id=1, source_target_pairs={{0,3},{1,2},{2,1},{3,0},{4,7},{5,6},{6,5},{7,4},{8,11},{9,10},{10,... | collective-permute-start | bytes 786440 | tf_op jit(solution)/shard_map/encoder_rows/ppermute | solution.py:18
  5.0 1.9 %copy-start = (bf16[1,3,512,1024]{3,2,1,0:T(8,128)(2,1)S(1)}, bf16[1,3,512,1024]{3,2,1,0:T(8,128)(2,1)}, u32[]{:S(2)}) copy-start(bf16[1,3,512,1024]{3,2,1,0:T(8,128)(2,1)} %param.9) | copy-start | bytes 9437188
  6.9 0.7 copy-start.3
  7.5 14.3 %copy-start.4 = (bf16[1,1024,1024]{2,1,0:T(8,128)(2,1)S(1)}, bf16[1,1024,1024]{2,1,0:T(8,128)(2,1)}, u32[]{:S(2)}) copy-start(bf16[1,1024,1024]{2,1,0:T(8,128)(2,1)} %param.6) | copy-start | bytes 6291460
  7.5 14.3 %copy-start.5 = (s32[1,16]{1,0:T(1,128)S(1)}, s32[1,16]{1,0:T(1,128)}, u32[]{:S(2)}) copy-start(s32[1,16]{1,0:T(1,128)} %param.11) | copy-start | bytes 196
  7.5 14.3 %copy-start.6 = (f32[1,128]{1,0:T(1,128)S(1)}, f32[1,128]{1,0:T(1,128)}, u32[]{:S(2)}) copy-start(f32[1,128]{1,0:T(1,128)} %bias_ref.1) | copy-start | bytes 1540
  7.7 46.5 %collective-permute-start = (bf16[528,1024]{1,0:T(8,128)(2,1)S(1)}, bf16[528,1024]{1,0:T(8,128)(2,1)S(1)}, u32[]{:S(2)}, u32[]{:S(2)}) collective-permute-start(bf16[528,1024]{1,0:T(8,128)(2,1)S(1)} %get-tuple-element.40), channel_id=1, source_target_pairs={{0,4},{4,8},{8,12},{12,16},{16,20},{20,24},{24,28},{1,5},{5,9},{9,... | collective-permute-start | bytes 3244040 | tf_op jit(solution)/shard_map/decoder_weights/ppermute | solution.py:23
  12.3 41.9 %collective-permute-start.1 = (bf16[528,1024]{1,0:T(8,128)(2,1)S(1)}, bf16[528,1024]{1,0:T(8,128)(2,1)S(1)}, u32[]{:S(2)}, u32[]{:S(2)}) collective-permute-start(bf16[528,1024]{1,0:T(8,128)(2,1)S(1)} %get-tuple-element.41), channel_id=1, source_target_pairs={{0,8},{4,12},{8,16},{12,20},{16,24},{20,28},{1,9},{5,13},{9,17},{1... | collective-permute-start | bytes 3244040 | tf_op jit(solution)/shard_map/decoder_weights/ppermute | solution.py:23
  21.9 32.4 %copy-start.1 = (bf16[1,3,512,1024]{3,2,1,0:T(8,128)(2,1)S(1)}, bf16[1,3,512,1024]{3,2,1,0:T(8,128)(2,1)}, u32[]{:S(2)}) copy-start(bf16[1,3,512,1024]{3,2,1,0:T(8,128)(2,1)} %param.9) | copy-start | bytes 9437188
  23.7 8.5 %collective-permute-start.5 = (bf16[4,2,64,128]{3,2,1,0:T(8,128)(2,1)S(1)}, bf16[4,2,64,128]{3,2,1,0:T(8,128)(2,1)S(1)}, u32[]{:S(2)}, u32[]{:S(2)}) collective-permute-start(bf16[4,2,64,128]{3,2,1,0:T(8,128)(2,1)S(1)} %get-tuple-element.49), channel_id=1, source_target_pairs={{0,1},{1,0},{2,3},{3,2},{4,5},{5,4},{6,7},{7,6},{8,9},{9,8},{10,11... | collective-permute-start | bytes 393224 | tf_op jit(solution)/shard_map/encode/ppermute | solution.py:18
  29.6 5.2 %collective-permute-start.7 = (bf16[4,2,64,128]{3,2,1,0:T(8,128)(2,1)S(1)}, bf16[4,2,64,128]{3,2,1,0:T(8,128)(2,1)S(1)}, u32[]{:S(2)}, u32[]{:S(2)}) collective-permute-start(bf16[4,2,64,128]{3,2,1,0:T(8,128)(2,1)S(1)} %get-tuple-element.53), channel_id=1, source_target_pairs={{0,1},{1,0},{2,3},{3,2},{4,5},{5,4},{6,7},{7,6},{8,9},{9,8},{10,11... | collective-permute-start | bytes 393224 | tf_op jit(solution)/shard_map/encode/ppermute | solution.py:18
  32.3 5.5 %collective-permute-start.6 = (bf16[4,2,64,128]{3,2,1,0:T(8,128)(2,1)S(1)}, bf16[4,2,64,128]{3,2,1,0:T(8,128)(2,1)S(1)}, u32[]{:S(2)}, u32[]{:S(2)}) collective-permute-start(bf16[4,2,64,128]{3,2,1,0:T(8,128)(2,1)S(1)} %get-tuple-element.51), channel_id=1, source_target_pairs={{0,2},{1,3},{2,0},{3,1},{4,6},{5,7},{6,4},{7,5},{8,10},{9,11},{10,... | collective-permute-start | bytes 393224 | tf_op jit(solution)/shard_map/encode/ppermute | solution.py:18
  37.8 7.3 %collective-permute-start.8 = (bf16[4,2,64,128]{3,2,1,0:T(8,128)(2,1)S(1)}, bf16[4,2,64,128]{3,2,1,0:T(8,128)(2,1)S(1)}, u32[]{:S(2)}, u32[]{:S(2)}) collective-permute-start(bf16[4,2,64,128]{3,2,1,0:T(8,128)(2,1)S(1)} %get-tuple-element.57), channel_id=1, source_target_pairs={{0,2},{1,3},{2,0},{3,1},{4,6},{5,7},{6,4},{7,5},{8,10},{9,11},{10,... | collective-permute-start | bytes 393224 | tf_op jit(solution)/shard_map/encode/ppermute | solution.py:18
  40.3 5.0 %collective-permute-start.9 = (bf16[4,2,64,128]{3,2,1,0:T(8,128)(2,1)S(1)}, bf16[4,2,64,128]{3,2,1,0:T(8,128)(2,1)S(1)}, u32[]{:S(2)}, u32[]{:S(2)}) collective-permute-start(bf16[4,2,64,128]{3,2,1,0:T(8,128)(2,1)S(1)} %activate.2.refs_0_), channel_id=1, source_target_pairs={{0,1},{1,0},{2,3},{3,2},{4,5},{5,4},{6,7},{7,6},{8,9},{9,8},{10,11... | collective-permute-start | bytes 393224 | tf_op jit(solution)/shard_map/spread/ppermute | solution.py:18
  40.4 10.1 %collective-permute-start.11 = (bf16[4,2,64,128]{3,2,1,0:T(8,128)(2,1)S(1)}, bf16[4,2,64,128]{3,2,1,0:T(8,128)(2,1)S(1)}, u32[]{:S(2)}, u32[]{:S(2)}) collective-permute-start(bf16[4,2,64,128]{3,2,1,0:T(8,128)(2,1)S(1)} %activate.2.refs_0_), channel_id=1, source_target_pairs={{0,8},{4,12},{8,16},{12,20},{16,24},{20,28},{1,9},{5,13},{9,17},{1... | collective-permute-start | bytes 393224 | tf_op jit(solution)/shard_map/spread/ppermute | solution.py:23
  45.2 5.9 %collective-permute-start.10 = (bf16[4,2,64,128]{3,2,1,0:T(8,128)(2,1)S(1)}, bf16[4,2,64,128]{3,2,1,0:T(8,128)(2,1)S(1)}, u32[]{:S(2)}, u32[]{:S(2)}) collective-permute-start(bf16[4,2,64,128]{3,2,1,0:T(8,128)(2,1)S(1)} %activate.3.refs_1_.first_ref), channel_id=1, source_target_pairs={{0,1},{1,0},{2,3},{3,2},{4,5},{5,4},{6,7},{7,6},{8,9},{9,8},{10,11... | collective-permute-start | bytes 393224 | tf_op jit(solution)/shard_map/spread/ppermute | solution.py:18
  45.3 12.3 %collective-permute-start.13 = (bf16[8,2,64,128]{3,2,1,0:T(8,128)(2,1)S(1)}, bf16[8,2,64,128]{3,2,1,0:T(8,128)(2,1)S(1)}, u32[]{:S(2)}, u32[]{:S(2)}) collective-permute-start(bf16[8,2,64,128]{3,2,1,0:T(8,128)(2,1)S(1)} %join.1), channel_id=1, source_target_pairs={{0,8},{4,12},{8,16},{12,20},{16,24},{20,28},{1,9},{5,13},{9,17},{1... | collective-permute-start | bytes 786440 | tf_op jit(solution)/shard_map/spread/ppermute | solution.py:23
  51.1 6.6 %collective-permute-start.12 = (bf16[4,2,64,128]{3,2,1,0:T(8,128)(2,1)S(1)}, bf16[4,2,64,128]{3,2,1,0:T(8,128)(2,1)S(1)}, u32[]{:S(2)}, u32[]{:S(2)}) collective-permute-start(bf16[4,2,64,128]{3,2,1,0:T(8,128)(2,1)S(1)} %collective-permute-done.10.refs_3_), channel_id=1, source_target_pairs={{0,8},{4,12},{8,16},{12,20},{16,24},{20,28},{1,9},{5,13},{9,17},{1... | collective-permute-start | bytes 393224 | tf_op jit(solution)/shard_map/spread/ppermute | solution.py:23
  57.7 7.9 %collective-permute-start.14 = (bf16[16,2,64,128]{3,2,1,0:T(8,128)(2,1)S(1)}, bf16[16,2,64,128]{3,2,1,0:T(8,128)(2,1)S(1)}, u32[]{:S(2)}, u32[]{:S(2)}) collective-permute-start(bf16[16,2,64,128]{3,2,1,0:T(8,128)(2,1)S(1)} %choose.1), channel_id=1, source_target_pairs={{0,4},{4,0},{8,12},{12,8},{16,20},{20,16},{24,28},{28,24},{1,5},{5... | collective-permute-start | bytes 1572872 | tf_op jit(solution)/shard_map/decode/ppermute | solution.py:28

commit v10 on v9

--- a/solution.py
+++ b/solution.py
@@ -16,6 +16,12 @@
 def swapped(value, step):
     count = lax.axis_size("latent")
     return lax.ppermute(value, "latent", [(i, i ^ step) for i in range(count)])
+
+
+def interleaved(parts):
+    across = list(range(parts - 1, parts // 2 - 1, -1))
+    within = list(range(parts // 2 - 1, 0, -1))
+    return [step for pair in zip(across, within + [None]) for step in pair if step]
 
 
 def passed_along(value, steps):
@@ -87,12 +93,13 @@
     width = bias_ref.shape[1]
     count, slots, rows, _ = out_refs[0].shape
     tiles = lists_ref.shape[1]
+    sources = [0] + interleaved(parts)
     for first in range(0, parts, 2):
         stacked = jnp.concatenate([ref[...] for ref in weight_refs[first : first + 2]], axis=1)
         product = jnp.dot(x_ref[...], stacked, preferred_element_type=jnp.float32)
-        for source in range(first, first + 2):
-            block = product[:, (source - first) * width : (source - first + 1) * width]
-            partial[source] = block if source else block + bias_ref[...]
+        for number in range(2):
+            block = product[:, number * width : (number + 1) * width]
+            partial[sources[first + number]] = block if first + number else block + bias_ref[...]
     for number, out_ref in enumerate(out_refs):
         for position in range(count):
             tile = held_tile(number * count + position, tiles, parts)
@@ -347,9 +354,7 @@
     with jax.named_scope("encoder_rows"):
         pieces = fetch_rows(encoder, parts)
         pieces, decoder = lax.optimization_barrier((pieces, decoder))
-        weights = [pieces[0]] + [None] * (parts - 1)
-        for step in sorted(range(1, parts), reverse=True):
-            weights[step] = swapped(pieces[step], step)
+        weights = [pieces[0]] + [swapped(pieces[step], step) for step in interleaved(parts)]
     with jax.named_scope("decoder_weights"):
         near_rows, far_rows = fetch_decoders(lists, decoder)
         near_decoder, far_decoder = passed_along(near_rows, 1), passed_along(far_rows, 2)

time: 69.1 us -> 70 us (1.013)
  waiting for transfers between devices: 18.7 us -> 25.9 us
  starting transfers between devices: 36.6 us -> 30.4 us
    ppermute x9, waiting for transfers between devices: 15.6 us -> 21.9 us  [swapped(): return lax.ppermute(value, 'latent', [(i, i ^ step) for i in range(count)])]
    ppermute x9, starting transfers between devices: 14.8 us -> 8.6 us  [swapped(): return lax.ppermute(value, 'latent', [(i, i ^ step) for i in range(count)])]
    ppermute x5, waiting for transfers between devices: 3.1 us -> 3.93 us  [passed_along(): lax.ppermute(value, 'layer', [(i, i + steps) for i in range(count - steps)])]
  transfers between devices with their start and end apart: 15 -> 15, of which waited for: 7 -> 9; matrix products, arithmetic and copies ran while one was open for 0% -> 0% of each run, Pallas kernels for 9% -> 9%
where the time goes in v10:
time: 70 us; the launch traced here: 69.7 us
  starting transfers between devices  30.4 us (43%)
  waiting for transfers between devices  25.9 us (37%)
  Pallas kernels  9.47 us (14%)
  local copies, waits for them, and re-layouts  3.81 us (5%)
    ppermute x9, waiting for transfers between devices, swapped(): return lax.ppermute(value, 'latent', [(i, i ^ step) for i in range(count)])  21.9 us
    ppermute x5, starting transfers between devices, passed_along(): lax.ppermute(value, 'layer', [(i, i + steps) for i in range(count - steps)])  14.9 us
    ppermute x9, starting transfers between devices, swapped(): return lax.ppermute(value, 'latent', [(i, i ^ step) for i in range(count)])  8.6 us
    ppermute x1, starting transfers between devices, across_cores(): return lax.ppermute(value, 'layer', [(i, i ^ 1) for i in range(count)])  6.91 us
    ppermute x5, waiting for transfers between devices, passed_along(): lax.ppermute(value, 'layer', [(i, i + steps) for i in range(count - steps)])  3.93 us
    unnamed x14, local copies, waits for them, and re-layouts  3.81 us
    pallas_call x1, Pallas kernels, decode_late(): pl.pallas_call(functools.partial(late_kernel, parts), out_shape=jax.Shape...  3.18 us
    pallas_call x1, Pallas kernels, decode_early(): pl.pallas_call(functools.partial(early_kernel, parts), out_shape=[jax.Sha...  2.38 us
  transfers between devices with their start and end apart: 15, of which 9 were waited for; matrix products, arithmetic and copies ran while one was open for 0% of the time, Pallas kernels for 9%

profile of v10, /device:TPU:5, one launch (start us, length us, event | category | flops | bytes accessed | tf_op | source)
XLA Modules:
  0.0 69.7 jit_solution(4453575949814617745)
XLA Ops:
  0.0 0.0 copy-start.2
  0.0 1.2 %copy-done.2 = bf16[1,4096,128]{2,1,0:T(8,128)(2,1)S(1)} copy-done((bf16[1,4096,128]{2,1,0:T(8,128)(2,1)S(1)}, bf16[1,4096,128]{2,1,0:T(8,128)(2,1)}, u32[]{:S(2)}) %copy-start.2) | copy-done | bytes 1048600
  1.2 0.1 fetch_rows.1
  1.3 3.4 %collective-permute-start.2 = (bf16[1024,128]{1,0:T(8,128)(2,1)S(1)}, bf16[1024,128]{1,0:T(8,128)(2,1)S(1)}, u32[]{:S(2)}, u32[]{:S(2)}) collective-permute-start(bf16[1024,128]{1,0:T(8,128)(2,1)S(1)} %get-tuple-element.45), channel_id=1, source_target_pairs={{0,3},{1,2},{2,1},{3,0},{4,7},{5,6},{6,5},{7,4},{8,11},{9,10},{10,... | collective-permute-start | bytes 786440 | tf_op jit(solution)/shard_map/encoder_rows/ppermute | solution.py:18
  4.7 0.0 collective-permute-start.3
  4.7 0.4 collective-permute-start.4
  5.0 0.0 copy-start
  5.0 1.9 %copy-done = bf16[1,3,512,1024]{3,2,1,0:T(8,128)(2,1)S(1)} copy-done((bf16[1,3,512,1024]{3,2,1,0:T(8,128)(2,1)S(1)}, bf16[1,3,512,1024]{3,2,1,0:T(8,128)(2,1)}, u32[]{:S(2)}) %copy-start) | copy-done | bytes 3145752
  6.9 0.0 copy-start.3
  6.9 0.7 copy-done.3
  7.6 0.0 copy-start.4
  7.6 0.1 fetch_decoders.1
  7.8 4.5 %collective-permute-start = (bf16[528,1024]{1,0:T(8,128)(2,1)S(1)}, bf16[528,1024]{1,0:T(8,128)(2,1)S(1)}, u32[]{:S(2)}, u32[]{:S(2)}) collective-permute-start(bf16[528,1024]{1,0:T(8,128)(2,1)S(1)} %get-tuple-element.40), channel_id=1, source_target_pairs={{0,4},{4,8},{8,12},{12,16},{16,20},{20,24},{24,28},{1,5},{5,9},{9,... | collective-permute-start | bytes 3244040 | tf_op jit(solution)/shard_map/decoder_weights/ppermute | solution.py:29
  12.3 1.9 %collective-permute-start.1 = (bf16[528,1024]{1,0:T(8,128)(2,1)S(1)}, bf16[528,1024]{1,0:T(8,128)(2,1)S(1)}, u32[]{:S(2)}, u32[]{:S(2)}) collective-permute-start(bf16[528,1024]{1,0:T(8,128)(2,1)S(1)} %get-tuple-element.41), channel_id=1, source_target_pairs={{0,8},{4,12},{8,16},{12,20},{16,24},{20,28},{1,9},{5,13},{9,17},{1... | collective-permute-start | bytes 3244040 | tf_op jit(solution)/shard_map/decoder_weights/ppermute | solution.py:29
  14.2 0.0 collective-permute-done.2.refs_1_
  14.2 3.8 %collective-permute-done.3.refs_2_ = bf16[1024,128]{1,0:T(8,128)(2,1)S(1)} collective-permute-done((bf16[1024,128]{1,0:T(8,128)(2,1)S(1)}, bf16[1024,128]{1,0:T(8,128)(2,1)S(1)}, u32[]{:S(2)}, u32[]{:S(2)}) %collective-permute-start.3) | collective-permute-done | bytes 262176 | tf_op jit(solution)/shard_map/encoder_rows/ppermute | solution.py:18
  18.1 8.5 %collective-permute-done.4.refs_3_ = bf16[1024,128]{1,0:T(8,128)(2,1)S(1)} collective-permute-done((bf16[1024,128]{1,0:T(8,128)(2,1)S(1)}, bf16[1024,128]{1,0:T(8,128)(2,1)S(1)}, u32[]{:S(2)}, u32[]{:S(2)}) %collective-permute-start.4) | collective-permute-done | bytes 262176 | tf_op jit(solution)/shard_map/encoder_rows/ppermute | solution.py:18
  26.6 0.0 copy-done.4
  26.6 0.0 copy-done.5
  26.6 0.0 copy-done.6
  26.6 0.0 copy-start.1
  26.6 1.9 %encode.1 = (f32[4,2,64,128]{3,2,1,0:T(8,128)S(1)}, f32[4,2,64,128]{3,2,1,0:T(8,128)S(1)}, bf16[4,2,64,128]{3,2,1,0:T(8,128)(2,1)S(1)}, bf16[4,2,64,128]{3,2,1,0:T(8,128)(2,1)S(1)}) custom-call(s32[2,16]{1,0:T(2,128)S(1)} %bitcast.12, s32[16]{0:T(128)S(1)} %bitcast.15, f32[1,128]{1,0:T(1,128)S(1)} %copy-done.6, bf16[1024,1024]{1,0:T(8,128)(2,1)S(1)} %bitcast.14, ...), custom_call_target="tpu_custom_call" | custom-call | flops 17179869184 | bytes 3145728 | tf_op jit(solution)/shard_map/encode/encode/pallas_call | solution.py:121
  28.5 0.1 collective-permute-start.5
  28.6 1.5 %collective-permute-start.7 = (bf16[4,2,64,128]{3,2,1,0:T(8,128)(2,1)S(1)}, bf16[4,2,64,128]{3,2,1,0:T(8,128)(2,1)S(1)}, u32[]{:S(2)}, u32[]{:S(2)}) collective-permute-start(bf16[4,2,64,128]{3,2,1,0:T(8,128)(2,1)S(1)} %get-tuple-element.53), channel_id=1, source_target_pairs={{0,1},{1,0},{2,3},{3,2},{4,5},{5,4},{6,7},{7,6},{8,9},{9,8},{10,11... | collective-permute-start | bytes 393224 | tf_op jit(solution)/shard_map/encode/ppermute | solution.py:18
  30.0 2.6 %collective-permute-done.5.arrived_ref = bf16[4,2,64,128]{3,2,1,0:T(8,128)(2,1)S(1)} collective-permute-done((bf16[4,2,64,128]{3,2,1,0:T(8,128)(2,1)S(1)}, bf16[4,2,64,128]{3,2,1,0:T(8,128)(2,1)S(1)}, u32[]{:S(2)}, u32[]{:S(2)}) %collective-permute-start.5) | collective-permute-done | bytes 131104 | tf_op jit(solution)/shard_map/encode/ppermute | solution.py:18
  32.7 0.9 %collective-permute-start.6 = (bf16[4,2,64,128]{3,2,1,0:T(8,128)(2,1)S(1)}, bf16[4,2,64,128]{3,2,1,0:T(8,128)(2,1)S(1)}, u32[]{:S(2)}, u32[]{:S(2)}) collective-permute-start(bf16[4,2,64,128]{3,2,1,0:T(8,128)(2,1)S(1)} %get-tuple-element.51), channel_id=1, source_target_pairs={{0,2},{1,3},{2,0},{3,1},{4,6},{5,7},{6,4},{7,5},{8,10},{9,11},{10,... | collective-permute-start | bytes 393224 | tf_op jit(solution)/shard_map/encode/ppermute | solution.py:18
  33.6 1.4 %collective-permute-done.7.arrived_ref = bf16[4,2,64,128]{3,2,1,0:T(8,128)(2,1)S(1)} collective-permute-done((bf16[4,2,64,128]{3,2,1,0:T(8,128)(2,1)S(1)}, bf16[4,2,64,128]{3,2,1,0:T(8,128)(2,1)S(1)}, u32[]{:S(2)}, u32[]{:S(2)}) %collective-permute-start.7) | collective-permute-done | bytes 131104 | tf_op jit(solution)/shard_map/encode/ppermute | solution.py:18
  35.0 4.0 %collective-permute-done.6.arrived_ref = bf16[4,2,64,128]{3,2,1,0:T(8,128)(2,1)S(1)} collective-permute-done((bf16[4,2,64,128]{3,2,1,0:T(8,128)(2,1)S(1)}, bf16[4,2,64,128]{3,2,1,0:T(8,128)(2,1)S(1)}, u32[]{:S(2)}, u32[]{:S(2)}) %collective-permute-start.6) | collective-permute-done | bytes 131104 | tf_op jit(solution)/shard_map/encode/ppermute | solution.py:18
  39.1 0.2 collective-permute-start.8
  39.3 2.2 %collective-permute-start.9 = (bf16[4,2,64,128]{3,2,1,0:T(8,128)(2,1)S(1)}, bf16[4,2,64,128]{3,2,1,0:T(8,128)(2,1)S(1)}, u32[]{:S(2)}, u32[]{:S(2)}) collective-permute-start(bf16[4,2,64,128]{3,2,1,0:T(8,128)(2,1)S(1)} %activate.2.refs_0_), channel_id=1, source_target_pairs={{0,1},{1,0},{2,3},{3,2},{4,5},{5,4},{6,7},{7,6},{8,9},{9,8},{10,11... | collective-permute-start | bytes 393224 | tf_op jit(solution)/shard_map/spread/ppermute | solution.py:18
  41.5 2.8 %collective-permute-start.11 = (bf16[4,2,64,128]{3,2,1,0:T(8,128)(2,1)S(1)}, bf16[4,2,64,128]{3,2,1,0:T(8,128)(2,1)S(1)}, u32[]{:S(2)}, u32[]{:S(2)}) collective-permute-start(bf16[4,2,64,128]{3,2,1,0:T(8,128)(2,1)S(1)} %activate.2.refs_0_), channel_id=1, source_target_pairs={{0,8},{4,12},{8,16},{12,20},{16,24},{20,28},{1,9},{5,13},{9,17},{1... | collective-permute-start | bytes 393224 | tf_op jit(solution)/shard_map/spread/ppermute | solution.py:29
  44.3 0.9 %collective-permute-done.8.arrived_ref = bf16[4,2,64,128]{3,2,1,0:T(8,128)(2,1)S(1)} collective-permute-done((bf16[4,2,64,128]{3,2,1,0:T(8,128)(2,1)S(1)}, bf16[4,2,64,128]{3,2,1,0:T(8,128)(2,1)S(1)}, u32[]{:S(2)}, u32[]{:S(2)}) %collective-permute-start.8) | collective-permute-done | bytes 131104 | tf_op jit(solution)/shard_map/encode/ppermute | solution.py:18
  45.3 0.1 collective-permute-start.10
  45.4 0.0 collective-permute-done.9.refs_2_.second_ref
  45.4 3.0 %collective-permute-start.13 = (bf16[8,2,64,128]{3,2,1,0:T(8,128)(2,1)S(1)}, bf16[8,2,64,128]{3,2,1,0:T(8,128)(2,1)S(1)}, u32[]{:S(2)}, u32[]{:S(2)}) collective-permute-start(bf16[8,2,64,128]{3,2,1,0:T(8,128)(2,1)S(1)} %join.1), channel_id=1, source_target_pairs={{0,8},{4,12},{8,16},{12,20},{16,24},{20,28},{1,9},{5,13},{9,17},{1... | collective-permute-start | bytes 786440 | tf_op jit(solution)/shard_map/spread/ppermute | solution.py:29
  48.5 2.4 %collective-permute-done.11.refs_4_ = bf16[4,2,64,128]{3,2,1,0:T(8,128)(2,1)S(1)} collective-permute-done((bf16[4,2,64,128]{3,2,1,0:T(8,128)(2,1)S(1)}, bf16[4,2,64,128]{3,2,1,0:T(8,128)(2,1)S(1)}, u32[]{:S(2)}, u32[]{:S(2)}) %collective-permute-start.11) | collective-permute-done | bytes 131104 | tf_op jit(solution)/shard_map/spread/ppermute | solution.py:29
  50.8 0.5 collective-permute-done.10.refs_3_
  51.4 2.6 %collective-permute-start.12 = (bf16[4,2,64,128]{3,2,1,0:T(8,128)(2,1)S(1)}, bf16[4,2,64,128]{3,2,1,0:T(8,128)(2,1)S(1)}, u32[]{:S(2)}, u32[]{:S(2)}) collective-permute-start(bf16[4,2,64,128]{3,2,1,0:T(8,128)(2,1)S(1)} %collective-permute-done.10.refs_3_), channel_id=1, source_target_pairs={{0,8},{4,12},{8,16},{12,20},{16,24},{20,28},{1,9},{5,13},{9,17},{1... | collective-permute-start | bytes 393224 | tf_op jit(solution)/shard_map/spread/ppermute | solution.py:29
  54.0 0.0 collective-permute-done.near_dec
  54.0 0.0 collective-permute-done.1.refs_6_.far_dec
  54.0 0.0 copy-done.1
  54.0 2.4 %decode_early.1 = (f32[256,1024]{1,0:T(8,128)S(1)}, f32[768,1024]{1,0:T(8,128)S(1)}) custom-call(s32[2,16]{1,0:T(2,128)S(1)} %bitcast.13, s32[2,16]{1,0:T(2,128)S(1)} %slice_convert_fusion.far_lists.lists_ref, bf16[4,2,64,128]{3,2,1,0:T(8,128)(2,1)S(1)} %activate.2.refs_0_, bf16[4,2,64,128]{3,2,1,0:T(8,128)(2,1)S(1)} %activate.3.refs_1_.first_ref, ...), custom_call_target="tpu_custom_call" | custom-call | flops 1342177280 | bytes 6291456 | tf_op jit(solution)/shard_map/decode/decode_early/pallas_call | solution.py:251
  56.4 1.6 %collective-permute-done.12.third.refs_6_ = bf16[4,2,64,128]{3,2,1,0:T(8,128)(2,1)S(1)} collective-permute-done((bf16[4,2,64,128]{3,2,1,0:T(8,128)(2,1)S(1)}, bf16[4,2,64,128]{3,2,1,0:T(8,128)(2,1)S(1)}, u32[]{:S(2)}, u32[]{:S(2)}) %collective-permute-start.12) | collective-permute-done | bytes 131104 | tf_op jit(solution)/shard_map/spread/ppermute | solution.py:29
  58.0 0.0 collective-permute-done.13.second.refs_5_
  58.0 6.9 %collective-permute-start.14 = (bf16[16,2,64,128]{3,2,1,0:T(8,128)(2,1)S(1)}, bf16[16,2,64,128]{3,2,1,0:T(8,128)(2,1)S(1)}, u32[]{:S(2)}, u32[]{:S(2)}) collective-permute-start(bf16[16,2,64,128]{3,2,1,0:T(8,128)(2,1)S(1)} %choose.1), channel_id=1, source_target_pairs={{0,4},{4,0},{8,12},{12,8},{16,20},{20,16},{24,28},{28,24},{1,5},{5... | collective-permute-start | bytes 1572872 | tf_op jit(solution)/shard_map/decode/ppermute | solution.py:34
  64.9 1.6 %decode_middle.1.rest_ref = f32[768,1024]{1,0:T(8,128)S(1)} custom-call(s32[2,16]{1,0:T(2,128)S(1)} %slice_convert_fusion.far_lists.lists_ref, f32[768,1024]{1,0:T(8,128)S(1)} %get-tuple-element.63.rest_ref, bf16[8,2,64,128]{3,2,1,0:T(8,128)(2,1)S(1)} %collective-permute-done.13.second.refs_5_, ...), custom_call_target="tpu_custom_call" | custom-call | flops 805306368 | bytes 7340032 | tf_op jit(solution)/shard_map/decode/decode_middle/pallas_call | solution.py:283
  66.6 0.0 collective-permute-done.14.near
  66.6 3.2 %decode_late.1 = bf16[1024,1024]{1,0:T(8,128)(2,1)} custom-call(s32[2,16]{1,0:T(2,128)S(1)} %slice_convert_fusion.1.lists_ref, f32[256,1024]{1,0:T(8,128)S(1)} %get-tuple-element.62.first_ref, f32[768,1024]{1,0:T(8,128)S(1)} %decode_middle.1.rest_ref, bf16[16,2,64,128]{3,2,1,0:T(8,128)(2,1)S(1)} %collective-permute-done.14.near, ...), custom_call_target="tpu_custom_call" | custom-call | flops 1073741824 | bytes 7340032 | tf_op jit(solution)/shard_map/decode/decode_late/pallas_call | solution.py:326
  (10 shorter events, 0.2 us)
Async XLA Ops:
  0.0 1.2 %copy-start.2 = (bf16[1,4096,128]{2,1,0:T(8,128)(2,1)S(1)}, bf16[1,4096,128]{2,1,0:T(8,128)(2,1)}, u32[]{:S(2)}) copy-start(bf16[1,4096,128]{2,1,0:T(8,128)(2,1)} %param.7) | copy-start | bytes 3145732
  1.3 12.9 %collective-permute-start.2 = (bf16[1024,128]{1,0:T(8,128)(2,1)S(1)}, bf16[1024,128]{1,0:T(8,128)(2,1)S(1)}, u32[]{:S(2)}, u32[]{:S(2)}) collective-permute-start(bf16[1024,128]{1,0:T(8,128)(2,1)S(1)} %get-tuple-element.45), channel_id=1, source_target_pairs={{0,3},{1,2},{2,1},{3,0},{4,7},{5,6},{6,5},{7,4},{8,11},{9,10},{10,... | collective-permute-start | bytes 786440 | tf_op jit(solution)/shard_map/encoder_rows/ppermute | solution.py:18
  4.7 13.4 %collective-permute-start.3 = (bf16[1024,128]{1,0:T(8,128)(2,1)S(1)}, bf16[1024,128]{1,0:T(8,128)(2,1)S(1)}, u32[]{:S(2)}, u32[]{:S(2)}) collective-permute-start(bf16[1024,128]{1,0:T(8,128)(2,1)S(1)} %get-tuple-element.46), channel_id=1, source_target_pairs={{0,1},{1,0},{2,3},{3,2},{4,5},{5,4},{6,7},{7,6},{8,9},{9,8},{10,11... | collective-permute-start | bytes 786440 | tf_op jit(solution)/shard_map/encoder_rows/ppermute | solution.py:18
  4.7 21.9 %collective-permute-start.4 = (bf16[1024,128]{1,0:T(8,128)(2,1)S(1)}, bf16[1024,128]{1,0:T(8,128)(2,1)S(1)}, u32[]{:S(2)}, u32[]{:S(2)}) collective-permute-start(bf16[1024,128]{1,0:T(8,128)(2,1)S(1)} %get-tuple-element.47), channel_id=1, source_target_pairs={{0,2},{1,3},{2,0},{3,1},{4,6},{5,7},{6,4},{7,5},{8,10},{9,11},{10,... | collective-permute-start | bytes 786440 | tf_op jit(solution)/shard_map/encoder_rows/ppermute | solution.py:18
  5.0 1.9 %copy-start = (bf16[1,3,512,1024]{3,2,1,0:T(8,128)(2,1)S(1)}, bf16[1,3,512,1024]{3,2,1,0:T(8,128)(2,1)}, u32[]{:S(2)}) copy-start(bf16[1,3,512,1024]{3,2,1,0:T(8,128)(2,1)} %param.9) | copy-start | bytes 9437188
  6.9 0.7 copy-start.3
  7.6 19.0 %copy-start.4 = (bf16[1,1024,1024]{2,1,0:T(8,128)(2,1)S(1)}, bf16[1,1024,1024]{2,1,0:T(8,128)(2,1)}, u32[]{:S(2)}) copy-start(bf16[1,1024,1024]{2,1,0:T(8,128)(2,1)} %param.6) | copy-start | bytes 6291460
  7.6 19.0 %copy-start.5 = (s32[1,16]{1,0:T(1,128)S(1)}, s32[1,16]{1,0:T(1,128)}, u32[]{:S(2)}) copy-start(s32[1,16]{1,0:T(1,128)} %param.11) | copy-start | bytes 196
  7.6 19.0 %copy-start.6 = (f32[1,128]{1,0:T(1,128)S(1)}, f32[1,128]{1,0:T(1,128)}, u32[]{:S(2)}) copy-start(f32[1,128]{1,0:T(1,128)} %bias_ref.1) | copy-start | bytes 1540
  7.8 46.2 %collective-permute-start = (bf16[528,1024]{1,0:T(8,128)(2,1)S(1)}, bf16[528,1024]{1,0:T(8,128)(2,1)S(1)}, u32[]{:S(2)}, u32[]{:S(2)}) collective-permute-start(bf16[528,1024]{1,0:T(8,128)(2,1)S(1)} %get-tuple-element.40), channel_id=1, source_target_pairs={{0,4},{4,8},{8,12},{12,16},{16,20},{20,24},{24,28},{1,5},{5,9},{9,... | collective-permute-start | bytes 3244040 | tf_op jit(solution)/shard_map/decoder_weights/ppermute | solution.py:29
  12.3 41.7 %collective-permute-start.1 = (bf16[528,1024]{1,0:T(8,128)(2,1)S(1)}, bf16[528,1024]{1,0:T(8,128)(2,1)S(1)}, u32[]{:S(2)}, u32[]{:S(2)}) collective-permute-start(bf16[528,1024]{1,0:T(8,128)(2,1)S(1)} %get-tuple-element.41), channel_id=1, source_target_pairs={{0,8},{4,12},{8,16},{12,20},{16,24},{20,28},{1,9},{5,13},{9,17},{1... | collective-permute-start | bytes 3244040 | tf_op jit(solution)/shard_map/decoder_weights/ppermute | solution.py:29
  26.6 27.4 %copy-start.1 = (bf16[1,3,512,1024]{3,2,1,0:T(8,128)(2,1)S(1)}, bf16[1,3,512,1024]{3,2,1,0:T(8,128)(2,1)}, u32[]{:S(2)}) copy-start(bf16[1,3,512,1024]{3,2,1,0:T(8,128)(2,1)} %param.9) | copy-start | bytes 9437188
  28.5 4.2 %collective-permute-start.5 = (bf16[4,2,64,128]{3,2,1,0:T(8,128)(2,1)S(1)}, bf16[4,2,64,128]{3,2,1,0:T(8,128)(2,1)S(1)}, u32[]{:S(2)}, u32[]{:S(2)}) collective-permute-start(bf16[4,2,64,128]{3,2,1,0:T(8,128)(2,1)S(1)} %get-tuple-element.49), channel_id=1, source_target_pairs={{0,1},{1,0},{2,3},{3,2},{4,5},{5,4},{6,7},{7,6},{8,9},{9,8},{10,11... | collective-permute-start | bytes 393224 | tf_op jit(solution)/shard_map/encode/ppermute | solution.py:18
  28.6 6.4 %collective-permute-start.7 = (bf16[4,2,64,128]{3,2,1,0:T(8,128)(2,1)S(1)}, bf16[4,2,64,128]{3,2,1,0:T(8,128)(2,1)S(1)}, u32[]{:S(2)}, u32[]{:S(2)}) collective-permute-start(bf16[4,2,64,128]{3,2,1,0:T(8,128)(2,1)S(1)} %get-tuple-element.53), channel_id=1, source_target_pairs={{0,1},{1,0},{2,3},{3,2},{4,5},{5,4},{6,7},{7,6},{8,9},{9,8},{10,11... | collective-permute-start | bytes 393224 | tf_op jit(solution)/shard_map/encode/ppermute | solution.py:18
  32.7 6.4 %collective-permute-start.6 = (bf16[4,2,64,128]{3,2,1,0:T(8,128)(2,1)S(1)}, bf16[4,2,64,128]{3,2,1,0:T(8,128)(2,1)S(1)}, u32[]{:S(2)}, u32[]{:S(2)}) collective-permute-start(bf16[4,2,64,128]{3,2,1,0:T(8,128)(2,1)S(1)} %get-tuple-element.51), channel_id=1, source_target_pairs={{0,2},{1,3},{2,0},{3,1},{4,6},{5,7},{6,4},{7,5},{8,10},{9,11},{10,... | collective-permute-start | bytes 393224 | tf_op jit(solution)/shard_map/encode/ppermute | solution.py:18
  39.1 6.2 %collective-permute-start.8 = (bf16[4,2,64,128]{3,2,1,0:T(8,128)(2,1)S(1)}, bf16[4,2,64,128]{3,2,1,0:T(8,128)(2,1)S(1)}, u32[]{:S(2)}, u32[]{:S(2)}) collective-permute-start(bf16[4,2,64,128]{3,2,1,0:T(8,128)(2,1)S(1)} %get-tuple-element.57), channel_id=1, source_target_pairs={{0,2},{1,3},{2,0},{3,1},{4,6},{5,7},{6,4},{7,5},{8,10},{9,11},{10,... | collective-permute-start | bytes 393224 | tf_op jit(solution)/shard_map/encode/ppermute | solution.py:18
  39.3 6.1 %collective-permute-start.9 = (bf16[4,2,64,128]{3,2,1,0:T(8,128)(2,1)S(1)}, bf16[4,2,64,128]{3,2,1,0:T(8,128)(2,1)S(1)}, u32[]{:S(2)}, u32[]{:S(2)}) collective-permute-start(bf16[4,2,64,128]{3,2,1,0:T(8,128)(2,1)S(1)} %activate.2.refs_0_), channel_id=1, source_target_pairs={{0,1},{1,0},{2,3},{3,2},{4,5},{5,4},{6,7},{7,6},{8,9},{9,8},{10,11... | collective-permute-start | bytes 393224 | tf_op jit(solution)/shard_map/spread/ppermute | solution.py:18
  41.5 9.3 %collective-permute-start.11 = (bf16[4,2,64,128]{3,2,1,0:T(8,128)(2,1)S(1)}, bf16[4,2,64,128]{3,2,1,0:T(8,128)(2,1)S(1)}, u32[]{:S(2)}, u32[]{:S(2)}) collective-permute-start(bf16[4,2,64,128]{3,2,1,0:T(8,128)(2,1)S(1)} %activate.2.refs_0_), channel_id=1, source_target_pairs={{0,8},{4,12},{8,16},{12,20},{16,24},{20,28},{1,9},{5,13},{9,17},{1... | collective-permute-start | bytes 393224 | tf_op jit(solution)/shard_map/spread/ppermute | solution.py:29
  45.3 6.1 %collective-permute-start.10 = (bf16[4,2,64,128]{3,2,1,0:T(8,128)(2,1)S(1)}, bf16[4,2,64,128]{3,2,1,0:T(8,128)(2,1)S(1)}, u32[]{:S(2)}, u32[]{:S(2)}) collective-permute-start(bf16[4,2,64,128]{3,2,1,0:T(8,128)(2,1)S(1)} %activate.3.refs_1_.first_ref), channel_id=1, source_target_pairs={{0,1},{1,0},{2,3},{3,2},{4,5},{5,4},{6,7},{7,6},{8,9},{9,8},{10,11... | collective-permute-start | bytes 393224 | tf_op jit(solution)/shard_map/spread/ppermute | solution.py:18
  45.4 12.6 %collective-permute-start.13 = (bf16[8,2,64,128]{3,2,1,0:T(8,128)(2,1)S(1)}, bf16[8,2,64,128]{3,2,1,0:T(8,128)(2,1)S(1)}, u32[]{:S(2)}, u32[]{:S(2)}) collective-permute-start(bf16[8,2,64,128]{3,2,1,0:T(8,128)(2,1)S(1)} %join.1), channel_id=1, source_target_pairs={{0,8},{4,12},{8,16},{12,20},{16,24},{20,28},{1,9},{5,13},{9,17},{1... | collective-permute-start | bytes 786440 | tf_op jit(solution)/shard_map/spread/ppermute | solution.py:29
  51.4 6.6 %collective-permute-start.12 = (bf16[4,2,64,128]{3,2,1,0:T(8,128)(2,1)S(1)}, bf16[4,2,64,128]{3,2,1,0:T(8,128)(2,1)S(1)}, u32[]{:S(2)}, u32[]{:S(2)}) collective-permute-start(bf16[4,2,64,128]{3,2,1,0:T(8,128)(2,1)S(1)} %collective-permute-done.10.refs_3_), channel_id=1, source_target_pairs={{0,8},{4,12},{8,16},{12,20},{16,24},{20,28},{1,9},{5,13},{9,17},{1... | collective-permute-start | bytes 393224 | tf_op jit(solution)/shard_map/spread/ppermute | solution.py:29
  58.0 8.5 %collective-permute-start.14 = (bf16[16,2,64,128]{3,2,1,0:T(8,128)(2,1)S(1)}, bf16[16,2,64,128]{3,2,1,0:T(8,128)(2,1)S(1)}, u32[]{:S(2)}, u32[]{:S(2)}) collective-permute-start(bf16[16,2,64,128]{3,2,1,0:T(8,128)(2,1)S(1)} %choose.1), channel_id=1, source_target_pairs={{0,4},{4,0},{8,12},{12,8},{16,20},{20,16},{24,28},{28,24},{1,5},{5... | collective-permute-start | bytes 1572872 | tf_op jit(solution)/shard_map/decode/ppermute | solution.py:34

commit v11 on v9

--- a/solution.py
+++ b/solution.py
@@ -161,17 +161,12 @@
     sources, out_ref = refs[:-1], refs[-1]
     count = sources[0].shape[0]
     odd = lax.bitwise_and(lax.axis_index("layer"), 1)
-
-    @pl.when(odd == 0)
-    def _():
-        for number in range(4):
-            out_ref[number * count : (number + 1) * count] = sources[number][...]
-
-    @pl.when(odd == 1)
-    def _():
-        out_ref[:count] = sources[4][...]
-        out_ref[count : 3 * count] = sources[5][...]
-        out_ref[3 * count :] = sources[6][...]
+    for parity in range(2):
+
+        @pl.when(odd == parity)
+        def _():
+            for number in range(4):
+                out_ref[number * count : (number + 1) * count] = sources[4 * parity + number][...]
 
 
 def choose(own, far):
@@ -179,26 +174,10 @@
     return pl.pallas_call(
         choose_kernel,
         out_shape=jax.ShapeDtypeStruct((4 * shape[0],) + shape[1:], own[0].dtype),
-        in_specs=[VMEM] * 7,
+        in_specs=[VMEM] * 8,
         out_specs=VMEM,
         **small("choose"),
     )(*own, *far)
-
-
-def join_kernel(first_ref, second_ref, out_ref):
-    count = first_ref.shape[0]
-    out_ref[:count] = first_ref[...]
-    out_ref[count:] = second_ref[...]
-
-
-def join(first, second):
-    return pl.pallas_call(
-        join_kernel,
-        out_shape=jax.ShapeDtypeStruct((2 * first.shape[0],) + first.shape[1:], first.dtype),
-        in_specs=[VMEM] * 2,
-        out_specs=VMEM,
-        **small("join"),
-    )(first, second)
 
 
 def expand(dense, lists_ref, parts, first, act_refs):
@@ -261,10 +240,11 @@
     )(lists, far_lists, *acts, decoder, far_decoder)
 
 
-def middle_kernel(parts, lists_ref, rest_ref, second, third, far_dec, total_ref, dense):
+def middle_kernel(parts, lists_ref, rest_ref, *refs):
+    far_refs, (far_dec, total_ref, dense) = refs[:3], refs[3:]
     latents = dense.shape[1]
     dense[...] = jnp.zeros_like(dense)
-    expand(dense, lists_ref, parts, third.shape[0], [second, third])
+    expand(dense, lists_ref, parts, far_refs[0].shape[0], far_refs)
     for lanes in column_tiles(rest_ref.shape[1]):
         total_ref[:, lanes] = rest_ref[:, lanes] + jnp.dot(
             dense[...], far_dec[:latents, lanes], preferred_element_type=jnp.float32
@@ -276,7 +256,7 @@
     return pl.pallas_call(
         functools.partial(middle_kernel, parts),
         out_shape=jax.ShapeDtypeStruct(rest.shape, rest.dtype),
-        in_specs=[SMEM] + [VMEM] * 4,
+        in_specs=[SMEM] + [VMEM] * 5,
         out_specs=VMEM,
         scratch_shapes=[pltpu.VMEM((rows, latents), jnp.bfloat16)],
         cost_estimate=pl.CostEstimate(
@@ -372,15 +352,16 @@
         own_a, own_b = activate(kept_a, arrived_a), activate(kept_b, arrived_b)
     with jax.named_scope("spread"):
         late_a = swapped(own_a, 1)
+        late_a, own_b = lax.optimization_barrier((late_a, own_b))
         far_a = passed_along(own_a, 2)
-        late_b = swapped(own_b, 1)
-        joined = join(own_b, late_a)
-        late_b, far_a = lax.optimization_barrier((late_b, far_a))
+        late_b, far_b = swapped(own_b, 1), passed_along(own_b, 2)
+        late_b, far_b = lax.optimization_barrier((late_b, far_b))
+        late_far_a, late_far_b = swapped(far_a, 1), swapped(far_b, 1)
         own = [own_a, own_b, late_a, late_b]
-        far = [far_a] + [passed_along(piece, 2) for piece in (joined, late_b)]
     with jax.named_scope("decode"):
-        first, rest = decode_early(lists, far_lists, own + far[:1], decoder, far_decoder, parts)
-        first, rest, far[2] = lax.optimization_barrier((first, rest, far[2]))
+        first, rest = decode_early(lists, far_lists, own + [far_a], decoder, far_decoder, parts)
+        first, rest, late_far_b = lax.optimization_barrier((first, rest, late_far_b))
+        far = [far_a, far_b, late_far_a, late_far_b]
         near = across_cores(choose(own, far))
         rest = decode_middle(far_lists, rest, far[1:], far_decoder, latents, parts)
         return decode_late(near_lists, [first, rest], near, near_decoder, latents, parts)[None]

time: 69.1 us -> 70.5 us (1.020)
  waiting for transfers between devices: 18.7 us -> 19.8 us
    ppermute x5 -> x4, starting transfers between devices: 15.6 us -> 12.3 us  [passed_along(): lax.ppermute(value, 'layer', [(i, i + steps) for i in range(count - steps)])]
    ppermute x9 -> x11, starting transfers between devices: 14.8 us -> 17.2 us  [swapped(): return lax.ppermute(value, 'latent', [(i, i ^ step) for i in range(count)])]
    ppermute x1, starting transfers between devices: 6.26 us -> 7.44 us  [across_cores(): return lax.ppermute(value, 'layer', [(i, i ^ 1) for i in range(count)])]
    ppermute x9 -> x11, waiting for transfers between devices: 15.6 us -> 16.8 us  [swapped(): return lax.ppermute(value, 'latent', [(i, i ^ step) for i in range(count)])]
    ppermute x5 -> x4, waiting for transfers between devices: 3.1 us -> 3.08 us  [passed_along(): lax.ppermute(value, 'layer', [(i, i + steps) for i in range(count - steps)])]
  transfers between devices with their start and end apart: 15 -> 16, of which waited for: 7 -> 8; matrix products, arithmetic and copies ran while one was open for 0% -> 0% of each run, Pallas kernels for 9% -> 9%
where the time goes in v11:
time: 70.5 us; the launch traced here: 70.3 us
  starting transfers between devices  37 us (52%)
  waiting for transfers between devices  19.8 us (28%)
  Pallas kernels  9.45 us (13%)
  local copies, waits for them, and re-layouts  3.81 us (5%)
    ppermute x11, starting transfers between devices, swapped(): return lax.ppermute(value, 'latent', [(i, i ^ step) for i in range(count)])  17.2 us
    ppermute x11, waiting for transfers between devices, swapped(): return lax.ppermute(value, 'latent', [(i, i ^ step) for i in range(count)])  16.8 us
    ppermute x4, starting transfers between devices, passed_along(): lax.ppermute(value, 'layer', [(i, i + steps) for i in range(count - steps)])  12.3 us
    ppermute x1, starting transfers between devices, across_cores(): return lax.ppermute(value, 'layer', [(i, i ^ 1) for i in range(count)])  7.44 us
    unnamed x14, local copies, waits for them, and re-layouts  3.81 us
    pallas_call x1, Pallas kernels, decode_late(): pl.pallas_call(functools.partial(late_kernel, parts), out_shape=jax.Shape...  3.17 us
    ppermute x4, waiting for transfers between devices, passed_along(): lax.ppermute(value, 'layer', [(i, i + steps) for i in range(count - steps)])  3.08 us
    pallas_call x1, Pallas kernels, decode_early(): pl.pallas_call(functools.partial(early_kernel, parts), out_shape=[jax.Sha...  2.38 us
  transfers between devices with their start and end apart: 16, of which 8 were waited for; matrix products, arithmetic and copies ran while one was open for 0% of the time, Pallas kernels for 9%

profile of v11, /device:TPU:5, one launch (start us, length us, event | category | flops | bytes accessed | tf_op | source)
XLA Modules:
  0.0 70.3 jit_solution(15623570069607906433)
XLA Ops:
  0.0 0.0 copy-start.2
  0.0 1.2 %copy-done.2 = bf16[1,4096,128]{2,1,0:T(8,128)(2,1)S(1)} copy-done((bf16[1,4096,128]{2,1,0:T(8,128)(2,1)S(1)}, bf16[1,4096,128]{2,1,0:T(8,128)(2,1)}, u32[]{:S(2)}) %copy-start.2) | copy-done | bytes 1048600
  1.2 0.1 fetch_rows.1
  1.3 1.4 %collective-permute-start.2 = (bf16[1024,128]{1,0:T(8,128)(2,1)S(1)}, bf16[1024,128]{1,0:T(8,128)(2,1)S(1)}, u32[]{:S(2)}, u32[]{:S(2)}) collective-permute-start(bf16[1024,128]{1,0:T(8,128)(2,1)S(1)} %get-tuple-element.47), channel_id=1, source_target_pairs={{0,1},{1,0},{2,3},{3,2},{4,5},{5,4},{6,7},{7,6},{8,9},{9,8},{10,11... | collective-permute-start | bytes 786440 | tf_op jit(solution)/shard_map/encoder_rows/ppermute | solution.py:18
  2.7 2.3 %collective-permute-start.3 = (bf16[1024,128]{1,0:T(8,128)(2,1)S(1)}, bf16[1024,128]{1,0:T(8,128)(2,1)S(1)}, u32[]{:S(2)}, u32[]{:S(2)}) collective-permute-start(bf16[1024,128]{1,0:T(8,128)(2,1)S(1)} %get-tuple-element.48), channel_id=1, source_target_pairs={{0,2},{1,3},{2,0},{3,1},{4,6},{5,7},{6,4},{7,5},{8,10},{9,11},{10,... | collective-permute-start | bytes 786440 | tf_op jit(solution)/shard_map/encoder_rows/ppermute | solution.py:18
  5.0 0.0 collective-permute-start.4
  5.0 0.0 copy-start
  5.0 1.9 %copy-done = bf16[1,3,512,1024]{3,2,1,0:T(8,128)(2,1)S(1)} copy-done((bf16[1,3,512,1024]{3,2,1,0:T(8,128)(2,1)S(1)}, bf16[1,3,512,1024]{3,2,1,0:T(8,128)(2,1)}, u32[]{:S(2)}) %copy-start) | copy-done | bytes 3145752
  6.9 0.7 copy-done.3
  7.5 0.1 fetch_decoders.1
  7.7 4.6 %collective-permute-start = (bf16[528,1024]{1,0:T(8,128)(2,1)S(1)}, bf16[528,1024]{1,0:T(8,128)(2,1)S(1)}, u32[]{:S(2)}, u32[]{:S(2)}) collective-permute-start(bf16[528,1024]{1,0:T(8,128)(2,1)S(1)} %get-tuple-element.42), channel_id=1, source_target_pairs={{0,4},{4,8},{8,12},{12,16},{16,20},{20,24},{24,28},{1,5},{5,9},{9,... | collective-permute-start | bytes 3244040 | tf_op jit(solution)/shard_map/decoder_weights/ppermute | solution.py:23
  12.3 1.9 %collective-permute-start.1 = (bf16[528,1024]{1,0:T(8,128)(2,1)S(1)}, bf16[528,1024]{1,0:T(8,128)(2,1)S(1)}, u32[]{:S(2)}, u32[]{:S(2)}) collective-permute-start(bf16[528,1024]{1,0:T(8,128)(2,1)S(1)} %get-tuple-element.43), channel_id=1, source_target_pairs={{0,8},{4,12},{8,16},{12,20},{16,24},{20,28},{1,9},{5,13},{9,17},{1... | collective-permute-start | bytes 3244040 | tf_op jit(solution)/shard_map/decoder_weights/ppermute | solution.py:23
  14.2 0.0 collective-permute-done.2.refs_1_
  14.2 0.0 collective-permute-done.3.refs_2_
  14.3 7.6 %collective-permute-done.4.refs_3_ = bf16[1024,128]{1,0:T(8,128)(2,1)S(1)} collective-permute-done((bf16[1024,128]{1,0:T(8,128)(2,1)S(1)}, bf16[1024,128]{1,0:T(8,128)(2,1)S(1)}, u32[]{:S(2)}, u32[]{:S(2)}) %collective-permute-start.4) | collective-permute-done | bytes 262176 | tf_op jit(solution)/shard_map/encoder_rows/ppermute | solution.py:18
  21.8 0.0 copy-done.4
  21.8 0.0 copy-done.5
  21.9 0.0 copy-done.6
  21.9 0.0 copy-start.1
  21.9 1.9 %encode.1 = (f32[4,2,64,128]{3,2,1,0:T(8,128)S(1)}, f32[4,2,64,128]{3,2,1,0:T(8,128)S(1)}, bf16[4,2,64,128]{3,2,1,0:T(8,128)(2,1)S(1)}, bf16[4,2,64,128]{3,2,1,0:T(8,128)(2,1)S(1)}) custom-call(s32[2,16]{1,0:T(2,128)S(1)} %bitcast.12, s32[16]{0:T(128)S(1)} %bitcast.15, f32[1,128]{1,0:T(1,128)S(1)} %copy-done.6, bf16[1024,1024]{1,0:T(8,128)(2,1)S(1)} %bitcast.14, ...), custom_call_target="tpu_custom_call" | custom-call | flops 17179869184 | bytes 3145728 | tf_op jit(solution)/shard_map/encode/encode/pallas_call | solution.py:114
  23.7 5.9 %collective-permute-start.5 = (bf16[4,2,64,128]{3,2,1,0:T(8,128)(2,1)S(1)}, bf16[4,2,64,128]{3,2,1,0:T(8,128)(2,1)S(1)}, u32[]{:S(2)}, u32[]{:S(2)}) collective-permute-start(bf16[4,2,64,128]{3,2,1,0:T(8,128)(2,1)S(1)} %get-tuple-element.51), channel_id=1, source_target_pairs={{0,1},{1,0},{2,3},{3,2},{4,5},{5,4},{6,7},{7,6},{8,9},{9,8},{10,11... | collective-permute-start | bytes 393224 | tf_op jit(solution)/shard_map/encode/ppermute | solution.py:18
  29.6 0.1 collective-permute-start.7
  29.7 2.6 %collective-permute-done.5.arrived_ref = bf16[4,2,64,128]{3,2,1,0:T(8,128)(2,1)S(1)} collective-permute-done((bf16[4,2,64,128]{3,2,1,0:T(8,128)(2,1)S(1)}, bf16[4,2,64,128]{3,2,1,0:T(8,128)(2,1)S(1)}, u32[]{:S(2)}, u32[]{:S(2)}) %collective-permute-start.5) | collective-permute-done | bytes 131104 | tf_op jit(solution)/shard_map/encode/ppermute | solution.py:18
  32.3 2.5 %collective-permute-start.6 = (bf16[4,2,64,128]{3,2,1,0:T(8,128)(2,1)S(1)}, bf16[4,2,64,128]{3,2,1,0:T(8,128)(2,1)S(1)}, u32[]{:S(2)}, u32[]{:S(2)}) collective-permute-start(bf16[4,2,64,128]{3,2,1,0:T(8,128)(2,1)S(1)} %get-tuple-element.53), channel_id=1, source_target_pairs={{0,2},{1,3},{2,0},{3,1},{4,6},{5,7},{6,4},{7,5},{8,10},{9,11},{10,... | collective-permute-start | bytes 393224 | tf_op jit(solution)/shard_map/encode/ppermute | solution.py:18
  34.8 0.0 collective-permute-done.7.arrived_ref
  34.9 3.0 %collective-permute-done.6.arrived_ref = bf16[4,2,64,128]{3,2,1,0:T(8,128)(2,1)S(1)} collective-permute-done((bf16[4,2,64,128]{3,2,1,0:T(8,128)(2,1)S(1)}, bf16[4,2,64,128]{3,2,1,0:T(8,128)(2,1)S(1)}, u32[]{:S(2)}, u32[]{:S(2)}) %collective-permute-start.6) | collective-permute-done | bytes 131104 | tf_op jit(solution)/shard_map/encode/ppermute | solution.py:18
  37.8 2.4 %collective-permute-start.9 = (bf16[4,2,64,128]{3,2,1,0:T(8,128)(2,1)S(1)}, bf16[4,2,64,128]{3,2,1,0:T(8,128)(2,1)S(1)}, u32[]{:S(2)}, u32[]{:S(2)}) collective-permute-start(bf16[4,2,64,128]{3,2,1,0:T(8,128)(2,1)S(1)} %get-tuple-element.59), channel_id=1, source_target_pairs={{0,2},{1,3},{2,0},{3,1},{4,6},{5,7},{6,4},{7,5},{8,10},{9,11},{10,... | collective-permute-start | bytes 393224 | tf_op jit(solution)/shard_map/encode/ppermute | solution.py:18
  40.3 0.1 collective-permute-start.8
  40.4 2.8 %collective-permute-start.12 = (bf16[4,2,64,128]{3,2,1,0:T(8,128)(2,1)S(1)}, bf16[4,2,64,128]{3,2,1,0:T(8,128)(2,1)S(1)}, u32[]{:S(2)}, u32[]{:S(2)}) collective-permute-start(bf16[4,2,64,128]{3,2,1,0:T(8,128)(2,1)S(1)} %activate.2.refs_0_), channel_id=1, source_target_pairs={{0,8},{4,12},{8,16},{12,20},{16,24},{20,28},{1,9},{5,13},{9,17},{1... | collective-permute-start | bytes 393224 | tf_op jit(solution)/shard_map/spread/ppermute | solution.py:23
  43.2 1.9 %collective-permute-done.9.arrived_ref = bf16[4,2,64,128]{3,2,1,0:T(8,128)(2,1)S(1)} collective-permute-done((bf16[4,2,64,128]{3,2,1,0:T(8,128)(2,1)S(1)}, bf16[4,2,64,128]{3,2,1,0:T(8,128)(2,1)S(1)}, u32[]{:S(2)}, u32[]{:S(2)}) %collective-permute-start.9) | collective-permute-done | bytes 131104 | tf_op jit(solution)/shard_map/encode/ppermute | solution.py:18
  45.2 0.0 collective-permute-done.8.refs_2_
  45.2 0.2 collective-permute-start.10
  45.5 3.0 %collective-permute-start.11 = (bf16[4,2,64,128]{3,2,1,0:T(8,128)(2,1)S(1)}, bf16[4,2,64,128]{3,2,1,0:T(8,128)(2,1)S(1)}, u32[]{:S(2)}, u32[]{:S(2)}) collective-permute-start(bf16[4,2,64,128]{3,2,1,0:T(8,128)(2,1)S(1)} %activate.3.refs_1_), channel_id=1, source_target_pairs={{0,8},{4,12},{8,16},{12,20},{16,24},{20,28},{1,9},{5,13},{9,17},{1... | collective-permute-start | bytes 393224 | tf_op jit(solution)/shard_map/spread/ppermute | solution.py:23
  48.4 2.1 %collective-permute-done.12.refs_4_ = bf16[4,2,64,128]{3,2,1,0:T(8,128)(2,1)S(1)} collective-permute-done((bf16[4,2,64,128]{3,2,1,0:T(8,128)(2,1)S(1)}, bf16[4,2,64,128]{3,2,1,0:T(8,128)(2,1)S(1)}, u32[]{:S(2)}, u32[]{:S(2)}) %collective-permute-start.12) | collective-permute-done | bytes 131104 | tf_op jit(solution)/shard_map/spread/ppermute | solution.py:23
  50.5 0.4 collective-permute-start.14
  50.9 0.1 collective-permute-done.10.refs_3_
  51.1 1.0 %collective-permute-done.11.refs_0_.refs_5_ = bf16[4,2,64,128]{3,2,1,0:T(8,128)(2,1)S(1)} collective-permute-done((bf16[4,2,64,128]{3,2,1,0:T(8,128)(2,1)S(1)}, bf16[4,2,64,128]{3,2,1,0:T(8,128)(2,1)S(1)}, u32[]{:S(2)}, u32[]{:S(2)}) %collective-permute-start.11) | collective-permute-done | bytes 131104 | tf_op jit(solution)/shard_map/spread/ppermute | solution.py:23
  52.1 1.9 %collective-permute-start.13 = (bf16[4,2,64,128]{3,2,1,0:T(8,128)(2,1)S(1)}, bf16[4,2,64,128]{3,2,1,0:T(8,128)(2,1)S(1)}, u32[]{:S(2)}, u32[]{:S(2)}) collective-permute-start(bf16[4,2,64,128]{3,2,1,0:T(8,128)(2,1)S(1)} %collective-permute-done.11.refs_0_.refs_5_), channel_id=1, source_target_pairs={{0,1},{1,0},{2,3},{3,2},{4,5},{5,4},{6,7},{7,6},{8,9},{9,8},{10,11... | collective-permute-start | bytes 393224 | tf_op jit(solution)/shard_map/spread/ppermute | solution.py:18
  54.0 0.0 collective-permute-done.near_dec
  54.0 0.0 collective-permute-done.1.refs_6_.refs_3_
  54.0 0.0 copy-done.1
  54.0 2.4 %decode_early.1 = (f32[256,1024]{1,0:T(8,128)S(1)}, f32[768,1024]{1,0:T(8,128)S(1)}) custom-call(s32[2,16]{1,0:T(2,128)S(1)} %bitcast.13, s32[2,16]{1,0:T(2,128)S(1)} %slice_convert_fusion.far_lists.lists_ref, bf16[4,2,64,128]{3,2,1,0:T(8,128)(2,1)S(1)} %activate.2.refs_0_, bf16[4,2,64,128]{3,2,1,0:T(8,128)(2,1)S(1)} %activate.3.refs_1_, ...), custom_call_target="tpu_custom_call" | custom-call | flops 1342177280 | bytes 6291456 | tf_op jit(solution)/shard_map/decode/decode_early/pallas_call | solution.py:223
  56.4 1.5 %collective-permute-done.13.refs_2_.refs_7_ = bf16[4,2,64,128]{3,2,1,0:T(8,128)(2,1)S(1)} collective-permute-done((bf16[4,2,64,128]{3,2,1,0:T(8,128)(2,1)S(1)}, bf16[4,2,64,128]{3,2,1,0:T(8,128)(2,1)S(1)}, u32[]{:S(2)}, u32[]{:S(2)}) %collective-permute-start.13) | collective-permute-done | bytes 131104 | tf_op jit(solution)/shard_map/spread/ppermute | solution.py:18
  57.9 0.0 collective-permute-done.14.refs_1_.refs_6_
  58.0 7.4 %collective-permute-start.15 = (bf16[16,2,64,128]{3,2,1,0:T(8,128)(2,1)S(1)}, bf16[16,2,64,128]{3,2,1,0:T(8,128)(2,1)S(1)}, u32[]{:S(2)}, u32[]{:S(2)}) collective-permute-start(bf16[16,2,64,128]{3,2,1,0:T(8,128)(2,1)S(1)} %choose.1), channel_id=1, source_target_pairs={{0,4},{4,0},{8,12},{12,8},{16,20},{20,16},{24,28},{28,24},{1,5},{5... | collective-permute-start | bytes 1572872 | tf_op jit(solution)/shard_map/decode/ppermute | solution.py:28
  65.4 1.6 %decode_middle.1.rest_ref = f32[768,1024]{1,0:T(8,128)S(1)} custom-call(s32[2,16]{1,0:T(2,128)S(1)} %slice_convert_fusion.far_lists.lists_ref, f32[768,1024]{1,0:T(8,128)S(1)} %get-tuple-element.67.rest_ref, bf16[4,2,64,128]{3,2,1,0:T(8,128)(2,1)S(1)} %collective-permute-done.11.refs_0_.refs_5_, ...), custom_call_target="tpu_custom_call" | custom-call | flops 805306368 | bytes 7340032 | tf_op jit(solution)/shard_map/decode/decode_middle/pallas_call | solution.py:256
  67.1 0.0 collective-permute-done.15.near
  67.1 3.2 %decode_late.1 = bf16[1024,1024]{1,0:T(8,128)(2,1)} custom-call(s32[2,16]{1,0:T(2,128)S(1)} %slice_convert_fusion.1.lists_ref, f32[256,1024]{1,0:T(8,128)S(1)} %get-tuple-element.66.first_ref, f32[768,1024]{1,0:T(8,128)S(1)} %decode_middle.1.rest_ref, bf16[16,2,64,128]{3,2,1,0:T(8,128)(2,1)S(1)} %collective-permute-done.15.near, ...), custom_call_target="tpu_custom_call" | custom-call | flops 1073741824 | bytes 7340032 | tf_op jit(solution)/shard_map/decode/decode_late/pallas_call | solution.py:299
  (11 shorter events, 0.2 us)
Async XLA Ops:
  0.0 1.2 %copy-start.2 = (bf16[1,4096,128]{2,1,0:T(8,128)(2,1)S(1)}, bf16[1,4096,128]{2,1,0:T(8,128)(2,1)}, u32[]{:S(2)}) copy-start(bf16[1,4096,128]{2,1,0:T(8,128)(2,1)} %param.7) | copy-start | bytes 3145732
  1.3 12.9 %collective-permute-start.2 = (bf16[1024,128]{1,0:T(8,128)(2,1)S(1)}, bf16[1024,128]{1,0:T(8,128)(2,1)S(1)}, u32[]{:S(2)}, u32[]{:S(2)}) collective-permute-start(bf16[1024,128]{1,0:T(8,128)(2,1)S(1)} %get-tuple-element.47), channel_id=1, source_target_pairs={{0,1},{1,0},{2,3},{3,2},{4,5},{5,4},{6,7},{7,6},{8,9},{9,8},{10,11... | collective-permute-start | bytes 786440 | tf_op jit(solution)/shard_map/encoder_rows/ppermute | solution.py:18
  2.7 11.6 %collective-permute-start.3 = (bf16[1024,128]{1,0:T(8,128)(2,1)S(1)}, bf16[1024,128]{1,0:T(8,128)(2,1)S(1)}, u32[]{:S(2)}, u32[]{:S(2)}) collective-permute-start(bf16[1024,128]{1,0:T(8,128)(2,1)S(1)} %get-tuple-element.48), channel_id=1, source_target_pairs={{0,2},{1,3},{2,0},{3,1},{4,6},{5,7},{6,4},{7,5},{8,10},{9,11},{10,... | collective-permute-start | bytes 786440 | tf_op jit(solution)/shard_map/encoder_rows/ppermute | solution.py:18
  5.0 16.9 %collective-permute-start.4 = (bf16[1024,128]{1,0:T(8,128)(2,1)S(1)}, bf16[1024,128]{1,0:T(8,128)(2,1)S(1)}, u32[]{:S(2)}, u32[]{:S(2)}) collective-permute-start(bf16[1024,128]{1,0:T(8,128)(2,1)S(1)} %get-tuple-element.49), channel_id=1, source_target_pairs={{0,3},{1,2},{2,1},{3,0},{4,7},{5,6},{6,5},{7,4},{8,11},{9,10},{10,... | collective-permute-start | bytes 786440 | tf_op jit(solution)/shard_map/encoder_rows/ppermute | solution.py:18
  5.0 1.9 %copy-start = (bf16[1,3,512,1024]{3,2,1,0:T(8,128)(2,1)S(1)}, bf16[1,3,512,1024]{3,2,1,0:T(8,128)(2,1)}, u32[]{:S(2)}) copy-start(bf16[1,3,512,1024]{3,2,1,0:T(8,128)(2,1)} %param.9) | copy-start | bytes 9437188
  6.9 0.7 copy-start.3
  7.5 14.3 %copy-start.4 = (bf16[1,1024,1024]{2,1,0:T(8,128)(2,1)S(1)}, bf16[1,1024,1024]{2,1,0:T(8,128)(2,1)}, u32[]{:S(2)}) copy-start(bf16[1,1024,1024]{2,1,0:T(8,128)(2,1)} %param.6) | copy-start | bytes 6291460
  7.5 14.3 %copy-start.5 = (s32[1,16]{1,0:T(1,128)S(1)}, s32[1,16]{1,0:T(1,128)}, u32[]{:S(2)}) copy-start(s32[1,16]{1,0:T(1,128)} %param.11) | copy-start | bytes 196
  7.5 14.3 %copy-start.6 = (f32[1,128]{1,0:T(1,128)S(1)}, f32[1,128]{1,0:T(1,128)}, u32[]{:S(2)}) copy-start(f32[1,128]{1,0:T(1,128)} %bias_ref.1) | copy-start | bytes 1540
  7.7 46.3 %collective-permute-start = (bf16[528,1024]{1,0:T(8,128)(2,1)S(1)}, bf16[528,1024]{1,0:T(8,128)(2,1)S(1)}, u32[]{:S(2)}, u32[]{:S(2)}) collective-permute-start(bf16[528,1024]{1,0:T(8,128)(2,1)S(1)} %get-tuple-element.42), channel_id=1, source_target_pairs={{0,4},{4,8},{8,12},{12,16},{16,20},{20,24},{24,28},{1,5},{5,9},{9,... | collective-permute-start | bytes 3244040 | tf_op jit(solution)/shard_map/decoder_weights/ppermute | solution.py:23
  12.3 41.7 %collective-permute-start.1 = (bf16[528,1024]{1,0:T(8,128)(2,1)S(1)}, bf16[528,1024]{1,0:T(8,128)(2,1)S(1)}, u32[]{:S(2)}, u32[]{:S(2)}) collective-permute-start(bf16[528,1024]{1,0:T(8,128)(2,1)S(1)} %get-tuple-element.43), channel_id=1, source_target_pairs={{0,8},{4,12},{8,16},{12,20},{16,24},{20,28},{1,9},{5,13},{9,17},{1... | collective-permute-start | bytes 3244040 | tf_op jit(solution)/shard_map/decoder_weights/ppermute | solution.py:23
  21.9 32.2 %copy-start.1 = (bf16[1,3,512,1024]{3,2,1,0:T(8,128)(2,1)S(1)}, bf16[1,3,512,1024]{3,2,1,0:T(8,128)(2,1)}, u32[]{:S(2)}) copy-start(bf16[1,3,512,1024]{3,2,1,0:T(8,128)(2,1)} %param.9) | copy-start | bytes 9437188
  23.7 8.5 %collective-permute-start.5 = (bf16[4,2,64,128]{3,2,1,0:T(8,128)(2,1)S(1)}, bf16[4,2,64,128]{3,2,1,0:T(8,128)(2,1)S(1)}, u32[]{:S(2)}, u32[]{:S(2)}) collective-permute-start(bf16[4,2,64,128]{3,2,1,0:T(8,128)(2,1)S(1)} %get-tuple-element.51), channel_id=1, source_target_pairs={{0,1},{1,0},{2,3},{3,2},{4,5},{5,4},{6,7},{7,6},{8,9},{9,8},{10,11... | collective-permute-start | bytes 393224 | tf_op jit(solution)/shard_map/encode/ppermute | solution.py:18
  29.6 5.2 %collective-permute-start.7 = (bf16[4,2,64,128]{3,2,1,0:T(8,128)(2,1)S(1)}, bf16[4,2,64,128]{3,2,1,0:T(8,128)(2,1)S(1)}, u32[]{:S(2)}, u32[]{:S(2)}) collective-permute-start(bf16[4,2,64,128]{3,2,1,0:T(8,128)(2,1)S(1)} %get-tuple-element.55), channel_id=1, source_target_pairs={{0,1},{1,0},{2,3},{3,2},{4,5},{5,4},{6,7},{7,6},{8,9},{9,8},{10,11... | collective-permute-start | bytes 393224 | tf_op jit(solution)/shard_map/encode/ppermute | solution.py:18
  32.3 5.5 %collective-permute-start.6 = (bf16[4,2,64,128]{3,2,1,0:T(8,128)(2,1)S(1)}, bf16[4,2,64,128]{3,2,1,0:T(8,128)(2,1)S(1)}, u32[]{:S(2)}, u32[]{:S(2)}) collective-permute-start(bf16[4,2,64,128]{3,2,1,0:T(8,128)(2,1)S(1)} %get-tuple-element.53), channel_id=1, source_target_pairs={{0,2},{1,3},{2,0},{3,1},{4,6},{5,7},{6,4},{7,5},{8,10},{9,11},{10,... | collective-permute-start | bytes 393224 | tf_op jit(solution)/shard_map/encode/ppermute | solution.py:18
  37.8 7.3 %collective-permute-start.9 = (bf16[4,2,64,128]{3,2,1,0:T(8,128)(2,1)S(1)}, bf16[4,2,64,128]{3,2,1,0:T(8,128)(2,1)S(1)}, u32[]{:S(2)}, u32[]{:S(2)}) collective-permute-start(bf16[4,2,64,128]{3,2,1,0:T(8,128)(2,1)S(1)} %get-tuple-element.59), channel_id=1, source_target_pairs={{0,2},{1,3},{2,0},{3,1},{4,6},{5,7},{6,4},{7,5},{8,10},{9,11},{10,... | collective-permute-start | bytes 393224 | tf_op jit(solution)/shard_map/encode/ppermute | solution.py:18
  40.3 4.9 %collective-permute-start.8 = (bf16[4,2,64,128]{3,2,1,0:T(8,128)(2,1)S(1)}, bf16[4,2,64,128]{3,2,1,0:T(8,128)(2,1)S(1)}, u32[]{:S(2)}, u32[]{:S(2)}) collective-permute-start(bf16[4,2,64,128]{3,2,1,0:T(8,128)(2,1)S(1)} %activate.2.refs_0_), channel_id=1, source_target_pairs={{0,1},{1,0},{2,3},{3,2},{4,5},{5,4},{6,7},{7,6},{8,9},{9,8},{10,11... | collective-permute-start | bytes 393224 | tf_op jit(solution)/shard_map/spread/ppermute | solution.py:18
  40.4 10.1 %collective-permute-start.12 = (bf16[4,2,64,128]{3,2,1,0:T(8,128)(2,1)S(1)}, bf16[4,2,64,128]{3,2,1,0:T(8,128)(2,1)S(1)}, u32[]{:S(2)}, u32[]{:S(2)}) collective-permute-start(bf16[4,2,64,128]{3,2,1,0:T(8,128)(2,1)S(1)} %activate.2.refs_0_), channel_id=1, source_target_pairs={{0,8},{4,12},{8,16},{12,20},{16,24},{20,28},{1,9},{5,13},{9,17},{1... | collective-permute-start | bytes 393224 | tf_op jit(solution)/shard_map/spread/ppermute | solution.py:23
  45.2 5.8 %collective-permute-start.10 = (bf16[4,2,64,128]{3,2,1,0:T(8,128)(2,1)S(1)}, bf16[4,2,64,128]{3,2,1,0:T(8,128)(2,1)S(1)}, u32[]{:S(2)}, u32[]{:S(2)}) collective-permute-start(bf16[4,2,64,128]{3,2,1,0:T(8,128)(2,1)S(1)} %activate.3.refs_1_), channel_id=1, source_target_pairs={{0,1},{1,0},{2,3},{3,2},{4,5},{5,4},{6,7},{7,6},{8,9},{9,8},{10,11... | collective-permute-start | bytes 393224 | tf_op jit(solution)/shard_map/spread/ppermute | solution.py:18
  45.5 6.6 %collective-permute-start.11 = (bf16[4,2,64,128]{3,2,1,0:T(8,128)(2,1)S(1)}, bf16[4,2,64,128]{3,2,1,0:T(8,128)(2,1)S(1)}, u32[]{:S(2)}, u32[]{:S(2)}) collective-permute-start(bf16[4,2,64,128]{3,2,1,0:T(8,128)(2,1)S(1)} %activate.3.refs_1_), channel_id=1, source_target_pairs={{0,8},{4,12},{8,16},{12,20},{16,24},{20,28},{1,9},{5,13},{9,17},{1... | collective-permute-start | bytes 393224 | tf_op jit(solution)/shard_map/spread/ppermute | solution.py:23
  50.5 7.4 %collective-permute-start.14 = (bf16[4,2,64,128]{3,2,1,0:T(8,128)(2,1)S(1)}, bf16[4,2,64,128]{3,2,1,0:T(8,128)(2,1)S(1)}, u32[]{:S(2)}, u32[]{:S(2)}) collective-permute-start(bf16[4,2,64,128]{3,2,1,0:T(8,128)(2,1)S(1)} %collective-permute-done.12.refs_4_), channel_id=1, source_target_pairs={{0,1},{1,0},{2,3},{3,2},{4,5},{5,4},{6,7},{7,6},{8,9},{9,8},{10,11... | collective-permute-start | bytes 393224 | tf_op jit(solution)/shard_map/spread/ppermute | solution.py:18
  52.1 5.9 %collective-permute-start.13 = (bf16[4,2,64,128]{3,2,1,0:T(8,128)(2,1)S(1)}, bf16[4,2,64,128]{3,2,1,0:T(8,128)(2,1)S(1)}, u32[]{:S(2)}, u32[]{:S(2)}) collective-permute-start(bf16[4,2,64,128]{3,2,1,0:T(8,128)(2,1)S(1)} %collective-permute-done.11.refs_0_.refs_5_), channel_id=1, source_target_pairs={{0,1},{1,0},{2,3},{3,2},{4,5},{5,4},{6,7},{7,6},{8,9},{9,8},{10,11... | collective-permute-start | bytes 393224 | tf_op jit(solution)/shard_map/spread/ppermute | solution.py:18
  58.0 9.1 %collective-permute-start.15 = (bf16[16,2,64,128]{3,2,1,0:T(8,128)(2,1)S(1)}, bf16[16,2,64,128]{3,2,1,0:T(8,128)(2,1)S(1)}, u32[]{:S(2)}, u32[]{:S(2)}) collective-permute-start(bf16[16,2,64,128]{3,2,1,0:T(8,128)(2,1)S(1)} %choose.1), channel_id=1, source_target_pairs={{0,4},{4,0},{8,12},{12,8},{16,20},{20,16},{24,28},{28,24},{1,5},{5... | collective-permute-start | bytes 1572872 | tf_op jit(solution)/shard_map/decode/ppermute | solution.py:28

commit v12 on v9

--- a/solution.py
+++ b/solution.py
@@ -82,43 +82,48 @@
     )(lists, decoder)
 
 
-def encode_kernel(parts, lists_ref, counts_ref, bias_ref, x_ref, *refs):
+def encode_kernel(parts, starts, lists_ref, counts_ref, bias_ref, x_ref, *refs):
     weight_refs, out_refs, partial = refs[:parts], refs[parts:-1], refs[-1]
     width = bias_ref.shape[1]
     count, slots, rows, _ = out_refs[0].shape
     tiles = lists_ref.shape[1]
+    held = [[held_tile(start + position, tiles, parts) for position in range(count)] for start in starts]
+    taken = [x_ref[pl.ds(pl.multiple_of(tile * rows, rows), rows), :] for group in held for tile in group]
+    taken = jnp.concatenate(taken, axis=0)
     for first in range(0, parts, 2):
         stacked = jnp.concatenate([ref[...] for ref in weight_refs[first : first + 2]], axis=1)
-        product = jnp.dot(x_ref[...], stacked, preferred_element_type=jnp.float32)
+        product = jnp.dot(taken, stacked, preferred_element_type=jnp.float32)
         for source in range(first, first + 2):
             block = product[:, (source - first) * width : (source - first + 1) * width]
             partial[source] = block if source else block + bias_ref[...]
-    for number, out_ref in enumerate(out_refs):
-        for position in range(count):
-            tile = held_tile(number * count + position, tiles, parts)
-            row = pl.multiple_of(tile * rows, rows)
+    row = 0
+    for start, group, out_ref in zip(starts, held, out_refs):
+        for position, tile in enumerate(group):
             for slot in range(slots):
                 source = lax.bitwise_xor(lax.axis_index("latent"), lists_ref[slot, tile])
-                kept = partial[source, pl.ds(row, rows), :]
-                if number < 2:
+                kept = partial[source, row : row + rows, :]
+                if start < tiles // 2:
                     kept = kept + jnp.where(slot < counts_ref[tile], 0.0, -1e30)
                 out_ref[position, slot] = kept.astype(out_ref.dtype)
-
-
-def encode(lists, counts, bias, x, weights):
+            row += rows
+
+
+def encode(starts, lists, counts, bias, x, weights, weight):
     parts = len(weights)
     tokens, depth = x.shape
     width = bias.shape[1]
     slots, tiles = lists.shape
     shape = (tiles // 4, slots, tokens // tiles, width)
-    return pl.pallas_call(
-        functools.partial(encode_kernel, parts),
-        out_shape=[jax.ShapeDtypeStruct(shape, jnp.float32)] * 2 + [jax.ShapeDtypeStruct(shape, jnp.bfloat16)] * 2,
+    dtypes = [jnp.float32 if start < tiles // 2 else jnp.bfloat16 for start in starts]
+    taken = tokens // 4 * len(starts)
+    return pl.pallas_call(
+        functools.partial(encode_kernel, parts, starts),
+        out_shape=[jax.ShapeDtypeStruct(shape, dtype) for dtype in dtypes],
         in_specs=[SMEM] * 2 + [VMEM] * (2 + parts),
-        out_specs=[VMEM] * 4,
-        scratch_shapes=[pltpu.VMEM((parts, tokens, width), jnp.float32)],
+        out_specs=[VMEM] * len(starts),
+        scratch_shapes=[pltpu.VMEM((parts, taken, width), jnp.float32)],
         cost_estimate=pl.CostEstimate(
-            flops=32 * tokens * depth * parts * width,
+            flops=weight * 2 * taken * depth * parts * width,
             bytes_accessed=2 * (tokens * depth + depth * parts * width),
             transcendentals=0,
         ),
@@ -359,8 +364,12 @@
         ]
 
     with jax.named_scope("encode"):
-        kept_a, kept_b, sent_a, sent_b = encode(lists, counts, enc_bias, x, weights)
-        arrived_a, arrived_b = swapped(sent_a, 1), swapped(sent_b, 1)
+        quarter = tiles // 4
+        (sent_a,) = encode([2 * quarter], lists, counts, enc_bias, x, weights, 64)
+        arrived_a = swapped(sent_a, 1)
+        starts = [3 * quarter, 0, quarter]
+        sent_b, kept_a, kept_b = encode(starts, lists, counts, enc_bias, x, weights, 1)
+        arrived_b = swapped(sent_b, 1)
         step = 2
         while step < parts:
             kept_a, sent_a = merge(kept_a, arrived_a)

time: 69.1 us -> 68.3 us (0.988)
  starting transfers between devices: 36.6 us -> 34.4 us
  Pallas kernels: 9.47 us -> 10.2 us
  waiting for transfers between devices: 18.7 us -> 19.4 us
    ppermute x5, waiting for transfers between devices: 3.1 us -> 6.06 us  [passed_along(): lax.ppermute(value, 'layer', [(i, i + steps) for i in range(count - steps)])]
    ppermute x9, waiting for transfers between devices: 15.6 us -> 13.4 us  [swapped(): return lax.ppermute(value, 'latent', [(i, i ^ step) for i in range(count)])]
    ppermute x1, starting transfers between devices: 6.26 us -> 4.04 us  [across_cores(): return lax.ppermute(value, 'layer', [(i, i ^ 1) for i in range(count)])]
    pallas_call x1 -> x2, Pallas kernels: 1.87 us -> 2.58 us  [encode(): pl.pallas_call(functools.partial(encode_kernel, parts, starts), out_shape...]
  transfers between devices with their start and end apart: 15 -> 15, of which waited for: 7 -> 7; matrix products, arithmetic and copies ran while one was open for 0% -> 0% of each run, Pallas kernels for 9% -> 10%
where the time goes in v12:
time: 68.3 us; the launch traced here: 68 us
  starting transfers between devices  34.4 us (50%)
  waiting for transfers between devices  19.4 us (28%)
  Pallas kernels  10.2 us (15%)
  local copies, waits for them, and re-layouts  3.81 us (6%)
    ppermute x5, starting transfers between devices, passed_along(): lax.ppermute(value, 'layer', [(i, i + steps) for i in range(count - steps)])  15.3 us
    ppermute x9, starting transfers between devices, swapped(): return lax.ppermute(value, 'latent', [(i, i ^ step) for i in range(count)])  15.1 us
    ppermute x9, waiting for transfers between devices, swapped(): return lax.ppermute(value, 'latent', [(i, i ^ step) for i in range(count)])  13.4 us
    ppermute x5, waiting for transfers between devices, passed_along(): lax.ppermute(value, 'layer', [(i, i + steps) for i in range(count - steps)])  6.06 us
    ppermute x1, starting transfers between devices, across_cores(): return lax.ppermute(value, 'layer', [(i, i ^ 1) for i in range(count)])  4.04 us
    unnamed x14, local copies, waits for them, and re-layouts  3.81 us
    pallas_call x1, Pallas kernels, decode_late(): pl.pallas_call(functools.partial(late_kernel, parts), out_shape=jax.Shape...  3.17 us
    pallas_call x2, Pallas kernels, encode(): pl.pallas_call(functools.partial(encode_kernel, parts, starts), out_shape...  2.58 us
  transfers between devices with their start and end apart: 15, of which 7 were waited for; matrix products, arithmetic and copies ran while one was open for 0% of the time, Pallas kernels for 10%

profile of v12, /device:TPU:5, one launch (start us, length us, event | category | flops | bytes accessed | tf_op | source)
XLA Modules:
  0.0 68.0 jit_solution(16027564701885612460)
XLA Ops:
  0.0 0.0 copy-start.3
  0.0 1.2 %copy-done.3 = bf16[1,4096,128]{2,1,0:T(8,128)(2,1)S(1)} copy-done((bf16[1,4096,128]{2,1,0:T(8,128)(2,1)S(1)}, bf16[1,4096,128]{2,1,0:T(8,128)(2,1)}, u32[]{:S(2)}) %copy-start.3) | copy-done | bytes 1048600
  1.2 0.1 fetch_rows.1
  1.3 1.4 %collective-permute-start.2 = (bf16[1024,128]{1,0:T(8,128)(2,1)S(1)}, bf16[1024,128]{1,0:T(8,128)(2,1)S(1)}, u32[]{:S(2)}, u32[]{:S(2)}) collective-permute-start(bf16[1024,128]{1,0:T(8,128)(2,1)S(1)} %get-tuple-element.44), channel_id=1, source_target_pairs={{0,1},{1,0},{2,3},{3,2},{4,5},{5,4},{6,7},{7,6},{8,9},{9,8},{10,11... | collective-permute-start | bytes 786440 | tf_op jit(solution)/shard_map/encoder_rows/ppermute | solution.py:18
  2.7 2.3 %collective-permute-start.3 = (bf16[1024,128]{1,0:T(8,128)(2,1)S(1)}, bf16[1024,128]{1,0:T(8,128)(2,1)S(1)}, u32[]{:S(2)}, u32[]{:S(2)}) collective-permute-start(bf16[1024,128]{1,0:T(8,128)(2,1)S(1)} %get-tuple-element.45), channel_id=1, source_target_pairs={{0,2},{1,3},{2,0},{3,1},{4,6},{5,7},{6,4},{7,5},{8,10},{9,11},{10,... | collective-permute-start | bytes 786440 | tf_op jit(solution)/shard_map/encoder_rows/ppermute | solution.py:18
  5.0 0.0 collective-permute-start.4
  5.0 0.0 copy-start
  5.0 1.9 %copy-done = bf16[1,3,512,1024]{3,2,1,0:T(8,128)(2,1)S(1)} copy-done((bf16[1,3,512,1024]{3,2,1,0:T(8,128)(2,1)S(1)}, bf16[1,3,512,1024]{3,2,1,0:T(8,128)(2,1)}, u32[]{:S(2)}) %copy-start) | copy-done | bytes 3145752
  6.9 0.0 copy-start.4
  6.9 0.7 copy-done.4
  7.5 0.0 copy-start.2
  7.5 0.1 fetch_decoders.1
  7.7 4.6 %collective-permute-start = (bf16[528,1024]{1,0:T(8,128)(2,1)S(1)}, bf16[528,1024]{1,0:T(8,128)(2,1)S(1)}, u32[]{:S(2)}, u32[]{:S(2)}) collective-permute-start(bf16[528,1024]{1,0:T(8,128)(2,1)S(1)} %get-tuple-element.39), channel_id=1, source_target_pairs={{0,4},{4,8},{8,12},{12,16},{16,20},{20,24},{24,28},{1,5},{5,9},{9,... | collective-permute-start | bytes 3244040 | tf_op jit(solution)/shard_map/decoder_weights/ppermute | solution.py:23
  12.3 1.9 %collective-permute-start.1 = (bf16[528,1024]{1,0:T(8,128)(2,1)S(1)}, bf16[528,1024]{1,0:T(8,128)(2,1)S(1)}, u32[]{:S(2)}, u32[]{:S(2)}) collective-permute-start(bf16[528,1024]{1,0:T(8,128)(2,1)S(1)} %get-tuple-element.40), channel_id=1, source_target_pairs={{0,8},{4,12},{8,16},{12,20},{16,24},{20,28},{1,9},{5,13},{9,17},{1... | collective-permute-start | bytes 3244040 | tf_op jit(solution)/shard_map/decoder_weights/ppermute | solution.py:23
  14.2 0.0 collective-permute-done.2.refs_1_
  14.2 0.0 collective-permute-done.3.refs_2_
  14.3 7.6 %collective-permute-done.4.refs_3_ = bf16[1024,128]{1,0:T(8,128)(2,1)S(1)} collective-permute-done((bf16[1024,128]{1,0:T(8,128)(2,1)S(1)}, bf16[1024,128]{1,0:T(8,128)(2,1)S(1)}, u32[]{:S(2)}, u32[]{:S(2)}) %collective-permute-start.4) | collective-permute-done | bytes 262176 | tf_op jit(solution)/shard_map/encoder_rows/ppermute | solution.py:18
  21.8 0.0 copy-done.2
  21.8 0.0 copy-done.5
  21.9 0.0 copy-done.6
  21.9 1.0 %encode.3 = bf16[4,2,64,128]{3,2,1,0:T(8,128)(2,1)S(1)} custom-call(s32[2,16]{1,0:T(2,128)S(1)} %bitcast.14, s32[16]{0:T(128)S(1)} %bitcast.17, f32[1,128]{1,0:T(1,128)S(1)} %copy-done.6, bf16[1024,1024]{1,0:T(8,128)(2,1)S(1)} %bitcast.10, bf16[1024,128]{1,0:T(8,128)(2,1)S(1)} %get-tuple-element.43.refs_0_, ...), custom_call_target="tpu_custom_call" | custom-call | flops 17179869184 | bytes 3145728 | tf_op jit(solution)/shard_map/encode/encode/pallas_call | solution.py:119
  22.9 5.9 %collective-permute-start.5 = (bf16[4,2,64,128]{3,2,1,0:T(8,128)(2,1)S(1)}, bf16[4,2,64,128]{3,2,1,0:T(8,128)(2,1)S(1)}, u32[]{:S(2)}, u32[]{:S(2)}) collective-permute-start(bf16[4,2,64,128]{3,2,1,0:T(8,128)(2,1)S(1)} %encode.3), channel_id=1, source_target_pairs={{0,1},{1,0},{2,3},{3,2},{4,5},{5,4},{6,7},{7,6},{8,9},{9,8},{10,11... | collective-permute-start | bytes 393224 | tf_op jit(solution)/shard_map/encode/ppermute | solution.py:18
  28.7 1.6 %encode.2 = (bf16[4,2,64,128]{3,2,1,0:T(8,128)(2,1)S(1)}, f32[4,2,64,128]{3,2,1,0:T(8,128)S(1)}, f32[4,2,64,128]{3,2,1,0:T(8,128)S(1)}) custom-call(s32[2,16]{1,0:T(2,128)S(1)} %bitcast.15, s32[16]{0:T(128)S(1)} %bitcast.18, f32[1,128]{1,0:T(1,128)S(1)} %copy-done.6, bf16[1024,1024]{1,0:T(8,128)(2,1)S(1)} %bitcast.11, ...), custom_call_target="tpu_custom_call" | custom-call | flops 805306368 | bytes 3145728 | tf_op jit(solution)/shard_map/encode/encode/pallas_call | solution.py:119
  30.3 0.1 collective-permute-start.7
  30.4 1.0 %collective-permute-done.5.arrived_ref = bf16[4,2,64,128]{3,2,1,0:T(8,128)(2,1)S(1)} collective-permute-done((bf16[4,2,64,128]{3,2,1,0:T(8,128)(2,1)S(1)}, bf16[4,2,64,128]{3,2,1,0:T(8,128)(2,1)S(1)}, u32[]{:S(2)}, u32[]{:S(2)}) %collective-permute-start.5) | collective-permute-done | bytes 131104 | tf_op jit(solution)/shard_map/encode/ppermute | solution.py:18
  31.4 2.5 %collective-permute-start.6 = (bf16[4,2,64,128]{3,2,1,0:T(8,128)(2,1)S(1)}, bf16[4,2,64,128]{3,2,1,0:T(8,128)(2,1)S(1)}, u32[]{:S(2)}, u32[]{:S(2)}) collective-permute-start(bf16[4,2,64,128]{3,2,1,0:T(8,128)(2,1)S(1)} %get-tuple-element.49), channel_id=1, source_target_pairs={{0,2},{1,3},{2,0},{3,1},{4,6},{5,7},{6,4},{7,5},{8,10},{9,11},{10,... | collective-permute-start | bytes 393224 | tf_op jit(solution)/shard_map/encode/ppermute | solution.py:18
  34.0 0.8 %collective-permute-done.7.arrived_ref = bf16[4,2,64,128]{3,2,1,0:T(8,128)(2,1)S(1)} collective-permute-done((bf16[4,2,64,128]{3,2,1,0:T(8,128)(2,1)S(1)}, bf16[4,2,64,128]{3,2,1,0:T(8,128)(2,1)S(1)}, u32[]{:S(2)}, u32[]{:S(2)}) %collective-permute-start.7) | collective-permute-done | bytes 131104 | tf_op jit(solution)/shard_map/encode/ppermute | solution.py:18
  34.8 2.1 %collective-permute-done.6.arrived_ref = bf16[4,2,64,128]{3,2,1,0:T(8,128)(2,1)S(1)} collective-permute-done((bf16[4,2,64,128]{3,2,1,0:T(8,128)(2,1)S(1)}, bf16[4,2,64,128]{3,2,1,0:T(8,128)(2,1)S(1)}, u32[]{:S(2)}, u32[]{:S(2)}) %collective-permute-start.6) | collective-permute-done | bytes 131104 | tf_op jit(solution)/shard_map/encode/ppermute | solution.py:18
  36.9 2.8 %collective-permute-start.8 = (bf16[4,2,64,128]{3,2,1,0:T(8,128)(2,1)S(1)}, bf16[4,2,64,128]{3,2,1,0:T(8,128)(2,1)S(1)}, u32[]{:S(2)}, u32[]{:S(2)}) collective-permute-start(bf16[4,2,64,128]{3,2,1,0:T(8,128)(2,1)S(1)} %get-tuple-element.55), channel_id=1, source_target_pairs={{0,2},{1,3},{2,0},{3,1},{4,6},{5,7},{6,4},{7,5},{8,10},{9,11},{10,... | collective-permute-start | bytes 393224 | tf_op jit(solution)/shard_map/encode/ppermute | solution.py:18
  39.7 0.1 collective-permute-start.9
  39.8 2.8 %collective-permute-start.11 = (bf16[4,2,64,128]{3,2,1,0:T(8,128)(2,1)S(1)}, bf16[4,2,64,128]{3,2,1,0:T(8,128)(2,1)S(1)}, u32[]{:S(2)}, u32[]{:S(2)}) collective-permute-start(bf16[4,2,64,128]{3,2,1,0:T(8,128)(2,1)S(1)} %activate.2.refs_0_), channel_id=1, source_target_pairs={{0,8},{4,12},{8,16},{12,20},{16,24},{20,28},{1,9},{5,13},{9,17},{1... | collective-permute-start | bytes 393224 | tf_op jit(solution)/shard_map/spread/ppermute | solution.py:23
  42.6 1.9 %collective-permute-done.8.arrived_ref = bf16[4,2,64,128]{3,2,1,0:T(8,128)(2,1)S(1)} collective-permute-done((bf16[4,2,64,128]{3,2,1,0:T(8,128)(2,1)S(1)}, bf16[4,2,64,128]{3,2,1,0:T(8,128)(2,1)S(1)}, u32[]{:S(2)}, u32[]{:S(2)}) %collective-permute-start.8) | collective-permute-done | bytes 131104 | tf_op jit(solution)/shard_map/encode/ppermute | solution.py:18
  44.5 0.1 collective-permute-start.10
  44.6 0.0 collective-permute-done.9.refs_2_.second_ref
  44.7 3.1 %collective-permute-start.13 = (bf16[8,2,64,128]{3,2,1,0:T(8,128)(2,1)S(1)}, bf16[8,2,64,128]{3,2,1,0:T(8,128)(2,1)S(1)}, u32[]{:S(2)}, u32[]{:S(2)}) collective-permute-start(bf16[8,2,64,128]{3,2,1,0:T(8,128)(2,1)S(1)} %join.1), channel_id=1, source_target_pairs={{0,8},{4,12},{8,16},{12,20},{16,24},{20,28},{1,9},{5,13},{9,17},{1... | collective-permute-start | bytes 786440 | tf_op jit(solution)/shard_map/spread/ppermute | solution.py:23
  47.8 3.7 %collective-permute-done.11.refs_4_ = bf16[4,2,64,128]{3,2,1,0:T(8,128)(2,1)S(1)} collective-permute-done((bf16[4,2,64,128]{3,2,1,0:T(8,128)(2,1)S(1)}, bf16[4,2,64,128]{3,2,1,0:T(8,128)(2,1)S(1)}, u32[]{:S(2)}, u32[]{:S(2)}) %collective-permute-start.11) | collective-permute-done | bytes 131104 | tf_op jit(solution)/shard_map/spread/ppermute | solution.py:23
  51.5 0.0 collective-permute-done.10.refs_3_
  51.5 2.8 %collective-permute-start.12 = (bf16[4,2,64,128]{3,2,1,0:T(8,128)(2,1)S(1)}, bf16[4,2,64,128]{3,2,1,0:T(8,128)(2,1)S(1)}, u32[]{:S(2)}, u32[]{:S(2)}) collective-permute-start(bf16[4,2,64,128]{3,2,1,0:T(8,128)(2,1)S(1)} %collective-permute-done.10.refs_3_), channel_id=1, source_target_pairs={{0,8},{4,12},{8,16},{12,20},{16,24},{20,28},{1,9},{5,13},{9,17},{1... | collective-permute-start | bytes 393224 | tf_op jit(solution)/shard_map/spread/ppermute | solution.py:23
  54.3 0.0 collective-permute-done.near_dec
  54.4 0.0 collective-permute-done.1.refs_6_.far_dec
  54.4 0.0 copy-done.1
  54.4 2.4 %decode_early.1 = (f32[256,1024]{1,0:T(8,128)S(1)}, f32[768,1024]{1,0:T(8,128)S(1)}) custom-call(s32[2,16]{1,0:T(2,128)S(1)} %bitcast.16, s32[2,16]{1,0:T(2,128)S(1)} %slice_convert_fusion.far_lists.lists_ref, bf16[4,2,64,128]{3,2,1,0:T(8,128)(2,1)S(1)} %activate.2.refs_0_, bf16[4,2,64,128]{3,2,1,0:T(8,128)(2,1)S(1)} %activate.3.refs_1_.first_ref, ...), custom_call_target="tpu_custom_call" | custom-call | flops 1342177280 | bytes 6291456 | tf_op jit(solution)/shard_map/decode/decode_early/pallas_call | solution.py:249
  56.8 2.3 %collective-permute-done.12.third.refs_6_ = bf16[4,2,64,128]{3,2,1,0:T(8,128)(2,1)S(1)} collective-permute-done((bf16[4,2,64,128]{3,2,1,0:T(8,128)(2,1)S(1)}, bf16[4,2,64,128]{3,2,1,0:T(8,128)(2,1)S(1)}, u32[]{:S(2)}, u32[]{:S(2)}) %collective-permute-start.12) | collective-permute-done | bytes 131104 | tf_op jit(solution)/shard_map/spread/ppermute | solution.py:23
  59.1 0.0 collective-permute-done.13.second.refs_5_
  59.1 4.0 %collective-permute-start.14 = (bf16[16,2,64,128]{3,2,1,0:T(8,128)(2,1)S(1)}, bf16[16,2,64,128]{3,2,1,0:T(8,128)(2,1)S(1)}, u32[]{:S(2)}, u32[]{:S(2)}) collective-permute-start(bf16[16,2,64,128]{3,2,1,0:T(8,128)(2,1)S(1)} %choose.1), channel_id=1, source_target_pairs={{0,4},{4,0},{8,12},{12,8},{16,20},{20,16},{24,28},{28,24},{1,5},{5... | collective-permute-start | bytes 1572872 | tf_op jit(solution)/shard_map/decode/ppermute | solution.py:28
  63.2 1.6 %decode_middle.1.rest_ref = f32[768,1024]{1,0:T(8,128)S(1)} custom-call(s32[2,16]{1,0:T(2,128)S(1)} %slice_convert_fusion.far_lists.lists_ref, f32[768,1024]{1,0:T(8,128)S(1)} %get-tuple-element.61.rest_ref, bf16[8,2,64,128]{3,2,1,0:T(8,128)(2,1)S(1)} %collective-permute-done.13.second.refs_5_, ...), custom_call_target="tpu_custom_call" | custom-call | flops 805306368 | bytes 7340032 | tf_op jit(solution)/shard_map/decode/decode_middle/pallas_call | solution.py:281
  64.8 0.0 collective-permute-done.14.near
  64.8 3.2 %decode_late.1 = bf16[1024,1024]{1,0:T(8,128)(2,1)} custom-call(s32[2,16]{1,0:T(2,128)S(1)} %slice_convert_fusion.1.lists_ref, f32[256,1024]{1,0:T(8,128)S(1)} %get-tuple-element.60.first_ref, f32[768,1024]{1,0:T(8,128)S(1)} %decode_middle.1.rest_ref, bf16[16,2,64,128]{3,2,1,0:T(8,128)(2,1)S(1)} %collective-permute-done.14.near, ...), custom_call_target="tpu_custom_call" | custom-call | flops 1073741824 | bytes 7340032 | tf_op jit(solution)/shard_map/decode/decode_late/pallas_call | solution.py:324
  (11 shorter events, 0.2 us)
Async XLA Ops:
  0.0 1.2 %copy-start.3 = (bf16[1,4096,128]{2,1,0:T(8,128)(2,1)S(1)}, bf16[1,4096,128]{2,1,0:T(8,128)(2,1)}, u32[]{:S(2)}) copy-start(bf16[1,4096,128]{2,1,0:T(8,128)(2,1)} %param.7) | copy-start | bytes 3145732
  1.3 12.9 %collective-permute-start.2 = (bf16[1024,128]{1,0:T(8,128)(2,1)S(1)}, bf16[1024,128]{1,0:T(8,128)(2,1)S(1)}, u32[]{:S(2)}, u32[]{:S(2)}) collective-permute-start(bf16[1024,128]{1,0:T(8,128)(2,1)S(1)} %get-tuple-element.44), channel_id=1, source_target_pairs={{0,1},{1,0},{2,3},{3,2},{4,5},{5,4},{6,7},{7,6},{8,9},{9,8},{10,11... | collective-permute-start | bytes 786440 | tf_op jit(solution)/shard_map/encoder_rows/ppermute | solution.py:18
  2.7 11.6 %collective-permute-start.3 = (bf16[1024,128]{1,0:T(8,128)(2,1)S(1)}, bf16[1024,128]{1,0:T(8,128)(2,1)S(1)}, u32[]{:S(2)}, u32[]{:S(2)}) collective-permute-start(bf16[1024,128]{1,0:T(8,128)(2,1)S(1)} %get-tuple-element.45), channel_id=1, source_target_pairs={{0,2},{1,3},{2,0},{3,1},{4,6},{5,7},{6,4},{7,5},{8,10},{9,11},{10,... | collective-permute-start | bytes 786440 | tf_op jit(solution)/shard_map/encoder_rows/ppermute | solution.py:18
  5.0 16.9 %collective-permute-start.4 = (bf16[1024,128]{1,0:T(8,128)(2,1)S(1)}, bf16[1024,128]{1,0:T(8,128)(2,1)S(1)}, u32[]{:S(2)}, u32[]{:S(2)}) collective-permute-start(bf16[1024,128]{1,0:T(8,128)(2,1)S(1)} %get-tuple-element.46), channel_id=1, source_target_pairs={{0,3},{1,2},{2,1},{3,0},{4,7},{5,6},{6,5},{7,4},{8,11},{9,10},{10,... | collective-permute-start | bytes 786440 | tf_op jit(solution)/shard_map/encoder_rows/ppermute | solution.py:18
  5.0 1.9 %copy-start = (bf16[1,3,512,1024]{3,2,1,0:T(8,128)(2,1)S(1)}, bf16[1,3,512,1024]{3,2,1,0:T(8,128)(2,1)}, u32[]{:S(2)}) copy-start(bf16[1,3,512,1024]{3,2,1,0:T(8,128)(2,1)} %param.9) | copy-start | bytes 9437188
  6.9 0.7 copy-start.4
  7.5 14.3 %copy-start.2 = (bf16[1,1024,1024]{2,1,0:T(8,128)(2,1)S(1)}, bf16[1,1024,1024]{2,1,0:T(8,128)(2,1)}, u32[]{:S(2)}) copy-start(bf16[1,1024,1024]{2,1,0:T(8,128)(2,1)} %param.6) | copy-start | bytes 6291460
  7.5 14.3 %copy-start.5 = (s32[1,16]{1,0:T(1,128)S(1)}, s32[1,16]{1,0:T(1,128)}, u32[]{:S(2)}) copy-start(s32[1,16]{1,0:T(1,128)} %param.11) | copy-start | bytes 196
  7.5 14.3 %copy-start.6 = (f32[1,128]{1,0:T(1,128)S(1)}, f32[1,128]{1,0:T(1,128)}, u32[]{:S(2)}) copy-start(f32[1,128]{1,0:T(1,128)} %bias_ref.3) | copy-start | bytes 1540
  7.7 46.7 %collective-permute-start = (bf16[528,1024]{1,0:T(8,128)(2,1)S(1)}, bf16[528,1024]{1,0:T(8,128)(2,1)S(1)}, u32[]{:S(2)}, u32[]{:S(2)}) collective-permute-start(bf16[528,1024]{1,0:T(8,128)(2,1)S(1)} %get-tuple-element.39), channel_id=1, source_target_pairs={{0,4},{4,8},{8,12},{12,16},{16,20},{20,24},{24,28},{1,5},{5,9},{9,... | collective-permute-start | bytes 3244040 | tf_op jit(solution)/shard_map/decoder_weights/ppermute | solution.py:23
  12.3 42.1 %collective-permute-start.1 = (bf16[528,1024]{1,0:T(8,128)(2,1)S(1)}, bf16[528,1024]{1,0:T(8,128)(2,1)S(1)}, u32[]{:S(2)}, u32[]{:S(2)}) collective-permute-start(bf16[528,1024]{1,0:T(8,128)(2,1)S(1)} %get-tuple-element.40), channel_id=1, source_target_pairs={{0,8},{4,12},{8,16},{12,20},{16,24},{20,28},{1,9},{5,13},{9,17},{1... | collective-permute-start | bytes 3244040 | tf_op jit(solution)/shard_map/decoder_weights/ppermute | solution.py:23
  22.9 8.5 %collective-permute-start.5 = (bf16[4,2,64,128]{3,2,1,0:T(8,128)(2,1)S(1)}, bf16[4,2,64,128]{3,2,1,0:T(8,128)(2,1)S(1)}, u32[]{:S(2)}, u32[]{:S(2)}) collective-permute-start(bf16[4,2,64,128]{3,2,1,0:T(8,128)(2,1)S(1)} %encode.3), channel_id=1, source_target_pairs={{0,1},{1,0},{2,3},{3,2},{4,5},{5,4},{6,7},{7,6},{8,9},{9,8},{10,11... | collective-permute-start | bytes 393224 | tf_op jit(solution)/shard_map/encode/ppermute | solution.py:18
  28.7 25.7 %copy-start.1 = (bf16[1,3,512,1024]{3,2,1,0:T(8,128)(2,1)S(1)}, bf16[1,3,512,1024]{3,2,1,0:T(8,128)(2,1)}, u32[]{:S(2)}) copy-start(bf16[1,3,512,1024]{3,2,1,0:T(8,128)(2,1)} %param.9) | copy-start | bytes 9437188
  30.3 4.5 %collective-permute-start.7 = (bf16[4,2,64,128]{3,2,1,0:T(8,128)(2,1)S(1)}, bf16[4,2,64,128]{3,2,1,0:T(8,128)(2,1)S(1)}, u32[]{:S(2)}, u32[]{:S(2)}) collective-permute-start(bf16[4,2,64,128]{3,2,1,0:T(8,128)(2,1)S(1)} %get-tuple-element.51), channel_id=1, source_target_pairs={{0,1},{1,0},{2,3},{3,2},{4,5},{5,4},{6,7},{7,6},{8,9},{9,8},{10,11... | collective-permute-start | bytes 393224 | tf_op jit(solution)/shard_map/encode/ppermute | solution.py:18
  31.4 5.5 %collective-permute-start.6 = (bf16[4,2,64,128]{3,2,1,0:T(8,128)(2,1)S(1)}, bf16[4,2,64,128]{3,2,1,0:T(8,128)(2,1)S(1)}, u32[]{:S(2)}, u32[]{:S(2)}) collective-permute-start(bf16[4,2,64,128]{3,2,1,0:T(8,128)(2,1)S(1)} %get-tuple-element.49), channel_id=1, source_target_pairs={{0,2},{1,3},{2,0},{3,1},{4,6},{5,7},{6,4},{7,5},{8,10},{9,11},{10,... | collective-permute-start | bytes 393224 | tf_op jit(solution)/shard_map/encode/ppermute | solution.py:18
  36.9 7.6 %collective-permute-start.8 = (bf16[4,2,64,128]{3,2,1,0:T(8,128)(2,1)S(1)}, bf16[4,2,64,128]{3,2,1,0:T(8,128)(2,1)S(1)}, u32[]{:S(2)}, u32[]{:S(2)}) collective-permute-start(bf16[4,2,64,128]{3,2,1,0:T(8,128)(2,1)S(1)} %get-tuple-element.55), channel_id=1, source_target_pairs={{0,2},{1,3},{2,0},{3,1},{4,6},{5,7},{6,4},{7,5},{8,10},{9,11},{10,... | collective-permute-start | bytes 393224 | tf_op jit(solution)/shard_map/encode/ppermute | solution.py:18
  39.7 4.9 %collective-permute-start.9 = (bf16[4,2,64,128]{3,2,1,0:T(8,128)(2,1)S(1)}, bf16[4,2,64,128]{3,2,1,0:T(8,128)(2,1)S(1)}, u32[]{:S(2)}, u32[]{:S(2)}) collective-permute-start(bf16[4,2,64,128]{3,2,1,0:T(8,128)(2,1)S(1)} %activate.2.refs_0_), channel_id=1, source_target_pairs={{0,1},{1,0},{2,3},{3,2},{4,5},{5,4},{6,7},{7,6},{8,9},{9,8},{10,11... | collective-permute-start | bytes 393224 | tf_op jit(solution)/shard_map/spread/ppermute | solution.py:18
  39.8 11.8 %collective-permute-start.11 = (bf16[4,2,64,128]{3,2,1,0:T(8,128)(2,1)S(1)}, bf16[4,2,64,128]{3,2,1,0:T(8,128)(2,1)S(1)}, u32[]{:S(2)}, u32[]{:S(2)}) collective-permute-start(bf16[4,2,64,128]{3,2,1,0:T(8,128)(2,1)S(1)} %activate.2.refs_0_), channel_id=1, source_target_pairs={{0,8},{4,12},{8,16},{12,20},{16,24},{20,28},{1,9},{5,13},{9,17},{1... | collective-permute-start | bytes 393224 | tf_op jit(solution)/shard_map/spread/ppermute | solution.py:23
  44.5 7.0 %collective-permute-start.10 = (bf16[4,2,64,128]{3,2,1,0:T(8,128)(2,1)S(1)}, bf16[4,2,64,128]{3,2,1,0:T(8,128)(2,1)S(1)}, u32[]{:S(2)}, u32[]{:S(2)}) collective-permute-start(bf16[4,2,64,128]{3,2,1,0:T(8,128)(2,1)S(1)} %activate.3.refs_1_.first_ref), channel_id=1, source_target_pairs={{0,1},{1,0},{2,3},{3,2},{4,5},{5,4},{6,7},{7,6},{8,9},{9,8},{10,11... | collective-permute-start | bytes 393224 | tf_op jit(solution)/shard_map/spread/ppermute | solution.py:18
  44.7 14.5 %collective-permute-start.13 = (bf16[8,2,64,128]{3,2,1,0:T(8,128)(2,1)S(1)}, bf16[8,2,64,128]{3,2,1,0:T(8,128)(2,1)S(1)}, u32[]{:S(2)}, u32[]{:S(2)}) collective-permute-start(bf16[8,2,64,128]{3,2,1,0:T(8,128)(2,1)S(1)} %join.1), channel_id=1, source_target_pairs={{0,8},{4,12},{8,16},{12,20},{16,24},{20,28},{1,9},{5,13},{9,17},{1... | collective-permute-start | bytes 786440 | tf_op jit(solution)/shard_map/spread/ppermute | solution.py:23
  51.5 7.6 %collective-permute-start.12 = (bf16[4,2,64,128]{3,2,1,0:T(8,128)(2,1)S(1)}, bf16[4,2,64,128]{3,2,1,0:T(8,128)(2,1)S(1)}, u32[]{:S(2)}, u32[]{:S(2)}) collective-permute-start(bf16[4,2,64,128]{3,2,1,0:T(8,128)(2,1)S(1)} %collective-permute-done.10.refs_3_), channel_id=1, source_target_pairs={{0,8},{4,12},{8,16},{12,20},{16,24},{20,28},{1,9},{5,13},{9,17},{1... | collective-permute-start | bytes 393224 | tf_op jit(solution)/shard_map/spread/ppermute | solution.py:23
  59.1 5.7 %collective-permute-start.14 = (bf16[16,2,64,128]{3,2,1,0:T(8,128)(2,1)S(1)}, bf16[16,2,64,128]{3,2,1,0:T(8,128)(2,1)S(1)}, u32[]{:S(2)}, u32[]{:S(2)}) collective-permute-start(bf16[16,2,64,128]{3,2,1,0:T(8,128)(2,1)S(1)} %choose.1), channel_id=1, source_target_pairs={{0,4},{4,0},{8,12},{12,8},{16,20},{20,16},{24,28},{28,24},{1,5},{5... | collective-permute-start | bytes 1572872 | tf_op jit(solution)/shard_map/decode/ppermute | solution.py:28

commit v13 on v12

--- a/solution.py
+++ b/solution.py
@@ -57,36 +57,46 @@
     )(encoder)
 
 
-def fetch_decoders_kernel(lists_ref, decoder_ref, *refs):
+def id_place(slot, tiles, features, width):
+    each = features // width
+    return slot // each * tiles, slice(slot % each * width, (slot % each + 1) * width)
+
+
+def fetch_decoders_kernel(parts, width, lists_ref, counts_ref, decoder_ref, *refs):
     out_refs, ids = refs[:-1], refs[-1]
-    latents = decoder_ref.shape[1]
+    _, latents, features = decoder_ref.shape
     slots, tiles = lists_ref.shape
     ids[...] = jnp.zeros_like(ids)
-    ids[:slots, :tiles] = lists_ref[...].astype(jnp.float32)
+    for slot in range(slots):
+        first, lanes = id_place(slot, tiles, features, width)
+        for position in range(tiles):
+            tile = held_tile(position, tiles, parts)
+            block = jnp.where(slot < counts_ref[tile], lists_ref[slot, tile], -1).astype(jnp.float32)
+            ids[first + position : first + position + 1, lanes] = jnp.full((1, width), block, jnp.float32)
     for number, out_ref in enumerate(out_refs):
         out_ref[:latents, :] = decoder_ref[number + 1]
         out_ref[latents:, :] = ids[...].astype(out_ref.dtype)
 
 
-def fetch_decoders(lists, decoder):
+def fetch_decoders(lists, counts, decoder, width, parts):
     targets, latents, features = decoder.shape
-    rows = lists.shape[0] + -lists.shape[0] % 16
+    slots, tiles = lists.shape
+    rows = -(-slots // (features // width)) * tiles
+    rows += -rows % 16
     shape = jax.ShapeDtypeStruct((latents + rows, features), decoder.dtype)
     return pl.pallas_call(
-        fetch_decoders_kernel,
-        out_shape=[shape] * (targets - 1),
-        in_specs=[VMEM, VMEM],
-        out_specs=[VMEM] * (targets - 1),
-        scratch_shapes=[pltpu.VMEM((rows, features), jnp.float32)],
+        functools.partial(fetch_decoders_kernel, parts, width),
+        out_shape=[shape] * (targets - 1) + [jax.ShapeDtypeStruct((rows, features), jnp.float32)],
+        in_specs=[SMEM, SMEM, VMEM],
+        out_specs=[VMEM] * targets,
         **small("fetch_decoders", 16),
-    )(lists, decoder)
-
-
-def encode_kernel(parts, starts, lists_ref, counts_ref, bias_ref, x_ref, *refs):
+    )(lists, counts, decoder)
+
+
+def encode_kernel(parts, starts, tiles, ids_ref, bias_ref, x_ref, *refs):
     weight_refs, out_refs, partial = refs[:parts], refs[parts:-1], refs[-1]
     width = bias_ref.shape[1]
     count, slots, rows, _ = out_refs[0].shape
-    tiles = lists_ref.shape[1]
     held = [[held_tile(start + position, tiles, parts) for position in range(count)] for start in starts]
     taken = [x_ref[pl.ds(pl.multiple_of(tile * rows, rows), rows), :] for group in held for tile in group]
     taken = jnp.concatenate(taken, axis=0)
@@ -96,30 +106,32 @@
         for source in range(first, first + 2):
             block = product[:, (source - first) * width : (source - first + 1) * width]
             partial[source] = block if source else block + bias_ref[...]
+    blocks = [lax.bitwise_xor(lax.axis_index("latent"), source).astype(jnp.float32) for source in range(parts)]
     row = 0
-    for start, group, out_ref in zip(starts, held, out_refs):
-        for position, tile in enumerate(group):
+    for start, out_ref in zip(starts, out_refs):
+        for position in range(count):
             for slot in range(slots):
-                source = lax.bitwise_xor(lax.axis_index("latent"), lists_ref[slot, tile])
-                kept = partial[source, row : row + rows, :]
-                if start < tiles // 2:
-                    kept = kept + jnp.where(slot < counts_ref[tile], 0.0, -1e30)
+                first, lanes = id_place(slot, tiles, ids_ref.shape[1], width)
+                first += start + position
+                wanted = ids_ref[first : first + 1, lanes]
+                kept = jnp.zeros((rows, width), jnp.float32)
+                for source in range(parts):
+                    kept = kept + jnp.where(wanted == blocks[source], 1.0, 0.0) * partial[source, row : row + rows, :]
                 out_ref[position, slot] = kept.astype(out_ref.dtype)
             row += rows
 
 
-def encode(starts, lists, counts, bias, x, weights, weight):
+def encode(starts, ids, bias, x, weights, slots, tiles, weight):
     parts = len(weights)
     tokens, depth = x.shape
     width = bias.shape[1]
-    slots, tiles = lists.shape
     shape = (tiles // 4, slots, tokens // tiles, width)
     dtypes = [jnp.float32 if start < tiles // 2 else jnp.bfloat16 for start in starts]
     taken = tokens // 4 * len(starts)
     return pl.pallas_call(
-        functools.partial(encode_kernel, parts, starts),
+        functools.partial(encode_kernel, parts, starts, tiles),
         out_shape=[jax.ShapeDtypeStruct(shape, dtype) for dtype in dtypes],
-        in_specs=[SMEM] * 2 + [VMEM] * (2 + parts),
+        in_specs=[VMEM] * (3 + parts),
         out_specs=[VMEM] * len(starts),
         scratch_shapes=[pltpu.VMEM((parts, taken, width), jnp.float32)],
         cost_estimate=pl.CostEstimate(
@@ -128,7 +140,7 @@
             transcendentals=0,
         ),
         **small("encode", 16),
-    )(lists, counts, bias, x, *weights)
+    )(ids, bias, x, *weights)
 
 
 def merge_kernel(kept_ref, arrived_ref, total_ref, sent_ref):
@@ -206,15 +218,23 @@
     )(first, second)
 
 
-def expand(dense, lists_ref, parts, first, act_refs):
+def expand(dense, ids_ref, tiles, first, act_refs):
     row = 0
     for act_ref in act_refs:
         count, slots, rows, width = act_ref.shape
         for position in range(count):
-            tile = held_tile(first + position, lists_ref.shape[1], parts)
+            wanted = []
             for slot in range(slots):
-                lanes = pl.ds(pl.multiple_of(lists_ref[slot, tile] * width, width), width)
-                dense[row : row + rows, lanes] = act_ref[position, slot]
+                start, lanes = id_place(slot, tiles, ids_ref.shape[1], width)
+                start += first + position
+                wanted.append(ids_ref[start : start + 1, lanes])
+            for block in range(dense.shape[1] // width):
+                total = None
+                for slot in range(slots):
+                    chosen = jnp.where(wanted[slot] == block, 1.0, 0.0).astype(dense.dtype)
+                    term = act_ref[position, slot] * chosen
+                    total = term if total is None else total + term
+                dense[row : row + rows, block * width : (block + 1) * width] = total
             row += rows
         first += count
 
@@ -224,16 +244,15 @@
     return [slice(first, first + columns) for first in range(0, features, columns)]
 
 
-def early_kernel(parts, lists_ref, far_lists, *refs):
+def early_kernel(tiles, ids_ref, *refs):
     own_refs, far_ref, (decoder_hbm, far_dec), refs = refs[:4], refs[4], refs[5:7], refs[7:]
-    first_ref, rest_ref, own, other, own_dec, sem = refs
+    first_ref, rest_ref, own, other, own_dec, far_ids, sem = refs
     copy = pltpu.make_async_copy(decoder_hbm.at[0], own_dec, sem)
     copy.start()
     quarter, latents = other.shape
-    own[...] = jnp.zeros_like(own)
-    other[...] = jnp.zeros_like(other)
-    expand(own, lists_ref, parts, 0, own_refs)
-    expand(other, far_lists, parts, 0, [far_ref])
+    far_ids[...] = far_dec[latents:, :].astype(far_ids.dtype)
+    expand(own, ids_ref, tiles, 0, own_refs)
+    expand(other, far_ids, tiles, 0, [far_ref])
     copy.wait()
     for lanes in column_tiles(first_ref.shape[1]):
         total = jnp.dot(own[...], own_dec[:, lanes], preferred_element_type=jnp.float32)
@@ -243,18 +262,19 @@
         )
 
 
-def decode_early(lists, far_lists, acts, decoder, far_decoder, parts):
+def decode_early(ids, acts, decoder, far_decoder, tiles):
     _, latents, features = decoder.shape
     quarter = acts[0].shape[0] * acts[0].shape[2]
     return pl.pallas_call(
-        functools.partial(early_kernel, parts),
+        functools.partial(early_kernel, tiles),
         out_shape=[jax.ShapeDtypeStruct((count * quarter, features), jnp.float32) for count in (1, 3)],
-        in_specs=[SMEM, SMEM] + [VMEM] * 5 + [ANY, VMEM],
+        in_specs=[VMEM] * 6 + [ANY, VMEM],
         out_specs=[VMEM] * 2,
         scratch_shapes=[
             pltpu.VMEM((4 * quarter, latents), jnp.bfloat16),
             pltpu.VMEM((quarter, latents), jnp.bfloat16),
             pltpu.VMEM((latents, features), jnp.bfloat16),
+            pltpu.VMEM(ids.shape, jnp.float32),
             pltpu.SemaphoreType.DMA,
         ],
         cost_estimate=pl.CostEstimate(
@@ -263,48 +283,50 @@
             transcendentals=0,
         ),
         **small("decode_early", 16),
-    )(lists, far_lists, *acts, decoder, far_decoder)
-
-
-def middle_kernel(parts, lists_ref, rest_ref, second, third, far_dec, total_ref, dense):
+    )(ids, *acts, decoder, far_decoder)
+
+
+def middle_kernel(tiles, rest_ref, second, third, far_dec, total_ref, dense, ids):
     latents = dense.shape[1]
-    dense[...] = jnp.zeros_like(dense)
-    expand(dense, lists_ref, parts, third.shape[0], [second, third])
+    ids[...] = far_dec[latents:, :].astype(ids.dtype)
+    expand(dense, ids, tiles, third.shape[0], [second, third])
     for lanes in column_tiles(rest_ref.shape[1]):
         total_ref[:, lanes] = rest_ref[:, lanes] + jnp.dot(
             dense[...], far_dec[:latents, lanes], preferred_element_type=jnp.float32
         )
 
 
-def decode_middle(lists, rest, far, decoder, latents, parts):
+def decode_middle(rest, far, decoder, latents, tiles):
     rows, features = rest.shape
     return pl.pallas_call(
-        functools.partial(middle_kernel, parts),
+        functools.partial(middle_kernel, tiles),
         out_shape=jax.ShapeDtypeStruct(rest.shape, rest.dtype),
-        in_specs=[SMEM] + [VMEM] * 4,
+        in_specs=[VMEM] * 4,
         out_specs=VMEM,
-        scratch_shapes=[pltpu.VMEM((rows, latents), jnp.bfloat16)],
+        scratch_shapes=[
+            pltpu.VMEM((rows, latents), jnp.bfloat16),
+            pltpu.VMEM((decoder.shape[0] - latents, features), jnp.float32),
+        ],
         cost_estimate=pl.CostEstimate(
             flops=2 * rows * latents * features,
             bytes_accessed=2 * (latents * features + 4 * rows * features),
             transcendentals=0,
         ),
         **small("decode_middle", 16),
-    )(lists, rest, *far, decoder)
-
-
-def late_kernel(parts, lists_ref, first_ref, rest_ref, near, near_dec, out_ref, dense, stage, sems):
+    )(rest, *far, decoder)
+
+
+def late_kernel(parts, tiles, first_ref, rest_ref, near, near_dec, out_ref, dense, stage, ids, sems):
     tokens, latents = dense.shape
     quarter, rows = tokens // 4, tokens // parts
-    dense[...] = jnp.zeros_like(dense)
-    expand(dense, lists_ref, parts, 0, [near])
+    ids[...] = near_dec[latents:, :].astype(ids.dtype)
+    expand(dense, ids, tiles, 0, [near])
     copies = []
     for number, lanes in enumerate(column_tiles(first_ref.shape[1])):
         total = jnp.dot(dense[...], near_dec[:latents, lanes], preferred_element_type=jnp.float32)
         stage[:quarter, lanes] = (total[:quarter] + first_ref[:, lanes]).astype(stage.dtype)
         stage[quarter:, lanes] = (total[quarter:] + rest_ref[:, lanes]).astype(stage.dtype)
         for held in range(parts):
-            tiles = lists_ref.shape[1]
             row = pl.multiple_of(held_tile(held * (tiles // parts), tiles, parts) * (tokens // tiles), rows)
             copies.append(
                 pltpu.make_async_copy(
@@ -318,17 +340,18 @@
         copy.wait()
 
 
-def decode_late(lists, partials, near, decoder, latents, parts):
+def decode_late(partials, near, decoder, latents, parts):
     features = decoder.shape[1]
     tokens = near.shape[0] * near.shape[2]
     return pl.pallas_call(
-        functools.partial(late_kernel, parts),
+        functools.partial(late_kernel, parts, near.shape[0]),
         out_shape=jax.ShapeDtypeStruct((tokens, features), jnp.bfloat16),
-        in_specs=[SMEM] + [VMEM] * 4,
+        in_specs=[VMEM] * 4,
         out_specs=ANY,
         scratch_shapes=[
             pltpu.VMEM((tokens, latents), jnp.bfloat16),
             pltpu.VMEM((tokens, features), jnp.bfloat16),
+            pltpu.VMEM((decoder.shape[0] - latents, features), jnp.float32),
             pltpu.SemaphoreType.DMA((len(column_tiles(features)), parts)),
         ],
         cost_estimate=pl.CostEstimate(
@@ -337,7 +360,7 @@
             transcendentals=0,
         ),
         **small("decode_late", 16),
-    )(lists, *partials, near, decoder)
+    )(*partials, near, decoder)
 
 
 def shards(layer_input, enc_weight, enc_bias, dec_weight, block_lists, block_counts):
@@ -356,19 +379,16 @@
         for step in sorted(range(1, parts), reverse=True):
             weights[step] = swapped(pieces[step], step)
     with jax.named_scope("decoder_weights"):
-        near_rows, far_rows = fetch_decoders(lists, decoder)
+        near_rows, far_rows, ids = fetch_decoders(lists, counts, decoder, encoder.shape[1], parts)
         near_decoder, far_decoder = passed_along(near_rows, 1), passed_along(far_rows, 2)
         near_decoder, far_decoder = lax.optimization_barrier((near_decoder, far_decoder))
-        near_lists, far_lists = [
-            rows[latents : latents + slots, :tiles].astype(jnp.int32) for rows in (near_decoder, far_decoder)
-        ]
 
     with jax.named_scope("encode"):
         quarter = tiles // 4
-        (sent_a,) = encode([2 * quarter], lists, counts, enc_bias, x, weights, 64)
+        (sent_a,) = encode([2 * quarter], ids, enc_bias, x, weights, slots, tiles, 64)
         arrived_a = swapped(sent_a, 1)
         starts = [3 * quarter, 0, quarter]
-        sent_b, kept_a, kept_b = encode(starts, lists, counts, enc_bias, x, weights, 1)
+        sent_b, kept_a, kept_b = encode(starts, ids, enc_bias, x, weights, slots, tiles, 1)
         arrived_b = swapped(sent_b, 1)
         step = 2
         while step < parts:
@@ -388,11 +408,11 @@
         own = [own_a, own_b, late_a, late_b]
         far = [far_a] + [passed_along(piece, 2) for piece in (joined, late_b)]
     with jax.named_scope("decode"):
-        first, rest = decode_early(lists, far_lists, own + far[:1], decoder, far_decoder, parts)
+        first, rest = decode_early(ids, own + far[:1], decoder, far_decoder, tiles)
         first, rest, far[2] = lax.optimization_barrier((first, rest, far[2]))
         near = across_cores(choose(own, far))
-        rest = decode_middle(far_lists, rest, far[1:], far_decoder, latents, parts)
-        return decode_late(near_lists, [first, rest], near, near_decoder, latents, parts)[None]
+        rest = decode_middle(rest, far[1:], far_decoder, latents, tiles)
+        return decode_late([first, rest], near, near_decoder, latents, parts)[None]
 
 
 def solution(mesh):

time: 68.3 us -> 67.8 us (level)
  waiting for transfers between devices: 19.4 us -> 22.1 us
  Pallas kernels: 10.2 us -> 7.83 us
  starting transfers between devices: 34.4 us -> 32.9 us
    ppermute x5, waiting for transfers between devices: 6.06 us -> 8.56 us  [passed_along(): lax.ppermute(value, 'layer', [(i, i + steps) for i in range(count - steps)])]
    pallas_call x6, Pallas kernels: 9.91 us -> 7.56 us  [the longest x1 2.48 us: decode_late(): pl.pallas_call(functools.partial(late_kernel, parts, near.shape[0]), out_...]
    ppermute x5, starting transfers between devices: 15.3 us -> 14.5 us  [passed_along(): lax.ppermute(value, 'layer', [(i, i + steps) for i in range(count - steps)])]
  transfers between devices with their start and end apart: 15 -> 15, of which waited for: 7 -> 8; matrix products, arithmetic and copies ran while one was open for 0% -> 0% of each run, Pallas kernels for 10% -> 8%
where the time goes in v13:
time: 67.8 us; the launch traced here: 67.5 us
  starting transfers between devices  32.9 us (49%)
  waiting for transfers between devices  22.1 us (33%)
  Pallas kernels  7.83 us (12%)
  local copies, waits for them, and re-layouts  4.46 us (7%)
    ppermute x9, starting transfers between devices, swapped(): return lax.ppermute(value, 'latent', [(i, i ^ step) for i in range(count)])  14.8 us
    ppermute x5, starting transfers between devices, passed_along(): lax.ppermute(value, 'layer', [(i, i + steps) for i in range(count - steps)])  14.5 us
    ppermute x9, waiting for transfers between devices, swapped(): return lax.ppermute(value, 'latent', [(i, i ^ step) for i in range(count)])  13 us
    ppermute x5, waiting for transfers between devices, passed_along(): lax.ppermute(value, 'layer', [(i, i + steps) for i in range(count - steps)])  8.56 us
    unnamed x14, local copies, waits for them, and re-layouts  4.46 us
    ppermute x1, starting transfers between devices, across_cores(): return lax.ppermute(value, 'layer', [(i, i ^ 1) for i in range(count)])  3.56 us
    pallas_call x1, Pallas kernels, decode_late(): pl.pallas_call(functools.partial(late_kernel, parts, near.shape[0]), out_...  2.48 us
    pallas_call x1, Pallas kernels, decode_early(): pl.pallas_call(functools.partial(early_kernel, tiles), out_shape=[jax.Sha...  1.93 us
  transfers between devices with their start and end apart: 15, of which 8 were waited for; matrix products, arithmetic and copies ran while one was open for 0% of the time, Pallas kernels for 8%

profile of v13, /device:TPU:5, one launch (start us, length us, event | category | flops | bytes accessed | tf_op | source)
XLA Modules:
  0.0 67.5 jit_solution(4168347132677310726)
XLA Ops:
  0.0 0.0 copy-start.3
  0.0 1.2 %copy-done.3 = bf16[1,4096,128]{2,1,0:T(8,128)(2,1)S(1)} copy-done((bf16[1,4096,128]{2,1,0:T(8,128)(2,1)S(1)}, bf16[1,4096,128]{2,1,0:T(8,128)(2,1)}, u32[]{:S(2)}) %copy-start.3) | copy-done | bytes 1048600
  1.2 0.0 copy-start.6
  1.2 0.1 fetch_rows.1
  1.3 1.4 %collective-permute-start = (bf16[1024,128]{1,0:T(8,128)(2,1)S(1)}, bf16[1024,128]{1,0:T(8,128)(2,1)S(1)}, u32[]{:S(2)}, u32[]{:S(2)}) collective-permute-start(bf16[1024,128]{1,0:T(8,128)(2,1)S(1)} %get-tuple-element.42), channel_id=1, source_target_pairs={{0,1},{1,0},{2,3},{3,2},{4,5},{5,4},{6,7},{7,6},{8,9},{9,8},{10,11... | collective-permute-start | bytes 786440 | tf_op jit(solution)/shard_map/encoder_rows/ppermute | solution.py:18
  2.7 2.3 %collective-permute-start.1 = (bf16[1024,128]{1,0:T(8,128)(2,1)S(1)}, bf16[1024,128]{1,0:T(8,128)(2,1)S(1)}, u32[]{:S(2)}, u32[]{:S(2)}) collective-permute-start(bf16[1024,128]{1,0:T(8,128)(2,1)S(1)} %get-tuple-element.43), channel_id=1, source_target_pairs={{0,2},{1,3},{2,0},{3,1},{4,6},{5,7},{6,4},{7,5},{8,10},{9,11},{10,... | collective-permute-start | bytes 786440 | tf_op jit(solution)/shard_map/encoder_rows/ppermute | solution.py:18
  5.0 0.0 collective-permute-start.2
  5.0 0.0 copy-start
  5.0 1.9 %copy-done = bf16[1,3,512,1024]{3,2,1,0:T(8,128)(2,1)S(1)} copy-done((bf16[1,3,512,1024]{3,2,1,0:T(8,128)(2,1)S(1)}, bf16[1,3,512,1024]{3,2,1,0:T(8,128)(2,1)}, u32[]{:S(2)}) %copy-start) | copy-done | bytes 3145752
  6.9 0.7 %copy-done.4 = s32[1,16,2]{1,2,0:T(2,128)S(1)} copy-done((s32[1,16,2]{1,2,0:T(2,128)S(1)}, s32[1,16,2]{1,2,0:T(2,128)}, u32[]{:S(2)}) %copy-start.4) | copy-done | bytes 152
  7.5 0.7 copy-done.5
  8.2 0.7 %fetch_decoders.1 = (bf16[528,1024]{1,0:T(8,128)(2,1)S(1)}, bf16[528,1024]{1,0:T(8,128)(2,1)S(1)}, f32[16,1024]{1,0:T(8,128)S(1)}) custom-call(s32[2,16]{1,0:T(2,128)S(1)} %bitcast.13, s32[16]{0:T(128)S(1)} %bitcast.14, bf16[3,512,1024]{2,1,0:T(8,128)(2,1)S(1)} %bitcast.8), custom_call_target="tpu_custom_call" | custom-call | tf_op jit(solution)/shard_map/decoder_weights/fetch_decoders/pallas_call | solution.py:87
  8.9 4.5 %collective-permute-start.10 = (bf16[528,1024]{1,0:T(8,128)(2,1)S(1)}, bf16[528,1024]{1,0:T(8,128)(2,1)S(1)}, u32[]{:S(2)}, u32[]{:S(2)}) collective-permute-start(bf16[528,1024]{1,0:T(8,128)(2,1)S(1)} %get-tuple-element.56), channel_id=1, source_target_pairs={{0,4},{4,8},{8,12},{12,16},{16,20},{20,24},{24,28},{1,5},{5,9},{9,... | collective-permute-start | bytes 3244040 | tf_op jit(solution)/shard_map/decoder_weights/ppermute | solution.py:23
  13.4 1.9 %collective-permute-start.11 = (bf16[528,1024]{1,0:T(8,128)(2,1)S(1)}, bf16[528,1024]{1,0:T(8,128)(2,1)S(1)}, u32[]{:S(2)}, u32[]{:S(2)}) collective-permute-start(bf16[528,1024]{1,0:T(8,128)(2,1)S(1)} %get-tuple-element.57), channel_id=1, source_target_pairs={{0,8},{4,12},{8,16},{12,20},{16,24},{20,28},{1,9},{5,13},{9,17},{1... | collective-permute-start | bytes 3244040 | tf_op jit(solution)/shard_map/decoder_weights/ppermute | solution.py:23
  15.3 0.0 collective-permute-done.refs_1_
  15.3 0.0 collective-permute-done.1.refs_2_
  15.3 6.5 %collective-permute-done.2.refs_3_ = bf16[1024,128]{1,0:T(8,128)(2,1)S(1)} collective-permute-done((bf16[1024,128]{1,0:T(8,128)(2,1)S(1)}, bf16[1024,128]{1,0:T(8,128)(2,1)S(1)}, u32[]{:S(2)}, u32[]{:S(2)}) %collective-permute-start.2) | collective-permute-done | bytes 262176 | tf_op jit(solution)/shard_map/encoder_rows/ppermute | solution.py:18
  21.8 0.0 copy-done.6
  21.9 0.0 copy-done.2
  21.9 0.4 encode.3
  22.3 0.0 copy-start.1
  22.3 5.9 %collective-permute-start.3 = (bf16[4,2,64,128]{3,2,1,0:T(8,128)(2,1)S(1)}, bf16[4,2,64,128]{3,2,1,0:T(8,128)(2,1)S(1)}, u32[]{:S(2)}, u32[]{:S(2)}) collective-permute-start(bf16[4,2,64,128]{3,2,1,0:T(8,128)(2,1)S(1)} %encode.3), channel_id=1, source_target_pairs={{0,1},{1,0},{2,3},{3,2},{4,5},{5,4},{6,7},{7,6},{8,9},{9,8},{10,11... | collective-permute-start | bytes 393224 | tf_op jit(solution)/shard_map/encode/ppermute | solution.py:18
  28.2 1.0 %encode.2 = (bf16[4,2,64,128]{3,2,1,0:T(8,128)(2,1)S(1)}, f32[4,2,64,128]{3,2,1,0:T(8,128)S(1)}, f32[4,2,64,128]{3,2,1,0:T(8,128)S(1)}) custom-call(f32[16,1024]{1,0:T(8,128)S(1)} %get-tuple-element.40.ids_ref, f32[1,128]{1,0:T(1,128)S(1)} %copy-done.6, bf16[1024,1024]{1,0:T(8,128)(2,1)S(1)} %bitcast.11, bf16[1024,128]{1,0:T(8,128)(2,1)S(1)} %get-tuple-element.41.refs_0_, ...), custom_call_target="tpu_custom_call" | custom-call | flops 805306368 | bytes 3145728 | tf_op jit(solution)/shard_map/encode/encode/pallas_call | solution.py:131
  29.2 0.1 collective-permute-start.5
  29.3 1.6 %collective-permute-done.3.arrived_ref = bf16[4,2,64,128]{3,2,1,0:T(8,128)(2,1)S(1)} collective-permute-done((bf16[4,2,64,128]{3,2,1,0:T(8,128)(2,1)S(1)}, bf16[4,2,64,128]{3,2,1,0:T(8,128)(2,1)S(1)}, u32[]{:S(2)}, u32[]{:S(2)}) %collective-permute-start.3) | collective-permute-done | bytes 131104 | tf_op jit(solution)/shard_map/encode/ppermute | solution.py:18
  30.9 2.5 %collective-permute-start.4 = (bf16[4,2,64,128]{3,2,1,0:T(8,128)(2,1)S(1)}, bf16[4,2,64,128]{3,2,1,0:T(8,128)(2,1)S(1)}, u32[]{:S(2)}, u32[]{:S(2)}) collective-permute-start(bf16[4,2,64,128]{3,2,1,0:T(8,128)(2,1)S(1)} %get-tuple-element.47), channel_id=1, source_target_pairs={{0,2},{1,3},{2,0},{3,1},{4,6},{5,7},{6,4},{7,5},{8,10},{9,11},{10,... | collective-permute-start | bytes 393224 | tf_op jit(solution)/shard_map/encode/ppermute | solution.py:18
  33.4 0.8 %collective-permute-done.5.arrived_ref = bf16[4,2,64,128]{3,2,1,0:T(8,128)(2,1)S(1)} collective-permute-done((bf16[4,2,64,128]{3,2,1,0:T(8,128)(2,1)S(1)}, bf16[4,2,64,128]{3,2,1,0:T(8,128)(2,1)S(1)}, u32[]{:S(2)}, u32[]{:S(2)}) %collective-permute-start.5) | collective-permute-done | bytes 131104 | tf_op jit(solution)/shard_map/encode/ppermute | solution.py:18
  34.3 2.1 %collective-permute-done.4.arrived_ref = bf16[4,2,64,128]{3,2,1,0:T(8,128)(2,1)S(1)} collective-permute-done((bf16[4,2,64,128]{3,2,1,0:T(8,128)(2,1)S(1)}, bf16[4,2,64,128]{3,2,1,0:T(8,128)(2,1)S(1)}, u32[]{:S(2)}, u32[]{:S(2)}) %collective-permute-start.4) | collective-permute-done | bytes 131104 | tf_op jit(solution)/shard_map/encode/ppermute | solution.py:18
  36.4 2.4 %collective-permute-start.6 = (bf16[4,2,64,128]{3,2,1,0:T(8,128)(2,1)S(1)}, bf16[4,2,64,128]{3,2,1,0:T(8,128)(2,1)S(1)}, u32[]{:S(2)}, u32[]{:S(2)}) collective-permute-start(bf16[4,2,64,128]{3,2,1,0:T(8,128)(2,1)S(1)} %get-tuple-element.53), channel_id=1, source_target_pairs={{0,2},{1,3},{2,0},{3,1},{4,6},{5,7},{6,4},{7,5},{8,10},{9,11},{10,... | collective-permute-start | bytes 393224 | tf_op jit(solution)/shard_map/encode/ppermute | solution.py:18
  38.8 0.1 collective-permute-start.7
  39.0 2.8 %collective-permute-start.9 = (bf16[4,2,64,128]{3,2,1,0:T(8,128)(2,1)S(1)}, bf16[4,2,64,128]{3,2,1,0:T(8,128)(2,1)S(1)}, u32[]{:S(2)}, u32[]{:S(2)}) collective-permute-start(bf16[4,2,64,128]{3,2,1,0:T(8,128)(2,1)S(1)} %activate.2.refs_0_), channel_id=1, source_target_pairs={{0,8},{4,12},{8,16},{12,20},{16,24},{20,28},{1,9},{5,13},{9,17},{1... | collective-permute-start | bytes 393224 | tf_op jit(solution)/shard_map/spread/ppermute | solution.py:23
  41.8 2.0 %collective-permute-done.6.arrived_ref = bf16[4,2,64,128]{3,2,1,0:T(8,128)(2,1)S(1)} collective-permute-done((bf16[4,2,64,128]{3,2,1,0:T(8,128)(2,1)S(1)}, bf16[4,2,64,128]{3,2,1,0:T(8,128)(2,1)S(1)}, u32[]{:S(2)}, u32[]{:S(2)}) %collective-permute-start.6) | collective-permute-done | bytes 131104 | tf_op jit(solution)/shard_map/encode/ppermute | solution.py:18
  43.8 0.1 collective-permute-start.8
  43.9 0.0 collective-permute-done.7.refs_2_.second_ref
  44.0 3.1 %collective-permute-start.13 = (bf16[8,2,64,128]{3,2,1,0:T(8,128)(2,1)S(1)}, bf16[8,2,64,128]{3,2,1,0:T(8,128)(2,1)S(1)}, u32[]{:S(2)}, u32[]{:S(2)}) collective-permute-start(bf16[8,2,64,128]{3,2,1,0:T(8,128)(2,1)S(1)} %join.1), channel_id=1, source_target_pairs={{0,8},{4,12},{8,16},{12,20},{16,24},{20,28},{1,9},{5,13},{9,17},{1... | collective-permute-start | bytes 786440 | tf_op jit(solution)/shard_map/spread/ppermute | solution.py:23
  47.1 4.5 %collective-permute-done.9.refs_4_ = bf16[4,2,64,128]{3,2,1,0:T(8,128)(2,1)S(1)} collective-permute-done((bf16[4,2,64,128]{3,2,1,0:T(8,128)(2,1)S(1)}, bf16[4,2,64,128]{3,2,1,0:T(8,128)(2,1)S(1)}, u32[]{:S(2)}, u32[]{:S(2)}) %collective-permute-start.9) | collective-permute-done | bytes 131104 | tf_op jit(solution)/shard_map/spread/ppermute | solution.py:23
  51.6 0.0 collective-permute-done.8.refs_3_
  51.6 2.2 %collective-permute-start.12 = (bf16[4,2,64,128]{3,2,1,0:T(8,128)(2,1)S(1)}, bf16[4,2,64,128]{3,2,1,0:T(8,128)(2,1)S(1)}, u32[]{:S(2)}, u32[]{:S(2)}) collective-permute-start(bf16[4,2,64,128]{3,2,1,0:T(8,128)(2,1)S(1)} %collective-permute-done.8.refs_3_), channel_id=1, source_target_pairs={{0,8},{4,12},{8,16},{12,20},{16,24},{20,28},{1,9},{5,13},{9,17},{1... | collective-permute-start | bytes 393224 | tf_op jit(solution)/shard_map/spread/ppermute | solution.py:23
  53.9 0.0 collective-permute-done.10.near_dec
  53.9 0.0 collective-permute-done.11.refs_6_.far_dec
  53.9 0.0 copy-done.1
  53.9 1.9 %decode_early.1 = (f32[256,1024]{1,0:T(8,128)S(1)}, f32[768,1024]{1,0:T(8,128)S(1)}) custom-call(f32[16,1024]{1,0:T(8,128)S(1)} %get-tuple-element.40.ids_ref, bf16[4,2,64,128]{3,2,1,0:T(8,128)(2,1)S(1)} %activate.2.refs_0_, bf16[4,2,64,128]{3,2,1,0:T(8,128)(2,1)S(1)} %activate.3.refs_1_.first_ref, ...), custom_call_target="tpu_custom_call" | custom-call | flops 1342177280 | bytes 6291456 | tf_op jit(solution)/shard_map/decode/decode_early/pallas_call | solution.py:268
  55.8 4.0 %collective-permute-done.12.third.refs_6_ = bf16[4,2,64,128]{3,2,1,0:T(8,128)(2,1)S(1)} collective-permute-done((bf16[4,2,64,128]{3,2,1,0:T(8,128)(2,1)S(1)}, bf16[4,2,64,128]{3,2,1,0:T(8,128)(2,1)S(1)}, u32[]{:S(2)}, u32[]{:S(2)}) %collective-permute-start.12) | collective-permute-done | bytes 131104 | tf_op jit(solution)/shard_map/spread/ppermute | solution.py:23
  59.8 0.0 collective-permute-done.13.second.refs_5_
  59.9 3.6 %collective-permute-start.14 = (bf16[16,2,64,128]{3,2,1,0:T(8,128)(2,1)S(1)}, bf16[16,2,64,128]{3,2,1,0:T(8,128)(2,1)S(1)}, u32[]{:S(2)}, u32[]{:S(2)}) collective-permute-start(bf16[16,2,64,128]{3,2,1,0:T(8,128)(2,1)S(1)} %choose.1), channel_id=1, source_target_pairs={{0,4},{4,0},{8,12},{12,8},{16,20},{20,16},{24,28},{28,24},{1,5},{5... | collective-permute-start | bytes 1572872 | tf_op jit(solution)/shard_map/decode/ppermute | solution.py:28
  63.4 1.0 %decode_middle.1.rest_ref = f32[768,1024]{1,0:T(8,128)S(1)} custom-call(f32[768,1024]{1,0:T(8,128)S(1)} %get-tuple-element.62.rest_ref, bf16[8,2,64,128]{3,2,1,0:T(8,128)(2,1)S(1)} %collective-permute-done.13.second.refs_5_, bf16[4,2,64,128]{3,2,1,0:T(8,128)(2,1)S(1)} %collective-permute-done.12.third.refs_6_, ...), custom_call_target="tpu_custom_call" | custom-call | flops 805306368 | bytes 7340032 | tf_op jit(solution)/shard_map/decode/decode_middle/pallas_call | solution.py:301
  64.5 0.5 collective-permute-done.14.near
  65.0 2.5 %decode_late.1 = bf16[1024,1024]{1,0:T(8,128)(2,1)} custom-call(f32[256,1024]{1,0:T(8,128)S(1)} %get-tuple-element.61.first_ref, f32[768,1024]{1,0:T(8,128)S(1)} %decode_middle.1.rest_ref, bf16[16,2,64,128]{3,2,1,0:T(8,128)(2,1)S(1)} %collective-permute-done.14.near, bf16[528,1024]{1,0:T(8,128)(2,1)S(1)} %collective-permute-done.10.near_dec), custom_call_target="tpu_custom_call" | custom-call | flops 1073741824 | bytes 7340032 | tf_op jit(solution)/shard_map/decode/decode_late/pallas_call | solution.py:346
  (9 shorter events, 0.2 us)
Async XLA Ops:
  0.0 1.2 %copy-start.3 = (bf16[1,4096,128]{2,1,0:T(8,128)(2,1)S(1)}, bf16[1,4096,128]{2,1,0:T(8,128)(2,1)}, u32[]{:S(2)}) copy-start(bf16[1,4096,128]{2,1,0:T(8,128)(2,1)} %param.7) | copy-start | bytes 3145732
  1.2 20.6 %copy-start.6 = (f32[1,128]{1,0:T(1,128)S(1)}, f32[1,128]{1,0:T(1,128)}, u32[]{:S(2)}) copy-start(f32[1,128]{1,0:T(1,128)} %bias_ref.3) | copy-start | bytes 1540
  1.3 14.0 %collective-permute-start = (bf16[1024,128]{1,0:T(8,128)(2,1)S(1)}, bf16[1024,128]{1,0:T(8,128)(2,1)S(1)}, u32[]{:S(2)}, u32[]{:S(2)}) collective-permute-start(bf16[1024,128]{1,0:T(8,128)(2,1)S(1)} %get-tuple-element.42), channel_id=1, source_target_pairs={{0,1},{1,0},{2,3},{3,2},{4,5},{5,4},{6,7},{7,6},{8,9},{9,8},{10,11... | collective-permute-start | bytes 786440 | tf_op jit(solution)/shard_map/encoder_rows/ppermute | solution.py:18
  2.7 12.7 %collective-permute-start.1 = (bf16[1024,128]{1,0:T(8,128)(2,1)S(1)}, bf16[1024,128]{1,0:T(8,128)(2,1)S(1)}, u32[]{:S(2)}, u32[]{:S(2)}) collective-permute-start(bf16[1024,128]{1,0:T(8,128)(2,1)S(1)} %get-tuple-element.43), channel_id=1, source_target_pairs={{0,2},{1,3},{2,0},{3,1},{4,6},{5,7},{6,4},{7,5},{8,10},{9,11},{10,... | collective-permute-start | bytes 786440 | tf_op jit(solution)/shard_map/encoder_rows/ppermute | solution.py:18
  5.0 16.9 %collective-permute-start.2 = (bf16[1024,128]{1,0:T(8,128)(2,1)S(1)}, bf16[1024,128]{1,0:T(8,128)(2,1)S(1)}, u32[]{:S(2)}, u32[]{:S(2)}) collective-permute-start(bf16[1024,128]{1,0:T(8,128)(2,1)S(1)} %get-tuple-element.44), channel_id=1, source_target_pairs={{0,3},{1,2},{2,1},{3,0},{4,7},{5,6},{6,5},{7,4},{8,11},{9,10},{10,... | collective-permute-start | bytes 786440 | tf_op jit(solution)/shard_map/encoder_rows/ppermute | solution.py:18
  5.0 1.9 %copy-start = (bf16[1,3,512,1024]{3,2,1,0:T(8,128)(2,1)S(1)}, bf16[1,3,512,1024]{3,2,1,0:T(8,128)(2,1)}, u32[]{:S(2)}) copy-start(bf16[1,3,512,1024]{3,2,1,0:T(8,128)(2,1)} %param.9) | copy-start | bytes 9437188
  6.9 0.7 %copy-start.4 = (s32[1,16,2]{1,2,0:T(2,128)S(1)}, s32[1,16,2]{1,2,0:T(2,128)}, u32[]{:S(2)}) copy-start(s32[1,16,2]{1,2,0:T(2,128)} %param.10) | copy-start | bytes 388
  7.5 0.7 copy-start.5
  8.2 13.7 %copy-start.2 = (bf16[1,1024,1024]{2,1,0:T(8,128)(2,1)S(1)}, bf16[1,1024,1024]{2,1,0:T(8,128)(2,1)}, u32[]{:S(2)}) copy-start(bf16[1,1024,1024]{2,1,0:T(8,128)(2,1)} %param.6) | copy-start | bytes 6291460
  8.9 44.9 %collective-permute-start.10 = (bf16[528,1024]{1,0:T(8,128)(2,1)S(1)}, bf16[528,1024]{1,0:T(8,128)(2,1)S(1)}, u32[]{:S(2)}, u32[]{:S(2)}) collective-permute-start(bf16[528,1024]{1,0:T(8,128)(2,1)S(1)} %get-tuple-element.56), channel_id=1, source_target_pairs={{0,4},{4,8},{8,12},{12,16},{16,20},{20,24},{24,28},{1,5},{5,9},{9,... | collective-permute-start | bytes 3244040 | tf_op jit(solution)/shard_map/decoder_weights/ppermute | solution.py:23
  13.4 40.5 %collective-permute-start.11 = (bf16[528,1024]{1,0:T(8,128)(2,1)S(1)}, bf16[528,1024]{1,0:T(8,128)(2,1)S(1)}, u32[]{:S(2)}, u32[]{:S(2)}) collective-permute-start(bf16[528,1024]{1,0:T(8,128)(2,1)S(1)} %get-tuple-element.57), channel_id=1, source_target_pairs={{0,8},{4,12},{8,16},{12,20},{16,24},{20,28},{1,9},{5,13},{9,17},{1... | collective-permute-start | bytes 3244040 | tf_op jit(solution)/shard_map/decoder_weights/ppermute | solution.py:23
  22.3 31.6 %copy-start.1 = (bf16[1,3,512,1024]{3,2,1,0:T(8,128)(2,1)S(1)}, bf16[1,3,512,1024]{3,2,1,0:T(8,128)(2,1)}, u32[]{:S(2)}) copy-start(bf16[1,3,512,1024]{3,2,1,0:T(8,128)(2,1)} %param.9) | copy-start | bytes 9437188
  22.3 8.5 %collective-permute-start.3 = (bf16[4,2,64,128]{3,2,1,0:T(8,128)(2,1)S(1)}, bf16[4,2,64,128]{3,2,1,0:T(8,128)(2,1)S(1)}, u32[]{:S(2)}, u32[]{:S(2)}) collective-permute-start(bf16[4,2,64,128]{3,2,1,0:T(8,128)(2,1)S(1)} %encode.3), channel_id=1, source_target_pairs={{0,1},{1,0},{2,3},{3,2},{4,5},{5,4},{6,7},{7,6},{8,9},{9,8},{10,11... | collective-permute-start | bytes 393224 | tf_op jit(solution)/shard_map/encode/ppermute | solution.py:18
  29.2 5.1 %collective-permute-start.5 = (bf16[4,2,64,128]{3,2,1,0:T(8,128)(2,1)S(1)}, bf16[4,2,64,128]{3,2,1,0:T(8,128)(2,1)S(1)}, u32[]{:S(2)}, u32[]{:S(2)}) collective-permute-start(bf16[4,2,64,128]{3,2,1,0:T(8,128)(2,1)S(1)} %get-tuple-element.49), channel_id=1, source_target_pairs={{0,1},{1,0},{2,3},{3,2},{4,5},{5,4},{6,7},{7,6},{8,9},{9,8},{10,11... | collective-permute-start | bytes 393224 | tf_op jit(solution)/shard_map/encode/ppermute | solution.py:18
  30.9 5.5 %collective-permute-start.4 = (bf16[4,2,64,128]{3,2,1,0:T(8,128)(2,1)S(1)}, bf16[4,2,64,128]{3,2,1,0:T(8,128)(2,1)S(1)}, u32[]{:S(2)}, u32[]{:S(2)}) collective-permute-start(bf16[4,2,64,128]{3,2,1,0:T(8,128)(2,1)S(1)} %get-tuple-element.47), channel_id=1, source_target_pairs={{0,2},{1,3},{2,0},{3,1},{4,6},{5,7},{6,4},{7,5},{8,10},{9,11},{10,... | collective-permute-start | bytes 393224 | tf_op jit(solution)/shard_map/encode/ppermute | solution.py:18
  36.4 7.4 %collective-permute-start.6 = (bf16[4,2,64,128]{3,2,1,0:T(8,128)(2,1)S(1)}, bf16[4,2,64,128]{3,2,1,0:T(8,128)(2,1)S(1)}, u32[]{:S(2)}, u32[]{:S(2)}) collective-permute-start(bf16[4,2,64,128]{3,2,1,0:T(8,128)(2,1)S(1)} %get-tuple-element.53), channel_id=1, source_target_pairs={{0,2},{1,3},{2,0},{3,1},{4,6},{5,7},{6,4},{7,5},{8,10},{9,11},{10,... | collective-permute-start | bytes 393224 | tf_op jit(solution)/shard_map/encode/ppermute | solution.py:18
  38.8 5.1 %collective-permute-start.7 = (bf16[4,2,64,128]{3,2,1,0:T(8,128)(2,1)S(1)}, bf16[4,2,64,128]{3,2,1,0:T(8,128)(2,1)S(1)}, u32[]{:S(2)}, u32[]{:S(2)}) collective-permute-start(bf16[4,2,64,128]{3,2,1,0:T(8,128)(2,1)S(1)} %activate.2.refs_0_), channel_id=1, source_target_pairs={{0,1},{1,0},{2,3},{3,2},{4,5},{5,4},{6,7},{7,6},{8,9},{9,8},{10,11... | collective-permute-start | bytes 393224 | tf_op jit(solution)/shard_map/spread/ppermute | solution.py:18
  39.0 12.6 %collective-permute-start.9 = (bf16[4,2,64,128]{3,2,1,0:T(8,128)(2,1)S(1)}, bf16[4,2,64,128]{3,2,1,0:T(8,128)(2,1)S(1)}, u32[]{:S(2)}, u32[]{:S(2)}) collective-permute-start(bf16[4,2,64,128]{3,2,1,0:T(8,128)(2,1)S(1)} %activate.2.refs_0_), channel_id=1, source_target_pairs={{0,8},{4,12},{8,16},{12,20},{16,24},{20,28},{1,9},{5,13},{9,17},{1... | collective-permute-start | bytes 393224 | tf_op jit(solution)/shard_map/spread/ppermute | solution.py:23
  43.8 7.8 %collective-permute-start.8 = (bf16[4,2,64,128]{3,2,1,0:T(8,128)(2,1)S(1)}, bf16[4,2,64,128]{3,2,1,0:T(8,128)(2,1)S(1)}, u32[]{:S(2)}, u32[]{:S(2)}) collective-permute-start(bf16[4,2,64,128]{3,2,1,0:T(8,128)(2,1)S(1)} %activate.3.refs_1_.first_ref), channel_id=1, source_target_pairs={{0,1},{1,0},{2,3},{3,2},{4,5},{5,4},{6,7},{7,6},{8,9},{9,8},{10,11... | collective-permute-start | bytes 393224 | tf_op jit(solution)/shard_map/spread/ppermute | solution.py:18
  44.0 15.9 %collective-permute-start.13 = (bf16[8,2,64,128]{3,2,1,0:T(8,128)(2,1)S(1)}, bf16[8,2,64,128]{3,2,1,0:T(8,128)(2,1)S(1)}, u32[]{:S(2)}, u32[]{:S(2)}) collective-permute-start(bf16[8,2,64,128]{3,2,1,0:T(8,128)(2,1)S(1)} %join.1), channel_id=1, source_target_pairs={{0,8},{4,12},{8,16},{12,20},{16,24},{20,28},{1,9},{5,13},{9,17},{1... | collective-permute-start | bytes 786440 | tf_op jit(solution)/shard_map/spread/ppermute | solution.py:23
  51.6 8.2 %collective-permute-start.12 = (bf16[4,2,64,128]{3,2,1,0:T(8,128)(2,1)S(1)}, bf16[4,2,64,128]{3,2,1,0:T(8,128)(2,1)S(1)}, u32[]{:S(2)}, u32[]{:S(2)}) collective-permute-start(bf16[4,2,64,128]{3,2,1,0:T(8,128)(2,1)S(1)} %collective-permute-done.8.refs_3_), channel_id=1, source_target_pairs={{0,8},{4,12},{8,16},{12,20},{16,24},{20,28},{1,9},{5,13},{9,17},{1... | collective-permute-start | bytes 393224 | tf_op jit(solution)/shard_map/spread/ppermute | solution.py:23
  59.9 5.1 %collective-permute-start.14 = (bf16[16,2,64,128]{3,2,1,0:T(8,128)(2,1)S(1)}, bf16[16,2,64,128]{3,2,1,0:T(8,128)(2,1)S(1)}, u32[]{:S(2)}, u32[]{:S(2)}) collective-permute-start(bf16[16,2,64,128]{3,2,1,0:T(8,128)(2,1)S(1)} %choose.1), channel_id=1, source_target_pairs={{0,4},{4,0},{8,12},{12,8},{16,20},{20,16},{24,28},{28,24},{1,5},{5... | collective-permute-start | bytes 1572872 | tf_op jit(solution)/shard_map/decode/ppermute | solution.py:28

commit v14 on v13

--- a/solution.py
+++ b/solution.py
@@ -16,6 +16,12 @@
 def swapped(value, step):
     count = lax.axis_size("latent")
     return lax.ppermute(value, "latent", [(i, i ^ step) for i in range(count)])
+
+
+def interleaved(parts):
+    across = list(range(parts // 2, parts))
+    within = list(range(1, parts // 2))
+    return [step for pair in zip(across, within + [None]) for step in pair if step]
 
 
 def passed_along(value, steps):
@@ -100,12 +106,13 @@
     held = [[held_tile(start + position, tiles, parts) for position in range(count)] for start in starts]
     taken = [x_ref[pl.ds(pl.multiple_of(tile * rows, rows), rows), :] for group in held for tile in group]
     taken = jnp.concatenate(taken, axis=0)
+    sources = [0] + interleaved(parts)
     for first in range(0, parts, 2):
         stacked = jnp.concatenate([ref[...] for ref in weight_refs[first : first + 2]], axis=1)
         product = jnp.dot(taken, stacked, preferred_element_type=jnp.float32)
-        for source in range(first, first + 2):
-            block = product[:, (source - first) * width : (source - first + 1) * width]
-            partial[source] = block if source else block + bias_ref[...]
+        for number in range(2):
+            block = product[:, number * width : (number + 1) * width]
+            partial[sources[first + number]] = block if first + number else block + bias_ref[...]
     blocks = [lax.bitwise_xor(lax.axis_index("latent"), source).astype(jnp.float32) for source in range(parts)]
     row = 0
     for start, out_ref in zip(starts, out_refs):
@@ -375,9 +382,7 @@
     with jax.named_scope("encoder_rows"):
         pieces = fetch_rows(encoder, parts)
         pieces, decoder = lax.optimization_barrier((pieces, decoder))
-        weights = [pieces[0]] + [None] * (parts - 1)
-        for step in sorted(range(1, parts), reverse=True):
-            weights[step] = swapped(pieces[step], step)
+        weights = [pieces[0]] + [swapped(pieces[step], step) for step in interleaved(parts)]
     with jax.named_scope("decoder_weights"):
         near_rows, far_rows, ids = fetch_decoders(lists, counts, decoder, encoder.shape[1], parts)
         near_decoder, far_decoder = passed_along(near_rows, 1), passed_along(far_rows, 2)

time: 67.8 us -> 67.1 us (0.990)
  waiting for transfers between devices: 22.1 us -> 19.7 us
  starting transfers between devices: 32.9 us -> 34.6 us
    ppermute x9, starting transfers between devices: 14.8 us -> 17.3 us  [swapped(): return lax.ppermute(value, 'latent', [(i, i ^ step) for i in range(count)])]
    ppermute x9, waiting for transfers between devices: 13 us -> 11.7 us  [swapped(): return lax.ppermute(value, 'latent', [(i, i ^ step) for i in range(count)])]
    ppermute x5, waiting for transfers between devices: 8.56 us -> 7.49 us  [passed_along(): lax.ppermute(value, 'layer', [(i, i + steps) for i in range(count - steps)])]
    ppermute x1, starting transfers between devices: 3.56 us -> 2.66 us  [across_cores(): return lax.ppermute(value, 'layer', [(i, i ^ 1) for i in range(count)])]
  transfers between devices with their start and end apart: 15 -> 15, of which waited for: 8 -> 6; matrix products, arithmetic and copies ran while one was open for 0% -> 0% of each run, Pallas kernels for 8% -> 8%
where the time goes in v14:
time: 67.1 us; the launch traced here: 66.8 us
  starting transfers between devices  34.6 us (52%)
  waiting for transfers between devices  19.7 us (29%)
  Pallas kernels  7.82 us (12%)
  local copies, waits for them, and re-layouts  4.46 us (7%)
    ppermute x9, starting transfers between devices, swapped(): return lax.ppermute(value, 'latent', [(i, i ^ step) for i in range(count)])  17.3 us
    ppermute x5, starting transfers between devices, passed_along(): lax.ppermute(value, 'layer', [(i, i + steps) for i in range(count - steps)])  14.7 us
    ppermute x9, waiting for transfers between devices, swapped(): return lax.ppermute(value, 'latent', [(i, i ^ step) for i in range(count)])  11.7 us
    ppermute x5, waiting for transfers between devices, passed_along(): lax.ppermute(value, 'layer', [(i, i + steps) for i in range(count - steps)])  7.49 us
    unnamed x14, local copies, waits for them, and re-layouts  4.46 us
    ppermute x1, starting transfers between devices, across_cores(): return lax.ppermute(value, 'layer', [(i, i ^ 1) for i in range(count)])  2.66 us
    pallas_call x1, Pallas kernels, decode_late(): pl.pallas_call(functools.partial(late_kernel, parts, near.shape[0]), out_...  2.47 us
    pallas_call x1, Pallas kernels, decode_early(): pl.pallas_call(functools.partial(early_kernel, tiles), out_shape=[jax.Sha...  1.93 us
  transfers between devices with their start and end apart: 15, of which 6 were waited for; matrix products, arithmetic and copies ran while one was open for 0% of the time, Pallas kernels for 8%

profile of v14, /device:TPU:5, one launch (start us, length us, event | category | flops | bytes accessed | tf_op | source)
XLA Modules:
  0.0 66.8 jit_solution(7824060961646604053)
XLA Ops:
  0.0 0.0 copy-start.3
  0.0 1.2 %copy-done.3 = bf16[1,4096,128]{2,1,0:T(8,128)(2,1)S(1)} copy-done((bf16[1,4096,128]{2,1,0:T(8,128)(2,1)S(1)}, bf16[1,4096,128]{2,1,0:T(8,128)(2,1)}, u32[]{:S(2)}) %copy-start.3) | copy-done | bytes 1048600
  1.2 0.0 copy-start.6
  1.2 0.1 fetch_rows.1
  1.3 2.4 %collective-permute-start = (bf16[1024,128]{1,0:T(8,128)(2,1)S(1)}, bf16[1024,128]{1,0:T(8,128)(2,1)S(1)}, u32[]{:S(2)}, u32[]{:S(2)}) collective-permute-start(bf16[1024,128]{1,0:T(8,128)(2,1)S(1)} %get-tuple-element.42), channel_id=1, source_target_pairs={{0,2},{1,3},{2,0},{3,1},{4,6},{5,7},{6,4},{7,5},{8,10},{9,11},{10,... | collective-permute-start | bytes 786440 | tf_op jit(solution)/shard_map/encoder_rows/ppermute | solution.py:18
  3.7 1.3 %collective-permute-start.1 = (bf16[1024,128]{1,0:T(8,128)(2,1)S(1)}, bf16[1024,128]{1,0:T(8,128)(2,1)S(1)}, u32[]{:S(2)}, u32[]{:S(2)}) collective-permute-start(bf16[1024,128]{1,0:T(8,128)(2,1)S(1)} %get-tuple-element.43), channel_id=1, source_target_pairs={{0,1},{1,0},{2,3},{3,2},{4,5},{5,4},{6,7},{7,6},{8,9},{9,8},{10,11... | collective-permute-start | bytes 786440 | tf_op jit(solution)/shard_map/encoder_rows/ppermute | solution.py:18
  5.0 0.0 collective-permute-start.2
  5.0 0.0 copy-start
  5.0 1.9 %copy-done = bf16[1,3,512,1024]{3,2,1,0:T(8,128)(2,1)S(1)} copy-done((bf16[1,3,512,1024]{3,2,1,0:T(8,128)(2,1)S(1)}, bf16[1,3,512,1024]{3,2,1,0:T(8,128)(2,1)}, u32[]{:S(2)}) %copy-start) | copy-done | bytes 3145752
  6.9 0.7 %copy-done.4 = s32[1,16,2]{1,2,0:T(2,128)S(1)} copy-done((s32[1,16,2]{1,2,0:T(2,128)S(1)}, s32[1,16,2]{1,2,0:T(2,128)}, u32[]{:S(2)}) %copy-start.4) | copy-done | bytes 152
  7.5 0.7 copy-done.5
  8.2 0.7 %fetch_decoders.1 = (bf16[528,1024]{1,0:T(8,128)(2,1)S(1)}, bf16[528,1024]{1,0:T(8,128)(2,1)S(1)}, f32[16,1024]{1,0:T(8,128)S(1)}) custom-call(s32[2,16]{1,0:T(2,128)S(1)} %bitcast.13, s32[16]{0:T(128)S(1)} %bitcast.14, bf16[3,512,1024]{2,1,0:T(8,128)(2,1)S(1)} %bitcast.8), custom_call_target="tpu_custom_call" | custom-call | tf_op jit(solution)/shard_map/decoder_weights/fetch_decoders/pallas_call | solution.py:93
  8.9 4.5 %collective-permute-start.10 = (bf16[528,1024]{1,0:T(8,128)(2,1)S(1)}, bf16[528,1024]{1,0:T(8,128)(2,1)S(1)}, u32[]{:S(2)}, u32[]{:S(2)}) collective-permute-start(bf16[528,1024]{1,0:T(8,128)(2,1)S(1)} %get-tuple-element.56), channel_id=1, source_target_pairs={{0,4},{4,8},{8,12},{12,16},{16,20},{20,24},{24,28},{1,5},{5,9},{9,... | collective-permute-start | bytes 3244040 | tf_op jit(solution)/shard_map/decoder_weights/ppermute | solution.py:29
  13.4 1.9 %collective-permute-start.11 = (bf16[528,1024]{1,0:T(8,128)(2,1)S(1)}, bf16[528,1024]{1,0:T(8,128)(2,1)S(1)}, u32[]{:S(2)}, u32[]{:S(2)}) collective-permute-start(bf16[528,1024]{1,0:T(8,128)(2,1)S(1)} %get-tuple-element.57), channel_id=1, source_target_pairs={{0,8},{4,12},{8,16},{12,20},{16,24},{20,28},{1,9},{5,13},{9,17},{1... | collective-permute-start | bytes 3244040 | tf_op jit(solution)/shard_map/decoder_weights/ppermute | solution.py:29
  15.3 0.0 collective-permute-done.refs_1_
  15.3 0.0 collective-permute-done.1.refs_2_
  15.3 6.5 %collective-permute-done.2.refs_3_ = bf16[1024,128]{1,0:T(8,128)(2,1)S(1)} collective-permute-done((bf16[1024,128]{1,0:T(8,128)(2,1)S(1)}, bf16[1024,128]{1,0:T(8,128)(2,1)S(1)}, u32[]{:S(2)}, u32[]{:S(2)}) %collective-permute-start.2) | collective-permute-done | bytes 262176 | tf_op jit(solution)/shard_map/encoder_rows/ppermute | solution.py:18
  21.8 0.0 copy-done.6
  21.8 0.0 copy-done.2
  21.8 0.4 encode.3
  22.3 0.0 copy-start.1
  22.3 6.0 %collective-permute-start.3 = (bf16[4,2,64,128]{3,2,1,0:T(8,128)(2,1)S(1)}, bf16[4,2,64,128]{3,2,1,0:T(8,128)(2,1)S(1)}, u32[]{:S(2)}, u32[]{:S(2)}) collective-permute-start(bf16[4,2,64,128]{3,2,1,0:T(8,128)(2,1)S(1)} %encode.3), channel_id=1, source_target_pairs={{0,1},{1,0},{2,3},{3,2},{4,5},{5,4},{6,7},{7,6},{8,9},{9,8},{10,11... | collective-permute-start | bytes 393224 | tf_op jit(solution)/shard_map/encode/ppermute | solution.py:18
  28.3 1.0 %encode.2 = (bf16[4,2,64,128]{3,2,1,0:T(8,128)(2,1)S(1)}, f32[4,2,64,128]{3,2,1,0:T(8,128)S(1)}, f32[4,2,64,128]{3,2,1,0:T(8,128)S(1)}) custom-call(f32[16,1024]{1,0:T(8,128)S(1)} %get-tuple-element.40.ids_ref, f32[1,128]{1,0:T(1,128)S(1)} %copy-done.6, bf16[1024,1024]{1,0:T(8,128)(2,1)S(1)} %bitcast.11, bf16[1024,128]{1,0:T(8,128)(2,1)S(1)} %get-tuple-element.41.refs_0_, ...), custom_call_target="tpu_custom_call" | custom-call | flops 805306368 | bytes 3145728 | tf_op jit(solution)/shard_map/encode/encode/pallas_call | solution.py:138
  29.3 0.1 collective-permute-start.5
  29.4 2.3 %collective-permute-done.3.arrived_ref = bf16[4,2,64,128]{3,2,1,0:T(8,128)(2,1)S(1)} collective-permute-done((bf16[4,2,64,128]{3,2,1,0:T(8,128)(2,1)S(1)}, bf16[4,2,64,128]{3,2,1,0:T(8,128)(2,1)S(1)}, u32[]{:S(2)}, u32[]{:S(2)}) %collective-permute-start.3) | collective-permute-done | bytes 131104 | tf_op jit(solution)/shard_map/encode/ppermute | solution.py:18
  31.7 3.1 %collective-permute-start.4 = (bf16[4,2,64,128]{3,2,1,0:T(8,128)(2,1)S(1)}, bf16[4,2,64,128]{3,2,1,0:T(8,128)(2,1)S(1)}, u32[]{:S(2)}, u32[]{:S(2)}) collective-permute-start(bf16[4,2,64,128]{3,2,1,0:T(8,128)(2,1)S(1)} %get-tuple-element.47), channel_id=1, source_target_pairs={{0,2},{1,3},{2,0},{3,1},{4,6},{5,7},{6,4},{7,5},{8,10},{9,11},{10,... | collective-permute-start | bytes 393224 | tf_op jit(solution)/shard_map/encode/ppermute | solution.py:18
  34.9 0.0 collective-permute-done.5.arrived_ref
  34.9 2.8 %collective-permute-done.4.arrived_ref = bf16[4,2,64,128]{3,2,1,0:T(8,128)(2,1)S(1)} collective-permute-done((bf16[4,2,64,128]{3,2,1,0:T(8,128)(2,1)S(1)}, bf16[4,2,64,128]{3,2,1,0:T(8,128)(2,1)S(1)}, u32[]{:S(2)}, u32[]{:S(2)}) %collective-permute-start.4) | collective-permute-done | bytes 131104 | tf_op jit(solution)/shard_map/encode/ppermute | solution.py:18
  37.8 2.2 %collective-permute-start.6 = (bf16[4,2,64,128]{3,2,1,0:T(8,128)(2,1)S(1)}, bf16[4,2,64,128]{3,2,1,0:T(8,128)(2,1)S(1)}, u32[]{:S(2)}, u32[]{:S(2)}) collective-permute-start(bf16[4,2,64,128]{3,2,1,0:T(8,128)(2,1)S(1)} %get-tuple-element.53), channel_id=1, source_target_pairs={{0,2},{1,3},{2,0},{3,1},{4,6},{5,7},{6,4},{7,5},{8,10},{9,11},{10,... | collective-permute-start | bytes 393224 | tf_op jit(solution)/shard_map/encode/ppermute | solution.py:18
  40.0 2.1 %collective-permute-start.7 = (bf16[4,2,64,128]{3,2,1,0:T(8,128)(2,1)S(1)}, bf16[4,2,64,128]{3,2,1,0:T(8,128)(2,1)S(1)}, u32[]{:S(2)}, u32[]{:S(2)}) collective-permute-start(bf16[4,2,64,128]{3,2,1,0:T(8,128)(2,1)S(1)} %activate.2.refs_0_), channel_id=1, source_target_pairs={{0,1},{1,0},{2,3},{3,2},{4,5},{5,4},{6,7},{7,6},{8,9},{9,8},{10,11... | collective-permute-start | bytes 393224 | tf_op jit(solution)/shard_map/spread/ppermute | solution.py:18
  42.1 3.1 %collective-permute-start.9 = (bf16[4,2,64,128]{3,2,1,0:T(8,128)(2,1)S(1)}, bf16[4,2,64,128]{3,2,1,0:T(8,128)(2,1)S(1)}, u32[]{:S(2)}, u32[]{:S(2)}) collective-permute-start(bf16[4,2,64,128]{3,2,1,0:T(8,128)(2,1)S(1)} %activate.2.refs_0_), channel_id=1, source_target_pairs={{0,8},{4,12},{8,16},{12,20},{16,24},{20,28},{1,9},{5,13},{9,17},{1... | collective-permute-start | bytes 393224 | tf_op jit(solution)/shard_map/spread/ppermute | solution.py:29
  45.2 0.0 collective-permute-done.6.arrived_ref
  45.3 0.1 collective-permute-start.8
  45.4 0.0 collective-permute-done.7.refs_2_.second_ref
  45.4 3.0 %collective-permute-start.13 = (bf16[8,2,64,128]{3,2,1,0:T(8,128)(2,1)S(1)}, bf16[8,2,64,128]{3,2,1,0:T(8,128)(2,1)S(1)}, u32[]{:S(2)}, u32[]{:S(2)}) collective-permute-start(bf16[8,2,64,128]{3,2,1,0:T(8,128)(2,1)S(1)} %join.1), channel_id=1, source_target_pairs={{0,8},{4,12},{8,16},{12,20},{16,24},{20,28},{1,9},{5,13},{9,17},{1... | collective-permute-start | bytes 786440 | tf_op jit(solution)/shard_map/spread/ppermute | solution.py:29
  48.4 4.0 %collective-permute-done.9.refs_4_ = bf16[4,2,64,128]{3,2,1,0:T(8,128)(2,1)S(1)} collective-permute-done((bf16[4,2,64,128]{3,2,1,0:T(8,128)(2,1)S(1)}, bf16[4,2,64,128]{3,2,1,0:T(8,128)(2,1)S(1)}, u32[]{:S(2)}, u32[]{:S(2)}) %collective-permute-start.9) | collective-permute-done | bytes 131104 | tf_op jit(solution)/shard_map/spread/ppermute | solution.py:29
  52.3 0.0 collective-permute-done.8.refs_3_
  52.3 2.2 %collective-permute-start.12 = (bf16[4,2,64,128]{3,2,1,0:T(8,128)(2,1)S(1)}, bf16[4,2,64,128]{3,2,1,0:T(8,128)(2,1)S(1)}, u32[]{:S(2)}, u32[]{:S(2)}) collective-permute-start(bf16[4,2,64,128]{3,2,1,0:T(8,128)(2,1)S(1)} %collective-permute-done.8.refs_3_), channel_id=1, source_target_pairs={{0,8},{4,12},{8,16},{12,20},{16,24},{20,28},{1,9},{5,13},{9,17},{1... | collective-permute-start | bytes 393224 | tf_op jit(solution)/shard_map/spread/ppermute | solution.py:29
  54.6 0.0 collective-permute-done.10.near_dec
  54.6 0.0 collective-permute-done.11.refs_6_.far_dec
  54.6 0.0 copy-done.1
  54.6 1.9 %decode_early.1 = (f32[256,1024]{1,0:T(8,128)S(1)}, f32[768,1024]{1,0:T(8,128)S(1)}) custom-call(f32[16,1024]{1,0:T(8,128)S(1)} %get-tuple-element.40.ids_ref, bf16[4,2,64,128]{3,2,1,0:T(8,128)(2,1)S(1)} %activate.2.refs_0_, bf16[4,2,64,128]{3,2,1,0:T(8,128)(2,1)S(1)} %activate.3.refs_1_.first_ref, ...), custom_call_target="tpu_custom_call" | custom-call | flops 1342177280 | bytes 6291456 | tf_op jit(solution)/shard_map/decode/decode_early/pallas_call | solution.py:275
  56.6 3.5 %collective-permute-done.12.third.refs_6_ = bf16[4,2,64,128]{3,2,1,0:T(8,128)(2,1)S(1)} collective-permute-done((bf16[4,2,64,128]{3,2,1,0:T(8,128)(2,1)S(1)}, bf16[4,2,64,128]{3,2,1,0:T(8,128)(2,1)S(1)}, u32[]{:S(2)}, u32[]{:S(2)}) %collective-permute-start.12) | collective-permute-done | bytes 131104 | tf_op jit(solution)/shard_map/spread/ppermute | solution.py:29
  60.0 0.0 collective-permute-done.13.second.refs_5_
  60.1 2.7 %collective-permute-start.14 = (bf16[16,2,64,128]{3,2,1,0:T(8,128)(2,1)S(1)}, bf16[16,2,64,128]{3,2,1,0:T(8,128)(2,1)S(1)}, u32[]{:S(2)}, u32[]{:S(2)}) collective-permute-start(bf16[16,2,64,128]{3,2,1,0:T(8,128)(2,1)S(1)} %choose.1), channel_id=1, source_target_pairs={{0,4},{4,0},{8,12},{12,8},{16,20},{20,16},{24,28},{28,24},{1,5},{5... | collective-permute-start | bytes 1572872 | tf_op jit(solution)/shard_map/decode/ppermute | solution.py:34
  62.8 1.0 %decode_middle.1.rest_ref = f32[768,1024]{1,0:T(8,128)S(1)} custom-call(f32[768,1024]{1,0:T(8,128)S(1)} %get-tuple-element.62.rest_ref, bf16[8,2,64,128]{3,2,1,0:T(8,128)(2,1)S(1)} %collective-permute-done.13.second.refs_5_, bf16[4,2,64,128]{3,2,1,0:T(8,128)(2,1)S(1)} %collective-permute-done.12.third.refs_6_, ...), custom_call_target="tpu_custom_call" | custom-call | flops 805306368 | bytes 7340032 | tf_op jit(solution)/shard_map/decode/decode_middle/pallas_call | solution.py:308
  63.8 0.5 collective-permute-done.14.near
  64.3 2.5 %decode_late.1 = bf16[1024,1024]{1,0:T(8,128)(2,1)} custom-call(f32[256,1024]{1,0:T(8,128)S(1)} %get-tuple-element.61.first_ref, f32[768,1024]{1,0:T(8,128)S(1)} %decode_middle.1.rest_ref, bf16[16,2,64,128]{3,2,1,0:T(8,128)(2,1)S(1)} %collective-permute-done.14.near, bf16[528,1024]{1,0:T(8,128)(2,1)S(1)} %collective-permute-done.10.near_dec), custom_call_target="tpu_custom_call" | custom-call | flops 1073741824 | bytes 7340032 | tf_op jit(solution)/shard_map/decode/decode_late/pallas_call | solution.py:353
  (9 shorter events, 0.2 us)
Async XLA Ops:
  0.0 1.2 %copy-start.3 = (bf16[1,4096,128]{2,1,0:T(8,128)(2,1)S(1)}, bf16[1,4096,128]{2,1,0:T(8,128)(2,1)}, u32[]{:S(2)}) copy-start(bf16[1,4096,128]{2,1,0:T(8,128)(2,1)} %param.7) | copy-start | bytes 3145732
  1.2 20.6 %copy-start.6 = (f32[1,128]{1,0:T(1,128)S(1)}, f32[1,128]{1,0:T(1,128)}, u32[]{:S(2)}) copy-start(f32[1,128]{1,0:T(1,128)} %bias_ref.3) | copy-start | bytes 1540
  1.3 14.0 %collective-permute-start = (bf16[1024,128]{1,0:T(8,128)(2,1)S(1)}, bf16[1024,128]{1,0:T(8,128)(2,1)S(1)}, u32[]{:S(2)}, u32[]{:S(2)}) collective-permute-start(bf16[1024,128]{1,0:T(8,128)(2,1)S(1)} %get-tuple-element.42), channel_id=1, source_target_pairs={{0,2},{1,3},{2,0},{3,1},{4,6},{5,7},{6,4},{7,5},{8,10},{9,11},{10,... | collective-permute-start | bytes 786440 | tf_op jit(solution)/shard_map/encoder_rows/ppermute | solution.py:18
  3.7 11.7 %collective-permute-start.1 = (bf16[1024,128]{1,0:T(8,128)(2,1)S(1)}, bf16[1024,128]{1,0:T(8,128)(2,1)S(1)}, u32[]{:S(2)}, u32[]{:S(2)}) collective-permute-start(bf16[1024,128]{1,0:T(8,128)(2,1)S(1)} %get-tuple-element.43), channel_id=1, source_target_pairs={{0,1},{1,0},{2,3},{3,2},{4,5},{5,4},{6,7},{7,6},{8,9},{9,8},{10,11... | collective-permute-start | bytes 786440 | tf_op jit(solution)/shard_map/encoder_rows/ppermute | solution.py:18
  5.0 16.8 %collective-permute-start.2 = (bf16[1024,128]{1,0:T(8,128)(2,1)S(1)}, bf16[1024,128]{1,0:T(8,128)(2,1)S(1)}, u32[]{:S(2)}, u32[]{:S(2)}) collective-permute-start(bf16[1024,128]{1,0:T(8,128)(2,1)S(1)} %get-tuple-element.44), channel_id=1, source_target_pairs={{0,3},{1,2},{2,1},{3,0},{4,7},{5,6},{6,5},{7,4},{8,11},{9,10},{10,... | collective-permute-start | bytes 786440 | tf_op jit(solution)/shard_map/encoder_rows/ppermute | solution.py:18
  5.0 1.9 %copy-start = (bf16[1,3,512,1024]{3,2,1,0:T(8,128)(2,1)S(1)}, bf16[1,3,512,1024]{3,2,1,0:T(8,128)(2,1)}, u32[]{:S(2)}) copy-start(bf16[1,3,512,1024]{3,2,1,0:T(8,128)(2,1)} %param.9) | copy-start | bytes 9437188
  6.9 0.7 %copy-start.4 = (s32[1,16,2]{1,2,0:T(2,128)S(1)}, s32[1,16,2]{1,2,0:T(2,128)}, u32[]{:S(2)}) copy-start(s32[1,16,2]{1,2,0:T(2,128)} %param.10) | copy-start | bytes 388
  7.5 0.7 copy-start.5
  8.2 13.6 %copy-start.2 = (bf16[1,1024,1024]{2,1,0:T(8,128)(2,1)S(1)}, bf16[1,1024,1024]{2,1,0:T(8,128)(2,1)}, u32[]{:S(2)}) copy-start(bf16[1,1024,1024]{2,1,0:T(8,128)(2,1)} %param.6) | copy-start | bytes 6291460
  8.9 45.7 %collective-permute-start.10 = (bf16[528,1024]{1,0:T(8,128)(2,1)S(1)}, bf16[528,1024]{1,0:T(8,128)(2,1)S(1)}, u32[]{:S(2)}, u32[]{:S(2)}) collective-permute-start(bf16[528,1024]{1,0:T(8,128)(2,1)S(1)} %get-tuple-element.56), channel_id=1, source_target_pairs={{0,4},{4,8},{8,12},{12,16},{16,20},{20,24},{24,28},{1,5},{5,9},{9,... | collective-permute-start | bytes 3244040 | tf_op jit(solution)/shard_map/decoder_weights/ppermute | solution.py:29
  13.4 41.2 %collective-permute-start.11 = (bf16[528,1024]{1,0:T(8,128)(2,1)S(1)}, bf16[528,1024]{1,0:T(8,128)(2,1)S(1)}, u32[]{:S(2)}, u32[]{:S(2)}) collective-permute-start(bf16[528,1024]{1,0:T(8,128)(2,1)S(1)} %get-tuple-element.57), channel_id=1, source_target_pairs={{0,8},{4,12},{8,16},{12,20},{16,24},{20,28},{1,9},{5,13},{9,17},{1... | collective-permute-start | bytes 3244040 | tf_op jit(solution)/shard_map/decoder_weights/ppermute | solution.py:29
  22.3 32.3 %copy-start.1 = (bf16[1,3,512,1024]{3,2,1,0:T(8,128)(2,1)S(1)}, bf16[1,3,512,1024]{3,2,1,0:T(8,128)(2,1)}, u32[]{:S(2)}) copy-start(bf16[1,3,512,1024]{3,2,1,0:T(8,128)(2,1)} %param.9) | copy-start | bytes 9437188
  22.3 9.4 %collective-permute-start.3 = (bf16[4,2,64,128]{3,2,1,0:T(8,128)(2,1)S(1)}, bf16[4,2,64,128]{3,2,1,0:T(8,128)(2,1)S(1)}, u32[]{:S(2)}, u32[]{:S(2)}) collective-permute-start(bf16[4,2,64,128]{3,2,1,0:T(8,128)(2,1)S(1)} %encode.3), channel_id=1, source_target_pairs={{0,1},{1,0},{2,3},{3,2},{4,5},{5,4},{6,7},{7,6},{8,9},{9,8},{10,11... | collective-permute-start | bytes 393224 | tf_op jit(solution)/shard_map/encode/ppermute | solution.py:18
  29.3 5.6 %collective-permute-start.5 = (bf16[4,2,64,128]{3,2,1,0:T(8,128)(2,1)S(1)}, bf16[4,2,64,128]{3,2,1,0:T(8,128)(2,1)S(1)}, u32[]{:S(2)}, u32[]{:S(2)}) collective-permute-start(bf16[4,2,64,128]{3,2,1,0:T(8,128)(2,1)S(1)} %get-tuple-element.49), channel_id=1, source_target_pairs={{0,1},{1,0},{2,3},{3,2},{4,5},{5,4},{6,7},{7,6},{8,9},{9,8},{10,11... | collective-permute-start | bytes 393224 | tf_op jit(solution)/shard_map/encode/ppermute | solution.py:18
  31.7 6.0 %collective-permute-start.4 = (bf16[4,2,64,128]{3,2,1,0:T(8,128)(2,1)S(1)}, bf16[4,2,64,128]{3,2,1,0:T(8,128)(2,1)S(1)}, u32[]{:S(2)}, u32[]{:S(2)}) collective-permute-start(bf16[4,2,64,128]{3,2,1,0:T(8,128)(2,1)S(1)} %get-tuple-element.47), channel_id=1, source_target_pairs={{0,2},{1,3},{2,0},{3,1},{4,6},{5,7},{6,4},{7,5},{8,10},{9,11},{10,... | collective-permute-start | bytes 393224 | tf_op jit(solution)/shard_map/encode/ppermute | solution.py:18
  37.8 7.5 %collective-permute-start.6 = (bf16[4,2,64,128]{3,2,1,0:T(8,128)(2,1)S(1)}, bf16[4,2,64,128]{3,2,1,0:T(8,128)(2,1)S(1)}, u32[]{:S(2)}, u32[]{:S(2)}) collective-permute-start(bf16[4,2,64,128]{3,2,1,0:T(8,128)(2,1)S(1)} %get-tuple-element.53), channel_id=1, source_target_pairs={{0,2},{1,3},{2,0},{3,1},{4,6},{5,7},{6,4},{7,5},{8,10},{9,11},{10,... | collective-permute-start | bytes 393224 | tf_op jit(solution)/shard_map/encode/ppermute | solution.py:18
  40.0 5.4 %collective-permute-start.7 = (bf16[4,2,64,128]{3,2,1,0:T(8,128)(2,1)S(1)}, bf16[4,2,64,128]{3,2,1,0:T(8,128)(2,1)S(1)}, u32[]{:S(2)}, u32[]{:S(2)}) collective-permute-start(bf16[4,2,64,128]{3,2,1,0:T(8,128)(2,1)S(1)} %activate.2.refs_0_), channel_id=1, source_target_pairs={{0,1},{1,0},{2,3},{3,2},{4,5},{5,4},{6,7},{7,6},{8,9},{9,8},{10,11... | collective-permute-start | bytes 393224 | tf_op jit(solution)/shard_map/spread/ppermute | solution.py:18
  42.1 10.2 %collective-permute-start.9 = (bf16[4,2,64,128]{3,2,1,0:T(8,128)(2,1)S(1)}, bf16[4,2,64,128]{3,2,1,0:T(8,128)(2,1)S(1)}, u32[]{:S(2)}, u32[]{:S(2)}) collective-permute-start(bf16[4,2,64,128]{3,2,1,0:T(8,128)(2,1)S(1)} %activate.2.refs_0_), channel_id=1, source_target_pairs={{0,8},{4,12},{8,16},{12,20},{16,24},{20,28},{1,9},{5,13},{9,17},{1... | collective-permute-start | bytes 393224 | tf_op jit(solution)/shard_map/spread/ppermute | solution.py:29
  45.3 7.1 %collective-permute-start.8 = (bf16[4,2,64,128]{3,2,1,0:T(8,128)(2,1)S(1)}, bf16[4,2,64,128]{3,2,1,0:T(8,128)(2,1)S(1)}, u32[]{:S(2)}, u32[]{:S(2)}) collective-permute-start(bf16[4,2,64,128]{3,2,1,0:T(8,128)(2,1)S(1)} %activate.3.refs_1_.first_ref), channel_id=1, source_target_pairs={{0,1},{1,0},{2,3},{3,2},{4,5},{5,4},{6,7},{7,6},{8,9},{9,8},{10,11... | collective-permute-start | bytes 393224 | tf_op jit(solution)/shard_map/spread/ppermute | solution.py:18
  45.4 14.7 %collective-permute-start.13 = (bf16[8,2,64,128]{3,2,1,0:T(8,128)(2,1)S(1)}, bf16[8,2,64,128]{3,2,1,0:T(8,128)(2,1)S(1)}, u32[]{:S(2)}, u32[]{:S(2)}) collective-permute-start(bf16[8,2,64,128]{3,2,1,0:T(8,128)(2,1)S(1)} %join.1), channel_id=1, source_target_pairs={{0,8},{4,12},{8,16},{12,20},{16,24},{20,28},{1,9},{5,13},{9,17},{1... | collective-permute-start | bytes 786440 | tf_op jit(solution)/shard_map/spread/ppermute | solution.py:29
  52.3 7.7 %collective-permute-start.12 = (bf16[4,2,64,128]{3,2,1,0:T(8,128)(2,1)S(1)}, bf16[4,2,64,128]{3,2,1,0:T(8,128)(2,1)S(1)}, u32[]{:S(2)}, u32[]{:S(2)}) collective-permute-start(bf16[4,2,64,128]{3,2,1,0:T(8,128)(2,1)S(1)} %collective-permute-done.8.refs_3_), channel_id=1, source_target_pairs={{0,8},{4,12},{8,16},{12,20},{16,24},{20,28},{1,9},{5,13},{9,17},{1... | collective-permute-start | bytes 393224 | tf_op jit(solution)/shard_map/spread/ppermute | solution.py:29
  60.1 4.2 %collective-permute-start.14 = (bf16[16,2,64,128]{3,2,1,0:T(8,128)(2,1)S(1)}, bf16[16,2,64,128]{3,2,1,0:T(8,128)(2,1)S(1)}, u32[]{:S(2)}, u32[]{:S(2)}) collective-permute-start(bf16[16,2,64,128]{3,2,1,0:T(8,128)(2,1)S(1)} %choose.1), channel_id=1, source_target_pairs={{0,4},{4,0},{8,12},{12,8},{16,20},{20,16},{24,28},{28,24},{1,5},{5... | collective-permute-start | bytes 1572872 | tf_op jit(solution)/shard_map/decode/ppermute | solution.py:34

commit v15 on v14

--- a/solution.py
+++ b/solution.py
@@ -383,6 +383,7 @@
         pieces = fetch_rows(encoder, parts)
         pieces, decoder = lax.optimization_barrier((pieces, decoder))
         weights = [pieces[0]] + [swapped(pieces[step], step) for step in interleaved(parts)]
+        weights[1], lists = lax.optimization_barrier((weights[1], lists))
     with jax.named_scope("decoder_weights"):
         near_rows, far_rows, ids = fetch_decoders(lists, counts, decoder, encoder.shape[1], parts)
         near_decoder, far_decoder = passed_along(near_rows, 1), passed_along(far_rows, 2)

time: 67.1 us -> 85.6 us (1.28)
  waiting for transfers between devices: 19.7 us -> 48 us
  starting transfers between devices: 34.6 us -> 24.8 us
    ppermute x9, waiting for transfers between devices: 11.7 us -> 28 us  [swapped(): return lax.ppermute(value, 'latent', [(i, i ^ step) for i in range(count)])]
    ppermute x9, starting transfers between devices: 17.3 us -> 5.48 us  [swapped(): return lax.ppermute(value, 'latent', [(i, i ^ step) for i in range(count)])]
    ppermute x5, waiting for transfers between devices: 7.49 us -> 19.1 us  [passed_along(): lax.ppermute(value, 'layer', [(i, i + steps) for i in range(count - steps)])]
    ppermute x5, starting transfers between devices: 14.7 us -> 19.2 us  [passed_along(): lax.ppermute(value, 'layer', [(i, i + steps) for i in range(count - steps)])]
    ppermute x1, starting transfers between devices: 2.66 us -> 0.07 us  [across_cores(): return lax.ppermute(value, 'layer', [(i, i ^ 1) for i in range(count)])]
  transfers between devices with their start and end apart: 15 -> 15, of which waited for: 6 -> 9; matrix products, arithmetic and copies ran while one was open for 0% -> 0% of each run, Pallas kernels for 8% -> 6%
where the time goes in v15:
time: 85.6 us; the launch traced here: 85.3 us
  waiting for transfers between devices  48 us (56%)
  starting transfers between devices  24.8 us (29%)
  Pallas kernels  7.84 us (9%)
  local copies, waits for them, and re-layouts  4.46 us (5%)
    ppermute x9, waiting for transfers between devices, swapped(): return lax.ppermute(value, 'latent', [(i, i ^ step) for i in range(count)])  28 us
    ppermute x5, starting transfers between devices, passed_along(): lax.ppermute(value, 'layer', [(i, i + steps) for i in range(count - steps)])  19.2 us
    ppermute x5, waiting for transfers between devices, passed_along(): lax.ppermute(value, 'layer', [(i, i + steps) for i in range(count - steps)])  19.1 us
    ppermute x9, starting transfers between devices, swapped(): return lax.ppermute(value, 'latent', [(i, i ^ step) for i in range(count)])  5.48 us
    unnamed x14, local copies, waits for them, and re-layouts  4.46 us
    pallas_call x1, Pallas kernels, decode_late(): pl.pallas_call(functools.partial(late_kernel, parts, near.shape[0]), out_...  2.48 us
    pallas_call x1, Pallas kernels, decode_early(): pl.pallas_call(functools.partial(early_kernel, tiles), out_shape=[jax.Sha...  1.93 us
  transfers between devices with their start and end apart: 15, of which 9 were waited for; matrix products, arithmetic and copies ran while one was open for 0% of the time, Pallas kernels for 6%

profile of v15, /device:TPU:5, one launch (start us, length us, event | category | flops | bytes accessed | tf_op | source)
XLA Modules:
  0.0 85.3 jit_solution(3164969778078857224)
XLA Ops:
  0.0 0.0 copy-start.3
  0.0 1.2 %copy-done.3 = bf16[1,4096,128]{2,1,0:T(8,128)(2,1)S(1)} copy-done((bf16[1,4096,128]{2,1,0:T(8,128)(2,1)S(1)}, bf16[1,4096,128]{2,1,0:T(8,128)(2,1)}, u32[]{:S(2)}) %copy-start.3) | copy-done | bytes 1048600
  1.2 0.0 copy-start.6
  1.2 0.1 fetch_rows.1
  1.3 2.4 %collective-permute-start = (bf16[1024,128]{1,0:T(8,128)(2,1)S(1)}, bf16[1024,128]{1,0:T(8,128)(2,1)S(1)}, u32[]{:S(2)}, u32[]{:S(2)}) collective-permute-start(bf16[1024,128]{1,0:T(8,128)(2,1)S(1)} %get-tuple-element.41), channel_id=1, source_target_pairs={{0,2},{1,3},{2,0},{3,1},{4,6},{5,7},{6,4},{7,5},{8,10},{9,11},{10,... | collective-permute-start | bytes 786440 | tf_op jit(solution)/shard_map/encoder_rows/ppermute | solution.py:18
  3.7 1.3 %collective-permute-start.1 = (bf16[1024,128]{1,0:T(8,128)(2,1)S(1)}, bf16[1024,128]{1,0:T(8,128)(2,1)S(1)}, u32[]{:S(2)}, u32[]{:S(2)}) collective-permute-start(bf16[1024,128]{1,0:T(8,128)(2,1)S(1)} %get-tuple-element.47), channel_id=1, source_target_pairs={{0,1},{1,0},{2,3},{3,2},{4,5},{5,4},{6,7},{7,6},{8,9},{9,8},{10,11... | collective-permute-start | bytes 786440 | tf_op jit(solution)/shard_map/encoder_rows/ppermute | solution.py:18
  5.0 0.0 collective-permute-start.2
  5.0 10.1 %collective-permute-done.refs_1_ = bf16[1024,128]{1,0:T(8,128)(2,1)S(1)} collective-permute-done((bf16[1024,128]{1,0:T(8,128)(2,1)S(1)}, bf16[1024,128]{1,0:T(8,128)(2,1)S(1)}, u32[]{:S(2)}, u32[]{:S(2)}) %collective-permute-start) | collective-permute-done | bytes 262176 | tf_op jit(solution)/shard_map/encoder_rows/ppermute | solution.py:18
  15.1 0.0 copy-start
  15.1 1.9 %copy-done = bf16[1,3,512,1024]{3,2,1,0:T(8,128)(2,1)S(1)} copy-done((bf16[1,3,512,1024]{3,2,1,0:T(8,128)(2,1)S(1)}, bf16[1,3,512,1024]{3,2,1,0:T(8,128)(2,1)}, u32[]{:S(2)}) %copy-start) | copy-done | bytes 3145752
  17.0 0.7 copy-done.4
  17.7 0.7 copy-done.5
  18.4 0.7 fetch_decoders.1
  19.1 11.3 %collective-permute-start.10 = (bf16[528,1024]{1,0:T(8,128)(2,1)S(1)}, bf16[528,1024]{1,0:T(8,128)(2,1)S(1)}, u32[]{:S(2)}, u32[]{:S(2)}) collective-permute-start(bf16[528,1024]{1,0:T(8,128)(2,1)S(1)} %get-tuple-element.60), channel_id=1, source_target_pairs={{0,4},{4,8},{8,12},{12,16},{16,20},{20,24},{24,28},{1,5},{5,9},{9,... | collective-permute-start | bytes 3244040 | tf_op jit(solution)/shard_map/decoder_weights/ppermute | solution.py:29
  30.3 1.9 %collective-permute-start.11 = (bf16[528,1024]{1,0:T(8,128)(2,1)S(1)}, bf16[528,1024]{1,0:T(8,128)(2,1)S(1)}, u32[]{:S(2)}, u32[]{:S(2)}) collective-permute-start(bf16[528,1024]{1,0:T(8,128)(2,1)S(1)} %get-tuple-element.61), channel_id=1, source_target_pairs={{0,8},{4,12},{8,16},{12,20},{16,24},{20,28},{1,9},{5,13},{9,17},{1... | collective-permute-start | bytes 3244040 | tf_op jit(solution)/shard_map/decoder_weights/ppermute | solution.py:29
  32.3 0.0 collective-permute-done.1.refs_2_
  32.3 0.0 collective-permute-done.2.refs_3_
  32.3 0.0 copy-done.6
  32.3 0.0 copy-done.2
  32.3 0.4 encode.3
  32.8 0.0 copy-start.1
  32.8 0.1 collective-permute-start.3
  32.9 1.0 %encode.2 = (bf16[4,2,64,128]{3,2,1,0:T(8,128)(2,1)S(1)}, f32[4,2,64,128]{3,2,1,0:T(8,128)S(1)}, f32[4,2,64,128]{3,2,1,0:T(8,128)S(1)}) custom-call(f32[16,1024]{1,0:T(8,128)S(1)} %get-tuple-element.44.ids_ref, f32[1,128]{1,0:T(1,128)S(1)} %copy-done.6, bf16[1024,1024]{1,0:T(8,128)(2,1)S(1)} %bitcast.11, bf16[1024,128]{1,0:T(8,128)(2,1)S(1)} %get-tuple-element.45.refs_0_, ...), custom_call_target="tpu_custom_call" | custom-call | flops 805306368 | bytes 3145728 | tf_op jit(solution)/shard_map/encode/encode/pallas_call | solution.py:138
  33.9 1.5 %collective-permute-start.5 = (bf16[4,2,64,128]{3,2,1,0:T(8,128)(2,1)S(1)}, bf16[4,2,64,128]{3,2,1,0:T(8,128)(2,1)S(1)}, u32[]{:S(2)}, u32[]{:S(2)}) collective-permute-start(bf16[4,2,64,128]{3,2,1,0:T(8,128)(2,1)S(1)} %get-tuple-element.53), channel_id=1, source_target_pairs={{0,1},{1,0},{2,3},{3,2},{4,5},{5,4},{6,7},{7,6},{8,9},{9,8},{10,11... | collective-permute-start | bytes 393224 | tf_op jit(solution)/shard_map/encode/ppermute | solution.py:18
  35.4 2.1 %collective-permute-done.3.arrived_ref = bf16[4,2,64,128]{3,2,1,0:T(8,128)(2,1)S(1)} collective-permute-done((bf16[4,2,64,128]{3,2,1,0:T(8,128)(2,1)S(1)}, bf16[4,2,64,128]{3,2,1,0:T(8,128)(2,1)S(1)}, u32[]{:S(2)}, u32[]{:S(2)}) %collective-permute-start.3) | collective-permute-done | bytes 131104 | tf_op jit(solution)/shard_map/encode/ppermute | solution.py:18
  37.6 0.1 collective-permute-start.4
  37.6 2.7 %collective-permute-done.5.arrived_ref = bf16[4,2,64,128]{3,2,1,0:T(8,128)(2,1)S(1)} collective-permute-done((bf16[4,2,64,128]{3,2,1,0:T(8,128)(2,1)S(1)}, bf16[4,2,64,128]{3,2,1,0:T(8,128)(2,1)S(1)}, u32[]{:S(2)}, u32[]{:S(2)}) %collective-permute-start.5) | collective-permute-done | bytes 131104 | tf_op jit(solution)/shard_map/encode/ppermute | solution.py:18
  40.4 7.7 %collective-permute-done.4.arrived_ref = bf16[4,2,64,128]{3,2,1,0:T(8,128)(2,1)S(1)} collective-permute-done((bf16[4,2,64,128]{3,2,1,0:T(8,128)(2,1)S(1)}, bf16[4,2,64,128]{3,2,1,0:T(8,128)(2,1)S(1)}, u32[]{:S(2)}, u32[]{:S(2)}) %collective-permute-start.4) | collective-permute-done | bytes 131104 | tf_op jit(solution)/shard_map/encode/ppermute | solution.py:18
  48.0 0.0 collective-permute-start.6
  48.1 0.1 collective-permute-start.7
  48.2 1.9 %collective-permute-start.9 = (bf16[4,2,64,128]{3,2,1,0:T(8,128)(2,1)S(1)}, bf16[4,2,64,128]{3,2,1,0:T(8,128)(2,1)S(1)}, u32[]{:S(2)}, u32[]{:S(2)}) collective-permute-start(bf16[4,2,64,128]{3,2,1,0:T(8,128)(2,1)S(1)} %activate.2.refs_0_), channel_id=1, source_target_pairs={{0,8},{4,12},{8,16},{12,20},{16,24},{20,28},{1,9},{5,13},{9,17},{1... | collective-permute-start | bytes 393224 | tf_op jit(solution)/shard_map/spread/ppermute | solution.py:29
  50.1 3.4 %collective-permute-done.6.arrived_ref = bf16[4,2,64,128]{3,2,1,0:T(8,128)(2,1)S(1)} collective-permute-done((bf16[4,2,64,128]{3,2,1,0:T(8,128)(2,1)S(1)}, bf16[4,2,64,128]{3,2,1,0:T(8,128)(2,1)S(1)}, u32[]{:S(2)}, u32[]{:S(2)}) %collective-permute-start.6) | collective-permute-done | bytes 131104 | tf_op jit(solution)/shard_map/encode/ppermute | solution.py:18
  53.5 0.1 collective-permute-start.8
  53.6 2.0 %collective-permute-done.7.refs_2_.second_ref = bf16[4,2,64,128]{3,2,1,0:T(8,128)(2,1)S(1)} collective-permute-done((bf16[4,2,64,128]{3,2,1,0:T(8,128)(2,1)S(1)}, bf16[4,2,64,128]{3,2,1,0:T(8,128)(2,1)S(1)}, u32[]{:S(2)}, u32[]{:S(2)}) %collective-permute-start.7) | collective-permute-done | bytes 131104 | tf_op jit(solution)/shard_map/spread/ppermute | solution.py:18
  55.6 1.9 %collective-permute-start.13 = (bf16[8,2,64,128]{3,2,1,0:T(8,128)(2,1)S(1)}, bf16[8,2,64,128]{3,2,1,0:T(8,128)(2,1)S(1)}, u32[]{:S(2)}, u32[]{:S(2)}) collective-permute-start(bf16[8,2,64,128]{3,2,1,0:T(8,128)(2,1)S(1)} %join.1), channel_id=1, source_target_pairs={{0,8},{4,12},{8,16},{12,20},{16,24},{20,28},{1,9},{5,13},{9,17},{1... | collective-permute-start | bytes 786440 | tf_op jit(solution)/shard_map/spread/ppermute | solution.py:29
  57.5 16.7 %collective-permute-done.9.refs_4_ = bf16[4,2,64,128]{3,2,1,0:T(8,128)(2,1)S(1)} collective-permute-done((bf16[4,2,64,128]{3,2,1,0:T(8,128)(2,1)S(1)}, bf16[4,2,64,128]{3,2,1,0:T(8,128)(2,1)S(1)}, u32[]{:S(2)}, u32[]{:S(2)}) %collective-permute-start.9) | collective-permute-done | bytes 131104 | tf_op jit(solution)/shard_map/spread/ppermute | solution.py:29
  74.2 0.0 collective-permute-done.8.refs_3_
  74.2 2.2 %collective-permute-start.12 = (bf16[4,2,64,128]{3,2,1,0:T(8,128)(2,1)S(1)}, bf16[4,2,64,128]{3,2,1,0:T(8,128)(2,1)S(1)}, u32[]{:S(2)}, u32[]{:S(2)}) collective-permute-start(bf16[4,2,64,128]{3,2,1,0:T(8,128)(2,1)S(1)} %collective-permute-done.8.refs_3_), channel_id=1, source_target_pairs={{0,8},{4,12},{8,16},{12,20},{16,24},{20,28},{1,9},{5,13},{9,17},{1... | collective-permute-start | bytes 393224 | tf_op jit(solution)/shard_map/spread/ppermute | solution.py:29
  76.4 0.0 collective-permute-done.10.near_dec
  76.4 0.0 collective-permute-done.11.refs_6_.far_dec
  76.4 0.0 copy-done.1
  76.5 1.9 %decode_early.1 = (f32[256,1024]{1,0:T(8,128)S(1)}, f32[768,1024]{1,0:T(8,128)S(1)}) custom-call(f32[16,1024]{1,0:T(8,128)S(1)} %get-tuple-element.44.ids_ref, bf16[4,2,64,128]{3,2,1,0:T(8,128)(2,1)S(1)} %activate.2.refs_0_, bf16[4,2,64,128]{3,2,1,0:T(8,128)(2,1)S(1)} %activate.3.refs_1_.first_ref, ...), custom_call_target="tpu_custom_call" | custom-call | flops 1342177280 | bytes 6291456 | tf_op jit(solution)/shard_map/decode/decode_early/pallas_call | solution.py:275
  78.4 2.4 %collective-permute-done.12.third.refs_6_ = bf16[4,2,64,128]{3,2,1,0:T(8,128)(2,1)S(1)} collective-permute-done((bf16[4,2,64,128]{3,2,1,0:T(8,128)(2,1)S(1)}, bf16[4,2,64,128]{3,2,1,0:T(8,128)(2,1)S(1)}, u32[]{:S(2)}, u32[]{:S(2)}) %collective-permute-start.12) | collective-permute-done | bytes 131104 | tf_op jit(solution)/shard_map/spread/ppermute | solution.py:29
  80.8 0.0 collective-permute-done.13.second.refs_5_
  80.8 0.1 collective-permute-start.14
  80.9 1.0 %decode_middle.1.rest_ref = f32[768,1024]{1,0:T(8,128)S(1)} custom-call(f32[768,1024]{1,0:T(8,128)S(1)} %get-tuple-element.66.rest_ref, bf16[8,2,64,128]{3,2,1,0:T(8,128)(2,1)S(1)} %collective-permute-done.13.second.refs_5_, bf16[4,2,64,128]{3,2,1,0:T(8,128)(2,1)S(1)} %collective-permute-done.12.third.refs_6_, ...), custom_call_target="tpu_custom_call" | custom-call | flops 805306368 | bytes 7340032 | tf_op jit(solution)/shard_map/decode/decode_middle/pallas_call | solution.py:308
  81.9 0.9 %collective-permute-done.14.near = bf16[16,2,64,128]{3,2,1,0:T(8,128)(2,1)S(1)} collective-permute-done((bf16[16,2,64,128]{3,2,1,0:T(8,128)(2,1)S(1)}, bf16[16,2,64,128]{3,2,1,0:T(8,128)(2,1)S(1)}, u32[]{:S(2)}, u32[]{:S(2)}) %collective-permute-start.14) | collective-permute-done | bytes 524320 | tf_op jit(solution)/shard_map/decode/ppermute | solution.py:34
  82.8 2.5 %decode_late.1 = bf16[1024,1024]{1,0:T(8,128)(2,1)} custom-call(f32[256,1024]{1,0:T(8,128)S(1)} %get-tuple-element.65.first_ref, f32[768,1024]{1,0:T(8,128)S(1)} %decode_middle.1.rest_ref, bf16[16,2,64,128]{3,2,1,0:T(8,128)(2,1)S(1)} %collective-permute-done.14.near, bf16[528,1024]{1,0:T(8,128)(2,1)S(1)} %collective-permute-done.10.near_dec), custom_call_target="tpu_custom_call" | custom-call | flops 1073741824 | bytes 7340032 | tf_op jit(solution)/shard_map/decode/decode_late/pallas_call | solution.py:353
  (9 shorter events, 0.2 us)
Async XLA Ops:
  0.0 1.2 %copy-start.3 = (bf16[1,4096,128]{2,1,0:T(8,128)(2,1)S(1)}, bf16[1,4096,128]{2,1,0:T(8,128)(2,1)}, u32[]{:S(2)}) copy-start(bf16[1,4096,128]{2,1,0:T(8,128)(2,1)} %param.7) | copy-start | bytes 3145732
  1.2 31.1 %copy-start.6 = (f32[1,128]{1,0:T(1,128)S(1)}, f32[1,128]{1,0:T(1,128)}, u32[]{:S(2)}) copy-start(f32[1,128]{1,0:T(1,128)} %bias_ref.3) | copy-start | bytes 1540
  1.3 13.8 %collective-permute-start = (bf16[1024,128]{1,0:T(8,128)(2,1)S(1)}, bf16[1024,128]{1,0:T(8,128)(2,1)S(1)}, u32[]{:S(2)}, u32[]{:S(2)}) collective-permute-start(bf16[1024,128]{1,0:T(8,128)(2,1)S(1)} %get-tuple-element.41), channel_id=1, source_target_pairs={{0,2},{1,3},{2,0},{3,1},{4,6},{5,7},{6,4},{7,5},{8,10},{9,11},{10,... | collective-permute-start | bytes 786440 | tf_op jit(solution)/shard_map/encoder_rows/ppermute | solution.py:18
  3.7 28.6 %collective-permute-start.1 = (bf16[1024,128]{1,0:T(8,128)(2,1)S(1)}, bf16[1024,128]{1,0:T(8,128)(2,1)S(1)}, u32[]{:S(2)}, u32[]{:S(2)}) collective-permute-start(bf16[1024,128]{1,0:T(8,128)(2,1)S(1)} %get-tuple-element.47), channel_id=1, source_target_pairs={{0,1},{1,0},{2,3},{3,2},{4,5},{5,4},{6,7},{7,6},{8,9},{9,8},{10,11... | collective-permute-start | bytes 786440 | tf_op jit(solution)/shard_map/encoder_rows/ppermute | solution.py:18
  5.0 27.3 %collective-permute-start.2 = (bf16[1024,128]{1,0:T(8,128)(2,1)S(1)}, bf16[1024,128]{1,0:T(8,128)(2,1)S(1)}, u32[]{:S(2)}, u32[]{:S(2)}) collective-permute-start(bf16[1024,128]{1,0:T(8,128)(2,1)S(1)} %get-tuple-element.48), channel_id=1, source_target_pairs={{0,3},{1,2},{2,1},{3,0},{4,7},{5,6},{6,5},{7,4},{8,11},{9,10},{10,... | collective-permute-start | bytes 786440 | tf_op jit(solution)/shard_map/encoder_rows/ppermute | solution.py:18
  15.1 1.9 %copy-start = (bf16[1,3,512,1024]{3,2,1,0:T(8,128)(2,1)S(1)}, bf16[1,3,512,1024]{3,2,1,0:T(8,128)(2,1)}, u32[]{:S(2)}) copy-start(bf16[1,3,512,1024]{3,2,1,0:T(8,128)(2,1)} %param.9) | copy-start | bytes 9437188
  17.0 0.7 copy-start.4
  17.7 0.7 copy-start.5
  18.3 14.0 %copy-start.2 = (bf16[1,1024,1024]{2,1,0:T(8,128)(2,1)S(1)}, bf16[1,1024,1024]{2,1,0:T(8,128)(2,1)}, u32[]{:S(2)}) copy-start(bf16[1,1024,1024]{2,1,0:T(8,128)(2,1)} %param.6) | copy-start | bytes 6291460
  19.1 57.4 %collective-permute-start.10 = (bf16[528,1024]{1,0:T(8,128)(2,1)S(1)}, bf16[528,1024]{1,0:T(8,128)(2,1)S(1)}, u32[]{:S(2)}, u32[]{:S(2)}) collective-permute-start(bf16[528,1024]{1,0:T(8,128)(2,1)S(1)} %get-tuple-element.60), channel_id=1, source_target_pairs={{0,4},{4,8},{8,12},{12,16},{16,20},{20,24},{24,28},{1,5},{5,9},{9,... | collective-permute-start | bytes 3244040 | tf_op jit(solution)/shard_map/decoder_weights/ppermute | solution.py:29
  30.3 46.1 %collective-permute-start.11 = (bf16[528,1024]{1,0:T(8,128)(2,1)S(1)}, bf16[528,1024]{1,0:T(8,128)(2,1)S(1)}, u32[]{:S(2)}, u32[]{:S(2)}) collective-permute-start(bf16[528,1024]{1,0:T(8,128)(2,1)S(1)} %get-tuple-element.61), channel_id=1, source_target_pairs={{0,8},{4,12},{8,16},{12,20},{16,24},{20,28},{1,9},{5,13},{9,17},{1... | collective-permute-start | bytes 3244040 | tf_op jit(solution)/shard_map/decoder_weights/ppermute | solution.py:29
  32.8 43.7 %copy-start.1 = (bf16[1,3,512,1024]{3,2,1,0:T(8,128)(2,1)S(1)}, bf16[1,3,512,1024]{3,2,1,0:T(8,128)(2,1)}, u32[]{:S(2)}) copy-start(bf16[1,3,512,1024]{3,2,1,0:T(8,128)(2,1)} %param.9) | copy-start | bytes 9437188
  32.8 4.7 %collective-permute-start.3 = (bf16[4,2,64,128]{3,2,1,0:T(8,128)(2,1)S(1)}, bf16[4,2,64,128]{3,2,1,0:T(8,128)(2,1)S(1)}, u32[]{:S(2)}, u32[]{:S(2)}) collective-permute-start(bf16[4,2,64,128]{3,2,1,0:T(8,128)(2,1)S(1)} %encode.3), channel_id=1, source_target_pairs={{0,1},{1,0},{2,3},{3,2},{4,5},{5,4},{6,7},{7,6},{8,9},{9,8},{10,11... | collective-permute-start | bytes 393224 | tf_op jit(solution)/shard_map/encode/ppermute | solution.py:18
  33.9 6.5 %collective-permute-start.5 = (bf16[4,2,64,128]{3,2,1,0:T(8,128)(2,1)S(1)}, bf16[4,2,64,128]{3,2,1,0:T(8,128)(2,1)S(1)}, u32[]{:S(2)}, u32[]{:S(2)}) collective-permute-start(bf16[4,2,64,128]{3,2,1,0:T(8,128)(2,1)S(1)} %get-tuple-element.53), channel_id=1, source_target_pairs={{0,1},{1,0},{2,3},{3,2},{4,5},{5,4},{6,7},{7,6},{8,9},{9,8},{10,11... | collective-permute-start | bytes 393224 | tf_op jit(solution)/shard_map/encode/ppermute | solution.py:18
  37.6 10.5 %collective-permute-start.4 = (bf16[4,2,64,128]{3,2,1,0:T(8,128)(2,1)S(1)}, bf16[4,2,64,128]{3,2,1,0:T(8,128)(2,1)S(1)}, u32[]{:S(2)}, u32[]{:S(2)}) collective-permute-start(bf16[4,2,64,128]{3,2,1,0:T(8,128)(2,1)S(1)} %get-tuple-element.51), channel_id=1, source_target_pairs={{0,2},{1,3},{2,0},{3,1},{4,6},{5,7},{6,4},{7,5},{8,10},{9,11},{10,... | collective-permute-start | bytes 393224 | tf_op jit(solution)/shard_map/encode/ppermute | solution.py:18
  48.0 5.4 %collective-permute-start.6 = (bf16[4,2,64,128]{3,2,1,0:T(8,128)(2,1)S(1)}, bf16[4,2,64,128]{3,2,1,0:T(8,128)(2,1)S(1)}, u32[]{:S(2)}, u32[]{:S(2)}) collective-permute-start(bf16[4,2,64,128]{3,2,1,0:T(8,128)(2,1)S(1)} %get-tuple-element.57), channel_id=1, source_target_pairs={{0,2},{1,3},{2,0},{3,1},{4,6},{5,7},{6,4},{7,5},{8,10},{9,11},{10,... | collective-permute-start | bytes 393224 | tf_op jit(solution)/shard_map/encode/ppermute | solution.py:18
  48.1 7.5 %collective-permute-start.7 = (bf16[4,2,64,128]{3,2,1,0:T(8,128)(2,1)S(1)}, bf16[4,2,64,128]{3,2,1,0:T(8,128)(2,1)S(1)}, u32[]{:S(2)}, u32[]{:S(2)}) collective-permute-start(bf16[4,2,64,128]{3,2,1,0:T(8,128)(2,1)S(1)} %activate.2.refs_0_), channel_id=1, source_target_pairs={{0,1},{1,0},{2,3},{3,2},{4,5},{5,4},{6,7},{7,6},{8,9},{9,8},{10,11... | collective-permute-start | bytes 393224 | tf_op jit(solution)/shard_map/spread/ppermute | solution.py:18
  48.2 26.0 %collective-permute-start.9 = (bf16[4,2,64,128]{3,2,1,0:T(8,128)(2,1)S(1)}, bf16[4,2,64,128]{3,2,1,0:T(8,128)(2,1)S(1)}, u32[]{:S(2)}, u32[]{:S(2)}) collective-permute-start(bf16[4,2,64,128]{3,2,1,0:T(8,128)(2,1)S(1)} %activate.2.refs_0_), channel_id=1, source_target_pairs={{0,8},{4,12},{8,16},{12,20},{16,24},{20,28},{1,9},{5,13},{9,17},{1... | collective-permute-start | bytes 393224 | tf_op jit(solution)/shard_map/spread/ppermute | solution.py:29
  53.5 20.7 %collective-permute-start.8 = (bf16[4,2,64,128]{3,2,1,0:T(8,128)(2,1)S(1)}, bf16[4,2,64,128]{3,2,1,0:T(8,128)(2,1)S(1)}, u32[]{:S(2)}, u32[]{:S(2)}) collective-permute-start(bf16[4,2,64,128]{3,2,1,0:T(8,128)(2,1)S(1)} %activate.3.refs_1_.first_ref), channel_id=1, source_target_pairs={{0,1},{1,0},{2,3},{3,2},{4,5},{5,4},{6,7},{7,6},{8,9},{9,8},{10,11... | collective-permute-start | bytes 393224 | tf_op jit(solution)/shard_map/spread/ppermute | solution.py:18
  55.6 25.2 %collective-permute-start.13 = (bf16[8,2,64,128]{3,2,1,0:T(8,128)(2,1)S(1)}, bf16[8,2,64,128]{3,2,1,0:T(8,128)(2,1)S(1)}, u32[]{:S(2)}, u32[]{:S(2)}) collective-permute-start(bf16[8,2,64,128]{3,2,1,0:T(8,128)(2,1)S(1)} %join.1), channel_id=1, source_target_pairs={{0,8},{4,12},{8,16},{12,20},{16,24},{20,28},{1,9},{5,13},{9,17},{1... | collective-permute-start | bytes 786440 | tf_op jit(solution)/shard_map/spread/ppermute | solution.py:29
  74.2 6.6 %collective-permute-start.12 = (bf16[4,2,64,128]{3,2,1,0:T(8,128)(2,1)S(1)}, bf16[4,2,64,128]{3,2,1,0:T(8,128)(2,1)S(1)}, u32[]{:S(2)}, u32[]{:S(2)}) collective-permute-start(bf16[4,2,64,128]{3,2,1,0:T(8,128)(2,1)S(1)} %collective-permute-done.8.refs_3_), channel_id=1, source_target_pairs={{0,8},{4,12},{8,16},{12,20},{16,24},{20,28},{1,9},{5,13},{9,17},{1... | collective-permute-start | bytes 393224 | tf_op jit(solution)/shard_map/spread/ppermute | solution.py:29
  80.8 2.0 %collective-permute-start.14 = (bf16[16,2,64,128]{3,2,1,0:T(8,128)(2,1)S(1)}, bf16[16,2,64,128]{3,2,1,0:T(8,128)(2,1)S(1)}, u32[]{:S(2)}, u32[]{:S(2)}) collective-permute-start(bf16[16,2,64,128]{3,2,1,0:T(8,128)(2,1)S(1)} %choose.1), channel_id=1, source_target_pairs={{0,4},{4,0},{8,12},{12,8},{16,20},{20,16},{24,28},{28,24},{1,5},{5... | collective-permute-start | bytes 1572872 | tf_op jit(solution)/shard_map/decode/ppermute | solution.py:34

commit v16 on v14

--- a/solution.py
+++ b/solution.py
@@ -107,10 +107,11 @@
     taken = [x_ref[pl.ds(pl.multiple_of(tile * rows, rows), rows), :] for group in held for tile in group]
     taken = jnp.concatenate(taken, axis=0)
     sources = [0] + interleaved(parts)
-    for first in range(0, parts, 2):
-        stacked = jnp.concatenate([ref[...] for ref in weight_refs[first : first + 2]], axis=1)
+    wide = min(parts, 4)
+    for first in range(0, parts, wide):
+        stacked = jnp.concatenate([ref[...] for ref in weight_refs[first : first + wide]], axis=1)
         product = jnp.dot(taken, stacked, preferred_element_type=jnp.float32)
-        for number in range(2):
+        for number in range(wide):
             block = product[:, number * width : (number + 1) * width]
             partial[sources[first + number]] = block if first + number else block + bias_ref[...]
     blocks = [lax.bitwise_xor(lax.axis_index("latent"), source).astype(jnp.float32) for source in range(parts)]
@@ -247,7 +248,7 @@
 
 
 def column_tiles(features):
-    columns = 256 if features % 256 == 0 else features
+    columns = 512 if features % 512 == 0 else features
     return [slice(first, first + columns) for first in range(0, features, columns)]
 
 

time: 67.1 us -> 66.9 us (level)
  no operation moved by 1% of the time
where the time goes in v16:
time: 66.9 us; the launch traced here: 66.6 us
  starting transfers between devices  34.6 us (52%)
  waiting for transfers between devices  19.7 us (29%)
  Pallas kernels  7.67 us (11%)
  local copies, waits for them, and re-layouts  4.46 us (7%)
    ppermute x9, starting transfers between devices, swapped(): return lax.ppermute(value, 'latent', [(i, i ^ step) for i in range(count)])  17.3 us
    ppermute x5, starting transfers between devices, passed_along(): lax.ppermute(value, 'layer', [(i, i + steps) for i in range(count - steps)])  14.7 us
    ppermute x9, waiting for transfers between devices, swapped(): return lax.ppermute(value, 'latent', [(i, i ^ step) for i in range(count)])  11.7 us
    ppermute x5, waiting for transfers between devices, passed_along(): lax.ppermute(value, 'layer', [(i, i + steps) for i in range(count - steps)])  7.49 us
    unnamed x14, local copies, waits for them, and re-layouts  4.46 us
    ppermute x1, starting transfers between devices, across_cores(): return lax.ppermute(value, 'layer', [(i, i ^ 1) for i in range(count)])  2.66 us
    pallas_call x1, Pallas kernels, decode_late(): pl.pallas_call(functools.partial(late_kernel, parts, near.shape[0]), out_...  2.32 us
    pallas_call x1, Pallas kernels, decode_early(): pl.pallas_call(functools.partial(early_kernel, tiles), out_shape=[jax.Sha...  1.93 us
  transfers between devices with their start and end apart: 15, of which 6 were waited for; matrix products, arithmetic and copies ran while one was open for 0% of the time, Pallas kernels for 8%

profile of v16, /device:TPU:5, one launch (start us, length us, event | category | flops | bytes accessed | tf_op | source)
XLA Modules:
  0.0 66.6 jit_solution(15918410311382972361)
XLA Ops:
  0.0 0.0 copy-start.3
  0.0 1.2 %copy-done.3 = bf16[1,4096,128]{2,1,0:T(8,128)(2,1)S(1)} copy-done((bf16[1,4096,128]{2,1,0:T(8,128)(2,1)S(1)}, bf16[1,4096,128]{2,1,0:T(8,128)(2,1)}, u32[]{:S(2)}) %copy-start.3) | copy-done | bytes 1048600
  1.2 0.0 copy-start.6
  1.2 0.1 fetch_rows.1
  1.3 2.4 %collective-permute-start = (bf16[1024,128]{1,0:T(8,128)(2,1)S(1)}, bf16[1024,128]{1,0:T(8,128)(2,1)S(1)}, u32[]{:S(2)}, u32[]{:S(2)}) collective-permute-start(bf16[1024,128]{1,0:T(8,128)(2,1)S(1)} %get-tuple-element.42), channel_id=1, source_target_pairs={{0,2},{1,3},{2,0},{3,1},{4,6},{5,7},{6,4},{7,5},{8,10},{9,11},{10,... | collective-permute-start | bytes 786440 | tf_op jit(solution)/shard_map/encoder_rows/ppermute | solution.py:18
  3.7 1.3 %collective-permute-start.1 = (bf16[1024,128]{1,0:T(8,128)(2,1)S(1)}, bf16[1024,128]{1,0:T(8,128)(2,1)S(1)}, u32[]{:S(2)}, u32[]{:S(2)}) collective-permute-start(bf16[1024,128]{1,0:T(8,128)(2,1)S(1)} %get-tuple-element.43), channel_id=1, source_target_pairs={{0,1},{1,0},{2,3},{3,2},{4,5},{5,4},{6,7},{7,6},{8,9},{9,8},{10,11... | collective-permute-start | bytes 786440 | tf_op jit(solution)/shard_map/encoder_rows/ppermute | solution.py:18
  5.0 0.0 collective-permute-start.2
  5.0 0.0 copy-start
  5.0 1.9 %copy-done = bf16[1,3,512,1024]{3,2,1,0:T(8,128)(2,1)S(1)} copy-done((bf16[1,3,512,1024]{3,2,1,0:T(8,128)(2,1)S(1)}, bf16[1,3,512,1024]{3,2,1,0:T(8,128)(2,1)}, u32[]{:S(2)}) %copy-start) | copy-done | bytes 3145752
  6.9 0.7 %copy-done.4 = s32[1,16,2]{1,2,0:T(2,128)S(1)} copy-done((s32[1,16,2]{1,2,0:T(2,128)S(1)}, s32[1,16,2]{1,2,0:T(2,128)}, u32[]{:S(2)}) %copy-start.4) | copy-done | bytes 152
  7.5 0.7 copy-done.5
  8.2 0.7 %fetch_decoders.1 = (bf16[528,1024]{1,0:T(8,128)(2,1)S(1)}, bf16[528,1024]{1,0:T(8,128)(2,1)S(1)}, f32[16,1024]{1,0:T(8,128)S(1)}) custom-call(s32[2,16]{1,0:T(2,128)S(1)} %bitcast.13, s32[16]{0:T(128)S(1)} %bitcast.14, bf16[3,512,1024]{2,1,0:T(8,128)(2,1)S(1)} %bitcast.8), custom_call_target="tpu_custom_call" | custom-call | tf_op jit(solution)/shard_map/decoder_weights/fetch_decoders/pallas_call | solution.py:93
  8.9 4.5 %collective-permute-start.10 = (bf16[528,1024]{1,0:T(8,128)(2,1)S(1)}, bf16[528,1024]{1,0:T(8,128)(2,1)S(1)}, u32[]{:S(2)}, u32[]{:S(2)}) collective-permute-start(bf16[528,1024]{1,0:T(8,128)(2,1)S(1)} %get-tuple-element.56), channel_id=1, source_target_pairs={{0,4},{4,8},{8,12},{12,16},{16,20},{20,24},{24,28},{1,5},{5,9},{9,... | collective-permute-start | bytes 3244040 | tf_op jit(solution)/shard_map/decoder_weights/ppermute | solution.py:29
  13.4 1.9 %collective-permute-start.11 = (bf16[528,1024]{1,0:T(8,128)(2,1)S(1)}, bf16[528,1024]{1,0:T(8,128)(2,1)S(1)}, u32[]{:S(2)}, u32[]{:S(2)}) collective-permute-start(bf16[528,1024]{1,0:T(8,128)(2,1)S(1)} %get-tuple-element.57), channel_id=1, source_target_pairs={{0,8},{4,12},{8,16},{12,20},{16,24},{20,28},{1,9},{5,13},{9,17},{1... | collective-permute-start | bytes 3244040 | tf_op jit(solution)/shard_map/decoder_weights/ppermute | solution.py:29
  15.3 0.0 collective-permute-done.refs_1_
  15.3 0.0 collective-permute-done.1.refs_2_
  15.3 6.5 %collective-permute-done.2.refs_3_ = bf16[1024,128]{1,0:T(8,128)(2,1)S(1)} collective-permute-done((bf16[1024,128]{1,0:T(8,128)(2,1)S(1)}, bf16[1024,128]{1,0:T(8,128)(2,1)S(1)}, u32[]{:S(2)}, u32[]{:S(2)}) %collective-permute-start.2) | collective-permute-done | bytes 262176 | tf_op jit(solution)/shard_map/encoder_rows/ppermute | solution.py:18
  21.8 0.0 copy-done.6
  21.8 0.0 copy-done.2
  21.8 0.4 encode.3
  22.3 0.0 copy-start.1
  22.3 6.0 %collective-permute-start.3 = (bf16[4,2,64,128]{3,2,1,0:T(8,128)(2,1)S(1)}, bf16[4,2,64,128]{3,2,1,0:T(8,128)(2,1)S(1)}, u32[]{:S(2)}, u32[]{:S(2)}) collective-permute-start(bf16[4,2,64,128]{3,2,1,0:T(8,128)(2,1)S(1)} %encode.3), channel_id=1, source_target_pairs={{0,1},{1,0},{2,3},{3,2},{4,5},{5,4},{6,7},{7,6},{8,9},{9,8},{10,11... | collective-permute-start | bytes 393224 | tf_op jit(solution)/shard_map/encode/ppermute | solution.py:18
  28.3 1.0 %encode.2 = (bf16[4,2,64,128]{3,2,1,0:T(8,128)(2,1)S(1)}, f32[4,2,64,128]{3,2,1,0:T(8,128)S(1)}, f32[4,2,64,128]{3,2,1,0:T(8,128)S(1)}) custom-call(f32[16,1024]{1,0:T(8,128)S(1)} %get-tuple-element.40.ids_ref, f32[1,128]{1,0:T(1,128)S(1)} %copy-done.6, bf16[1024,1024]{1,0:T(8,128)(2,1)S(1)} %bitcast.11, bf16[1024,128]{1,0:T(8,128)(2,1)S(1)} %get-tuple-element.41.refs_0_, ...), custom_call_target="tpu_custom_call" | custom-call | flops 805306368 | bytes 3145728 | tf_op jit(solution)/shard_map/encode/encode/pallas_call | solution.py:139
  29.3 0.1 collective-permute-start.5
  29.4 2.3 %collective-permute-done.3.arrived_ref = bf16[4,2,64,128]{3,2,1,0:T(8,128)(2,1)S(1)} collective-permute-done((bf16[4,2,64,128]{3,2,1,0:T(8,128)(2,1)S(1)}, bf16[4,2,64,128]{3,2,1,0:T(8,128)(2,1)S(1)}, u32[]{:S(2)}, u32[]{:S(2)}) %collective-permute-start.3) | collective-permute-done | bytes 131104 | tf_op jit(solution)/shard_map/encode/ppermute | solution.py:18
  31.7 3.1 %collective-permute-start.4 = (bf16[4,2,64,128]{3,2,1,0:T(8,128)(2,1)S(1)}, bf16[4,2,64,128]{3,2,1,0:T(8,128)(2,1)S(1)}, u32[]{:S(2)}, u32[]{:S(2)}) collective-permute-start(bf16[4,2,64,128]{3,2,1,0:T(8,128)(2,1)S(1)} %get-tuple-element.47), channel_id=1, source_target_pairs={{0,2},{1,3},{2,0},{3,1},{4,6},{5,7},{6,4},{7,5},{8,10},{9,11},{10,... | collective-permute-start | bytes 393224 | tf_op jit(solution)/shard_map/encode/ppermute | solution.py:18
  34.9 0.0 collective-permute-done.5.arrived_ref
  34.9 2.8 %collective-permute-done.4.arrived_ref = bf16[4,2,64,128]{3,2,1,0:T(8,128)(2,1)S(1)} collective-permute-done((bf16[4,2,64,128]{3,2,1,0:T(8,128)(2,1)S(1)}, bf16[4,2,64,128]{3,2,1,0:T(8,128)(2,1)S(1)}, u32[]{:S(2)}, u32[]{:S(2)}) %collective-permute-start.4) | collective-permute-done | bytes 131104 | tf_op jit(solution)/shard_map/encode/ppermute | solution.py:18
  37.8 2.2 %collective-permute-start.6 = (bf16[4,2,64,128]{3,2,1,0:T(8,128)(2,1)S(1)}, bf16[4,2,64,128]{3,2,1,0:T(8,128)(2,1)S(1)}, u32[]{:S(2)}, u32[]{:S(2)}) collective-permute-start(bf16[4,2,64,128]{3,2,1,0:T(8,128)(2,1)S(1)} %get-tuple-element.53), channel_id=1, source_target_pairs={{0,2},{1,3},{2,0},{3,1},{4,6},{5,7},{6,4},{7,5},{8,10},{9,11},{10,... | collective-permute-start | bytes 393224 | tf_op jit(solution)/shard_map/encode/ppermute | solution.py:18
  40.0 2.1 %collective-permute-start.7 = (bf16[4,2,64,128]{3,2,1,0:T(8,128)(2,1)S(1)}, bf16[4,2,64,128]{3,2,1,0:T(8,128)(2,1)S(1)}, u32[]{:S(2)}, u32[]{:S(2)}) collective-permute-start(bf16[4,2,64,128]{3,2,1,0:T(8,128)(2,1)S(1)} %activate.2.refs_0_), channel_id=1, source_target_pairs={{0,1},{1,0},{2,3},{3,2},{4,5},{5,4},{6,7},{7,6},{8,9},{9,8},{10,11... | collective-permute-start | bytes 393224 | tf_op jit(solution)/shard_map/spread/ppermute | solution.py:18
  42.1 3.1 %collective-permute-start.9 = (bf16[4,2,64,128]{3,2,1,0:T(8,128)(2,1)S(1)}, bf16[4,2,64,128]{3,2,1,0:T(8,128)(2,1)S(1)}, u32[]{:S(2)}, u32[]{:S(2)}) collective-permute-start(bf16[4,2,64,128]{3,2,1,0:T(8,128)(2,1)S(1)} %activate.2.refs_0_), channel_id=1, source_target_pairs={{0,8},{4,12},{8,16},{12,20},{16,24},{20,28},{1,9},{5,13},{9,17},{1... | collective-permute-start | bytes 393224 | tf_op jit(solution)/shard_map/spread/ppermute | solution.py:29
  45.2 0.0 collective-permute-done.6.arrived_ref
  45.3 0.1 collective-permute-start.8
  45.4 0.0 collective-permute-done.7.refs_2_.second_ref
  45.4 3.0 %collective-permute-start.13 = (bf16[8,2,64,128]{3,2,1,0:T(8,128)(2,1)S(1)}, bf16[8,2,64,128]{3,2,1,0:T(8,128)(2,1)S(1)}, u32[]{:S(2)}, u32[]{:S(2)}) collective-permute-start(bf16[8,2,64,128]{3,2,1,0:T(8,128)(2,1)S(1)} %join.1), channel_id=1, source_target_pairs={{0,8},{4,12},{8,16},{12,20},{16,24},{20,28},{1,9},{5,13},{9,17},{1... | collective-permute-start | bytes 786440 | tf_op jit(solution)/shard_map/spread/ppermute | solution.py:29
  48.4 4.0 %collective-permute-done.9.refs_4_ = bf16[4,2,64,128]{3,2,1,0:T(8,128)(2,1)S(1)} collective-permute-done((bf16[4,2,64,128]{3,2,1,0:T(8,128)(2,1)S(1)}, bf16[4,2,64,128]{3,2,1,0:T(8,128)(2,1)S(1)}, u32[]{:S(2)}, u32[]{:S(2)}) %collective-permute-start.9) | collective-permute-done | bytes 131104 | tf_op jit(solution)/shard_map/spread/ppermute | solution.py:29
  52.3 0.0 collective-permute-done.8.refs_3_
  52.3 2.2 %collective-permute-start.12 = (bf16[4,2,64,128]{3,2,1,0:T(8,128)(2,1)S(1)}, bf16[4,2,64,128]{3,2,1,0:T(8,128)(2,1)S(1)}, u32[]{:S(2)}, u32[]{:S(2)}) collective-permute-start(bf16[4,2,64,128]{3,2,1,0:T(8,128)(2,1)S(1)} %collective-permute-done.8.refs_3_), channel_id=1, source_target_pairs={{0,8},{4,12},{8,16},{12,20},{16,24},{20,28},{1,9},{5,13},{9,17},{1... | collective-permute-start | bytes 393224 | tf_op jit(solution)/shard_map/spread/ppermute | solution.py:29
  54.6 0.0 collective-permute-done.10.near_dec
  54.6 0.0 collective-permute-done.11.refs_6_.far_dec
  54.6 0.0 copy-done.1
  54.6 1.9 %decode_early.1 = (f32[256,1024]{1,0:T(8,128)S(1)}, f32[768,1024]{1,0:T(8,128)S(1)}) custom-call(f32[16,1024]{1,0:T(8,128)S(1)} %get-tuple-element.40.ids_ref, bf16[4,2,64,128]{3,2,1,0:T(8,128)(2,1)S(1)} %activate.2.refs_0_, bf16[4,2,64,128]{3,2,1,0:T(8,128)(2,1)S(1)} %activate.3.refs_1_.first_ref, ...), custom_call_target="tpu_custom_call" | custom-call | flops 1342177280 | bytes 6291456 | tf_op jit(solution)/shard_map/decode/decode_early/pallas_call | solution.py:276
  56.6 3.5 %collective-permute-done.12.third.refs_6_ = bf16[4,2,64,128]{3,2,1,0:T(8,128)(2,1)S(1)} collective-permute-done((bf16[4,2,64,128]{3,2,1,0:T(8,128)(2,1)S(1)}, bf16[4,2,64,128]{3,2,1,0:T(8,128)(2,1)S(1)}, u32[]{:S(2)}, u32[]{:S(2)}) %collective-permute-start.12) | collective-permute-done | bytes 131104 | tf_op jit(solution)/shard_map/spread/ppermute | solution.py:29
  60.0 0.0 collective-permute-done.13.second.refs_5_
  60.1 2.7 %collective-permute-start.14 = (bf16[16,2,64,128]{3,2,1,0:T(8,128)(2,1)S(1)}, bf16[16,2,64,128]{3,2,1,0:T(8,128)(2,1)S(1)}, u32[]{:S(2)}, u32[]{:S(2)}) collective-permute-start(bf16[16,2,64,128]{3,2,1,0:T(8,128)(2,1)S(1)} %choose.1), channel_id=1, source_target_pairs={{0,4},{4,0},{8,12},{12,8},{16,20},{20,16},{24,28},{28,24},{1,5},{5... | collective-permute-start | bytes 1572872 | tf_op jit(solution)/shard_map/decode/ppermute | solution.py:34
  62.8 1.0 %decode_middle.1.rest_ref = f32[768,1024]{1,0:T(8,128)S(1)} custom-call(f32[768,1024]{1,0:T(8,128)S(1)} %get-tuple-element.62.rest_ref, bf16[8,2,64,128]{3,2,1,0:T(8,128)(2,1)S(1)} %collective-permute-done.13.second.refs_5_, bf16[4,2,64,128]{3,2,1,0:T(8,128)(2,1)S(1)} %collective-permute-done.12.third.refs_6_, ...), custom_call_target="tpu_custom_call" | custom-call | flops 805306368 | bytes 7340032 | tf_op jit(solution)/shard_map/decode/decode_middle/pallas_call | solution.py:309
  63.8 0.5 collective-permute-done.14.near
  64.3 2.3 %decode_late.1 = bf16[1024,1024]{1,0:T(8,128)(2,1)} custom-call(f32[256,1024]{1,0:T(8,128)S(1)} %get-tuple-element.61.first_ref, f32[768,1024]{1,0:T(8,128)S(1)} %decode_middle.1.rest_ref, bf16[16,2,64,128]{3,2,1,0:T(8,128)(2,1)S(1)} %collective-permute-done.14.near, bf16[528,1024]{1,0:T(8,128)(2,1)S(1)} %collective-permute-done.10.near_dec), custom_call_target="tpu_custom_call" | custom-call | flops 1073741824 | bytes 7340032 | tf_op jit(solution)/shard_map/decode/decode_late/pallas_call | solution.py:354
  (9 shorter events, 0.2 us)
Async XLA Ops:
  0.0 1.2 %copy-start.3 = (bf16[1,4096,128]{2,1,0:T(8,128)(2,1)S(1)}, bf16[1,4096,128]{2,1,0:T(8,128)(2,1)}, u32[]{:S(2)}) copy-start(bf16[1,4096,128]{2,1,0:T(8,128)(2,1)} %param.7) | copy-start | bytes 3145732
  1.2 20.6 %copy-start.6 = (f32[1,128]{1,0:T(1,128)S(1)}, f32[1,128]{1,0:T(1,128)}, u32[]{:S(2)}) copy-start(f32[1,128]{1,0:T(1,128)} %bias_ref.3) | copy-start | bytes 1540
  1.3 14.0 %collective-permute-start = (bf16[1024,128]{1,0:T(8,128)(2,1)S(1)}, bf16[1024,128]{1,0:T(8,128)(2,1)S(1)}, u32[]{:S(2)}, u32[]{:S(2)}) collective-permute-start(bf16[1024,128]{1,0:T(8,128)(2,1)S(1)} %get-tuple-element.42), channel_id=1, source_target_pairs={{0,2},{1,3},{2,0},{3,1},{4,6},{5,7},{6,4},{7,5},{8,10},{9,11},{10,... | collective-permute-start | bytes 786440 | tf_op jit(solution)/shard_map/encoder_rows/ppermute | solution.py:18
  3.7 11.7 %collective-permute-start.1 = (bf16[1024,128]{1,0:T(8,128)(2,1)S(1)}, bf16[1024,128]{1,0:T(8,128)(2,1)S(1)}, u32[]{:S(2)}, u32[]{:S(2)}) collective-permute-start(bf16[1024,128]{1,0:T(8,128)(2,1)S(1)} %get-tuple-element.43), channel_id=1, source_target_pairs={{0,1},{1,0},{2,3},{3,2},{4,5},{5,4},{6,7},{7,6},{8,9},{9,8},{10,11... | collective-permute-start | bytes 786440 | tf_op jit(solution)/shard_map/encoder_rows/ppermute | solution.py:18
  5.0 16.8 %collective-permute-start.2 = (bf16[1024,128]{1,0:T(8,128)(2,1)S(1)}, bf16[1024,128]{1,0:T(8,128)(2,1)S(1)}, u32[]{:S(2)}, u32[]{:S(2)}) collective-permute-start(bf16[1024,128]{1,0:T(8,128)(2,1)S(1)} %get-tuple-element.44), channel_id=1, source_target_pairs={{0,3},{1,2},{2,1},{3,0},{4,7},{5,6},{6,5},{7,4},{8,11},{9,10},{10,... | collective-permute-start | bytes 786440 | tf_op jit(solution)/shard_map/encoder_rows/ppermute | solution.py:18
  5.0 1.9 %copy-start = (bf16[1,3,512,1024]{3,2,1,0:T(8,128)(2,1)S(1)}, bf16[1,3,512,1024]{3,2,1,0:T(8,128)(2,1)}, u32[]{:S(2)}) copy-start(bf16[1,3,512,1024]{3,2,1,0:T(8,128)(2,1)} %param.9) | copy-start | bytes 9437188
  6.9 0.7 %copy-start.4 = (s32[1,16,2]{1,2,0:T(2,128)S(1)}, s32[1,16,2]{1,2,0:T(2,128)}, u32[]{:S(2)}) copy-start(s32[1,16,2]{1,2,0:T(2,128)} %param.10) | copy-start | bytes 388
  7.5 0.7 copy-start.5
  8.2 13.6 %copy-start.2 = (bf16[1,1024,1024]{2,1,0:T(8,128)(2,1)S(1)}, bf16[1,1024,1024]{2,1,0:T(8,128)(2,1)}, u32[]{:S(2)}) copy-start(bf16[1,1024,1024]{2,1,0:T(8,128)(2,1)} %param.6) | copy-start | bytes 6291460
  8.9 45.7 %collective-permute-start.10 = (bf16[528,1024]{1,0:T(8,128)(2,1)S(1)}, bf16[528,1024]{1,0:T(8,128)(2,1)S(1)}, u32[]{:S(2)}, u32[]{:S(2)}) collective-permute-start(bf16[528,1024]{1,0:T(8,128)(2,1)S(1)} %get-tuple-element.56), channel_id=1, source_target_pairs={{0,4},{4,8},{8,12},{12,16},{16,20},{20,24},{24,28},{1,5},{5,9},{9,... | collective-permute-start | bytes 3244040 | tf_op jit(solution)/shard_map/decoder_weights/ppermute | solution.py:29
  13.4 41.2 %collective-permute-start.11 = (bf16[528,1024]{1,0:T(8,128)(2,1)S(1)}, bf16[528,1024]{1,0:T(8,128)(2,1)S(1)}, u32[]{:S(2)}, u32[]{:S(2)}) collective-permute-start(bf16[528,1024]{1,0:T(8,128)(2,1)S(1)} %get-tuple-element.57), channel_id=1, source_target_pairs={{0,8},{4,12},{8,16},{12,20},{16,24},{20,28},{1,9},{5,13},{9,17},{1... | collective-permute-start | bytes 3244040 | tf_op jit(solution)/shard_map/decoder_weights/ppermute | solution.py:29
  22.3 32.3 %copy-start.1 = (bf16[1,3,512,1024]{3,2,1,0:T(8,128)(2,1)S(1)}, bf16[1,3,512,1024]{3,2,1,0:T(8,128)(2,1)}, u32[]{:S(2)}) copy-start(bf16[1,3,512,1024]{3,2,1,0:T(8,128)(2,1)} %param.9) | copy-start | bytes 9437188
  22.3 9.4 %collective-permute-start.3 = (bf16[4,2,64,128]{3,2,1,0:T(8,128)(2,1)S(1)}, bf16[4,2,64,128]{3,2,1,0:T(8,128)(2,1)S(1)}, u32[]{:S(2)}, u32[]{:S(2)}) collective-permute-start(bf16[4,2,64,128]{3,2,1,0:T(8,128)(2,1)S(1)} %encode.3), channel_id=1, source_target_pairs={{0,1},{1,0},{2,3},{3,2},{4,5},{5,4},{6,7},{7,6},{8,9},{9,8},{10,11... | collective-permute-start | bytes 393224 | tf_op jit(solution)/shard_map/encode/ppermute | solution.py:18
  29.3 5.6 %collective-permute-start.5 = (bf16[4,2,64,128]{3,2,1,0:T(8,128)(2,1)S(1)}, bf16[4,2,64,128]{3,2,1,0:T(8,128)(2,1)S(1)}, u32[]{:S(2)}, u32[]{:S(2)}) collective-permute-start(bf16[4,2,64,128]{3,2,1,0:T(8,128)(2,1)S(1)} %get-tuple-element.49), channel_id=1, source_target_pairs={{0,1},{1,0},{2,3},{3,2},{4,5},{5,4},{6,7},{7,6},{8,9},{9,8},{10,11... | collective-permute-start | bytes 393224 | tf_op jit(solution)/shard_map/encode/ppermute | solution.py:18
  31.7 6.0 %collective-permute-start.4 = (bf16[4,2,64,128]{3,2,1,0:T(8,128)(2,1)S(1)}, bf16[4,2,64,128]{3,2,1,0:T(8,128)(2,1)S(1)}, u32[]{:S(2)}, u32[]{:S(2)}) collective-permute-start(bf16[4,2,64,128]{3,2,1,0:T(8,128)(2,1)S(1)} %get-tuple-element.47), channel_id=1, source_target_pairs={{0,2},{1,3},{2,0},{3,1},{4,6},{5,7},{6,4},{7,5},{8,10},{9,11},{10,... | collective-permute-start | bytes 393224 | tf_op jit(solution)/shard_map/encode/ppermute | solution.py:18
  37.8 7.5 %collective-permute-start.6 = (bf16[4,2,64,128]{3,2,1,0:T(8,128)(2,1)S(1)}, bf16[4,2,64,128]{3,2,1,0:T(8,128)(2,1)S(1)}, u32[]{:S(2)}, u32[]{:S(2)}) collective-permute-start(bf16[4,2,64,128]{3,2,1,0:T(8,128)(2,1)S(1)} %get-tuple-element.53), channel_id=1, source_target_pairs={{0,2},{1,3},{2,0},{3,1},{4,6},{5,7},{6,4},{7,5},{8,10},{9,11},{10,... | collective-permute-start | bytes 393224 | tf_op jit(solution)/shard_map/encode/ppermute | solution.py:18
  40.0 5.4 %collective-permute-start.7 = (bf16[4,2,64,128]{3,2,1,0:T(8,128)(2,1)S(1)}, bf16[4,2,64,128]{3,2,1,0:T(8,128)(2,1)S(1)}, u32[]{:S(2)}, u32[]{:S(2)}) collective-permute-start(bf16[4,2,64,128]{3,2,1,0:T(8,128)(2,1)S(1)} %activate.2.refs_0_), channel_id=1, source_target_pairs={{0,1},{1,0},{2,3},{3,2},{4,5},{5,4},{6,7},{7,6},{8,9},{9,8},{10,11... | collective-permute-start | bytes 393224 | tf_op jit(solution)/shard_map/spread/ppermute | solution.py:18
  42.1 10.2 %collective-permute-start.9 = (bf16[4,2,64,128]{3,2,1,0:T(8,128)(2,1)S(1)}, bf16[4,2,64,128]{3,2,1,0:T(8,128)(2,1)S(1)}, u32[]{:S(2)}, u32[]{:S(2)}) collective-permute-start(bf16[4,2,64,128]{3,2,1,0:T(8,128)(2,1)S(1)} %activate.2.refs_0_), channel_id=1, source_target_pairs={{0,8},{4,12},{8,16},{12,20},{16,24},{20,28},{1,9},{5,13},{9,17},{1... | collective-permute-start | bytes 393224 | tf_op jit(solution)/shard_map/spread/ppermute | solution.py:29
  45.3 7.1 %collective-permute-start.8 = (bf16[4,2,64,128]{3,2,1,0:T(8,128)(2,1)S(1)}, bf16[4,2,64,128]{3,2,1,0:T(8,128)(2,1)S(1)}, u32[]{:S(2)}, u32[]{:S(2)}) collective-permute-start(bf16[4,2,64,128]{3,2,1,0:T(8,128)(2,1)S(1)} %activate.3.refs_1_.first_ref), channel_id=1, source_target_pairs={{0,1},{1,0},{2,3},{3,2},{4,5},{5,4},{6,7},{7,6},{8,9},{9,8},{10,11... | collective-permute-start | bytes 393224 | tf_op jit(solution)/shard_map/spread/ppermute | solution.py:18
  45.4 14.7 %collective-permute-start.13 = (bf16[8,2,64,128]{3,2,1,0:T(8,128)(2,1)S(1)}, bf16[8,2,64,128]{3,2,1,0:T(8,128)(2,1)S(1)}, u32[]{:S(2)}, u32[]{:S(2)}) collective-permute-start(bf16[8,2,64,128]{3,2,1,0:T(8,128)(2,1)S(1)} %join.1), channel_id=1, source_target_pairs={{0,8},{4,12},{8,16},{12,20},{16,24},{20,28},{1,9},{5,13},{9,17},{1... | collective-permute-start | bytes 786440 | tf_op jit(solution)/shard_map/spread/ppermute | solution.py:29
  52.3 7.7 %collective-permute-start.12 = (bf16[4,2,64,128]{3,2,1,0:T(8,128)(2,1)S(1)}, bf16[4,2,64,128]{3,2,1,0:T(8,128)(2,1)S(1)}, u32[]{:S(2)}, u32[]{:S(2)}) collective-permute-start(bf16[4,2,64,128]{3,2,1,0:T(8,128)(2,1)S(1)} %collective-permute-done.8.refs_3_), channel_id=1, source_target_pairs={{0,8},{4,12},{8,16},{12,20},{16,24},{20,28},{1,9},{5,13},{9,17},{1... | collective-permute-start | bytes 393224 | tf_op jit(solution)/shard_map/spread/ppermute | solution.py:29
  60.1 4.2 %collective-permute-start.14 = (bf16[16,2,64,128]{3,2,1,0:T(8,128)(2,1)S(1)}, bf16[16,2,64,128]{3,2,1,0:T(8,128)(2,1)S(1)}, u32[]{:S(2)}, u32[]{:S(2)}) collective-permute-start(bf16[16,2,64,128]{3,2,1,0:T(8,128)(2,1)S(1)} %choose.1), channel_id=1, source_target_pairs={{0,4},{4,0},{8,12},{12,8},{16,20},{20,16},{24,28},{28,24},{1,5},{5... | collective-permute-start | bytes 1572872 | tf_op jit(solution)/shard_map/decode/ppermute | solution.py:34

commit v17 on v16

--- a/solution.py
+++ b/solution.py
@@ -386,8 +386,8 @@
         weights = [pieces[0]] + [swapped(pieces[step], step) for step in interleaved(parts)]
     with jax.named_scope("decoder_weights"):
         near_rows, far_rows, ids = fetch_decoders(lists, counts, decoder, encoder.shape[1], parts)
-        near_decoder, far_decoder = passed_along(near_rows, 1), passed_along(far_rows, 2)
-        near_decoder, far_decoder = lax.optimization_barrier((near_decoder, far_decoder))
+        far_decoder, near_decoder = passed_along(far_rows, 2), passed_along(near_rows, 1)
+        far_decoder, near_decoder = lax.optimization_barrier((far_decoder, near_decoder))
 
     with jax.named_scope("encode"):
         quarter = tiles // 4

time: 66.9 us -> 66.9 us (level)
  waiting for transfers between devices: 19.7 us -> 18.5 us
  starting transfers between devices: 34.6 us -> 35.8 us
    ppermute x5, waiting for transfers between devices: 7.49 us -> 5.39 us  [passed_along(): lax.ppermute(value, 'layer', [(i, i + steps) for i in range(count - steps)])]
    ppermute x1, starting transfers between devices: 2.66 us -> 3.83 us  [across_cores(): return lax.ppermute(value, 'layer', [(i, i ^ 1) for i in range(count)])]
    ppermute x9, waiting for transfers between devices: 11.7 us -> 12.6 us  [swapped(): return lax.ppermute(value, 'latent', [(i, i ^ step) for i in range(count)])]
  transfers between devices with their start and end apart: 15 -> 15, of which waited for: 6 -> 8; matrix products, arithmetic and copies ran while one was open for 0% -> 0% of each run, Pallas kernels for 8% -> 8%
where the time goes in v17:
time: 66.9 us; the launch traced here: 66.6 us
  starting transfers between devices  35.8 us (54%)
  waiting for transfers between devices  18.5 us (28%)
  Pallas kernels  7.67 us (11%)
  local copies, waits for them, and re-layouts  4.46 us (7%)
    ppermute x9, starting transfers between devices, swapped(): return lax.ppermute(value, 'latent', [(i, i ^ step) for i in range(count)])  17.4 us
    ppermute x5, starting transfers between devices, passed_along(): lax.ppermute(value, 'layer', [(i, i + steps) for i in range(count - steps)])  14.6 us
    ppermute x9, waiting for transfers between devices, swapped(): return lax.ppermute(value, 'latent', [(i, i ^ step) for i in range(count)])  12.6 us
    ppermute x5, waiting for transfers between devices, passed_along(): lax.ppermute(value, 'layer', [(i, i + steps) for i in range(count - steps)])  5.39 us
    unnamed x14, local copies, waits for them, and re-layouts  4.46 us
    ppermute x1, starting transfers between devices, across_cores(): return lax.ppermute(value, 'layer', [(i, i ^ 1) for i in range(count)])  3.83 us
    pallas_call x1, Pallas kernels, decode_late(): pl.pallas_call(functools.partial(late_kernel, parts, near.shape[0]), out_...  2.32 us
    pallas_call x1, Pallas kernels, decode_early(): pl.pallas_call(functools.partial(early_kernel, tiles), out_shape=[jax.Sha...  1.93 us
  transfers between devices with their start and end apart: 15, of which 8 were waited for; matrix products, arithmetic and copies ran while one was open for 0% of the time, Pallas kernels for 8%

profile of v17, /device:TPU:5, one launch (start us, length us, event | category | flops | bytes accessed | tf_op | source)
XLA Modules:
  0.0 66.6 jit_solution(6566250693335585425)
XLA Ops:
  0.0 0.0 copy-start.3
  0.0 1.2 %copy-done.3 = bf16[1,4096,128]{2,1,0:T(8,128)(2,1)S(1)} copy-done((bf16[1,4096,128]{2,1,0:T(8,128)(2,1)S(1)}, bf16[1,4096,128]{2,1,0:T(8,128)(2,1)}, u32[]{:S(2)}) %copy-start.3) | copy-done | bytes 1048600
  1.2 0.0 copy-start.6
  1.2 0.1 fetch_rows.1
  1.3 2.4 %collective-permute-start = (bf16[1024,128]{1,0:T(8,128)(2,1)S(1)}, bf16[1024,128]{1,0:T(8,128)(2,1)S(1)}, u32[]{:S(2)}, u32[]{:S(2)}) collective-permute-start(bf16[1024,128]{1,0:T(8,128)(2,1)S(1)} %get-tuple-element.42), channel_id=1, source_target_pairs={{0,2},{1,3},{2,0},{3,1},{4,6},{5,7},{6,4},{7,5},{8,10},{9,11},{10,... | collective-permute-start | bytes 786440 | tf_op jit(solution)/shard_map/encoder_rows/ppermute | solution.py:18
  3.7 1.3 %collective-permute-start.1 = (bf16[1024,128]{1,0:T(8,128)(2,1)S(1)}, bf16[1024,128]{1,0:T(8,128)(2,1)S(1)}, u32[]{:S(2)}, u32[]{:S(2)}) collective-permute-start(bf16[1024,128]{1,0:T(8,128)(2,1)S(1)} %get-tuple-element.43), channel_id=1, source_target_pairs={{0,1},{1,0},{2,3},{3,2},{4,5},{5,4},{6,7},{7,6},{8,9},{9,8},{10,11... | collective-permute-start | bytes 786440 | tf_op jit(solution)/shard_map/encoder_rows/ppermute | solution.py:18
  5.0 0.0 collective-permute-start.2
  5.0 0.0 copy-start
  5.0 1.9 %copy-done = bf16[1,3,512,1024]{3,2,1,0:T(8,128)(2,1)S(1)} copy-done((bf16[1,3,512,1024]{3,2,1,0:T(8,128)(2,1)S(1)}, bf16[1,3,512,1024]{3,2,1,0:T(8,128)(2,1)}, u32[]{:S(2)}) %copy-start) | copy-done | bytes 3145752
  6.9 0.7 %copy-done.4 = s32[1,16,2]{1,2,0:T(2,128)S(1)} copy-done((s32[1,16,2]{1,2,0:T(2,128)S(1)}, s32[1,16,2]{1,2,0:T(2,128)}, u32[]{:S(2)}) %copy-start.4) | copy-done | bytes 152
  7.5 0.7 copy-done.5
  8.2 0.7 %fetch_decoders.1 = (bf16[528,1024]{1,0:T(8,128)(2,1)S(1)}, bf16[528,1024]{1,0:T(8,128)(2,1)S(1)}, f32[16,1024]{1,0:T(8,128)S(1)}) custom-call(s32[2,16]{1,0:T(2,128)S(1)} %bitcast.13, s32[16]{0:T(128)S(1)} %bitcast.14, bf16[3,512,1024]{2,1,0:T(8,128)(2,1)S(1)} %bitcast.8), custom_call_target="tpu_custom_call" | custom-call | tf_op jit(solution)/shard_map/decoder_weights/fetch_decoders/pallas_call | solution.py:93
  8.9 3.1 %collective-permute-start.10 = (bf16[528,1024]{1,0:T(8,128)(2,1)S(1)}, bf16[528,1024]{1,0:T(8,128)(2,1)S(1)}, u32[]{:S(2)}, u32[]{:S(2)}) collective-permute-start(bf16[528,1024]{1,0:T(8,128)(2,1)S(1)} %get-tuple-element.56), channel_id=1, source_target_pairs={{0,8},{4,12},{8,16},{12,20},{16,24},{20,28},{1,9},{5,13},{9,17},{1... | collective-permute-start | bytes 3244040 | tf_op jit(solution)/shard_map/decoder_weights/ppermute | solution.py:29
  12.0 2.6 %collective-permute-start.11 = (bf16[528,1024]{1,0:T(8,128)(2,1)S(1)}, bf16[528,1024]{1,0:T(8,128)(2,1)S(1)}, u32[]{:S(2)}, u32[]{:S(2)}) collective-permute-start(bf16[528,1024]{1,0:T(8,128)(2,1)S(1)} %get-tuple-element.57), channel_id=1, source_target_pairs={{0,4},{4,8},{8,12},{12,16},{16,20},{20,24},{24,28},{1,5},{5,9},{9,... | collective-permute-start | bytes 3244040 | tf_op jit(solution)/shard_map/decoder_weights/ppermute | solution.py:29
  14.7 0.4 collective-permute-done.refs_1_
  15.1 0.0 collective-permute-done.1.refs_2_
  15.1 6.7 %collective-permute-done.2.refs_3_ = bf16[1024,128]{1,0:T(8,128)(2,1)S(1)} collective-permute-done((bf16[1024,128]{1,0:T(8,128)(2,1)S(1)}, bf16[1024,128]{1,0:T(8,128)(2,1)S(1)}, u32[]{:S(2)}, u32[]{:S(2)}) %collective-permute-start.2) | collective-permute-done | bytes 262176 | tf_op jit(solution)/shard_map/encoder_rows/ppermute | solution.py:18
  21.8 0.0 copy-done.6
  21.8 0.0 copy-done.2
  21.8 0.4 encode.3
  22.3 0.0 copy-start.1
  22.3 6.0 %collective-permute-start.3 = (bf16[4,2,64,128]{3,2,1,0:T(8,128)(2,1)S(1)}, bf16[4,2,64,128]{3,2,1,0:T(8,128)(2,1)S(1)}, u32[]{:S(2)}, u32[]{:S(2)}) collective-permute-start(bf16[4,2,64,128]{3,2,1,0:T(8,128)(2,1)S(1)} %encode.3), channel_id=1, source_target_pairs={{0,1},{1,0},{2,3},{3,2},{4,5},{5,4},{6,7},{7,6},{8,9},{9,8},{10,11... | collective-permute-start | bytes 393224 | tf_op jit(solution)/shard_map/encode/ppermute | solution.py:18
  28.3 1.0 %encode.2 = (bf16[4,2,64,128]{3,2,1,0:T(8,128)(2,1)S(1)}, f32[4,2,64,128]{3,2,1,0:T(8,128)S(1)}, f32[4,2,64,128]{3,2,1,0:T(8,128)S(1)}) custom-call(f32[16,1024]{1,0:T(8,128)S(1)} %get-tuple-element.40.ids_ref, f32[1,128]{1,0:T(1,128)S(1)} %copy-done.6, bf16[1024,1024]{1,0:T(8,128)(2,1)S(1)} %bitcast.11, bf16[1024,128]{1,0:T(8,128)(2,1)S(1)} %get-tuple-element.41.refs_0_, ...), custom_call_target="tpu_custom_call" | custom-call | flops 805306368 | bytes 3145728 | tf_op jit(solution)/shard_map/encode/encode/pallas_call | solution.py:139
  29.3 0.1 collective-permute-start.5
  29.4 2.3 %collective-permute-done.3.arrived_ref = bf16[4,2,64,128]{3,2,1,0:T(8,128)(2,1)S(1)} collective-permute-done((bf16[4,2,64,128]{3,2,1,0:T(8,128)(2,1)S(1)}, bf16[4,2,64,128]{3,2,1,0:T(8,128)(2,1)S(1)}, u32[]{:S(2)}, u32[]{:S(2)}) %collective-permute-start.3) | collective-permute-done | bytes 131104 | tf_op jit(solution)/shard_map/encode/ppermute | solution.py:18
  31.7 3.1 %collective-permute-start.4 = (bf16[4,2,64,128]{3,2,1,0:T(8,128)(2,1)S(1)}, bf16[4,2,64,128]{3,2,1,0:T(8,128)(2,1)S(1)}, u32[]{:S(2)}, u32[]{:S(2)}) collective-permute-start(bf16[4,2,64,128]{3,2,1,0:T(8,128)(2,1)S(1)} %get-tuple-element.47), channel_id=1, source_target_pairs={{0,2},{1,3},{2,0},{3,1},{4,6},{5,7},{6,4},{7,5},{8,10},{9,11},{10,... | collective-permute-start | bytes 393224 | tf_op jit(solution)/shard_map/encode/ppermute | solution.py:18
  34.9 0.0 collective-permute-done.5.arrived_ref
  34.9 2.8 %collective-permute-done.4.arrived_ref = bf16[4,2,64,128]{3,2,1,0:T(8,128)(2,1)S(1)} collective-permute-done((bf16[4,2,64,128]{3,2,1,0:T(8,128)(2,1)S(1)}, bf16[4,2,64,128]{3,2,1,0:T(8,128)(2,1)S(1)}, u32[]{:S(2)}, u32[]{:S(2)}) %collective-permute-start.4) | collective-permute-done | bytes 131104 | tf_op jit(solution)/shard_map/encode/ppermute | solution.py:18
  37.8 2.2 %collective-permute-start.6 = (bf16[4,2,64,128]{3,2,1,0:T(8,128)(2,1)S(1)}, bf16[4,2,64,128]{3,2,1,0:T(8,128)(2,1)S(1)}, u32[]{:S(2)}, u32[]{:S(2)}) collective-permute-start(bf16[4,2,64,128]{3,2,1,0:T(8,128)(2,1)S(1)} %get-tuple-element.53), channel_id=1, source_target_pairs={{0,2},{1,3},{2,0},{3,1},{4,6},{5,7},{6,4},{7,5},{8,10},{9,11},{10,... | collective-permute-start | bytes 393224 | tf_op jit(solution)/shard_map/encode/ppermute | solution.py:18
  40.0 2.1 %collective-permute-start.7 = (bf16[4,2,64,128]{3,2,1,0:T(8,128)(2,1)S(1)}, bf16[4,2,64,128]{3,2,1,0:T(8,128)(2,1)S(1)}, u32[]{:S(2)}, u32[]{:S(2)}) collective-permute-start(bf16[4,2,64,128]{3,2,1,0:T(8,128)(2,1)S(1)} %activate.2.refs_0_), channel_id=1, source_target_pairs={{0,1},{1,0},{2,3},{3,2},{4,5},{5,4},{6,7},{7,6},{8,9},{9,8},{10,11... | collective-permute-start | bytes 393224 | tf_op jit(solution)/shard_map/spread/ppermute | solution.py:18
  42.1 3.1 %collective-permute-start.9 = (bf16[4,2,64,128]{3,2,1,0:T(8,128)(2,1)S(1)}, bf16[4,2,64,128]{3,2,1,0:T(8,128)(2,1)S(1)}, u32[]{:S(2)}, u32[]{:S(2)}) collective-permute-start(bf16[4,2,64,128]{3,2,1,0:T(8,128)(2,1)S(1)} %activate.2.refs_0_), channel_id=1, source_target_pairs={{0,8},{4,12},{8,16},{12,20},{16,24},{20,28},{1,9},{5,13},{9,17},{1... | collective-permute-start | bytes 393224 | tf_op jit(solution)/shard_map/spread/ppermute | solution.py:29
  45.2 0.0 collective-permute-done.6.arrived_ref
  45.3 0.2 collective-permute-start.8
  45.5 0.0 collective-permute-done.7.refs_2_.second_ref
  45.5 2.8 %collective-permute-start.13 = (bf16[8,2,64,128]{3,2,1,0:T(8,128)(2,1)S(1)}, bf16[8,2,64,128]{3,2,1,0:T(8,128)(2,1)S(1)}, u32[]{:S(2)}, u32[]{:S(2)}) collective-permute-start(bf16[8,2,64,128]{3,2,1,0:T(8,128)(2,1)S(1)} %join.1), channel_id=1, source_target_pairs={{0,8},{4,12},{8,16},{12,20},{16,24},{20,28},{1,9},{5,13},{9,17},{1... | collective-permute-start | bytes 786440 | tf_op jit(solution)/shard_map/spread/ppermute | solution.py:29
  48.4 1.9 %collective-permute-done.9.refs_4_ = bf16[4,2,64,128]{3,2,1,0:T(8,128)(2,1)S(1)} collective-permute-done((bf16[4,2,64,128]{3,2,1,0:T(8,128)(2,1)S(1)}, bf16[4,2,64,128]{3,2,1,0:T(8,128)(2,1)S(1)}, u32[]{:S(2)}, u32[]{:S(2)}) %collective-permute-start.9) | collective-permute-done | bytes 131104 | tf_op jit(solution)/shard_map/spread/ppermute | solution.py:29
  50.3 0.3 collective-permute-done.8.refs_3_
  50.6 2.9 %collective-permute-start.12 = (bf16[4,2,64,128]{3,2,1,0:T(8,128)(2,1)S(1)}, bf16[4,2,64,128]{3,2,1,0:T(8,128)(2,1)S(1)}, u32[]{:S(2)}, u32[]{:S(2)}) collective-permute-start(bf16[4,2,64,128]{3,2,1,0:T(8,128)(2,1)S(1)} %collective-permute-done.8.refs_3_), channel_id=1, source_target_pairs={{0,8},{4,12},{8,16},{12,20},{16,24},{20,28},{1,9},{5,13},{9,17},{1... | collective-permute-start | bytes 393224 | tf_op jit(solution)/shard_map/spread/ppermute | solution.py:29
  53.5 0.0 collective-permute-done.10.refs_6_.far_dec
  53.5 0.0 collective-permute-done.11.near_dec
  53.5 0.0 copy-done.1
  53.5 1.9 %decode_early.1 = (f32[256,1024]{1,0:T(8,128)S(1)}, f32[768,1024]{1,0:T(8,128)S(1)}) custom-call(f32[16,1024]{1,0:T(8,128)S(1)} %get-tuple-element.40.ids_ref, bf16[4,2,64,128]{3,2,1,0:T(8,128)(2,1)S(1)} %activate.2.refs_0_, bf16[4,2,64,128]{3,2,1,0:T(8,128)(2,1)S(1)} %activate.3.refs_1_.first_ref, ...), custom_call_target="tpu_custom_call" | custom-call | flops 1342177280 | bytes 6291456 | tf_op jit(solution)/shard_map/decode/decode_early/pallas_call | solution.py:276
  55.4 3.4 %collective-permute-done.12.third.refs_6_ = bf16[4,2,64,128]{3,2,1,0:T(8,128)(2,1)S(1)} collective-permute-done((bf16[4,2,64,128]{3,2,1,0:T(8,128)(2,1)S(1)}, bf16[4,2,64,128]{3,2,1,0:T(8,128)(2,1)S(1)}, u32[]{:S(2)}, u32[]{:S(2)}) %collective-permute-start.12) | collective-permute-done | bytes 131104 | tf_op jit(solution)/shard_map/spread/ppermute | solution.py:29
  58.9 0.0 collective-permute-done.13.second.refs_5_
  58.9 3.8 %collective-permute-start.14 = (bf16[16,2,64,128]{3,2,1,0:T(8,128)(2,1)S(1)}, bf16[16,2,64,128]{3,2,1,0:T(8,128)(2,1)S(1)}, u32[]{:S(2)}, u32[]{:S(2)}) collective-permute-start(bf16[16,2,64,128]{3,2,1,0:T(8,128)(2,1)S(1)} %choose.1), channel_id=1, source_target_pairs={{0,4},{4,0},{8,12},{12,8},{16,20},{20,16},{24,28},{28,24},{1,5},{5... | collective-permute-start | bytes 1572872 | tf_op jit(solution)/shard_map/decode/ppermute | solution.py:34
  62.8 1.0 %decode_middle.1.rest_ref = f32[768,1024]{1,0:T(8,128)S(1)} custom-call(f32[768,1024]{1,0:T(8,128)S(1)} %get-tuple-element.62.rest_ref, bf16[8,2,64,128]{3,2,1,0:T(8,128)(2,1)S(1)} %collective-permute-done.13.second.refs_5_, bf16[4,2,64,128]{3,2,1,0:T(8,128)(2,1)S(1)} %collective-permute-done.12.third.refs_6_, ...), custom_call_target="tpu_custom_call" | custom-call | flops 805306368 | bytes 7340032 | tf_op jit(solution)/shard_map/decode/decode_middle/pallas_call | solution.py:309
  63.8 0.5 collective-permute-done.14.near
  64.3 2.3 %decode_late.1 = bf16[1024,1024]{1,0:T(8,128)(2,1)} custom-call(f32[256,1024]{1,0:T(8,128)S(1)} %get-tuple-element.61.first_ref, f32[768,1024]{1,0:T(8,128)S(1)} %decode_middle.1.rest_ref, bf16[16,2,64,128]{3,2,1,0:T(8,128)(2,1)S(1)} %collective-permute-done.14.near, bf16[528,1024]{1,0:T(8,128)(2,1)S(1)} %collective-permute-done.11.near_dec), custom_call_target="tpu_custom_call" | custom-call | flops 1073741824 | bytes 7340032 | tf_op jit(solution)/shard_map/decode/decode_late/pallas_call | solution.py:354
  (9 shorter events, 0.2 us)
Async XLA Ops:
  0.0 1.2 %copy-start.3 = (bf16[1,4096,128]{2,1,0:T(8,128)(2,1)S(1)}, bf16[1,4096,128]{2,1,0:T(8,128)(2,1)}, u32[]{:S(2)}) copy-start(bf16[1,4096,128]{2,1,0:T(8,128)(2,1)} %param.7) | copy-start | bytes 3145732
  1.2 20.6 %copy-start.6 = (f32[1,128]{1,0:T(1,128)S(1)}, f32[1,128]{1,0:T(1,128)}, u32[]{:S(2)}) copy-start(f32[1,128]{1,0:T(1,128)} %bias_ref.3) | copy-start | bytes 1540
  1.3 13.8 %collective-permute-start = (bf16[1024,128]{1,0:T(8,128)(2,1)S(1)}, bf16[1024,128]{1,0:T(8,128)(2,1)S(1)}, u32[]{:S(2)}, u32[]{:S(2)}) collective-permute-start(bf16[1024,128]{1,0:T(8,128)(2,1)S(1)} %get-tuple-element.42), channel_id=1, source_target_pairs={{0,2},{1,3},{2,0},{3,1},{4,6},{5,7},{6,4},{7,5},{8,10},{9,11},{10,... | collective-permute-start | bytes 786440 | tf_op jit(solution)/shard_map/encoder_rows/ppermute | solution.py:18
  3.7 11.5 %collective-permute-start.1 = (bf16[1024,128]{1,0:T(8,128)(2,1)S(1)}, bf16[1024,128]{1,0:T(8,128)(2,1)S(1)}, u32[]{:S(2)}, u32[]{:S(2)}) collective-permute-start(bf16[1024,128]{1,0:T(8,128)(2,1)S(1)} %get-tuple-element.43), channel_id=1, source_target_pairs={{0,1},{1,0},{2,3},{3,2},{4,5},{5,4},{6,7},{7,6},{8,9},{9,8},{10,11... | collective-permute-start | bytes 786440 | tf_op jit(solution)/shard_map/encoder_rows/ppermute | solution.py:18
  5.0 16.8 %collective-permute-start.2 = (bf16[1024,128]{1,0:T(8,128)(2,1)S(1)}, bf16[1024,128]{1,0:T(8,128)(2,1)S(1)}, u32[]{:S(2)}, u32[]{:S(2)}) collective-permute-start(bf16[1024,128]{1,0:T(8,128)(2,1)S(1)} %get-tuple-element.44), channel_id=1, source_target_pairs={{0,3},{1,2},{2,1},{3,0},{4,7},{5,6},{6,5},{7,4},{8,11},{9,10},{10,... | collective-permute-start | bytes 786440 | tf_op jit(solution)/shard_map/encoder_rows/ppermute | solution.py:18
  5.0 1.9 %copy-start = (bf16[1,3,512,1024]{3,2,1,0:T(8,128)(2,1)S(1)}, bf16[1,3,512,1024]{3,2,1,0:T(8,128)(2,1)}, u32[]{:S(2)}) copy-start(bf16[1,3,512,1024]{3,2,1,0:T(8,128)(2,1)} %param.9) | copy-start | bytes 9437188
  6.9 0.7 %copy-start.4 = (s32[1,16,2]{1,2,0:T(2,128)S(1)}, s32[1,16,2]{1,2,0:T(2,128)}, u32[]{:S(2)}) copy-start(s32[1,16,2]{1,2,0:T(2,128)} %param.10) | copy-start | bytes 388
  7.5 0.7 copy-start.5
  8.2 13.6 %copy-start.2 = (bf16[1,1024,1024]{2,1,0:T(8,128)(2,1)S(1)}, bf16[1,1024,1024]{2,1,0:T(8,128)(2,1)}, u32[]{:S(2)}) copy-start(bf16[1,1024,1024]{2,1,0:T(8,128)(2,1)} %param.6) | copy-start | bytes 6291460
  8.9 44.6 %collective-permute-start.10 = (bf16[528,1024]{1,0:T(8,128)(2,1)S(1)}, bf16[528,1024]{1,0:T(8,128)(2,1)S(1)}, u32[]{:S(2)}, u32[]{:S(2)}) collective-permute-start(bf16[528,1024]{1,0:T(8,128)(2,1)S(1)} %get-tuple-element.56), channel_id=1, source_target_pairs={{0,8},{4,12},{8,16},{12,20},{16,24},{20,28},{1,9},{5,13},{9,17},{1... | collective-permute-start | bytes 3244040 | tf_op jit(solution)/shard_map/decoder_weights/ppermute | solution.py:29
  12.0 41.4 %collective-permute-start.11 = (bf16[528,1024]{1,0:T(8,128)(2,1)S(1)}, bf16[528,1024]{1,0:T(8,128)(2,1)S(1)}, u32[]{:S(2)}, u32[]{:S(2)}) collective-permute-start(bf16[528,1024]{1,0:T(8,128)(2,1)S(1)} %get-tuple-element.57), channel_id=1, source_target_pairs={{0,4},{4,8},{8,12},{12,16},{16,20},{20,24},{24,28},{1,5},{5,9},{9,... | collective-permute-start | bytes 3244040 | tf_op jit(solution)/shard_map/decoder_weights/ppermute | solution.py:29
  22.3 31.2 %copy-start.1 = (bf16[1,3,512,1024]{3,2,1,0:T(8,128)(2,1)S(1)}, bf16[1,3,512,1024]{3,2,1,0:T(8,128)(2,1)}, u32[]{:S(2)}) copy-start(bf16[1,3,512,1024]{3,2,1,0:T(8,128)(2,1)} %param.9) | copy-start | bytes 9437188
  22.3 9.4 %collective-permute-start.3 = (bf16[4,2,64,128]{3,2,1,0:T(8,128)(2,1)S(1)}, bf16[4,2,64,128]{3,2,1,0:T(8,128)(2,1)S(1)}, u32[]{:S(2)}, u32[]{:S(2)}) collective-permute-start(bf16[4,2,64,128]{3,2,1,0:T(8,128)(2,1)S(1)} %encode.3), channel_id=1, source_target_pairs={{0,1},{1,0},{2,3},{3,2},{4,5},{5,4},{6,7},{7,6},{8,9},{9,8},{10,11... | collective-permute-start | bytes 393224 | tf_op jit(solution)/shard_map/encode/ppermute | solution.py:18
  29.3 5.6 %collective-permute-start.5 = (bf16[4,2,64,128]{3,2,1,0:T(8,128)(2,1)S(1)}, bf16[4,2,64,128]{3,2,1,0:T(8,128)(2,1)S(1)}, u32[]{:S(2)}, u32[]{:S(2)}) collective-permute-start(bf16[4,2,64,128]{3,2,1,0:T(8,128)(2,1)S(1)} %get-tuple-element.49), channel_id=1, source_target_pairs={{0,1},{1,0},{2,3},{3,2},{4,5},{5,4},{6,7},{7,6},{8,9},{9,8},{10,11... | collective-permute-start | bytes 393224 | tf_op jit(solution)/shard_map/encode/ppermute | solution.py:18
  31.7 6.0 %collective-permute-start.4 = (bf16[4,2,64,128]{3,2,1,0:T(8,128)(2,1)S(1)}, bf16[4,2,64,128]{3,2,1,0:T(8,128)(2,1)S(1)}, u32[]{:S(2)}, u32[]{:S(2)}) collective-permute-start(bf16[4,2,64,128]{3,2,1,0:T(8,128)(2,1)S(1)} %get-tuple-element.47), channel_id=1, source_target_pairs={{0,2},{1,3},{2,0},{3,1},{4,6},{5,7},{6,4},{7,5},{8,10},{9,11},{10,... | collective-permute-start | bytes 393224 | tf_op jit(solution)/shard_map/encode/ppermute | solution.py:18
  37.8 7.5 %collective-permute-start.6 = (bf16[4,2,64,128]{3,2,1,0:T(8,128)(2,1)S(1)}, bf16[4,2,64,128]{3,2,1,0:T(8,128)(2,1)S(1)}, u32[]{:S(2)}, u32[]{:S(2)}) collective-permute-start(bf16[4,2,64,128]{3,2,1,0:T(8,128)(2,1)S(1)} %get-tuple-element.53), channel_id=1, source_target_pairs={{0,2},{1,3},{2,0},{3,1},{4,6},{5,7},{6,4},{7,5},{8,10},{9,11},{10,... | collective-permute-start | bytes 393224 | tf_op jit(solution)/shard_map/encode/ppermute | solution.py:18
  40.0 5.5 %collective-permute-start.7 = (bf16[4,2,64,128]{3,2,1,0:T(8,128)(2,1)S(1)}, bf16[4,2,64,128]{3,2,1,0:T(8,128)(2,1)S(1)}, u32[]{:S(2)}, u32[]{:S(2)}) collective-permute-start(bf16[4,2,64,128]{3,2,1,0:T(8,128)(2,1)S(1)} %activate.2.refs_0_), channel_id=1, source_target_pairs={{0,1},{1,0},{2,3},{3,2},{4,5},{5,4},{6,7},{7,6},{8,9},{9,8},{10,11... | collective-permute-start | bytes 393224 | tf_op jit(solution)/shard_map/spread/ppermute | solution.py:18
  42.1 8.2 %collective-permute-start.9 = (bf16[4,2,64,128]{3,2,1,0:T(8,128)(2,1)S(1)}, bf16[4,2,64,128]{3,2,1,0:T(8,128)(2,1)S(1)}, u32[]{:S(2)}, u32[]{:S(2)}) collective-permute-start(bf16[4,2,64,128]{3,2,1,0:T(8,128)(2,1)S(1)} %activate.2.refs_0_), channel_id=1, source_target_pairs={{0,8},{4,12},{8,16},{12,20},{16,24},{20,28},{1,9},{5,13},{9,17},{1... | collective-permute-start | bytes 393224 | tf_op jit(solution)/shard_map/spread/ppermute | solution.py:29
  45.3 5.3 %collective-permute-start.8 = (bf16[4,2,64,128]{3,2,1,0:T(8,128)(2,1)S(1)}, bf16[4,2,64,128]{3,2,1,0:T(8,128)(2,1)S(1)}, u32[]{:S(2)}, u32[]{:S(2)}) collective-permute-start(bf16[4,2,64,128]{3,2,1,0:T(8,128)(2,1)S(1)} %activate.3.refs_1_.first_ref), channel_id=1, source_target_pairs={{0,1},{1,0},{2,3},{3,2},{4,5},{5,4},{6,7},{7,6},{8,9},{9,8},{10,11... | collective-permute-start | bytes 393224 | tf_op jit(solution)/shard_map/spread/ppermute | solution.py:18
  45.5 13.4 %collective-permute-start.13 = (bf16[8,2,64,128]{3,2,1,0:T(8,128)(2,1)S(1)}, bf16[8,2,64,128]{3,2,1,0:T(8,128)(2,1)S(1)}, u32[]{:S(2)}, u32[]{:S(2)}) collective-permute-start(bf16[8,2,64,128]{3,2,1,0:T(8,128)(2,1)S(1)} %join.1), channel_id=1, source_target_pairs={{0,8},{4,12},{8,16},{12,20},{16,24},{20,28},{1,9},{5,13},{9,17},{1... | collective-permute-start | bytes 786440 | tf_op jit(solution)/shard_map/spread/ppermute | solution.py:29
  50.6 8.3 %collective-permute-start.12 = (bf16[4,2,64,128]{3,2,1,0:T(8,128)(2,1)S(1)}, bf16[4,2,64,128]{3,2,1,0:T(8,128)(2,1)S(1)}, u32[]{:S(2)}, u32[]{:S(2)}) collective-permute-start(bf16[4,2,64,128]{3,2,1,0:T(8,128)(2,1)S(1)} %collective-permute-done.8.refs_3_), channel_id=1, source_target_pairs={{0,8},{4,12},{8,16},{12,20},{16,24},{20,28},{1,9},{5,13},{9,17},{1... | collective-permute-start | bytes 393224 | tf_op jit(solution)/shard_map/spread/ppermute | solution.py:29
  58.9 5.4 %collective-permute-start.14 = (bf16[16,2,64,128]{3,2,1,0:T(8,128)(2,1)S(1)}, bf16[16,2,64,128]{3,2,1,0:T(8,128)(2,1)S(1)}, u32[]{:S(2)}, u32[]{:S(2)}) collective-permute-start(bf16[16,2,64,128]{3,2,1,0:T(8,128)(2,1)S(1)} %choose.1), channel_id=1, source_target_pairs={{0,4},{4,0},{8,12},{12,8},{16,20},{20,16},{24,28},{28,24},{1,5},{5... | collective-permute-start | bytes 1572872 | tf_op jit(solution)/shard_map/decode/ppermute | solution.py:34
